TPU v7x, 32 devices: a whole 2x2x4 slice. The times are simulated.
32 devices in a mesh: stream: 2 (over x), dp: 16 (over z, y, core).
Axes of the slice: x: 2, y: 2, z: 4, core: 2. Of those that a mesh axis runs over, the one named last changes fastest.
Arguments:
- tokens_in: bfloat16 [32, 1024, 768], P('dp', 'stream'), may hold values from -6 to 6
- char_ids: int32 [32, 4096], P('dp'), may hold values from 0 to 255
- char_lengths: int32 [32, 1024], P('dp'), may hold values from 1 to 8, 4096 in all within a row
- out_grad: bfloat16 [32, 1024, 768], P('dp', 'stream'), may hold values from -6 to 6
- w_qkv: float32 [768, 2304], P(('stream', 'dp')), may hold values from -0.21875 to 0.21875
- first_qkv: float32 [768, 2304], P(('stream', 'dp')), may hold values from -640 to 640
- second_qkv: float32 [768, 2304], P(('stream', 'dp')), may hold values from 5898.24 to 95027.2
- w_out: float32 [768, 768], P(('stream', 'dp')), may hold values from -4 to 4
- first_out: float32 [768, 768], P(('stream', 'dp')), may hold values from -32 to 32
- second_out: float32 [768, 768], P(('stream', 'dp')), may hold values from 12.8 to 208
- w_up: float32 [768, 3072], P(('stream', 'dp')), may hold values from -0.21875 to 0.21875
- first_up: float32 [768, 3072], P(('stream', 'dp')), may hold values from -224 to 224
- second_up: float32 [768, 3072], P(('stream', 'dp')), may hold values from 655.36 to 10485.76
- w_down: float32 [3072, 768], P(('stream', 'dp')), may hold values from -0.109375 to 0.109375
- first_down: float32 [3072, 768], P(('stream', 'dp')), may hold values from -448 to 448
- second_down: float32 [3072, 768], P(('stream', 'dp')), may hold values from 2621.44 to 41943.04
- w_gru: float32 [768, 1536], P(('stream', 'dp')), may hold values from -0.21875 to 0.21875
- first_gru: float32 [768, 1536], P(('stream', 'dp')), may hold values from -112 to 112
- second_gru: float32 [768, 1536], P(('stream', 'dp')), may hold values from 163.84 to 2621.44
- w_blend: float32 [4608, 768], P(('stream', 'dp')), may hold values from -0.09375 to 0.09375
- first_blend: float32 [4608, 768], P(('stream', 'dp')), may hold values from -384 to 384
- second_blend: float32 [4608, 768], P(('stream', 'dp')), may hold values from 1966.08 to 32112.64
- char_table: float32 [256, 768], P(('stream', 'dp')), may hold values from -5 to 5
- first_table: float32 [256, 768], P(('stream', 'dp')), may hold values from -10 to 10
- second_table: float32 [256, 768], P(('stream', 'dp')), may hold values from 1.28 to 20.48
- gains: float32 [3, 768], P(None, ('stream', 'dp')), may hold values from 0.5 to 1.5
- first_gains: float32 [3, 768], P(None, ('stream', 'dp')), may hold values from -896 to 896
- second_gains: float32 [3, 768], P(None, ('stream', 'dp')), may hold values from 10485.76 to 167116.8
Outputs:
- block_out: bfloat16 [32, 1024, 768], P('dp', 'stream')
- tokens_grad: bfloat16 [32, 1024, 768], P('dp', 'stream')
- fresh_qkv: float32 [768, 2304], P(('stream', 'dp'))
- mean_qkv: float32 [768, 2304], P(('stream', 'dp'))
- power_qkv: float32 [768, 2304], P(('stream', 'dp'))
- fresh_out: float32 [768, 768], P(('stream', 'dp'))
- mean_out: float32 [768, 768], P(('stream', 'dp'))
- power_out: float32 [768, 768], P(('stream', 'dp'))
- fresh_up: float32 [768, 3072], P(('stream', 'dp'))
- mean_up: float32 [768, 3072], P(('stream', 'dp'))
- power_up: float32 [768, 3072], P(('stream', 'dp'))
- fresh_down: float32 [3072, 768], P(('stream', 'dp'))
- mean_down: float32 [3072, 768], P(('stream', 'dp'))
- power_down: float32 [3072, 768], P(('stream', 'dp'))
- fresh_gru: float32 [768, 1536], P(('stream', 'dp'))
- mean_gru: float32 [768, 1536], P(('stream', 'dp'))
- power_gru: float32 [768, 1536], P(('stream', 'dp'))
- fresh_blend: float32 [4608, 768], P(('stream', 'dp'))
- mean_blend: float32 [4608, 768], P(('stream', 'dp'))
- power_blend: float32 [4608, 768], P(('stream', 'dp'))
- fresh_table: float32 [256, 768], P(('stream', 'dp'))
- mean_table: float32 [256, 768], P(('stream', 'dp'))
- power_table: float32 [256, 768], P(('stream', 'dp'))
- fresh_gains: float32 [3, 768], P(None, ('stream', 'dp'))
- mean_gains: float32 [3, 768], P(None, ('stream', 'dp'))
- power_gains: float32 [3, 768], P(None, ('stream', 'dp'))
Inputs may be any that keep to these rules, and one draw needn't show every extreme that they name: `char_lengths`: the 1024 lengths of a sequence sum to 4096, and one of them is 8.
All inputs are finite; a program needn't handle non-finite values.
Results may differ from a plain program's by a relative error of at most 0.017.
The roundings to bfloat16 on the way count: a program that leaves them out, or rounds other values in their place, can miss the bound.
Values may be sent and summed in bfloat16 or wider, within the bound.
No kernel may reach another device: no remote copies, remote signals or barrier semaphores. Data moves between devices by JAX's collectives and lax.ppermute only.
A program may use at most 320 MiB of HBM per device.

v0:
```python
import jax
import jax.numpy as jnp
from jax import lax
from jax.sharding import PartitionSpec as P

D = 768
HEADS = 12
FF = 3072
LEN = 1024
STEP = 5


def partner(block, axis, apart):
    count = lax.axis_size(axis)
    route = []
    for low in range(count):
        high = low | 1 << apart
        if high != low and high < count:
            route += [(low, high), (high, low)]
    return lax.ppermute(block, axis, route)


def product(former, latter):
    return jnp.dot(former, latter, preferred_element_type=jnp.float32)


def inner_rows(former, latter):
    return lax.dot_general(
        former, latter, (((0,), (0,)), ((), ())), preferred_element_type=jnp.float32
    )


def inner_cols(former, latter):
    return lax.dot_general(
        former, latter, (((1,), (1,)), ((), ())), preferred_element_type=jnp.float32
    )


def norm_gain(values, scales):
    center = jnp.mean(values, axis=-1, keepdims=True)
    shifted = values - center
    spread = jnp.mean(shifted * shifted, axis=-1, keepdims=True)
    return shifted * lax.rsqrt(spread + 1e-05) * scales


def combine(earlier, latter):
    return (earlier[0] * latter[0], latter[0] * earlier[1] + latter[1])


def linear_chain(factor, inject):
    return lax.associative_scan(combine, (factor, inject), axis=0)[1]


def chain_states(logits, candidate):
    update = jax.nn.sigmoid(logits)
    return linear_chain(1.0 - update, update * candidate)


def chain_grads(logits, candidate, states, upstream):
    update = jax.nn.sigmoid(logits)
    keep_next = jnp.concatenate([1.0 - update[1:], jnp.zeros_like(update[:1])], 0)
    carried = jnp.flip(linear_chain(jnp.flip(keep_next, 0), jnp.flip(upstream, 0)), 0)
    before = jnp.concatenate([jnp.zeros_like(states[:1]), states[:-1]], 0)
    return (carried * (candidate - before) * update * (1.0 - update), carried * update)


def rows_before(matrix):
    return jnp.concatenate([jnp.zeros_like(matrix[:1]), matrix[:-1]], 0)


def rows_after(matrix):
    return jnp.concatenate([matrix[1:], jnp.zeros_like(matrix[:1])], 0)


def char_segments(lengths, char_count):
    starts = jnp.cumsum(lengths) - lengths
    markers = jnp.zeros((char_count,), jnp.int32).at[starts].add(1)
    return jnp.cumsum(markers) - 1


def step_rates():
    return (
        0.5 * D ** (-0.5),
        0.5 * (3 * D // LEN) ** (-0.5),
        0.5 * D ** (-0.5),
        0.5 * FF ** (-0.5),
        0.5 * D ** (-0.5),
        0.5 * (6 * D) ** (-0.5),
        0.5,
        0.2,
    )


def adamw(master, first_m, second_m, grad_sum, step_rate):
    mean_new = 0.5 * first_m + 0.5 * grad_sum
    power = 0.5 * second_m + 0.5 * grad_sum * grad_sum
    correct = 1.0 - 0.5**STEP
    fresh_w = master - step_rate * (
        mean_new / correct / (jnp.sqrt(power / correct) + 1e-08) + 0.01 * master
    )
    return (fresh_w, mean_new, power)


def split_heads(qkv):
    length = qkv.shape[0]
    model_width = qkv.shape[1] // 3
    head_size = model_width // HEADS
    block_rows = min(512, length)
    block_count = length // block_rows
    queries = qkv[:, :model_width].reshape(block_count, block_rows, HEADS, head_size)
    key_rows = qkv[:, model_width : 2 * model_width].reshape(length, HEADS, head_size)
    value_rows = qkv[:, 2 * model_width :].reshape(length, HEADS, head_size)
    return (queries, key_rows, value_rows, head_size ** (-0.5))


def attention(qkv):
    length = qkv.shape[0]
    model_width = qkv.shape[1] // 3
    queries, key_rows, value_rows, scale = split_heads(qkv)
    block_rows = queries.shape[1]

    def one_block(row_block):
        scores = (
            jnp.einsum("qhd,khd->hqk", row_block, key_rows, preferred_element_type=jnp.float32)
            * scale
        )
        row_max = jnp.max(scores, axis=-1, keepdims=True)
        exponent = jnp.exp(scores - row_max)
        row_total = jnp.sum(exponent, axis=-1, keepdims=True)
        attn_probs = (exponent / row_total).astype(jnp.bfloat16)
        context = jnp.einsum(
            "hqk,khd->qhd", attn_probs, value_rows, preferred_element_type=jnp.float32
        )
        return (
            context.reshape(block_rows, model_width).astype(jnp.bfloat16),
            (row_max + jnp.log(row_total))[..., 0],
        )

    context, logsum = lax.map(one_block, queries)
    return (context.reshape(length, model_width), logsum)


def attention_grad(qkv, logsum, context_grad):
    length = qkv.shape[0]
    model_width = qkv.shape[1] // 3
    queries, key_rows, value_rows, scale = split_heads(qkv)
    block_rows = queries.shape[1]
    grad_blocks = context_grad.reshape(queries.shape)

    def one_block(running, pieces):
        row_block, grad_rows, row_logsum = pieces
        key_grad, value_grad = running
        scores = (
            jnp.einsum("qhd,khd->hqk", row_block, key_rows, preferred_element_type=jnp.float32)
            * scale
        )
        attn_probs = jnp.exp(scores - row_logsum[..., None])
        value_grad = value_grad + jnp.einsum(
            "hqk,qhd->khd",
            attn_probs.astype(jnp.bfloat16),
            grad_rows,
            preferred_element_type=jnp.float32,
        )
        prob_grad = jnp.einsum(
            "qhd,khd->hqk", grad_rows, value_rows, preferred_element_type=jnp.float32
        )
        score_grad = (
            attn_probs * (prob_grad - jnp.sum(prob_grad * attn_probs, axis=-1, keepdims=True))
        ).astype(jnp.bfloat16)
        query_grad = (
            jnp.einsum("hqk,khd->qhd", score_grad, key_rows, preferred_element_type=jnp.float32)
            * scale
        )
        key_grad = (
            key_grad
            + jnp.einsum("hqk,qhd->khd", score_grad, row_block, preferred_element_type=jnp.float32)
            * scale
        )
        return ((key_grad, value_grad), query_grad.reshape(block_rows, model_width))

    zero_rows = jnp.zeros(key_rows.shape, jnp.float32)
    sums, query_grad = lax.scan(one_block, (zero_rows, zero_rows), (queries, grad_blocks, logsum))
    return jnp.concatenate(
        [
            query_grad.reshape(length, model_width),
            sums[0].reshape(length, model_width),
            sums[1].reshape(length, model_width),
        ],
        1,
    ).astype(jnp.bfloat16)


def token_forward(tokens, weights):
    qkv = product(tokens, weights[0]).astype(jnp.bfloat16)
    context, logsum = attention(qkv)
    mixed_sum = tokens.astype(jnp.float32) + product(context, weights[1])
    normed = norm_gain(mixed_sum, weights[7][0].astype(jnp.float32))
    hidden = product(normed.astype(jnp.bfloat16), weights[2])
    summed = normed + product(jax.nn.gelu(hidden).astype(jnp.bfloat16), weights[3])
    feature = norm_gain(summed, weights[7][1].astype(jnp.float32)).astype(jnp.bfloat16)
    return (feature, (qkv, logsum, context, mixed_sum, normed, hidden, summed))


def token_backward(tokens, stored, feature_grad, weights):
    qkv, logsum, context, mixed_sum, normed, kept_hidden, summed = stored
    summed_grad, gain_ffn = jax.vjp(norm_gain, summed, weights[7][1].astype(jnp.float32))[1](
        feature_grad.astype(jnp.float32)
    )
    ffn_grad = summed_grad.astype(jnp.bfloat16)
    active = jax.nn.gelu(kept_hidden).astype(jnp.bfloat16)
    grad_down = inner_rows(active, ffn_grad)
    hidden_grad = jax.vjp(jax.nn.gelu, kept_hidden)[1](inner_cols(ffn_grad, weights[3]))[0].astype(
        jnp.bfloat16
    )
    grad_up = inner_rows(normed.astype(jnp.bfloat16), hidden_grad)
    normed_grad = summed_grad + inner_cols(hidden_grad, weights[2])
    mixed_grad, gain_attn = jax.vjp(norm_gain, mixed_sum, weights[7][0].astype(jnp.float32))[1](
        normed_grad
    )
    attended_grad = mixed_grad.astype(jnp.bfloat16)
    grad_out = inner_rows(context, attended_grad)
    context_grad = inner_cols(attended_grad, weights[1]).astype(jnp.bfloat16)
    qkv_grad = attention_grad(qkv, logsum, context_grad)
    grad_qkv = inner_rows(tokens, qkv_grad)
    tokens_grad = (mixed_grad + inner_cols(qkv_grad, weights[0])).astype(jnp.bfloat16)
    return (tokens_grad, (grad_qkv, grad_out, grad_up, grad_down, gain_attn, gain_ffn))


def char_section(feature, out_rows, ids_row, lengths_row, weights):
    w_gru, w_blend, table_copy = (weights[4], weights[5], weights[6])
    embedded = table_copy[ids_row]
    gate_logits = product(embedded, w_gru)
    hidden_width = gate_logits.shape[1] // 4
    forward_states = chain_states(
        gate_logits[:, :hidden_width], gate_logits[:, hidden_width : 2 * hidden_width]
    )
    reversed_logits = jnp.flip(gate_logits[:, 2 * hidden_width :], 0)
    reversed_states = chain_states(
        reversed_logits[:, :hidden_width], reversed_logits[:, hidden_width:]
    )
    states = jnp.concatenate([forward_states, jnp.flip(reversed_states, 0)], 1)
    length = lengths_row.shape[0]
    segment = char_segments(lengths_row, ids_row.shape[0])
    span_len = lengths_row.astype(jnp.float32)[:, None]
    pooled = (
        jax.ops.segment_sum(states, segment, num_segments=length, indices_are_sorted=True)
        / span_len
    ).astype(jnp.bfloat16)
    joined = jnp.concatenate([feature, pooled], 1)
    stacked = jnp.concatenate([rows_before(joined), joined, rows_after(joined)], 1)
    blend_in = product(stacked, w_blend)
    blended, gelu_pull = jax.vjp(jax.nn.gelu, blend_in)
    result, norm_pull = jax.vjp(
        norm_gain, feature.astype(jnp.float32) + blended, weights[7][2].astype(jnp.float32)
    )
    total_grad, gain_blend = norm_pull(out_rows.astype(jnp.float32))
    blend_grad = gelu_pull(total_grad)[0].astype(jnp.bfloat16)
    grad_blend = inner_rows(stacked, blend_grad)
    stacked_grad = inner_cols(blend_grad, w_blend)
    pair_width = joined.shape[1]
    model_width = pair_width // 2
    joined_grad = (
        stacked_grad[:, pair_width : 2 * pair_width]
        + rows_after(stacked_grad[:, :pair_width])
        + rows_before(stacked_grad[:, 2 * pair_width :])
    )
    feature_grad = (total_grad + joined_grad[:, :model_width]).astype(jnp.bfloat16)
    state_grad = (joined_grad[:, model_width:] / span_len)[segment]
    forward_gate, forward_cand = chain_grads(
        gate_logits[:, :hidden_width],
        gate_logits[:, hidden_width : 2 * hidden_width],
        forward_states,
        state_grad[:, :hidden_width],
    )
    reversed_gate, reversed_cand = chain_grads(
        reversed_logits[:, :hidden_width],
        reversed_logits[:, hidden_width:],
        reversed_states,
        jnp.flip(state_grad[:, hidden_width:], 0),
    )
    gate_grad = jnp.concatenate(
        [forward_gate, forward_cand, jnp.flip(reversed_gate, 0), jnp.flip(reversed_cand, 0)], 1
    ).astype(jnp.bfloat16)
    grad_gru = inner_rows(embedded, gate_grad)
    grad_table = jax.ops.segment_sum(
        inner_cols(gate_grad, w_gru), ids_row, num_segments=table_copy.shape[0]
    )
    return (
        result.astype(jnp.bfloat16),
        feature_grad,
        (grad_gru, grad_blend, grad_table, gain_blend),
    )


def on_device(
    tokens_in,
    char_ids,
    char_lengths,
    out_grad,
    w_qkv,
    first_qkv,
    second_qkv,
    w_out,
    first_out,
    second_out,
    w_up,
    first_up,
    second_up,
    w_down,
    first_down,
    second_down,
    w_gru,
    first_gru,
    second_gru,
    w_blend,
    first_blend,
    second_blend,
    char_table,
    first_table,
    second_table,
    gains,
    first_gains,
    second_gains,
):
    masters = (w_qkv, w_out, w_up, w_down, w_gru, w_blend, char_table, gains)
    firsts = (
        first_qkv,
        first_out,
        first_up,
        first_down,
        first_gru,
        first_blend,
        first_table,
        first_gains,
    )
    seconds = (
        second_qkv,
        second_out,
        second_up,
        second_down,
        second_gru,
        second_blend,
        second_table,
        second_gains,
    )
    on_first = lax.axis_index("stream") == 0
    half_len = tokens_in.shape[1]
    current = (
        lax.all_gather(w_qkv.astype(jnp.bfloat16), ("stream", "dp"), axis=0, tiled=True),
        lax.all_gather(w_out.astype(jnp.bfloat16), ("stream", "dp"), axis=0, tiled=True),
        lax.all_gather(w_up.astype(jnp.bfloat16), ("stream", "dp"), axis=0, tiled=True),
        lax.all_gather(w_down.astype(jnp.bfloat16), ("stream", "dp"), axis=0, tiled=True),
        lax.all_gather(w_gru.astype(jnp.bfloat16), ("stream", "dp"), axis=0, tiled=True),
        lax.all_gather(w_blend.astype(jnp.bfloat16), ("stream", "dp"), axis=0, tiled=True),
        lax.all_gather(char_table.astype(jnp.bfloat16), ("stream", "dp"), axis=0, tiled=True),
        lax.all_gather(gains.astype(jnp.bfloat16), ("stream", "dp"), axis=1, tiled=True),
    )
    block_parts = []
    grad_parts = []
    other_tokens = jnp.where(on_first, tokens_in[1], tokens_in[0])
    other_grad = jnp.where(on_first, out_grad[1], out_grad[0])
    keep_tokens = jnp.where(on_first, tokens_in[0], tokens_in[1])
    keep_grad = jnp.where(on_first, out_grad[0], out_grad[1])
    got_tokens, got_grad = partner((other_tokens, other_grad), "stream", 0)
    whole_tokens = jnp.where(
        on_first,
        jnp.concatenate([keep_tokens, got_tokens], 0),
        jnp.concatenate([got_tokens, keep_tokens], 0),
    )
    whole_grad = jnp.where(
        on_first,
        jnp.concatenate([keep_grad, got_grad], 0),
        jnp.concatenate([got_grad, keep_grad], 0),
    )
    ids_row = jnp.where(on_first, char_ids[0], char_ids[1])
    lengths_row = jnp.where(on_first, char_lengths[0], char_lengths[1])
    feature, stored = token_forward(whole_tokens, current)
    result, feature_grad, char_grads = char_section(
        feature, whole_grad, ids_row, lengths_row, current
    )
    tokens_grad, token_grads = token_backward(whole_tokens, stored, feature_grad, current)
    send_result = jnp.where(on_first, result[half_len:], result[:half_len])
    send_grad = jnp.where(on_first, tokens_grad[half_len:], tokens_grad[:half_len])
    back_result, back_grad = partner((send_result, send_grad), "stream", 0)
    block_parts.append(jnp.where(on_first, result[:half_len], back_result))
    block_parts.append(jnp.where(on_first, back_result, result[half_len:]))
    grad_parts.append(jnp.where(on_first, tokens_grad[:half_len], back_grad))
    grad_parts.append(jnp.where(on_first, back_grad, tokens_grad[half_len:]))
    gain_grads = jnp.stack([token_grads[4], token_grads[5], char_grads[3]])
    shares = (
        lax.psum_scatter(token_grads[0], ("stream", "dp"), scatter_dimension=0, tiled=True),
        lax.psum_scatter(token_grads[1], ("stream", "dp"), scatter_dimension=0, tiled=True),
        lax.psum_scatter(token_grads[2], ("stream", "dp"), scatter_dimension=0, tiled=True),
        lax.psum_scatter(token_grads[3], ("stream", "dp"), scatter_dimension=0, tiled=True),
        lax.psum_scatter(char_grads[0], ("stream", "dp"), scatter_dimension=0, tiled=True),
        lax.psum_scatter(char_grads[1], ("stream", "dp"), scatter_dimension=0, tiled=True),
        lax.psum_scatter(char_grads[2], ("stream", "dp"), scatter_dimension=0, tiled=True),
        lax.psum_scatter(gain_grads, ("stream", "dp"), scatter_dimension=1, tiled=True),
    )
    rates = step_rates()
    results = [
        adamw(masters[number], firsts[number], seconds[number], shares[number], rates[number])
        for number in range(8)
    ]
    return (
        jnp.stack(block_parts),
        jnp.stack(grad_parts),
        results[0][0],
        results[0][1],
        results[0][2],
        results[1][0],
        results[1][1],
        results[1][2],
        results[2][0],
        results[2][1],
        results[2][2],
        results[3][0],
        results[3][1],
        results[3][2],
        results[4][0],
        results[4][1],
        results[4][2],
        results[5][0],
        results[5][1],
        results[5][2],
        results[6][0],
        results[6][1],
        results[6][2],
        results[7][0],
        results[7][1],
        results[7][2],
    )


def solution(mesh):
    in_specs = (
        P("dp", "stream", None),
        P("dp", None),
        P("dp", None),
        P("dp", "stream", None),
        P(("stream", "dp"), None),
        P(("stream", "dp"), None),
        P(("stream", "dp"), None),
        P(("stream", "dp"), None),
        P(("stream", "dp"), None),
        P(("stream", "dp"), None),
        P(("stream", "dp"), None),
        P(("stream", "dp"), None),
        P(("stream", "dp"), None),
        P(("stream", "dp"), None),
        P(("stream", "dp"), None),
        P(("stream", "dp"), None),
        P(("stream", "dp"), None),
        P(("stream", "dp"), None),
        P(("stream", "dp"), None),
        P(("stream", "dp"), None),
        P(("stream", "dp"), None),
        P(("stream", "dp"), None),
        P(("stream", "dp"), None),
        P(("stream", "dp"), None),
        P(("stream", "dp"), None),
        P(None, ("stream", "dp")),
        P(None, ("stream", "dp")),
        P(None, ("stream", "dp")),
    )
    out_specs = (
        P("dp", "stream", None),
        P("dp", "stream", None),
        P(("stream", "dp"), None),
        P(("stream", "dp"), None),
        P(("stream", "dp"), None),
        P(("stream", "dp"), None),
        P(("stream", "dp"), None),
        P(("stream", "dp"), None),
        P(("stream", "dp"), None),
        P(("stream", "dp"), None),
        P(("stream", "dp"), None),
        P(("stream", "dp"), None),
        P(("stream", "dp"), None),
        P(("stream", "dp"), None),
        P(("stream", "dp"), None),
        P(("stream", "dp"), None),
        P(("stream", "dp"), None),
        P(("stream", "dp"), None),
        P(("stream", "dp"), None),
        P(("stream", "dp"), None),
        P(("stream", "dp"), None),
        P(("stream", "dp"), None),
        P(("stream", "dp"), None),
        P(None, ("stream", "dp")),
        P(None, ("stream", "dp")),
        P(None, ("stream", "dp")),
    )
    return jax.shard_map(
        on_device, mesh=mesh, in_specs=in_specs, out_specs=out_specs, check_vma=False
    )
```

profile of v0, /device:TPU:0, one launch (start us, length us, event | category | flops | bytes accessed | tf_op | source)
XLA Modules:
  0.0 3034.4 jit_solution(9658484704899617812)
XLA Ops:
  34.9 41.7 %all-gather = bf16[32,24,3]{1,2,0:T(4,128)(2,1)S(1)} all-gather(bf16[1,24,3]{1,2,0:T(4,128)(2,1)S(1)} %convert_bitcast_fusion), channel_id=1, replica_groups=mesh['stream'=2,'dp'=16] {'stream','dp'}, dimensions={0}, use_global_device_ids=true | all-gather | bytes 4752 | tf_op jit(solution)/shard_map/all_gather | solution.py:356
  77.9 38.1 %all_gather.29 = bf16[256,768]{1,0:T(8,128)(2,1)S(1)} all-gather(bf16[8,768]{1,0:T(8,128)(2,1)S(1)} %convert_element_type.133), channel_id=1, replica_groups=mesh['stream'=2,'dp'=16] {'stream','dp'}, dimensions={0}, use_global_device_ids=true | all-gather | bytes 405504 | tf_op jit(solution)/shard_map/all_gather | solution.py:355
  151.4 18.7 fusion.50
  348.8 48.5 %slice.1406 = f32[4096,384]{1,0:T(8,128)} reverse(f32[4096,384]{1,0:T(8,128)} %get-tuple-element.392), dimensions={0} | reverse | bytes 12582912 | tf_op jit(solution)/shard_map/slice | solution.py:239
  397.3 48.4 %slice.1404 = f32[4096,384]{1,0:T(8,128)} reverse(f32[4096,384]{1,0:T(8,128)} %get-tuple-element.393), dimensions={0} | reverse | bytes 12582912 | tf_op jit(solution)/shard_map/slice | solution.py:239
  676.2 19.1 pad.322
  749.5 18.7 pad.347
  919.1 25.6 slice.1515
  960.2 24.6 slice.1623
  984.8 25.6 slice.1615
  1026.0 48.4 %rev.23 = f32[4096,384]{1,0:T(8,128)} reverse(f32[4096,384]{1,0:T(8,128)} %add.1017), dimensions={0} | reverse | bytes 12582912 | tf_op jit(solution)/shard_map/jit(_flip)/rev | solution.py:241
  1074.3 30.1 scatter_custom_fusion.1
  1127.8 76.0 %while.27 = (s32[]{:T(128)}, bf16[2,512,768]{2,1,0:T(8,128)(2,1)}, f32[2,12,512]{2,1,0:T(8,128)}, bf16[2,512,12,64]{1,3,2,0:T(8,128)(2,1)S(1)}, bf16[1024,12,64]...) while((s32[]{:T(128)}, bf16[2,512,768]{2,1,0:T(8,128)(2,1)}, f32[2,12,512]{2,1,0:T(8,128)}, ...), condition=%wide.region_3.4_spmd, body=%wide.region_0.3_spmd.sunk | while | flops 1667622912 | bytes 89858160 | solution.py:139
  1380.3 24.7 slice.1520
  1681.8 25.8 slice.1610
  1736.8 18.7 pad.371
  1836.0 18.6 pad.370
  1862.4 48.5 %rev.24 = f32[4096,384]{1,0:T(8,128)} reverse(f32[4096,384]{1,0:T(8,128)} %add.1084), dimensions={0} | reverse | bytes 12582912 | tf_op jit(solution)/shard_map/jit(_flip)/rev | solution.py:62
  1921.6 18.6 pad.394
  1948.0 48.3 %rev.25 = f32[4096,384]{1,0:T(8,128)} reverse(f32[4096,384]{1,0:T(8,128)} %add.1119), dimensions={0} | reverse | bytes 12582912 | tf_op jit(solution)/shard_map/jit(_flip)/rev | solution.py:62
  2008.0 45.2 %rev.26 = bf16[4096,384]{1,0:T(8,128)(2,1)} reverse(bf16[4096,384]{1,0:T(8,128)(2,1)} %get-tuple-element.401), dimensions={0} | reverse | bytes 6291456 | tf_op jit(solution)/shard_map/jit(_flip)/rev | solution.py:282
  2053.2 30.4 %rev.27 = bf16[4096,384]{1,0:T(8,128)(2,1)} reverse(bf16[4096,384]{1,0:T(8,128)(2,1)S(1)} %get-tuple-element.402), dimensions={0} | reverse | bytes 6291456 | tf_op jit(solution)/shard_map/jit(_flip)/rev | solution.py:282
  2112.9 28.6 scatter_custom_fusion.2
  2174.8 171.0 %while.28 = (s32[]{:T(128)}, f32[1024,12,64]{0,2,1:T(8,128)}, f32[1024,12,64]{0,2,1:T(8,128)}, bf16[2,512,768]{2,1,0:T(8,128)(2,1)}, bf16[2,512,12,64]{1,3,2,0:T...) while((s32[]{:T(128)}, f32[1024,12,64]{0,2,1:T(8,128)}, ...), condition=%wide.region_24.25_spmd.clone, body=%wide.region_22.24_spmd.clone.sunk | while | flops 4106741760 | bytes 219594928 | solution.py:182
  2214.9 21.7 multiply_convert_fusion.12
  2300.5 21.8 multiply_convert_fusion.12
  2394.1 19.4 fusion.151
  2427.5 60.8 %all-reduce.104 = f32[3,768]{1,0:T(4,128)S(1)} all-reduce(f32[3,768]{1,0:T(4,128)S(1)} %pad_maximum_fusion.46), channel_id=9, replica_groups=mesh['stream'=2,'dp'=16] {'stream','dp'}, use_global_device_ids=true, to_apply=%region_36.37.clone | all-reduce | flops 2304 | bytes 18432
  2500.3 73.8 %reduce-scatter.9.cloned.1.call-done = f32[24,2304]{1,0:T(8,128)} async-done(((f32[768,2304]{1,0:T(8,128)}), f32[24,2304]{1,0:T(8,128)}) %reduce-scatter.9.cloned.1.call-update) | async-done | bytes 221200 | tf_op jit(solution)/shard_map/reduce_scatter | solution.py:391
  2576.1 139.8 %reduce-scatter.15.cloned.1.call-done = f32[96,768]{1,0:T(8,128)} async-done(((f32[3072,768]{1,0:T(8,128)}), f32[96,768]{1,0:T(8,128)}) %reduce-scatter.15.cloned.1.call-update) | async-done | bytes 294928 | tf_op jit(solution)/shard_map/reduce_scatter | solution.py:394
  2717.9 138.5 %reduce-scatter.13.cloned.1.call-done = f32[24,3072]{1,0:T(8,128)} async-done(((f32[768,3072]{1,0:T(8,128)}), f32[24,3072]{1,0:T(8,128)}) %reduce-scatter.13.cloned.1.call-update) | async-done | bytes 294928 | tf_op jit(solution)/shard_map/reduce_scatter | solution.py:393
  2858.5 166.8 %reduce-scatter.19.cloned.1.call-done = f32[144,768]{1,0:T(8,128)} async-done(((f32[4608,768]{1,0:T(8,128)}), f32[144,768]{1,0:T(8,128)}) %reduce-scatter.19.cloned.1.call-update) | async-done | bytes 442384 | tf_op jit(solution)/shard_map/reduce_scatter | solution.py:396
  (1222 shorter events, 1678.0 us)
Async XLA Ops:
  7.2 126.7 %all-gather.16.cloned.1.call-start = ((), (), s32[]{:S(2)}) async-start(), calls=%async_computation.11 | async-start | bytes 2433024 | tf_op jit(solution)/shard_map/all_gather | solution.py:353
  8.9 1099.9 %all-gather.8.cloned.1.call-start = ((), (), s32[]{:S(2)}) async-start(), calls=%async_computation.7 | async-start | bytes 3649536 | tf_op jit(solution)/shard_map/all_gather | solution.py:349
  10.6 1193.2 %all-gather.10.cloned.1.call-start = ((), (), s32[]{:S(2)}) async-start(), calls=%async_computation.8 | async-start | bytes 1216512 | tf_op jit(solution)/shard_map/all_gather | solution.py:350
  12.2 1199.7 %all-gather.12.cloned.1.call-start = ((), (), s32[]{:S(2)}) async-start(), calls=%async_computation.9 | async-start | bytes 4866048 | tf_op jit(solution)/shard_map/all_gather | solution.py:351
  13.9 1209.0 %all-gather.14.cloned.1.call-start = ((), (), s32[]{:S(2)}) async-start(), calls=%async_computation.10 | async-start | bytes 4866048 | tf_op jit(solution)/shard_map/all_gather | solution.py:352
  15.6 1226.7 %all-gather.18.cloned.1.call-start = ((), (), s32[]{:S(2)}) async-start(), calls=%async_computation.12 | async-start | bytes 7299072 | tf_op jit(solution)/shard_map/all_gather | solution.py:354
  17.6 1091.2 %collective-permute-start = (bf16[512,768]{0,1:T(8,128)(2,1)}, bf16[512,768]{0,1:T(8,128)(2,1)}, u32[]{:S(2)}, u32[]{:S(2)}) collective-permute-start(bf16[512,768]{0,1:T(8,128)(2,1)} %get-tuple-element.432), channel_id=1, source_target_pairs={{0,16},{16,0},{1,17},{17,1},{2,18},{18,2},{3,19},{19,3},{4,20},{20... | collective-permute-start | bytes 2359304 | tf_op jit(solution)/shard_map/ppermute | solution.py:20
  22.7 1237.6 %collective-permute-start.2 = (bf16[512,768]{0,1:T(8,128)(2,1)}, bf16[512,768]{0,1:T(8,128)(2,1)}, u32[]{:S(2)}, u32[]{:S(2)}) collective-permute-start(bf16[512,768]{0,1:T(8,128)(2,1)} %get-tuple-element.427), channel_id=1, source_target_pairs={{0,16},{16,0},{1,17},{17,1},{2,18},{18,2},{3,19},{19,3},{4,20},{20... | collective-permute-start | bytes 2359304 | tf_op jit(solution)/shard_map/ppermute | solution.py:20
  24.1 2471.0 %reduce-scatter.21.cloned.1.call-start = ((), (), s32[]{:S(2)}) async-start(), calls=%async_computation.19 | async-start | bytes 811008 | tf_op jit(solution)/shard_map/reduce_scatter | solution.py:397
  1234.1 67.4 %copy-start.7 = (f32[1024,768]{0,1:T(8,128)}, f32[1024,768]{0,1:T(8,128)S(1)}, u32[]{:S(2)}) copy-start(f32[1024,768]{0,1:T(8,128)S(1)} %get-tuple-element.522) | copy-start | bytes 9437188
  1234.1 435.7 %copy-start.115 = (f32[1024]{0:T(1024)}, f32[1024]{0:T(1024)S(1)}, u32[]{:S(2)}) copy-start(f32[1024]{0:T(1024)S(1)} %broadcast_multiply_fusion.1) | copy-start | bytes 12292
  2141.5 355.1 %reduce-scatter.11.cloned.1.call-start = ((), (), s32[]{:S(2)}) async-start(), calls=%async_computation.14 | async-start | bytes 2433024 | tf_op jit(solution)/shard_map/reduce_scatter | solution.py:392
  2149.0 349.2 %reduce-scatter.17.cloned.1.call-start = ((), (), s32[]{:S(2)}) async-start(), calls=%async_computation.17 | async-start | bytes 4866048 | tf_op jit(solution)/shard_map/reduce_scatter | solution.py:395
  2172.9 401.2 %reduce-scatter.9.cloned.1.call-start = ((), (), s32[]{:S(2)}) async-start(), calls=%async_computation.13 | async-start | bytes 7299072 | tf_op jit(solution)/shard_map/reduce_scatter | solution.py:391
  2362.8 353.1 %reduce-scatter.15.cloned.1.call-start = ((), (), s32[]{:S(2)}) async-start(), calls=%async_computation.16 | async-start | bytes 9732096 | tf_op jit(solution)/shard_map/reduce_scatter | solution.py:394
  2379.2 477.2 %reduce-scatter.13.cloned.1.call-start = ((), (), s32[]{:S(2)}) async-start(), calls=%async_computation.15 | async-start | bytes 9732096 | tf_op jit(solution)/shard_map/reduce_scatter | solution.py:393
  2391.7 633.6 %reduce-scatter.19.cloned.1.call-start = ((), (), s32[]{:S(2)}) async-start(), calls=%async_computation.18 | async-start | bytes 14598144 | tf_op jit(solution)/shard_map/reduce_scatter | solution.py:396
  2415.9 72.4 %copy-start.168 = (f32[3,24]{1,0:T(4,128)S(1)}, f32[3,24]{1,0:T(4,128)}, u32[]{:S(2)}) copy-start(f32[3,24]{1,0:T(4,128)} %param.57) | copy-start | bytes 868
  2415.9 72.4 %copy-start.213 = (f32[3,24]{1,0:T(4,128)S(1)}, f32[3,24]{1,0:T(4,128)}, u32[]{:S(2)}) copy-start(f32[3,24]{1,0:T(4,128)} %param.58) | copy-start | bytes 868
  2415.9 72.4 %copy-start.214 = (f32[3,24]{1,0:T(4,128)S(1)}, f32[3,24]{1,0:T(4,128)}, u32[]{:S(2)}) copy-start(f32[3,24]{1,0:T(4,128)} %param.59) | copy-start | bytes 868
  2415.9 73.0 %collective-permute-start.1 = (bf16[512,768]{0,1:T(8,128)(2,1)}, bf16[512,768]{0,1:T(8,128)(2,1)}, u32[]{:S(2)}, u32[]{:S(2)}) collective-permute-start(bf16[512,768]{0,1:T(8,128)(2,1)} %broadcast_select_fusion.1), channel_id=1, source_target_pairs={{0,16},{16,0},{1,17},{17,1},{2,18},{18,2},{3,19},{19,3},{4,20},{20... | collective-permute-start | bytes 2359304 | tf_op jit(solution)/shard_map/ppermute | solution.py:20
  2425.6 66.4 %collective-permute-start.3 = (bf16[512,768]{0,1:T(8,128)(2,1)}, bf16[512,768]{0,1:T(8,128)(2,1)}, u32[]{:S(2)}, u32[]{:S(2)}) collective-permute-start(bf16[512,768]{0,1:T(8,128)(2,1)} %broadcast_select_fusion), channel_id=1, source_target_pairs={{0,16},{16,0},{1,17},{17,1},{2,18},{18,2},{3,19},{19,3},{4,20},{20... | collective-permute-start | bytes 2359304 | tf_op jit(solution)/shard_map/ppermute | solution.py:20
  2493.5 80.6 %copy-start.76 = (f32[24,2304]{1,0:T(8,128)S(1)}, f32[24,2304]{1,0:T(8,128)}, u32[]{:S(2)}) copy-start(f32[24,2304]{1,0:T(8,128)} %param.36) | copy-start | bytes 663556
  2493.5 80.5 %copy-start.106 = (f32[24,2304]{1,0:T(8,128)S(1)}, f32[24,2304]{1,0:T(8,128)}, u32[]{:S(2)}) copy-start(f32[24,2304]{1,0:T(8,128)} %param.37) | copy-start | bytes 663556
  2493.6 222.3 %copy-start.74 = (f32[96,768]{1,0:T(8,128)S(1)}, f32[96,768]{1,0:T(8,128)}, u32[]{:S(2)}) copy-start(f32[96,768]{1,0:T(8,128)} %param.45) | copy-start | bytes 884740
  2493.6 222.3 %copy-start.103 = (f32[96,768]{1,0:T(8,128)S(1)}, f32[96,768]{1,0:T(8,128)}, u32[]{:S(2)}) copy-start(f32[96,768]{1,0:T(8,128)} %param.46) | copy-start | bytes 884740
  2493.6 222.3 %copy-start.104 = (f32[96,768]{1,0:T(8,128)S(1)}, f32[96,768]{1,0:T(8,128)}, u32[]{:S(2)}) copy-start(f32[96,768]{1,0:T(8,128)} %param.47) | copy-start | bytes 884740
  2495.2 361.2 %copy-start.75 = (f32[24,3072]{1,0:T(8,128)S(1)}, f32[24,3072]{1,0:T(8,128)}, u32[]{:S(2)}) copy-start(f32[24,3072]{1,0:T(8,128)} %param.42) | copy-start | bytes 884740
  2495.2 361.2 %copy-start.105 = (f32[24,3072]{1,0:T(8,128)S(1)}, f32[24,3072]{1,0:T(8,128)}, u32[]{:S(2)}) copy-start(f32[24,3072]{1,0:T(8,128)} %param.43) | copy-start | bytes 884740
  2498.2 527.1 %copy-start.63 = (f32[144,768]{1,0:T(8,128)S(1)}, f32[144,768]{1,0:T(8,128)}, u32[]{:S(2)}) copy-start(f32[144,768]{1,0:T(8,128)} %param.51) | copy-start | bytes 1327108
  2498.2 527.1 %copy-start.85 = (f32[144,768]{1,0:T(8,128)S(1)}, f32[144,768]{1,0:T(8,128)}, u32[]{:S(2)}) copy-start(f32[144,768]{1,0:T(8,128)} %param.52) | copy-start | bytes 1327108
  2498.2 527.1 %copy-start.86 = (f32[144,768]{1,0:T(8,128)S(1)}, f32[144,768]{1,0:T(8,128)}, u32[]{:S(2)}) copy-start(f32[144,768]{1,0:T(8,128)} %param.53) | copy-start | bytes 1327108
  (210 other events, 1919.7 us)
Sparse Core Ops, SparseCore 0:
  11.5 61.4 all-gather.15
  76.5 59.1 all-gather.7
  138.6 52.8 all-gather.9
  194.8 62.3 all-gather.11
  260.6 62.3 all-gather.13
  326.3 71.4 all-gather.17
  2141.7 92.7 reduce-scatter.20
  2239.7 98.1 reduce-scatter.10
  2344.3 106.3 reduce-scatter.16
  2456.3 117.7 reduce-scatter.8
  2581.0 134.8 reduce-scatter.14
  2721.6 134.6 reduce-scatter.12
  2863.4 161.8 reduce-scatter.18
where the time goes:
time: 3090 us; the launch traced here: 3030 us
  local copies, waits for them, and re-layouts  1540 us (50%)
  waiting for transfers between devices  519 us (17%)
  other arithmetic  438 us (14%)
  matrix products  371 us (12%)
  blocking collectives  141 us (5%)
    slice x304, local copies, waits for them, and re-layouts, linear_chain(): return lax.associative_scan(combine, (factor, inject), axis=0)[1]  858 us
    pad x88, local copies, waits for them, and re-layouts, linear_chain(): return lax.associative_scan(combine, (factor, inject), axis=0)[1]  220 us
    reduce_scatter x1, waiting for transfers between devices, on_device(): lax.psum_scatter(char_grads[1], ('stream', 'dp'), scatter_dimension=0, ti...  167 us
    reduce_scatter x1, waiting for transfers between devices, on_device(): lax.psum_scatter(token_grads[3], ('stream', 'dp'), scatter_dimension=0, t...  140 us
    reduce_scatter x1, waiting for transfers between devices, on_device(): lax.psum_scatter(token_grads[2], ('stream', 'dp'), scatter_dimension=0, t...  138 us
    rev x2, local copies, waits for them, and re-layouts, chain_grads(): jnp.flip(linear_chain(jnp.flip(keep_next, 0), jnp.flip(upstream, 0)), 0)  96.8 us
    add x50, other arithmetic, linear_chain(): return lax.associative_scan(combine, (factor, inject), axis=0)[1]  76.2 us
    reduce_scatter x1, waiting for transfers between devices, on_device(): lax.psum_scatter(token_grads[0], ('stream', 'dp'), scatter_dimension=0, t...  73.8 us
  transfers between devices with their start and end apart: 17, of which 4 were waited for; matrix products, arithmetic and copies ran while one was open for 47% of the time, Pallas kernels for 0%

commit v1 on v0

v1 whole, which is shorter than its diff:
```python
import jax
import jax.numpy as jnp
from jax import lax
from jax.experimental import pallas as pl
from jax.experimental.pallas import tpu as pltpu
from jax.sharding import PartitionSpec as P

D = 768
HEADS = 12
FF = 3072
LEN = 1024
STEP = 5


def partner(block, axis, apart):
    count = lax.axis_size(axis)
    route = []
    for low in range(count):
        high = low | 1 << apart
        if high != low and high < count:
            route += [(low, high), (high, low)]
    return lax.ppermute(block, axis, route)


def to_rows(matrix, parts):
    side = matrix.shape[1] // D
    own = matrix.shape[0] // parts
    blocks = matrix.astype(jnp.bfloat16).reshape(parts, own, side, D)
    return blocks.transpose(0, 2, 1, 3).reshape(parts, side * own, D)


def from_rows(rows, offset, own, side):
    parts = rows.shape[0]
    blocks = rows[:, offset : offset + own * side].reshape(parts, side, own, D)
    return blocks.transpose(0, 2, 1, 3).reshape(parts * own, side * D)


def gains_row(gains):
    return jnp.pad(gains.reshape(1, -1), ((0, 7), (0, D - gains.size)))


def gather_rows(shards, axes):
    packed = jnp.concatenate([to_rows(shard, 1)[0] for shard in shards], 0)
    rows = lax.all_gather(packed, axes, axis=0, tiled=False)
    pieces = []
    offset = 0
    for shard in shards:
        own, side = shard.shape[0], shard.shape[1] // D
        pieces.append(from_rows(rows, offset, own, side))
        offset += own * side
    return pieces


def scatter_rows(grads, axes):
    parts = lax.axis_size(axes)
    packed = jnp.concatenate([to_rows(grad, parts) for grad in grads], 1)
    high = packed.shape[1]
    total = lax.psum_scatter(packed.reshape(parts * high, D), axes, scatter_dimension=0, tiled=True)
    pieces = []
    offset = 0
    for grad in grads:
        own, side = grad.shape[0] // parts, grad.shape[1] // D
        pieces.append(from_rows(total[None], offset, own, side).astype(jnp.float32))
        offset += own * side
    return pieces


def product(former, latter):
    return jnp.dot(former, latter, preferred_element_type=jnp.float32)


def inner_rows(former, latter):
    return lax.dot_general(
        former, latter, (((0,), (0,)), ((), ())), preferred_element_type=jnp.float32
    )


def inner_cols(former, latter):
    return lax.dot_general(
        former, latter, (((1,), (1,)), ((), ())), preferred_element_type=jnp.float32
    )


def norm_gain(values, scales):
    center = jnp.mean(values, axis=-1, keepdims=True)
    shifted = values - center
    spread = jnp.mean(shifted * shifted, axis=-1, keepdims=True)
    return shifted * lax.rsqrt(spread + 1e-05) * scales


def rows_before(matrix):
    return jnp.concatenate([jnp.zeros_like(matrix[:1]), matrix[:-1]], 0)


def rows_after(matrix):
    return jnp.concatenate([matrix[1:], jnp.zeros_like(matrix[:1])], 0)


def char_segments(lengths, char_count):
    starts = jnp.cumsum(lengths) - lengths
    markers = jnp.zeros((char_count,), jnp.int32).at[starts].add(1)
    return jnp.cumsum(markers) - 1


def step_rates():
    return (
        0.5 * D ** (-0.5),
        0.5 * (3 * D // LEN) ** (-0.5),
        0.5 * D ** (-0.5),
        0.5 * FF ** (-0.5),
        0.5 * D ** (-0.5),
        0.5 * (6 * D) ** (-0.5),
        0.5,
        0.2,
    )


def adamw(master, first_m, second_m, grad_sum, step_rate):
    mean_new = 0.5 * first_m + 0.5 * grad_sum
    power = 0.5 * second_m + 0.5 * grad_sum * grad_sum
    correct = 1.0 - 0.5**STEP
    fresh_w = master - step_rate * (
        mean_new / correct / (jnp.sqrt(power / correct) + 1e-08) + 0.01 * master
    )
    return (fresh_w, mean_new, power)


STEP_ROWS = 512
UNROLL = 8


def lane_blocks(count):
    half = count // 2
    return [(number, number if number < half else number - half + 4) for number in range(count)]


def chars_ahead(ids, owners, table, w_gru, shares, keep, inject, before, pooled, sums, carry):
    block = pl.program_id(0)
    total = ids.shape[0]
    width = w_gru.shape[1] // 4

    @pl.when(block == 0)
    def start():
        logits = jnp.dot(table[...], w_gru[...], preferred_element_type=jnp.float32)
        keep[...] = jnp.zeros_like(keep)
        inject[...] = jnp.zeros_like(inject)
        carry[...] = jnp.zeros_like(carry)
        for number, place in lane_blocks(6):
            left = number * 128 if number < 3 else 2 * width + (number - 3) * 128
            update = jax.nn.sigmoid(logits[:, left : left + 128])
            keep[:, place, :] = 1.0 - update
            inject[:, place, :] = update * logits[:, left + width : left + width + 128]

    leading = lax.broadcasted_iota(jnp.int32, (8, 128), 0) < 4

    def one(step, state, running, owner_f, owner_b):
        place = block * STEP_ROWS + step
        mirror = total - 1 - place
        id_f, id_b = ids[place], ids[mirror]
        now_f, now_b = owners[place], owners[mirror]
        before[step] = state
        state = jnp.where(leading, keep[id_f], keep[id_b]) * state + jnp.where(
            leading, inject[id_f], inject[id_b]
        )
        stay_f = jnp.where(now_f == owner_f, 1.0, 0.0)
        stay_b = jnp.where(now_b == owner_b, 1.0, 0.0)
        running = running * jnp.where(leading, stay_f, stay_b) + state
        sums[now_f, 0:4] = running[0:4]
        sums[now_b, 4:8] = running[4:8]
        return state, running, now_f, now_b

    def several(group, held):
        for inner in range(UNROLL):
            held = one(group * UNROLL + inner, *held)
        return held

    first = block * STEP_ROWS
    last_f = jnp.where(block == 0, -1, owners[jnp.maximum(first - 1, 0)])
    last_b = jnp.where(block == 0, -1, owners[jnp.minimum(total - first, total - 1)])
    state, running, _, _ = lax.fori_loop(
        0, STEP_ROWS // UNROLL, several, (carry[0], carry[1], last_f, last_b)
    )
    carry[0] = state
    carry[1] = running

    @pl.when(block == pl.num_programs(0) - 1)
    def finish():
        for number, place in lane_blocks(6):
            pooled[:, number * 128 : number * 128 + 128] = (
                sums[:, place, :] * shares[...]
            ).astype(pooled.dtype)


def chars_back(
    ids, owners, upstream, shares, table, w_gru, keep, inject, before, grad_gru, grad_table, spread, zs, cs, full, carry
):
    block = pl.num_programs(0) - 1 - pl.program_id(0)
    total = ids.shape[0]

    @pl.when(pl.program_id(0) == 0)
    def start():
        zs[...] = jnp.zeros_like(zs)
        cs[...] = jnp.zeros_like(cs)
        carry[...] = jnp.zeros_like(carry)
        for number, place in lane_blocks(6):
            spread[:, place, :] = upstream[:, number * 128 : number * 128 + 128] * shares[...]
        for place in (3, 7):
            spread[:, place, :] = jnp.zeros((spread.shape[0], 128), jnp.float32)

    leading = lax.broadcasted_iota(jnp.int32, (8, 128), 0) < 4

    def one(step, passed):
        place = block * STEP_ROWS + step
        mirror = total - 1 - place
        id_f, id_b = ids[place], ids[mirror]
        now_f, now_b = owners[place], owners[mirror]
        kept = jnp.where(leading, keep[id_f], keep[id_b])
        came = jnp.where(leading, inject[id_f], inject[id_b])
        carried = jnp.where(leading, spread[now_f], spread[now_b]) + passed
        passed = kept * carried
        update = 1.0 - kept
        cand_grad = carried * update
        gate_grad = passed * (came - before[step] * update)
        cand_grad = cand_grad.astype(jnp.bfloat16).astype(jnp.float32)
        gate_grad = gate_grad.astype(jnp.bfloat16).astype(jnp.float32)
        zs[id_f, 0:4] += gate_grad[0:4]
        zs[id_b, 4:8] += gate_grad[4:8]
        cs[id_f, 0:4] += cand_grad[0:4]
        cs[id_b, 4:8] += cand_grad[4:8]
        return passed

    def several(group, held):
        for inner in range(UNROLL):
            held = one(STEP_ROWS - 1 - group * UNROLL - inner, held)
        return held

    carry[...] = lax.fori_loop(0, STEP_ROWS // UNROLL, several, carry[...])

    @pl.when(block == 0)
    def finish():
        width = full.shape[1] // 4
        for number, place in lane_blocks(6):
            left = number * 128 if number < 3 else 2 * width + (number - 3) * 128
            full[:, left : left + 128] = zs[:, place, :]
            full[:, left + width : left + width + 128] = cs[:, place, :]
        upper = full[...].astype(jnp.bfloat16)
        lower = (full[...] - upper.astype(jnp.float32)).astype(jnp.bfloat16)
        grad_gru[...] = (
            contract(table[...], upper, 0, 0) + contract(table[...], lower, 0, 0)
        ).astype(grad_gru.dtype)
        grad_table[...] = (
            contract(upper, w_gru[...], 1, 1) + contract(lower, w_gru[...], 1, 1)
        ).astype(grad_table.dtype)


def whole(array):
    return pl.BlockSpec(array.shape, lambda block: (0,) * len(array.shape))


def scalars():
    return pl.BlockSpec(memory_space=pltpu.SMEM)


def run_chars(ids, owners, table, w_gru, shares):
    total, count = ids.shape[0], shares.shape[0]
    letters = table.shape[0]
    f32 = jnp.float32
    tile = jax.ShapeDtypeStruct((letters, 8, 128), f32)
    outs = (
        tile,
        tile,
        jax.ShapeDtypeStruct((total, 8, 128), f32),
        jax.ShapeDtypeStruct((count, w_gru.shape[1] // 2), jnp.bfloat16),
    )
    return pl.pallas_call(
        chars_ahead,
        grid=(total // STEP_ROWS,),
        in_specs=[scalars(), scalars(), whole(table), whole(w_gru), whole(shares)],
        out_specs=[
            whole(tile),
            whole(tile),
            pl.BlockSpec((STEP_ROWS, 8, 128), lambda block: (block, 0, 0)),
            whole(outs[3]),
        ],
        out_shape=outs,
        scratch_shapes=[pltpu.VMEM((count, 8, 128), f32), pltpu.VMEM((2, 8, 128), f32)],
        compiler_params=pltpu.CompilerParams(vmem_limit_bytes=40 << 20),
        cost_estimate=pl.CostEstimate(flops=2 * 256 * 768 * 1536, bytes_accessed=40 << 20, transcendentals=0),
    )(ids, owners, table, w_gru, shares)


def run_chars_back(ids, owners, upstream, shares, table, w_gru, keep, inject, before):
    total, count = ids.shape[0], shares.shape[0]
    letters = keep.shape[0]
    f32 = jnp.float32
    blocks = total // STEP_ROWS
    outs = (
        jax.ShapeDtypeStruct(w_gru.shape, jnp.bfloat16),
        jax.ShapeDtypeStruct(table.shape, jnp.bfloat16),
    )
    return pl.pallas_call(
        chars_back,
        grid=(blocks,),
        in_specs=[
            scalars(),
            scalars(),
            whole(upstream),
            whole(shares),
            whole(table),
            whole(w_gru),
            whole(keep),
            whole(inject),
            pl.BlockSpec((STEP_ROWS, 8, 128), lambda block: (blocks - 1 - block, 0, 0)),
        ],
        out_specs=[whole(outs[0]), whole(outs[1])],
        out_shape=outs,
        scratch_shapes=[
            pltpu.VMEM((count, 8, 128), f32),
            pltpu.VMEM((letters, 8, 128), f32),
            pltpu.VMEM((letters, 8, 128), f32),
            pltpu.VMEM((letters, w_gru.shape[1]), f32),
            pltpu.VMEM((8, 128), f32),
        ],
        compiler_params=pltpu.CompilerParams(vmem_limit_bytes=48 << 20),
        cost_estimate=pl.CostEstimate(
            flops=20_000_000_000, bytes_accessed=40 << 20, transcendentals=0
        ),
    )(ids, owners, upstream, shares, table, w_gru, keep, inject, before)


ROWS = 256


def contract(former, latter, left, right):
    return lax.dot_general(
        former, latter, (((left,), (right,)), ((), ())), preferred_element_type=jnp.float32
    )


def attend(queries, key_rows, value_rows, context, logsum):
    size = key_rows.shape[1] // 2
    lanes = lax.broadcasted_iota(jnp.int32, (1, 2 * size), 1)
    scale = size ** (-0.5)

    def some_rows(number, _):
        at = pl.ds(pl.multiple_of(number * ROWS, ROWS), ROWS)
        row_block = queries[at, :]
        parts = []
        sums = []
        for head in range(2):
            own = (lanes < size) if head == 0 else (lanes >= size)
            scores = contract(jnp.where(own, row_block, 0) * scale, key_rows[...], 1, 1)
            row_max = jnp.max(scores, axis=-1, keepdims=True)
            exponent = jnp.exp(scores - row_max)
            row_total = jnp.sum(exponent, axis=-1, keepdims=True)
            probs = (exponent * (1.0 / row_total)).astype(jnp.bfloat16)
            parts.append(contract(probs, value_rows[...], 1, 0))
            sums.append(row_max + jnp.log(row_total))
        context[at, :] = jnp.where(lanes < size, parts[0], parts[1]).astype(context.dtype)
        both = jnp.where(lanes < size, sums[0], sums[1])
        turned = jnp.transpose(both)
        logsum[0:8, at] = turned[0:8]
        logsum[8:16, at] = turned[size : size + 8]
        return 0

    lax.fori_loop(0, queries.shape[0] // ROWS, some_rows, 0)


def attend_back(queries, key_rows, value_rows, logsum, grads, query_grad, key_grad, value_grad, key_sum, value_sum):
    size = key_rows.shape[1] // 2
    lanes = lax.broadcasted_iota(jnp.int32, (1, 2 * size), 1)
    scale = size ** (-0.5)
    key_sum[...] = jnp.zeros_like(key_sum)
    value_sum[...] = jnp.zeros_like(value_sum)

    def some_rows(number, _):
        at = pl.ds(pl.multiple_of(number * ROWS, ROWS), ROWS)
        row_block = queries[at, :]
        grad_block = grads[at, :]
        parts = []
        for head in range(2):
            own = (lanes < size) if head == 0 else (lanes >= size)
            own_rows = jnp.where(own, row_block, 0) * scale
            own_grads = jnp.where(own, grad_block, 0)
            scores = contract(key_rows[...], own_rows, 1, 1)
            probs = jnp.exp(scores - logsum[8 * head : 8 * head + 1, at])
            value_sum[...] += contract(probs.astype(jnp.bfloat16), own_grads, 1, 0)
            prob_grad = contract(value_rows[...], own_grads, 1, 1)
            center = jnp.sum(prob_grad * probs, axis=0, keepdims=True)
            score_grad = (probs * (prob_grad - center)).astype(jnp.bfloat16)
            key_sum[...] += contract(score_grad, own_rows, 1, 0)
            parts.append(contract(score_grad, key_rows[...], 0, 0))
        query_grad[at, :] = (
            jnp.where(lanes < size, parts[0], parts[1]) * scale
        ).astype(query_grad.dtype)
        return 0

    lax.fori_loop(0, queries.shape[0] // ROWS, some_rows, 0)
    key_grad[...] = key_sum[...].astype(key_grad.dtype)
    value_grad[...] = value_sum[...].astype(value_grad.dtype)


def column(rows, width, offset):
    return pl.BlockSpec((rows, width), lambda pair: (0, offset + pair))


def run_attend(qkv):
    length, across = qkv.shape
    model = across // 3
    pairs = model // 128
    return pl.pallas_call(
        attend,
        grid=(pairs,),
        in_specs=[column(length, 128, pairs * part) for part in range(3)],
        out_specs=[column(length, 128, 0), pl.BlockSpec((16, length), lambda pair: (pair, 0))],
        out_shape=(
            jax.ShapeDtypeStruct((length, model), jnp.bfloat16),
            jax.ShapeDtypeStruct((16 * pairs, length), jnp.float32),
        ),
        compiler_params=pltpu.CompilerParams(vmem_limit_bytes=40 << 20),
        cost_estimate=pl.CostEstimate(flops=4 * length * length * model, bytes_accessed=8 * length * model, transcendentals=length * length * 12),
    )(qkv, qkv, qkv)


def run_attend_back(qkv, logsum, grads):
    length, across = qkv.shape
    model = across // 3
    pairs = model // 128
    part = jax.ShapeDtypeStruct((length, model), jnp.bfloat16)
    return pl.pallas_call(
        attend_back,
        grid=(pairs,),
        in_specs=[column(length, 128, pairs * part) for part in range(3)]
        + [pl.BlockSpec((16, length), lambda pair: (pair, 0)), column(length, 128, 0)],
        out_specs=[column(length, 128, 0)] * 3,
        out_shape=(part, part, part),
        scratch_shapes=[pltpu.VMEM((length, 128), jnp.float32)] * 2,
        compiler_params=pltpu.CompilerParams(vmem_limit_bytes=40 << 20),
        cost_estimate=pl.CostEstimate(flops=10 * length * length * model, bytes_accessed=16 * length * model, transcendentals=length * length * 12),
    )(qkv, qkv, qkv, logsum, grads)


def token_forward(tokens, weights):
    qkv = product(tokens, weights[0]).astype(jnp.bfloat16)
    context, logsum = run_attend(qkv)
    mixed_sum = tokens.astype(jnp.float32) + product(context, weights[1])
    normed = norm_gain(mixed_sum, weights[7][0].astype(jnp.float32))
    hidden = product(normed.astype(jnp.bfloat16), weights[2])
    summed = normed + product(jax.nn.gelu(hidden).astype(jnp.bfloat16), weights[3])
    feature = norm_gain(summed, weights[7][1].astype(jnp.float32)).astype(jnp.bfloat16)
    return (feature, (qkv, logsum, context, mixed_sum, normed, hidden, summed))


def token_backward(tokens, stored, feature_grad, weights):
    qkv, logsum, context, mixed_sum, normed, kept_hidden, summed = stored
    summed_grad, gain_ffn = jax.vjp(norm_gain, summed, weights[7][1].astype(jnp.float32))[1](
        feature_grad.astype(jnp.float32)
    )
    ffn_grad = summed_grad.astype(jnp.bfloat16)
    active = jax.nn.gelu(kept_hidden).astype(jnp.bfloat16)
    grad_down = inner_rows(active, ffn_grad)
    hidden_grad = jax.vjp(jax.nn.gelu, kept_hidden)[1](inner_cols(ffn_grad, weights[3]))[0].astype(
        jnp.bfloat16
    )
    grad_up = inner_rows(normed.astype(jnp.bfloat16), hidden_grad)
    normed_grad = summed_grad + inner_cols(hidden_grad, weights[2])
    mixed_grad, gain_attn = jax.vjp(norm_gain, mixed_sum, weights[7][0].astype(jnp.float32))[1](
        normed_grad
    )
    attended_grad = mixed_grad.astype(jnp.bfloat16)
    grad_out = inner_rows(context, attended_grad)
    context_grad = inner_cols(attended_grad, weights[1]).astype(jnp.bfloat16)
    qkv_grad = jnp.concatenate(run_attend_back(qkv, logsum, context_grad), 1)
    grad_qkv = inner_rows(tokens, qkv_grad)
    tokens_grad = (mixed_grad + inner_cols(qkv_grad, weights[0])).astype(jnp.bfloat16)
    return (tokens_grad, (grad_qkv, grad_out, grad_up, grad_down, gain_attn, gain_ffn))


def char_section(feature, pooled, kept, out_rows, weights):
    ids_row, segment, shares, keep, inject, before = kept
    w_gru, w_blend, table_copy = (weights[4], weights[5], weights[6])
    joined = jnp.concatenate([feature, pooled], 1)
    stacked = jnp.concatenate([rows_before(joined), joined, rows_after(joined)], 1)
    blend_in = product(stacked, w_blend)
    blended, gelu_pull = jax.vjp(jax.nn.gelu, blend_in)
    result, norm_pull = jax.vjp(
        norm_gain, feature.astype(jnp.float32) + blended, weights[7][2].astype(jnp.float32)
    )
    total_grad, gain_blend = norm_pull(out_rows.astype(jnp.float32))
    blend_grad = gelu_pull(total_grad)[0].astype(jnp.bfloat16)
    grad_blend = inner_rows(stacked, blend_grad)
    stacked_grad = inner_cols(blend_grad, w_blend)
    pair_width = joined.shape[1]
    model_width = pair_width // 2
    joined_grad = (
        stacked_grad[:, pair_width : 2 * pair_width]
        + rows_after(stacked_grad[:, :pair_width])
        + rows_before(stacked_grad[:, 2 * pair_width :])
    )
    feature_grad = (total_grad + joined_grad[:, :model_width]).astype(jnp.bfloat16)
    grad_gru, grad_table = run_chars_back(
        ids_row, segment, joined_grad[:, model_width:], shares, table_copy, w_gru, keep, inject, before
    )
    return (
        result.astype(jnp.bfloat16),
        feature_grad,
        (grad_gru, grad_blend, grad_table, gain_blend),
    )


def on_device(
    tokens_in,
    char_ids,
    char_lengths,
    out_grad,
    w_qkv,
    first_qkv,
    second_qkv,
    w_out,
    first_out,
    second_out,
    w_up,
    first_up,
    second_up,
    w_down,
    first_down,
    second_down,
    w_gru,
    first_gru,
    second_gru,
    w_blend,
    first_blend,
    second_blend,
    char_table,
    first_table,
    second_table,
    gains,
    first_gains,
    second_gains,
):
    masters = (w_qkv, w_out, w_up, w_down, w_gru, w_blend, char_table, gains)
    firsts = (
        first_qkv,
        first_out,
        first_up,
        first_down,
        first_gru,
        first_blend,
        first_table,
        first_gains,
    )
    seconds = (
        second_qkv,
        second_out,
        second_up,
        second_down,
        second_gru,
        second_blend,
        second_table,
        second_gains,
    )
    on_first = lax.axis_index("stream") == 0
    half_len = tokens_in.shape[1]
    everyone = ("stream", "dp")
    early = gather_rows((char_table, w_gru, w_qkv), everyone)
    late = gather_rows((w_out, w_up, w_down, w_blend, gains_row(gains)), everyone)
    count = late[4].shape[0] // 8
    all_gains = late[4][::8, : gains.size].reshape(count, 3, -1).transpose(1, 0, 2).reshape(3, -1)
    current = (early[2], late[0], late[1], late[2], early[1], late[3], early[0], all_gains)
    block_parts = []
    grad_parts = []
    other_tokens = jnp.where(on_first, tokens_in[1], tokens_in[0])
    other_grad = jnp.where(on_first, out_grad[1], out_grad[0])
    keep_tokens = jnp.where(on_first, tokens_in[0], tokens_in[1])
    keep_grad = jnp.where(on_first, out_grad[0], out_grad[1])
    got_tokens, got_grad = partner((other_tokens, other_grad), "stream", 0)
    whole_tokens = jnp.where(
        on_first,
        jnp.concatenate([keep_tokens, got_tokens], 0),
        jnp.concatenate([got_tokens, keep_tokens], 0),
    )
    whole_grad = jnp.where(
        on_first,
        jnp.concatenate([keep_grad, got_grad], 0),
        jnp.concatenate([got_grad, keep_grad], 0),
    )
    ids_row = jnp.where(on_first, char_ids[0], char_ids[1])
    lengths_row = jnp.where(on_first, char_lengths[0], char_lengths[1])
    segment = char_segments(lengths_row, ids_row.shape[0])
    shares = 1.0 / lengths_row.astype(jnp.float32)[:, None]
    keep, inject, before, pooled = run_chars(ids_row, segment, current[6], current[4], shares)
    feature, stored = token_forward(whole_tokens, current)
    result, feature_grad, char_grads = char_section(
        feature, pooled, (ids_row, segment, shares, keep, inject, before), whole_grad, current
    )
    tokens_grad, token_grads = token_backward(whole_tokens, stored, feature_grad, current)
    send_result = jnp.where(on_first, result[half_len:], result[:half_len])
    send_grad = jnp.where(on_first, tokens_grad[half_len:], tokens_grad[:half_len])
    back_result, back_grad = partner((send_result, send_grad), "stream", 0)
    block_parts.append(jnp.where(on_first, result[:half_len], back_result))
    block_parts.append(jnp.where(on_first, back_result, result[half_len:]))
    grad_parts.append(jnp.where(on_first, tokens_grad[:half_len], back_grad))
    grad_parts.append(jnp.where(on_first, back_grad, tokens_grad[half_len:]))
    gain_grads = jnp.stack([token_grads[4], token_grads[5], char_grads[3]])
    gain_rows = gain_grads.reshape(3, count, -1).transpose(1, 0, 2).reshape(count, -1)
    gain_rows = jnp.pad(gain_rows[:, None], ((0, 0), (0, 7), (0, D - gain_rows.shape[1])))
    gain_rows = gain_rows.reshape(8 * count, D)
    blend_sum = scatter_rows((char_grads[1],), everyone)
    middle = scatter_rows((token_grads[3], token_grads[2], char_grads[0], char_grads[2]), everyone)
    final = scatter_rows((token_grads[0], token_grads[1], gain_rows), everyone)
    gain_sum = final[2][0, : gains.size].reshape(gains.shape)
    sums = (final[0], final[1], middle[1], middle[0], middle[2], blend_sum[0], middle[3], gain_sum)
    rates = step_rates()
    results = [
        adamw(masters[number], firsts[number], seconds[number], sums[number], rates[number])
        for number in range(8)
    ]
    return (
        jnp.stack(block_parts),
        jnp.stack(grad_parts),
        results[0][0],
        results[0][1],
        results[0][2],
        results[1][0],
        results[1][1],
        results[1][2],
        results[2][0],
        results[2][1],
        results[2][2],
        results[3][0],
        results[3][1],
        results[3][2],
        results[4][0],
        results[4][1],
        results[4][2],
        results[5][0],
        results[5][1],
        results[5][2],
        results[6][0],
        results[6][1],
        results[6][2],
        results[7][0],
        results[7][1],
        results[7][2],
    )


def solution(mesh):
    in_specs = (
        P("dp", "stream", None),
        P("dp", None),
        P("dp", None),
        P("dp", "stream", None),
        P(("stream", "dp"), None),
        P(("stream", "dp"), None),
        P(("stream", "dp"), None),
        P(("stream", "dp"), None),
        P(("stream", "dp"), None),
        P(("stream", "dp"), None),
        P(("stream", "dp"), None),
        P(("stream", "dp"), None),
        P(("stream", "dp"), None),
        P(("stream", "dp"), None),
        P(("stream", "dp"), None),
        P(("stream", "dp"), None),
        P(("stream", "dp"), None),
        P(("stream", "dp"), None),
        P(("stream", "dp"), None),
        P(("stream", "dp"), None),
        P(("stream", "dp"), None),
        P(("stream", "dp"), None),
        P(("stream", "dp"), None),
        P(("stream", "dp"), None),
        P(("stream", "dp"), None),
        P(None, ("stream", "dp")),
        P(None, ("stream", "dp")),
        P(None, ("stream", "dp")),
    )
    out_specs = (
        P("dp", "stream", None),
        P("dp", "stream", None),
        P(("stream", "dp"), None),
        P(("stream", "dp"), None),
        P(("stream", "dp"), None),
        P(("stream", "dp"), None),
        P(("stream", "dp"), None),
        P(("stream", "dp"), None),
        P(("stream", "dp"), None),
        P(("stream", "dp"), None),
        P(("stream", "dp"), None),
        P(("stream", "dp"), None),
        P(("stream", "dp"), None),
        P(("stream", "dp"), None),
        P(("stream", "dp"), None),
        P(("stream", "dp"), None),
        P(("stream", "dp"), None),
        P(("stream", "dp"), None),
        P(("stream", "dp"), None),
        P(("stream", "dp"), None),
        P(("stream", "dp"), None),
        P(("stream", "dp"), None),
        P(("stream", "dp"), None),
        P(None, ("stream", "dp")),
        P(None, ("stream", "dp")),
        P(None, ("stream", "dp")),
    )
    return jax.shard_map(
        on_device, mesh=mesh, in_specs=in_specs, out_specs=out_specs, check_vma=False
    )
```

time: 3090 us -> 877 us (0.28); the launches traced: 3030 us -> 869 us
  local copies, waits for them, and re-layouts: 1540 us -> 103 us
  other arithmetic: 438 us -> 77.5 us
  matrix products: 371 us -> 149 us
  waiting for transfers between devices: 519 us -> 333 us
  Pallas kernels: 0 us -> 184 us
  blocking collectives: 141 us -> 0 us
    slice x314 -> x11, local copies, waits for them, and re-layouts: 971 us -> 20.7 us  [the longest x8 19.7 us: from_rows(): blocks = rows[:, offset:offset + own * side].reshape(parts, side, own, D)]
    reduce_scatter x7 -> x3, waiting for transfers between devices: 519 us -> 209 us  [scatter_rows(): lax.psum_scatter(packed.reshape(parts * high, D), axes, scatter_dimension...]
    rev x5 -> x0, local copies, waits for them, and re-layouts: 221 us -> none  [the longest x2 96.8 us: chain_grads(): jnp.flip(linear_chain(jnp.flip(keep_next, 0), jnp.flip(upstream, 0)), 0)]
    pad x88 -> x0, local copies, waits for them, and re-layouts: 220 us -> none  [linear_chain(): return lax.associative_scan(combine, (factor, inject), axis=0)[1]]
    pallas_call x0 -> x4, Pallas kernels: none -> 184 us  [the longest x1 57.2 us: run_attend_back(): pl.pallas_call(attend_back, grid=(pairs,), in_specs=[column(length, 128,...]
    dot_general x14 -> x0, matrix products: 162 us -> none  [the longest x4 40.7 us: one_block(): jnp.einsum('qhd,khd->hqk', row_block, key_rows, preferred_element_type=jn...]
    add x95 -> x0, other arithmetic: 91.1 us -> none  [the longest x50 76.2 us: linear_chain(): return lax.associative_scan(combine, (factor, inject), axis=0)[1]]
    all_gather x6 -> x2, waiting for transfers between devices: 0.03 us -> 87 us  [gather_rows(): rows = lax.all_gather(packed, axes, axis=0, tiled=False)]
  transfers between devices with their start and end apart: 17 -> 9, of which waited for: 4 -> 6; matrix products, arithmetic and copies ran while one was open for 47% -> 22% of each run, Pallas kernels for 0% -> 15%
where the time goes in v1:
time: 877 us; the launch traced here: 869 us
  waiting for transfers between devices  333 us (38%)
  Pallas kernels  184 us (21%)
  matrix products  149 us (17%)
  local copies, waits for them, and re-layouts  103 us (12%)
  other arithmetic  77.5 us (9%)
  between operations  15.7 us (2%)
    reduce_scatter x3, waiting for transfers between devices, scatter_rows(): lax.psum_scatter(packed.reshape(parts * high, D), axes, scatter_dimension...  209 us
    all_gather x2, waiting for transfers between devices, gather_rows(): rows = lax.all_gather(packed, axes, axis=0, tiled=False)  87 us
    pallas_call x1, Pallas kernels, run_attend_back(): pl.pallas_call(attend_back, grid=(pairs,), in_specs=[column(length, 128,...  57.2 us
    dot_general x5, matrix products, inner_rows(): lax.dot_general(former, latter, (((0,), (0,)), ((), ())), preferred_eleme...  53.9 us
    pallas_call x1, Pallas kernels, run_chars_back(): pl.pallas_call(chars_back, grid=(blocks,), in_specs=[scalars(), scalars()...  53.5 us
    dot_general x5, matrix products, inner_cols(): lax.dot_general(former, latter, (((1,), (1,)), ((), ())), preferred_eleme...  52.5 us
    dot_general x5, matrix products, product(): return jnp.dot(former, latter, preferred_element_type=jnp.float32)  42.3 us
    pallas_call x1, Pallas kernels, run_chars(): pl.pallas_call(chars_ahead, grid=(total // STEP_ROWS,), in_specs=[scalars...  38.5 us
  transfers between devices with their start and end apart: 9, of which 6 were waited for; matrix products, arithmetic and copies ran while one was open for 22% of the time, Pallas kernels for 15%

profile of v1, /device:TPU:0, one launch (start us, length us, event | category | flops | bytes accessed | tf_op | source)
XLA Modules:
  0.0 869.0 jit_solution(5038353880091275259)
XLA Ops:
  21.2 7.6 scatter_custom_fusion
  29.8 59.7 %all-gather.5.cloned.1.call-done = bf16[4096,768]{1,0:T(8,128)(2,1)} async-done(((bf16[128,768]{1,0:T(8,128)(2,1)}), bf16[4096,768]{1,0:T(8,128)(2,1)}) %all-gather.5.cloned.1.call-update) | async-done | bytes 6291472 | tf_op jit(solution)/shard_map/all_gather | solution.py:44
  100.1 38.5 %shard_map.468 = (f32[256,8,128]{2,1,0:T(8,128)S(1)}, f32[256,8,128]{2,1,0:T(8,128)S(1)}, f32[4096,8,128]{2,1,0:T(8,128)}, bf16[1024,768]{1,0:T(8,128)(2,1)S(1)}) custom-call(s32[4096]{0:T(1024)S(1)} %bitcast.147, s32[4096]{0:T(1024)S(1)} %add_bitcast_fusion.owners, bf16[256,768]{1,0:T(8,128)(2,1)S(1)} %slice_bitcast_fusion.table, ...), custom_call_target="tpu_custom_call" | custom-call | flops 603979776 | bytes 41943040 | tf_op jit(solution)/shard_map/pallas_call | solution.py:275
  142.0 5.9 convolution_convert_fusion.1.queries.key_rows.value_rows
  147.9 34.7 %shard_map.467 = (bf16[1024,768]{1,0:T(8,128)(2,1)S(1)}, f32[96,1024]{1,0:T(8,128)S(1)}) custom-call(bf16[1024,2304]{1,0:T(8,128)(2,1)S(1)} %convolution_convert_fusion.1.queries.key_rows.value_rows, bf16[1024,2304]{1,0:T(8,128)(2,1)S(1)} %convolution_convert_fusion.1.queries.key_rows.value_rows, ...), custom_call_target="tpu_custom_call" | custom-call | flops 3221225472 | bytes 6291456 | tf_op jit(solution)/shard_map/pallas_call | solution.py:411
  184.7 27.3 %all-gather.7.cloned.1.call-done = bf16[11776,768]{1,0:T(8,128)(2,1)} async-done(((bf16[368,768]{1,0:T(8,128)(2,1)}), bf16[11776,768]{1,0:T(8,128)(2,1)}) %all-gather.7.cloned.1.call-update) | async-done | bytes 18087952 | tf_op jit(solution)/shard_map/all_gather | solution.py:44
  215.4 8.1 fusion.69
  237.7 8.4 fusion.50
  246.2 10.2 %fusion.70 = (f32[1024]{0:T(1024)S(1)}, f32[1024,768]{1,0:T(8,128)S(1)}) fusion(bf16[3072,768]{1,0:T(8,128)(2,1)S(1)} %bitcast.182, f32[1024,3072]{1,0:T(8,128)} %fusion.50, f32[768]{0:T(1024)S(1)} %reshape.384, f32[1024]{0:T(1024)S(1)} %fusion.42, f32[1024,768]{1,0:T(8,128)S(1)} %copy-done.21, f32[1024]{0:T(1024)S(1)} %broadcast_multiply_fusion.2), kind=kOutput, calls=%fused_computation.179 | convolution fusion | flops 4864080896 | bytes 23608320 | tf_op jit(solution)/shard_map/dot_general | solution.py:69
  269.4 14.8 %fusion.66 = (f32[1024]{0:T(1024)}, f32[1024,768]{1,0:T(8,128)}, f32[1024,768]{1,0:T(8,128)}) fusion(bf16[1024,768]{1,0:T(8,128)(2,1)S(1)} %multiply_convert_fusion.2, bf16[4608,768]{1,0:T(8,128)(2,1)S(1)} %bitcast.170, bf16[1023,1536]{1,0:T(8,128)(2,1)} %slice_maximum_fusion, bf16[1024,1536]{1,0:T(8,128)(2,1)} %fusion.31, ...), kind=kOutput, calls=%fused_computation.175 | convolution fusion | flops 7303592960 | bytes 22807552 | tf_op jit(solution)/shard_map/dot_general | solution.py:69
  294.4 5.2 fusion.65
  299.6 16.8 %fusion.52 = f32[1024,4608]{1,0:T(8,128)} fusion(bf16[4608,768]{1,0:T(8,128)(2,1)} %bitcast.171, f32[1024,768]{1,0:T(8,128)S(1)} %copy-done.85, f32[1024,768]{1,0:T(8,128)S(1)} %get-tuple-element.84, f32[1024]{0:T(1024)S(1)} %negate_multiply_fusion.2), kind=kOutput, calls=%fused_computation.171 | convolution fusion | flops 7264272384 | bytes 32247808 | tf_op jit(solution)/shard_map/dot_general | solution.py:79
  316.4 10.7 %fusion.68 = (f32[1023,1536]{1,0:T(8,128)}, f32[1023,1536]{1,0:T(8,128)}) fusion(f32[1024,4608]{1,0:T(8,128)} %fusion.52), kind=kLoop, calls=%fused_computation.177 | loop fusion | bytes 25141248 | tf_op jit(solution)/shard_map/slice | solution.py:96
  327.0 7.3 fusion.12
  340.5 18.1 %fusion.7 = bf16[1024,3072]{1,0:T(8,128)(2,1)} fusion(f32[1024,3072]{1,0:T(8,128)} %fusion.50, bf16[3072,768]{1,0:T(8,128)(2,1)} %bitcast.179, f32[1024,768]{1,0:T(8,128)} %get-tuple-element.81, f32[1024]{0:T(1024)S(1)} %negate_multiply_fusion.1), kind=kOutput, calls=%fused_computation.11 | convolution fusion | flops 4896325632 | bytes 26742784 | tf_op jit(solution)/shard_map/dot_general | solution.py:79
  358.7 9.0 %multiply_reduce_fusion = (bf16[768]{0:T(1024)(128)(2,1)}, f32[1024]{0:T(1024)S(1)}, f32[1024,768]{1,0:T(8,128)S(1)}) fusion(f32[1024,768]{1,0:T(8,128)S(1)} %copy-done.22, f32[1024]{0:T(1024)S(1)} %copy-done.74, f32[1024]{0:T(1024)S(1)} %copy-done.63, f32[768]{0:T(1024)S(1)} %copy-done.72, bf16[1024,3072]{1,0:T(8,128)(2,1)} %fusion.7, ...), kind=kOutput, calls=%fused_computation.58 | convolution fusion | flops 4838914048 | bytes 20468224 | tf_op jit(solution)/shard_map/dot_general | solution.py:79
  374.3 57.2 %shard_map.469 = (bf16[1024,768]{1,0:T(8,128)(2,1)S(1)}, bf16[1024,768]{1,0:T(8,128)(2,1)S(1)}, bf16[1024,768]{1,0:T(8,128)(2,1)S(1)}) custom-call(bf16[1024,2304]{1,0:T(8,128)(2,1)S(1)} %bitcast.150, bf16[1024,2304]{1,0:T(8,128)(2,1)S(1)} %bitcast.150, bf16[1024,2304]{1,0:T(8,128)(2,1)S(1)} %bitcast.150, f32[96,1024]{1,0:T(8,128)S(1)} %get-tuple-element.39.logsum, ...), custom_call_target="tpu_custom_call" | custom-call | flops 8053063680 | bytes 12582912 | tf_op jit(solution)/shard_map/pallas_call | solution.py:430
  434.1 7.3 convolution_convert_fusion.4
  441.4 8.7 %reshape.376 = bf16[32,24,3,768]{3,2,1,0:T(4,128)(2,1)} reshape(bf16[768,2304]{1,0:T(8,128)(2,1)} %convolution_convert_fusion.4) | data formatting | bytes 7077888 | tf_op jit(solution)/shard_map/reshape | solution.py:28
  455.5 5.7 fusion.15
  461.3 22.1 %convolution_convert_fusion = bf16[4608,768]{1,0:T(8,128)(2,1)} fusion(bf16[1023,1536]{1,0:T(8,128)(2,1)} %slice_maximum_fusion, bf16[1024,1536]{1,0:T(8,128)(2,1)} %fusion.31, bf16[1024,768]{1,0:T(8,128)(2,1)S(1)} %get-tuple-element.38, bf16[1024,768]{1,0:T(8,128)(2,1)S(1)} %multiply_convert_fusion.2, f32[1024,768]{1,0:T(8,128)} %get-tuple-element.108, ...), kind=kOutput, calls=%fused_computation.19 | convolution fusion | flops 7314997248 | bytes 22807552 | tf_op jit(solution)/shard_map/dot_general | solution.py:73
  485.4 10.3 %convolution_convert_fusion.2 = bf16[768,3072]{1,0:T(8,128)(2,1)} fusion(bf16[1024,3072]{1,0:T(8,128)(2,1)} %fusion.7, f32[1024,768]{1,0:T(8,128)S(1)} %copy-done.23, f32[768]{0:T(1024)S(1)} %copy-done.72, f32[1024]{0:T(1024)S(1)} %copy-done.74, f32[1024]{0:T(1024)S(1)} %copy-done.63), kind=kOutput, calls=%fused_computation.27 | convolution fusion | flops 4837343232 | bytes 14167040 | tf_op jit(solution)/shard_map/dot_general | solution.py:73
  495.6 9.8 %reshape.379 = bf16[32,24,4,768]{3,2,1,0:T(4,128)(2,1)} reshape(bf16[768,3072]{1,0:T(8,128)(2,1)} %convolution_convert_fusion.2) | data formatting | bytes 9437184 | tf_op jit(solution)/shard_map/reshape | solution.py:28
  505.5 5.6 copy.147
  511.1 53.5 %shard_map.470 = (bf16[768,1536]{1,0:T(8,128)(2,1)S(1)}, bf16[256,768]{1,0:T(8,128)(2,1)S(1)}) custom-call(s32[4096]{0:T(1024)S(1)} %bitcast.148, s32[4096]{0:T(1024)S(1)} %copy-done.8, f32[1024,768]{1,0:T(8,128)} %get-tuple-element.93.upstream, f32[1024,1]{1,0:T(8,128)S(1)} %copy-done.2, bf16[256,768]{1,0:T(8,128)(2,1)S(1)} %copy-done.4, ...), custom_call_target="tpu_custom_call" | custom-call | flops 20000000000 | bytes 41943040 | tf_op jit(solution)/shard_map/pallas_call | solution.py:301
  569.0 11.7 %convolution_convert_fusion.3 = bf16[3072,768]{1,0:T(8,128)(2,1)S(1)} fusion(f32[1024,768]{1,0:T(8,128)} %get-tuple-element.81, f32[1024]{0:T(1024)S(1)} %copy-done.79, f32[1024,3072]{1,0:T(8,128)} %fusion.50), kind=kOutput, calls=%fused_computation.28 | convolution fusion | flops 4864081920 | bytes 20451328 | tf_op jit(solution)/shard_map/dot_general | solution.py:73
  580.8 5.4 pad_maximum_fusion
  588.3 7.2 add_convert_fusion
  598.4 17.6 %collective-permute-done.3 = bf16[512,768]{1,0:T(8,128)(2,1)S(1)} collective-permute-done((bf16[512,768]{1,0:T(8,128)(2,1)S(1)}, bf16[512,768]{1,0:T(8,128)(2,1)S(1)}, u32[]{:S(2)}, u32[]{:S(2)}) %collective-permute-start.3) | collective-permute-done | bytes 786464 | tf_op jit(solution)/shard_map/ppermute | solution.py:22
  617.5 19.9 %collective-permute-done.1 = bf16[512,768]{1,0:T(8,128)(2,1)S(1)} collective-permute-done((bf16[512,768]{1,0:T(8,128)(2,1)S(1)}, bf16[512,768]{1,0:T(8,128)(2,1)S(1)}, u32[]{:S(2)}, u32[]{:S(2)}) %collective-permute-start.1) | collective-permute-done | bytes 786464 | tf_op jit(solution)/shard_map/ppermute | solution.py:22
  643.9 53.2 %reduce-scatter.8.cloned.1.call-done = bf16[144,768]{1,0:T(8,128)(2,1)} async-done(((bf16[4608,768]{1,0:T(8,128)(2,1)}), bf16[144,768]{1,0:T(8,128)(2,1)}) %reduce-scatter.8.cloned.1.call-update) | async-done | bytes 221200 | tf_op jit(solution)/shard_map/reduce_scatter | solution.py:58
  699.3 155.3 %reduce-scatter.6.cloned.1.call-done = bf16[248,768]{1,0:T(8,128)(2,1)} async-done(((bf16[7936,768]{1,0:T(8,128)(2,1)}), bf16[248,768]{1,0:T(8,128)(2,1)}) %reduce-scatter.6.cloned.1.call-update) | async-done | bytes 380944 | tf_op jit(solution)/shard_map/reduce_scatter | solution.py:58
  (332 shorter events, 120.5 us)
Async XLA Ops:
  7.2 82.3 %all-gather.5.cloned.1.call-start = ((), (), s32[]{:S(2)}) async-start(), calls=%async_computation.6 | async-start | bytes 6488064 | tf_op jit(solution)/shard_map/all_gather | solution.py:44
  10.9 201.1 %all-gather.7.cloned.1.call-start = ((), (), s32[]{:S(2)}) async-start(), calls=%async_computation.7 | async-start | bytes 18653184 | tf_op jit(solution)/shard_map/all_gather | solution.py:44
  14.6 624.3 %reduce-scatter.4.cloned.1.call-start = ((), (), s32[]{:S(2)}) async-start(), calls=%async_computation.3 | async-start | bytes 5271552 | tf_op jit(solution)/shard_map/reduce_scatter | solution.py:58
  15.7 126.3 %copy-start.41 = (bf16[512,768]{1,0:T(8,128)(2,1)}, bf16[512,768]{1,0:T(8,128)(2,1)S(1)}, u32[]{:S(2)}) copy-start(bf16[512,768]{1,0:T(8,128)(2,1)S(1)} %get-tuple-element.101) | copy-start | bytes 2359300
  15.7 126.3 %collective-permute-start = (bf16[512,768]{1,0:T(8,128)(2,1)}, bf16[512,768]{1,0:T(8,128)(2,1)}, u32[]{:S(2)}, u32[]{:S(2)}) collective-permute-start(bf16[512,768]{1,0:T(8,128)(2,1)} %get-tuple-element.102), channel_id=1, source_target_pairs={{0,16},{16,0},{1,17},{17,1},{2,18},{18,2},{3,19},{19,3},{4,20},{20... | collective-permute-start | bytes 2359304 | tf_op jit(solution)/shard_map/ppermute | solution.py:22
  19.9 269.8 %collective-permute-start.2 = (bf16[512,768]{1,0:T(8,128)(2,1)}, bf16[512,768]{1,0:T(8,128)(2,1)}, u32[]{:S(2)}, u32[]{:S(2)}) collective-permute-start(bf16[512,768]{1,0:T(8,128)(2,1)} %get-tuple-element.99), channel_id=1, source_target_pairs={{0,16},{16,0},{1,17},{17,1},{2,18},{18,2},{3,19},{19,3},{4,20},{20... | collective-permute-start | bytes 2359304 | tf_op jit(solution)/shard_map/ppermute | solution.py:22
  29.3 70.8 %copy-start.5 = (s32[1,4096]{1,0:T(1,128)}, s32[1,4096]{1,0:T(1,128)S(1)}, u32[]{:S(2)}) copy-start(s32[1,4096]{1,0:T(1,128)S(1)} %broadcast_select_fusion.2) | copy-start | bytes 49156
  29.7 70.4 %copy-start.7 = (s32[4096]{0:T(1024)}, s32[4096]{0:T(1024)S(1)}, u32[]{:S(2)}) copy-start(s32[4096]{0:T(1024)S(1)} %add_bitcast_fusion.owners) | copy-start | bytes 49156
  29.8 70.3 %copy-start.1 = (f32[1024,1]{1,0:T(8,128)}, f32[1024,1]{1,0:T(8,128)S(1)}, u32[]{:S(2)}) copy-start(f32[1024,1]{1,0:T(8,128)S(1)} %convert_divide_fusion.shares) | copy-start | bytes 12292
  96.7 45.3 %copy-start.28 = (bf16[96,8,3,768]{3,1,2,0:T(8,128)(2,1)}, bf16[96,8,3,768]{3,1,2,0:T(8,128)(2,1)S(1)}, u32[]{:S(2)}) copy-start(bf16[96,8,3,768]{3,1,2,0:T(8,128)(2,1)S(1)} %copy.155) | copy-start | bytes 10616836
  100.1 38.6 %copy-start.3 = (bf16[256,768]{1,0:T(8,128)(2,1)}, bf16[256,768]{1,0:T(8,128)(2,1)S(1)}, u32[]{:S(2)}) copy-start(bf16[256,768]{1,0:T(8,128)(2,1)S(1)} %slice_bitcast_fusion.table) | copy-start | bytes 1179652
  184.7 38.8 %copy-start.13 = (bf16[1024,768]{1,0:T(8,128)(2,1)}, bf16[1024,768]{1,0:T(8,128)(2,1)S(1)}, u32[]{:S(2)}) copy-start(bf16[1024,768]{1,0:T(8,128)(2,1)S(1)} %get-tuple-element.37) | copy-start | bytes 4718596
  226.5 19.6 %copy-start.62 = (f32[1024]{0:T(1024)}, f32[1024]{0:T(1024)S(1)}, u32[]{:S(2)}) copy-start(f32[1024]{0:T(1024)S(1)} %broadcast_multiply_fusion.2) | copy-start | bytes 12292
  299.6 34.7 %copy-start.24 = (f32[1024,768]{1,0:T(8,128)}, f32[1024,768]{1,0:T(8,128)S(1)}, u32[]{:S(2)}) copy-start(f32[1024,768]{1,0:T(8,128)S(1)} %get-tuple-element.84) | copy-start | bytes 9437188
  337.9 20.7 %slice-start.4 = ((s8[4718592]{0:T(1024)(128)(4,1)}), s8[4194304]{0:T(1024)(128)(4,1)S(1)}, s32[]{:S(2)}) async-start(s8[4718592]{0:T(1024)(128)(4,1)} %bitcast.176), calls=%async_computation.12 | async-start | bytes 8388608
  340.5 18.1 %copy-start.63 = (f32[1024]{0:T(1024)S(1)}, f32[1024]{0:T(1024)}, u32[]{:S(2)}) copy-start(f32[1024]{0:T(1024)} %copy-done.62) | copy-start | bytes 12292
  461.2 235.9 %reduce-scatter.8.cloned.1.call-start = ((), (), s32[]{:S(2)}) async-start(), calls=%async_computation.5 | async-start | bytes 7299072 | tf_op jit(solution)/shard_map/reduce_scatter | solution.py:58
  483.4 371.2 %reduce-scatter.6.cloned.1.call-start = ((), (), s32[]{:S(2)}) async-start(), calls=%async_computation.4 | async-start | bytes 12570624 | tf_op jit(solution)/shard_map/reduce_scatter | solution.py:58
  595.6 20.4 %collective-permute-start.3 = (bf16[512,768]{1,0:T(8,128)(2,1)S(1)}, bf16[512,768]{1,0:T(8,128)(2,1)S(1)}, u32[]{:S(2)}, u32[]{:S(2)}) collective-permute-start(bf16[512,768]{1,0:T(8,128)(2,1)S(1)} %broadcast_select_fusion), channel_id=1, source_target_pairs={{0,16},{16,0},{1,17},{17,1},{2,18},{18,2},{3,19},{19,3},{4,20},{20... | collective-permute-start | bytes 2359304 | tf_op jit(solution)/shard_map/ppermute | solution.py:22
  597.1 40.4 %collective-permute-start.1 = (bf16[512,768]{1,0:T(8,128)(2,1)S(1)}, bf16[512,768]{1,0:T(8,128)(2,1)S(1)}, u32[]{:S(2)}, u32[]{:S(2)}) collective-permute-start(bf16[512,768]{1,0:T(8,128)(2,1)S(1)} %broadcast_select_fusion.1), channel_id=1, source_target_pairs={{0,16},{16,0},{1,17},{17,1},{2,18},{18,2},{3,19},{19,3},{4,20},{20... | collective-permute-start | bytes 2359304 | tf_op jit(solution)/shard_map/ppermute | solution.py:22
  637.7 59.5 %copy-start.32 = (f32[144,768]{1,0:T(8,128)S(1)}, f32[144,768]{1,0:T(8,128)}, u32[]{:S(2)}) copy-start(f32[144,768]{1,0:T(8,128)} %param.47) | copy-start | bytes 1327108
  637.7 59.5 %copy-start.47 = (f32[144,768]{1,0:T(8,128)S(1)}, f32[144,768]{1,0:T(8,128)}, u32[]{:S(2)}) copy-start(f32[144,768]{1,0:T(8,128)} %param.48) | copy-start | bytes 1327108
  637.7 59.4 %copy-start.48 = (f32[144,768]{1,0:T(8,128)S(1)}, f32[144,768]{1,0:T(8,128)}, u32[]{:S(2)}) copy-start(f32[144,768]{1,0:T(8,128)} %param.49) | copy-start | bytes 1327108
  643.9 212.9 %copy-start.39 = (f32[96,768]{1,0:T(8,128)S(1)}, f32[96,768]{1,0:T(8,128)}, u32[]{:S(2)}) copy-start(f32[96,768]{1,0:T(8,128)} %param.41) | copy-start | bytes 884740
  643.9 212.9 %copy-start.52 = (f32[96,768]{1,0:T(8,128)S(1)}, f32[96,768]{1,0:T(8,128)}, u32[]{:S(2)}) copy-start(f32[96,768]{1,0:T(8,128)} %param.42) | copy-start | bytes 884740
  643.9 212.9 %copy-start.53 = (f32[96,768]{1,0:T(8,128)S(1)}, f32[96,768]{1,0:T(8,128)}, u32[]{:S(2)}) copy-start(f32[96,768]{1,0:T(8,128)} %param.43) | copy-start | bytes 884740
  643.9 214.9 %copy-start.58 = (f32[8,768]{1,0:T(8,128)S(1)}, f32[8,768]{1,0:T(8,128)}, u32[]{:S(2)}) copy-start(f32[8,768]{1,0:T(8,128)} %param.50) | copy-start | bytes 73732
  643.9 214.9 %copy-start.69 = (f32[8,768]{1,0:T(8,128)S(1)}, f32[8,768]{1,0:T(8,128)}, u32[]{:S(2)}) copy-start(f32[8,768]{1,0:T(8,128)} %param.51) | copy-start | bytes 73732
  643.9 214.9 %copy-start.70 = (f32[8,768]{1,0:T(8,128)S(1)}, f32[8,768]{1,0:T(8,128)}, u32[]{:S(2)}) copy-start(f32[8,768]{1,0:T(8,128)} %param.52) | copy-start | bytes 73732
  699.3 160.8 %copy-start.37 = (f32[24,3072]{1,0:T(8,128)S(1)}, f32[24,3072]{1,0:T(8,128)}, u32[]{:S(2)}) copy-start(f32[24,3072]{1,0:T(8,128)} %param.38) | copy-start | bytes 884740
  699.3 160.8 %copy-start.49 = (f32[24,3072]{1,0:T(8,128)S(1)}, f32[24,3072]{1,0:T(8,128)}, u32[]{:S(2)}) copy-start(f32[24,3072]{1,0:T(8,128)} %param.39) | copy-start | bytes 884740
  699.3 160.8 %copy-start.50 = (f32[24,3072]{1,0:T(8,128)S(1)}, f32[24,3072]{1,0:T(8,128)}, u32[]{:S(2)}) copy-start(f32[24,3072]{1,0:T(8,128)} %param.40) | copy-start | bytes 884740
  (71 other events, 429.4 us)
Sparse Core Ops, SparseCore 0:
  11.5 77.9 all-gather.4
  92.4 119.5 all-gather.6
  461.3 107.2 reduce-scatter.3
  575.1 121.9 reduce-scatter.7
  703.1 151.4 reduce-scatter.5

commit v2 on v1

v2 whole, which is shorter than its diff:
```python
import functools

import jax
import jax.numpy as jnp
from jax import lax
from jax.experimental import pallas as pl
from jax.experimental.pallas import tpu as pltpu
from jax.sharding import PartitionSpec as P

D = 768
HEADS = 12
FF = 3072
LEN = 1024
STEP = 5


def partner(block, axis, apart):
    count = lax.axis_size(axis)
    route = []
    for low in range(count):
        high = low | 1 << apart
        if high != low and high < count:
            route += [(low, high), (high, low)]
    return lax.ppermute(block, axis, route)


def to_rows(matrix, parts):
    side = matrix.shape[1] // D
    own = matrix.shape[0] // parts
    blocks = matrix.astype(jnp.bfloat16).reshape(parts, own, side, D)
    return blocks.transpose(0, 2, 1, 3).reshape(parts, side * own, D)


def from_rows(rows, offset, own, side):
    parts = rows.shape[0]
    blocks = rows[:, offset : offset + own * side].reshape(parts, side, own, D)
    return blocks.transpose(0, 2, 1, 3).reshape(parts * own, side * D)


def gains_row(gains):
    return jnp.pad(gains.reshape(1, -1), ((0, 7), (0, D - gains.size)))


def swap_bit(block, bit):
    inner = lax.axis_size("dp").bit_length() - 1
    if bit < inner:
        return partner(block, "dp", bit)
    return partner(block, "stream", bit - inner)


def pair_bits():
    return (lax.axis_size("dp") * lax.axis_size("stream")).bit_length() - 2


def hop_order(turned):
    top = pair_bits()
    order = list(range(2, top)) + ([1, top] if turned else [top, 1])
    return order


def in_pairs(shapes):
    parts = lax.axis_size("dp") * lax.axis_size("stream")
    return parts >= 8 and parts & (parts - 1) == 0 and all(rows % 8 == 0 for rows, _ in shapes)


def my_place():
    return (lax.axis_index("stream") * lax.axis_size("dp") + lax.axis_index("dp")).reshape(1)


def shapes_of(matrices, parts):
    return [(matrix.shape[0] // parts, matrix.shape[1] // D) for matrix in matrices]


def assemble(shapes, place, mine, theirs, *weights):
    core = place[0] & 1
    low = (place[0] >> 1) & 3
    pieces = []
    for pair in range(4):
        own = mine[pair ^ low].astype(jnp.float32)
        other = theirs[pair ^ low].astype(jnp.float32)
        pieces.append(jnp.where(core == 0, own, other))
        pieces.append(jnp.where(core == 0, other, own))
    offset = 0
    for (rows, side), weight in zip(shapes, weights):
        for number in range(side):
            block = jnp.concatenate([piece[offset : offset + rows] for piece in pieces], 0)
            weight[:, number * D : number * D + D] = block.astype(weight.dtype)
            offset += rows


def apart(shapes, place, *refs):
    grads, keep, send = refs[: len(shapes)], refs[-2], refs[-1]
    core = place[0] & 1
    low = (place[0] >> 1) & 3
    for pair in range(4):
        halves = []
        for side in range(2):
            pieces = []
            for (rows, across), grad in zip(shapes, grads):
                first = (2 * pair + side) * rows
                for number in range(across):
                    pieces.append(
                        grad[first : first + rows, number * D : number * D + D].astype(jnp.float32)
                    )
            halves.append(jnp.concatenate(pieces, 0))
        keep[pair ^ low] = jnp.where(core == 0, halves[0], halves[1]).astype(keep.dtype)
        send[pair ^ low] = jnp.where(core == 0, halves[1], halves[0]).astype(send.dtype)


def turned_block(high):
    return pl.BlockSpec((4, high, D), lambda group, place: (group ^ (place[0] >> 3), 0, 0))


def natural_block(shape):
    return pl.BlockSpec((8 * shape[0], shape[1] * D), lambda group, place: (group, 0))


class Flow:
    def __init__(self):
        self.live = {}
        self.ended = {}

    def begin(self, name, chain, skips=()):
        self.step(name, chain, None, list(skips))

    def step(self, name, chain, arrays, skips):
        try:
            waiting = chain.send(arrays)
            self.live[name] = [chain, waiting, skips, skips.pop(0) if skips else 0]
        except StopIteration as stop:
            self.ended[name] = stop.value

    def slot(self, values):
        due = [name for name, entry in self.live.items() if entry[3] == 0]
        for entry in self.live.values():
            entry[3] -= 1
        values, waited = lax.optimization_barrier(
            (values, [self.live[name][1] for name in due])
        )
        for name, arrays in zip(due, waited):
            chain, _, skips, _ = self.live.pop(name)
            self.step(name, chain, arrays, skips)
        return values

    def end(self, name):
        return self.ended.pop(name)


def gather_chain(shards, turned):
    shapes = shapes_of(shards, 1)
    packed = jnp.concatenate([to_rows(shard, 1)[0] for shard in shards], 0)
    if not in_pairs(shapes):
        return gather_whole(packed, shapes)
    top = pair_bits()
    held = packed.reshape((1,) * top + packed.shape)
    for bit in hop_order(turned):
        other = swap_bit(held, bit)
        held, other = yield (held, other)
        held = jnp.concatenate([held, other], top - bit)
    other = swap_bit(held, 0)
    held, other = yield (held, other)
    return join_halves(shapes, held, other)


def gather_whole(packed, shapes):
    rows = lax.all_gather(packed, ("stream", "dp"), axis=0, tiled=False)
    pieces = []
    offset = 0
    for own, side in shapes:
        pieces.append(from_rows(rows, offset, own, side))
        offset += own * side
    return pieces


def join_halves(shapes, mine, theirs):
    high = mine.shape[-2]
    pairs = 1 << pair_bits()
    parts = 2 * pairs
    return pl.pallas_call(
        functools.partial(assemble, shapes),
        grid_spec=pltpu.PrefetchScalarGridSpec(
            num_scalar_prefetch=1,
            grid=(pairs // 4,),
            in_specs=[turned_block(high)] * 2,
            out_specs=[natural_block(shape) for shape in shapes],
        ),
        out_shape=[
            jax.ShapeDtypeStruct((parts * rows, side * D), jnp.bfloat16) for rows, side in shapes
        ],
        compiler_params=pltpu.CompilerParams(vmem_limit_bytes=40 << 20),
        cost_estimate=pl.CostEstimate(
            flops=0, bytes_accessed=4 * parts * high * D, transcendentals=0
        ),
    )(my_place(), mine.reshape(pairs, high, D), theirs.reshape(pairs, high, D))


def scatter_whole(grads):
    parts = lax.axis_size("dp") * lax.axis_size("stream")
    packed = jnp.concatenate([to_rows(grad, parts) for grad in grads], 1)
    total = lax.psum_scatter(
        packed.reshape(-1, D), ("stream", "dp"), scatter_dimension=0, tiled=True
    ).astype(jnp.float32)
    return own_pieces(total, shapes_of(grads, parts))


def own_pieces(total, shapes):
    pieces = []
    offset = 0
    for own, side in shapes:
        pieces.append(from_rows(total[None], offset, own, side))
        offset += own * side
    return pieces


def scatter_chain(grads, turned):
    parts = lax.axis_size("dp") * lax.axis_size("stream")
    shapes = shapes_of(grads, parts)
    if not in_pairs(shapes):
        return scatter_whole(grads)
    pairs = parts // 2
    high = sum(rows * side for rows, side in shapes)
    half = jax.ShapeDtypeStruct((pairs, high, D), jnp.bfloat16)
    kept, sent = pl.pallas_call(
        functools.partial(apart, shapes),
        grid_spec=pltpu.PrefetchScalarGridSpec(
            num_scalar_prefetch=1,
            grid=(pairs // 4,),
            in_specs=[natural_block(shape) for shape in shapes],
            out_specs=[turned_block(high)] * 2,
        ),
        out_shape=[half, half],
        compiler_params=pltpu.CompilerParams(vmem_limit_bytes=40 << 20),
        cost_estimate=pl.CostEstimate(
            flops=0, bytes_accessed=4 * parts * high * D, transcendentals=0
        ),
    )(my_place(), *[grad.astype(jnp.bfloat16) for grad in grads])
    other = swap_bit(sent, 0)
    kept, other = yield (kept, other)
    total = kept.astype(jnp.float32) + other.astype(jnp.float32)
    top = pair_bits()
    total = total.reshape((2,) * top + (high, D))
    for bit in reversed(hop_order(turned)):
        axis = top - bit
        other = swap_bit(lax.slice_in_dim(total, 1, 2, axis=axis).astype(jnp.bfloat16), bit)
        kept, other = yield (lax.slice_in_dim(total, 0, 1, axis=axis), other)
        total = kept + other.astype(jnp.float32)
    return own_pieces(total.reshape(high, D), shapes)


def swap_chain(block):
    other = yield partner(block, "stream", 0)
    return other


def product(former, latter):
    return jnp.dot(former, latter, preferred_element_type=jnp.float32)


def inner_rows(former, latter):
    return lax.dot_general(
        former, latter, (((0,), (0,)), ((), ())), preferred_element_type=jnp.float32
    )


def inner_cols(former, latter):
    return lax.dot_general(
        former, latter, (((1,), (1,)), ((), ())), preferred_element_type=jnp.float32
    )


def norm_gain(values, scales):
    center = jnp.mean(values, axis=-1, keepdims=True)
    shifted = values - center
    spread = jnp.mean(shifted * shifted, axis=-1, keepdims=True)
    return shifted * lax.rsqrt(spread + 1e-05) * scales


def rows_before(matrix):
    return jnp.concatenate([jnp.zeros_like(matrix[:1]), matrix[:-1]], 0)


def rows_after(matrix):
    return jnp.concatenate([matrix[1:], jnp.zeros_like(matrix[:1])], 0)


def char_segments(lengths, char_count):
    starts = jnp.cumsum(lengths) - lengths
    markers = jnp.zeros((char_count,), jnp.int32).at[starts].add(1)
    return jnp.cumsum(markers) - 1


def step_rates():
    return (
        0.5 * D ** (-0.5),
        0.5 * (3 * D // LEN) ** (-0.5),
        0.5 * D ** (-0.5),
        0.5 * FF ** (-0.5),
        0.5 * D ** (-0.5),
        0.5 * (6 * D) ** (-0.5),
        0.5,
        0.2,
    )


def adamw(master, first_m, second_m, grad_sum, step_rate):
    mean_new = 0.5 * first_m + 0.5 * grad_sum
    power = 0.5 * second_m + 0.5 * grad_sum * grad_sum
    correct = 1.0 - 0.5**STEP
    fresh_w = master - step_rate * (
        mean_new / correct / (jnp.sqrt(power / correct) + 1e-08) + 0.01 * master
    )
    return (fresh_w, mean_new, power)


STEP_ROWS = 512
UNROLL = 8


def contract(former, latter, left, right):
    return lax.dot_general(
        former, latter, (((left,), (right,)), ((), ())), preferred_element_type=jnp.float32
    )


def lane_blocks(width):
    blocks = []
    for number in range(2 * width // 128):
        side, lane = divmod(number * 128, width)
        blocks.append((number * 128, 2 * side * width + lane, 4 * side + lane // 128))
    return blocks


def eight(offset):
    return pl.ds(pl.multiple_of(offset, 8), 8)


def chars_ahead(rows_f, rows_b, ends, table, w_gru, shares, letters, before, pooled, running, spans, carry):
    block = pl.program_id(0)
    total = rows_f.shape[0]
    width = w_gru.shape[1] // 4

    @pl.when(block == 0)
    def start():
        logits = jnp.dot(table[...], w_gru[...], preferred_element_type=jnp.float32)
        letters[...] = jnp.zeros_like(letters)
        carry[...] = jnp.zeros_like(carry)
        for _, left, place in lane_blocks(width):
            update = jax.nn.sigmoid(logits[:, left : left + 128])
            letters[:, place, :] = 1.0 - update
            letters[:, 8 + place, :] = update * logits[:, left + width : left + width + 128]

    leading = lax.broadcasted_iota(jnp.int32, (8, 128), 0) < 4

    def several(group, held):
        state, total_state = held
        first = block * STEP_ROWS + group * UNROLL
        factors, adds = [], []
        for inner in range(UNROLL):
            id_f, id_b = rows_f[first + inner], rows_b[first + inner]
            factors.append(jnp.where(leading, letters[id_f, 0:8], letters[id_b, 0:8]))
            adds.append(jnp.where(leading, letters[id_f, 8:16], letters[id_b, 8:16]))
        for inner in range(UNROLL):
            before[group * UNROLL + inner] = state
            running[first + inner] = total_state
            state = factors[inner] * state + adds[inner]
            total_state = total_state + state
        return state, total_state

    state, total_state = lax.fori_loop(0, STEP_ROWS // UNROLL, several, (carry[0], carry[1]))
    carry[0] = state
    carry[1] = total_state

    @pl.when(block == pl.num_programs(0) - 1)
    def finish():
        running[total] = total_state

        def tokens(group, prior):
            found = []
            for inner in range(UNROLL):
                end = ends[group * UNROLL + inner]
                found.append(jnp.where(leading, running[end], -running[total - end]))
            for inner in range(UNROLL):
                spans[group * UNROLL + inner] = found[inner] - prior
                prior = found[inner]
            return prior

        lax.fori_loop(0, ends.shape[0] // UNROLL, tokens, jnp.where(leading, running[0], -running[total]))
        for at, _, place in lane_blocks(width):
            pooled[:, at : at + 128] = (spans[:, place, :] * shares[...]).astype(pooled.dtype)


def chars_back(
    rows_f, rows_b, owners_f, owners_b, upstream, shares, table, w_gru, letters, before,
    grad_gru, grad_table, spread, sums_f, sums_b, more_f, more_b, full, carry
):
    block = pl.num_programs(0) - 1 - pl.program_id(0)
    width = full.shape[1] // 4

    @pl.when(pl.program_id(0) == 0)
    def start():
        for held in (sums_f, sums_b, more_f, more_b):
            held[...] = jnp.zeros_like(held)
        carry[...] = jnp.zeros_like(carry)
        for at, _, place in lane_blocks(width):
            spread[:, place, :] = upstream[:, at : at + 128] * shares[...]
        for place in (3, 7):
            spread[:, place, :] = jnp.zeros((spread.shape[0], 128), jnp.float32)

    leading = lax.broadcasted_iota(jnp.int32, (8, 128), 0) < 4

    def several(group, passed):
        steps = [STEP_ROWS - 1 - group * UNROLL - inner for inner in range(UNROLL)]
        kept, given, priors, owned = [], [], [], []
        for step in steps:
            place = block * STEP_ROWS + step
            id_f, id_b = rows_f[place], rows_b[place]
            owned.append((id_f, id_b))
            kept.append(jnp.where(leading, letters[id_f, 0:8], letters[id_b, 0:8]))
            given.append(jnp.where(leading, spread[owners_f[place]], spread[owners_b[place]]))
            priors.append(before[step])
        for inner in range(UNROLL):
            carried = given[inner] + passed
            passed = kept[inner] * carried
            moved = carried * priors[inner]
            id_f, id_b = owned[inner]
            for held, row, value in (
                ((sums_f, more_f)[inner % 2], id_f, jnp.where(leading, carried, pltpu.roll(moved, 4, 0))),
                ((sums_b, more_b)[inner % 2], id_b, jnp.where(leading, pltpu.roll(carried, 4, 0), moved)),
            ):
                held[row] += value
        return passed

    carry[...] = lax.fori_loop(0, STEP_ROWS // UNROLL, several, carry[...])

    @pl.when(block == 0)
    def finish():
        sums_f[...] += more_f[...]
        sums_b[...] += more_b[...]
        for _, left, place in lane_blocks(width):
            found = sums_f if place < 4 else sums_b
            lane = place % 4
            kept = letters[:, place, :]
            update = 1.0 - kept
            total = found[:, lane, :]
            full[:, left : left + 128] = kept * (
                letters[:, 8 + place, :] * total - update * found[:, 4 + lane, :]
            )
            full[:, left + width : left + width + 128] = update * total
        upper = full[...].astype(jnp.bfloat16)
        lower = (full[...] - upper.astype(jnp.float32)).astype(jnp.bfloat16)
        grad_gru[...] = (
            contract(table[...], upper, 0, 0) + contract(table[...], lower, 0, 0)
        ).astype(grad_gru.dtype)
        grad_table[...] = (
            contract(upper, w_gru[...], 1, 1) + contract(lower, w_gru[...], 1, 1)
        ).astype(grad_table.dtype)


def whole(array):
    return pl.BlockSpec(array.shape, lambda block: (0,) * len(array.shape))


def scalars():
    return pl.BlockSpec(memory_space=pltpu.SMEM)


def run_chars(ids, ends, table, w_gru, shares):
    total, count = ids.shape[0], shares.shape[0]
    f32 = jnp.float32
    outs = (
        jax.ShapeDtypeStruct((table.shape[0], 16, 128), f32),
        jax.ShapeDtypeStruct((total, 8, 128), f32),
        jax.ShapeDtypeStruct((count, w_gru.shape[1] // 2), jnp.bfloat16),
    )
    return pl.pallas_call(
        chars_ahead,
        grid=(total // STEP_ROWS,),
        in_specs=[scalars(), scalars(), scalars(), whole(table), whole(w_gru), whole(shares)],
        out_specs=[
            whole(outs[0]),
            pl.BlockSpec((STEP_ROWS, 8, 128), lambda block: (block, 0, 0)),
            whole(outs[2]),
        ],
        out_shape=outs,
        scratch_shapes=[
            pltpu.VMEM((total + 1, 8, 128), f32),
            pltpu.VMEM((count, 8, 128), f32),
            pltpu.VMEM((2, 8, 128), f32),
        ],
        compiler_params=pltpu.CompilerParams(vmem_limit_bytes=56 << 20),
        cost_estimate=pl.CostEstimate(
            flops=20_000_000_000, bytes_accessed=40 << 20, transcendentals=0
        ),
    )(ids, jnp.flip(ids), ends, table, w_gru, shares)


def run_chars_back(ids, owners, upstream, shares, table, w_gru, letters, before):
    total, count = ids.shape[0], shares.shape[0]
    f32 = jnp.float32
    blocks = total // STEP_ROWS
    outs = (
        jax.ShapeDtypeStruct(w_gru.shape, jnp.bfloat16),
        jax.ShapeDtypeStruct(table.shape, jnp.bfloat16),
    )
    return pl.pallas_call(
        chars_back,
        grid=(blocks,),
        in_specs=[scalars()] * 4
        + [
            whole(upstream),
            whole(shares),
            whole(table),
            whole(w_gru),
            whole(letters),
            pl.BlockSpec((STEP_ROWS, 8, 128), lambda block: (blocks - 1 - block, 0, 0)),
        ],
        out_specs=[whole(outs[0]), whole(outs[1])],
        out_shape=outs,
        scratch_shapes=[
            pltpu.VMEM((count, 8, 128), f32),
            pltpu.VMEM((table.shape[0], 8, 128), f32),
            pltpu.VMEM((table.shape[0], 8, 128), f32),
            pltpu.VMEM((table.shape[0], 8, 128), f32),
            pltpu.VMEM((table.shape[0], 8, 128), f32),
            pltpu.VMEM((table.shape[0], w_gru.shape[1]), f32),
            pltpu.VMEM((8, 128), f32),
        ],
        compiler_params=pltpu.CompilerParams(vmem_limit_bytes=56 << 20),
        cost_estimate=pl.CostEstimate(
            flops=20_000_000_000, bytes_accessed=40 << 20, transcendentals=0
        ),
    )(ids, jnp.flip(ids), owners, jnp.flip(owners), upstream, shares, table, w_gru, letters, before)


ROWS = 256


def attend(queries, key_rows, value_rows, context, logsum):
    size = key_rows.shape[1] // 2
    lanes = lax.broadcasted_iota(jnp.int32, (1, 2 * size), 1)
    scale = size ** (-0.5)

    def some_rows(number, _):
        at = pl.ds(pl.multiple_of(number * ROWS, ROWS), ROWS)
        row_block = queries[at, :]
        parts = []
        sums = []
        for head in range(2):
            own = (lanes < size) if head == 0 else (lanes >= size)
            scores = contract(jnp.where(own, row_block, 0) * scale, key_rows[...], 1, 1)
            row_max = jnp.max(scores, axis=-1, keepdims=True)
            exponent = jnp.exp(scores - row_max)
            row_total = jnp.sum(exponent, axis=-1, keepdims=True)
            probs = (exponent * (1.0 / row_total)).astype(jnp.bfloat16)
            parts.append(contract(probs, value_rows[...], 1, 0))
            sums.append(row_max + jnp.log(row_total))
        context[at, :] = jnp.where(lanes < size, parts[0], parts[1]).astype(context.dtype)
        both = jnp.where(lanes < size, sums[0], sums[1])
        turned = jnp.transpose(both)
        logsum[0:8, at] = turned[0:8]
        logsum[8:16, at] = turned[size : size + 8]
        return 0

    lax.fori_loop(0, queries.shape[0] // ROWS, some_rows, 0)


def attend_back(queries, key_rows, value_rows, logsum, grads, query_grad, key_grad, value_grad, key_sum, value_sum):
    size = key_rows.shape[1] // 2
    lanes = lax.broadcasted_iota(jnp.int32, (1, 2 * size), 1)
    scale = size ** (-0.5)
    key_sum[...] = jnp.zeros_like(key_sum)
    value_sum[...] = jnp.zeros_like(value_sum)

    def some_rows(number, _):
        at = pl.ds(pl.multiple_of(number * ROWS, ROWS), ROWS)
        row_block = queries[at, :]
        grad_block = grads[at, :]
        parts = []
        for head in range(2):
            own = (lanes < size) if head == 0 else (lanes >= size)
            own_rows = jnp.where(own, row_block, 0) * scale
            own_grads = jnp.where(own, grad_block, 0)
            scores = contract(key_rows[...], own_rows, 1, 1)
            probs = jnp.exp(scores - logsum[8 * head : 8 * head + 1, at])
            value_sum[...] += contract(probs.astype(jnp.bfloat16), own_grads, 1, 0)
            prob_grad = contract(value_rows[...], own_grads, 1, 1)
            center = jnp.sum(prob_grad * probs, axis=0, keepdims=True)
            score_grad = (probs * (prob_grad - center)).astype(jnp.bfloat16)
            key_sum[...] += contract(score_grad, own_rows, 1, 0)
            parts.append(contract(score_grad, key_rows[...], 0, 0))
        query_grad[at, :] = (
            jnp.where(lanes < size, parts[0], parts[1]) * scale
        ).astype(query_grad.dtype)
        return 0

    lax.fori_loop(0, queries.shape[0] // ROWS, some_rows, 0)
    key_grad[...] = key_sum[...].astype(key_grad.dtype)
    value_grad[...] = value_sum[...].astype(value_grad.dtype)


def column(rows, width, offset):
    return pl.BlockSpec((rows, width), lambda pair: (0, offset + pair))


def run_attend(qkv):
    length, across = qkv.shape
    model = across // 3
    pairs = model // 128
    return pl.pallas_call(
        attend,
        grid=(pairs,),
        in_specs=[column(length, 128, pairs * part) for part in range(3)],
        out_specs=[column(length, 128, 0), pl.BlockSpec((16, length), lambda pair: (pair, 0))],
        out_shape=(
            jax.ShapeDtypeStruct((length, model), jnp.bfloat16),
            jax.ShapeDtypeStruct((16 * pairs, length), jnp.float32),
        ),
        compiler_params=pltpu.CompilerParams(vmem_limit_bytes=40 << 20),
        cost_estimate=pl.CostEstimate(flops=4 * length * length * model, bytes_accessed=8 * length * model, transcendentals=length * length * 12),
    )(qkv, qkv, qkv)


def run_attend_back(qkv, logsum, grads):
    length, across = qkv.shape
    model = across // 3
    pairs = model // 128
    part = jax.ShapeDtypeStruct((length, model), jnp.bfloat16)
    return pl.pallas_call(
        attend_back,
        grid=(pairs,),
        in_specs=[column(length, 128, pairs * part) for part in range(3)]
        + [pl.BlockSpec((16, length), lambda pair: (pair, 0)), column(length, 128, 0)],
        out_specs=[column(length, 128, 0)] * 3,
        out_shape=(part, part, part),
        scratch_shapes=[pltpu.VMEM((length, 128), jnp.float32)] * 2,
        compiler_params=pltpu.CompilerParams(vmem_limit_bytes=40 << 20),
        cost_estimate=pl.CostEstimate(flops=10 * length * length * model, bytes_accessed=16 * length * model, transcendentals=length * length * 12),
    )(qkv, qkv, qkv, logsum, grads)


def on_device(
    tokens_in,
    char_ids,
    char_lengths,
    out_grad,
    w_qkv,
    first_qkv,
    second_qkv,
    w_out,
    first_out,
    second_out,
    w_up,
    first_up,
    second_up,
    w_down,
    first_down,
    second_down,
    w_gru,
    first_gru,
    second_gru,
    w_blend,
    first_blend,
    second_blend,
    char_table,
    first_table,
    second_table,
    gains,
    first_gains,
    second_gains,
):
    masters = (w_qkv, w_out, w_up, w_down, w_gru, w_blend, char_table, gains)
    firsts = (
        first_qkv,
        first_out,
        first_up,
        first_down,
        first_gru,
        first_blend,
        first_table,
        first_gains,
    )
    seconds = (
        second_qkv,
        second_out,
        second_up,
        second_down,
        second_gru,
        second_blend,
        second_table,
        second_gains,
    )
    parts = lax.axis_size("stream") * lax.axis_size("dp")
    on_first = lax.axis_index("stream") == 0
    half_len = tokens_in.shape[1]
    flow = Flow()

    def both_halves(pair, got):
        kept = jnp.where(on_first, pair[0], pair[1])
        return jnp.where(
            on_first, jnp.concatenate([kept, got], 0), jnp.concatenate([got, kept], 0)
        )

    groups = 3
    by_group = w_qkv.reshape(w_qkv.shape[0], 3, groups, -1).transpose(0, 2, 1, 3)
    by_group = by_group.reshape(w_qkv.shape[0], groups, -1)
    ids_row = jnp.where(on_first, char_ids[0], char_ids[1])
    lengths_row = jnp.where(on_first, char_lengths[0], char_lengths[1])
    segment = char_segments(lengths_row, ids_row.shape[0])
    shares = 1.0 / lengths_row.astype(jnp.float32)[:, None]
    ends = jnp.cumsum(lengths_row)

    flow.begin("tokens", swap_chain(jnp.where(on_first, tokens_in[1], tokens_in[0])), [4])
    flow.begin("first", gather_chain([by_group[:, 0]], False))
    flow.begin("second", gather_chain([by_group[:, 1]], True))
    flow.slot(())
    flow.slot(())
    flow.begin("third", gather_chain([by_group[:, 2], w_out], True))
    flow.slot(())
    shards = flow.slot((char_table, w_gru, gains_row(gains), w_blend))
    flow.begin("up", gather_chain([w_up], True), [0, 0, 0, 1, 0])
    shapes = shapes_of(shards[:3], 1)
    packed = jnp.concatenate([to_rows(shard, 1)[0] for shard in shards[:3]], 0)
    rest = gather_whole(packed, shapes)
    blend_all = lax.all_gather(
        shards[3].astype(jnp.bfloat16), ("stream", "dp"), axis=0, tiled=True
    )
    flow.slot(())
    tokens = both_halves(tokens_in, flow.end("tokens"))
    (w_first,) = flow.end("first")
    (w_second,) = flow.end("second")
    flow.begin("down", gather_chain([w_down], True), [0, 0, 0, 1, 0])
    flow.begin("out_grad", swap_chain(jnp.where(on_first, out_grad[1], out_grad[0])), [2])
    qkv_parts, contexts, logsums = [], [], []

    def attend_group(w_group):
        qkv = product(tokens, w_group).astype(jnp.bfloat16)
        context, logsum = run_attend(qkv)
        return qkv, context, logsum

    qkv, context, logsum = attend_group(w_first)
    qkv, context, logsum, tokens = flow.slot((qkv, context, logsum, tokens))
    qkv_parts.append(qkv)
    contexts.append(context)
    logsums.append(logsum)
    qkv, context, logsum = attend_group(w_second)
    qkv, context, logsum, tokens = flow.slot((qkv, context, logsum, tokens))
    qkv_parts.append(qkv)
    contexts.append(context)
    logsums.append(logsum)
    w_third, out_all = flow.end("third")
    qkv, context, logsum = attend_group(w_third)
    qkv, context, logsum, tokens = flow.slot((qkv, context, logsum, tokens))
    qkv_parts.append(qkv)
    contexts.append(context)
    logsums.append(logsum)
    context = jnp.concatenate(contexts, 1)
    mixed_sum = tokens.astype(jnp.float32) + product(context, out_all)
    mixed_sum, rest = flow.slot((mixed_sum, rest))
    table_all, gru_all, gain_all = rest
    gain_all = gain_all.reshape(parts, -1, D)[:, 0, : gains.size]
    gain_all = gain_all.reshape(parts, 3, -1).transpose(1, 0, 2).reshape(3, -1).astype(jnp.float32)
    letters, before, pooled = run_chars(ids_row, ends, table_all, gru_all, shares)
    letters, before, pooled, mixed_sum = flow.slot((letters, before, pooled, mixed_sum))
    normed = norm_gain(mixed_sum, gain_all[0])
    (up_all,) = flow.end("up")
    hidden = product(normed.astype(jnp.bfloat16), up_all)
    active = jax.nn.gelu(hidden).astype(jnp.bfloat16)
    active, hidden, normed = flow.slot((active, hidden, normed))
    (down_all,) = flow.end("down")
    summed = normed + product(active, down_all)
    feature = norm_gain(summed, gain_all[1]).astype(jnp.bfloat16)

    whole_grad = both_halves(out_grad, flow.end("out_grad"))
    joined = jnp.concatenate([feature, pooled], 1)
    stacked = jnp.concatenate([rows_before(joined), joined, rows_after(joined)], 1)
    blend_in = product(stacked, blend_all)
    blended, gelu_pull = jax.vjp(jax.nn.gelu, blend_in)
    result, norm_pull = jax.vjp(norm_gain, feature.astype(jnp.float32) + blended, gain_all[2])
    total_grad, gain_blend = norm_pull(whole_grad.astype(jnp.float32))
    blend_grad = gelu_pull(total_grad)[0].astype(jnp.bfloat16)
    grad_blend = inner_rows(stacked, blend_grad)
    stacked_grad = inner_cols(blend_grad, blend_all)
    pair_width = joined.shape[1]
    joined_grad = (
        stacked_grad[:, pair_width : 2 * pair_width]
        + rows_after(stacked_grad[:, :pair_width])
        + rows_before(stacked_grad[:, 2 * pair_width :])
    )
    feature_grad = (total_grad + joined_grad[:, :D]).astype(jnp.bfloat16)
    result = result.astype(jnp.bfloat16)
    flow.begin(
        "result", swap_chain(jnp.where(on_first, result[half_len:], result[:half_len])), [2]
    )
    (blend_sum,) = scatter_whole([grad_blend])

    summed_grad, gain_ffn = jax.vjp(norm_gain, summed, gain_all[1])[1](
        feature_grad.astype(jnp.float32)
    )
    ffn_grad = summed_grad.astype(jnp.bfloat16)
    grad_down = inner_rows(active, ffn_grad).astype(jnp.bfloat16)
    hidden_grad = jax.vjp(jax.nn.gelu, hidden)[1](inner_cols(ffn_grad, down_all))[0].astype(
        jnp.bfloat16
    )
    grad_up = inner_rows(normed.astype(jnp.bfloat16), hidden_grad).astype(jnp.bfloat16)
    normed_grad = summed_grad + inner_cols(hidden_grad, up_all)
    flow.begin("down", scatter_chain([grad_down], True))
    flow.begin("up", scatter_chain([grad_up], False))
    mixed_grad, gain_attn = jax.vjp(norm_gain, mixed_sum, gain_all[0])[1](normed_grad)
    attended_grad = mixed_grad.astype(jnp.bfloat16)
    grad_out = inner_rows(context, attended_grad).astype(jnp.bfloat16)
    context_grad = inner_cols(attended_grad, out_all).astype(jnp.bfloat16)
    gain_grads = jnp.stack([gain_attn, gain_ffn, gain_blend])
    state_grad = joined_grad[:, D:]
    context_grad, grad_out, gain_grads, mixed_grad, state_grad = flow.slot(
        (context_grad, grad_out, gain_grads, mixed_grad, state_grad)
    )
    grad_gru, grad_table = run_chars_back(
        ids_row, segment, state_grad, shares, table_all, gru_all, letters, before
    )
    context_grad, grad_gru, grad_table = flow.slot((context_grad, grad_gru, grad_table))
    flow.begin("letters", scatter_chain([grad_gru, grad_table, grad_out], True))
    gain_rows = gain_grads.reshape(3, parts, -1).transpose(1, 0, 2).reshape(parts, -1)
    gain_rows = jnp.pad(gain_rows[:, None], ((0, 0), (0, 7), (0, D - gain_rows.shape[1])))
    gain_rows = gain_rows.reshape(8 * parts, D)
    tokens_grad = mixed_grad
    weights = (w_first, w_second, w_third)
    for number in range(groups):
        width = context_grad.shape[1] // groups
        qkv_grad = jnp.concatenate(
            run_attend_back(
                qkv_parts[number],
                logsums[number],
                context_grad[:, number * width : number * width + width],
            ),
            1,
        )
        grad_group = inner_rows(tokens, qkv_grad).astype(jnp.bfloat16)
        tokens_grad = tokens_grad + inner_cols(qkv_grad, weights[number])
        if number < 2:
            context_grad, grad_group, tokens_grad = flow.slot(
                (context_grad, grad_group, tokens_grad)
            )
        grads = [grad_group, gain_rows] if number == 0 else [grad_group]
        flow.begin("qkv%d" % number, scatter_chain(grads, number % 2 == 1))
    tokens_grad = tokens_grad.astype(jnp.bfloat16)
    flow.begin(
        "tokens", swap_chain(jnp.where(on_first, tokens_grad[half_len:], tokens_grad[:half_len])), [4]
    )
    while flow.live:
        flow.slot(())
    own_result = jnp.where(on_first, result[:half_len], result[half_len:])
    own_grad = jnp.where(on_first, tokens_grad[:half_len], tokens_grad[half_len:])
    back_result, back_grad = flow.end("result"), flow.end("tokens")
    block_parts = [
        jnp.where(on_first, own_result, back_result),
        jnp.where(on_first, back_result, own_result),
    ]
    grad_parts = [
        jnp.where(on_first, own_grad, back_grad),
        jnp.where(on_first, back_grad, own_grad),
    ]
    first_sum, gain_sum = flow.end("qkv0")
    group_sums = jnp.stack([first_sum, flow.end("qkv1")[0], flow.end("qkv2")[0]], 1)
    qkv_sum = group_sums.reshape(w_qkv.shape[0], groups, 3, -1).transpose(0, 2, 1, 3)
    letter_sums = flow.end("letters")
    sums = (
        qkv_sum.reshape(w_qkv.shape),
        letter_sums[2],
        flow.end("up")[0],
        flow.end("down")[0],
        letter_sums[0],
        blend_sum,
        letter_sums[1],
        gain_sum[0, : gains.size].reshape(gains.shape),
    )
    rates = step_rates()
    results = [
        adamw(masters[number], firsts[number], seconds[number], sums[number], rates[number])
        for number in range(8)
    ]
    return (
        jnp.stack(block_parts),
        jnp.stack(grad_parts),
        results[0][0],
        results[0][1],
        results[0][2],
        results[1][0],
        results[1][1],
        results[1][2],
        results[2][0],
        results[2][1],
        results[2][2],
        results[3][0],
        results[3][1],
        results[3][2],
        results[4][0],
        results[4][1],
        results[4][2],
        results[5][0],
        results[5][1],
        results[5][2],
        results[6][0],
        results[6][1],
        results[6][2],
        results[7][0],
        results[7][1],
        results[7][2],
    )


def solution(mesh):
    in_specs = (
        P("dp", "stream", None),
        P("dp", None),
        P("dp", None),
        P("dp", "stream", None),
        P(("stream", "dp"), None),
        P(("stream", "dp"), None),
        P(("stream", "dp"), None),
        P(("stream", "dp"), None),
        P(("stream", "dp"), None),
        P(("stream", "dp"), None),
        P(("stream", "dp"), None),
        P(("stream", "dp"), None),
        P(("stream", "dp"), None),
        P(("stream", "dp"), None),
        P(("stream", "dp"), None),
        P(("stream", "dp"), None),
        P(("stream", "dp"), None),
        P(("stream", "dp"), None),
        P(("stream", "dp"), None),
        P(("stream", "dp"), None),
        P(("stream", "dp"), None),
        P(("stream", "dp"), None),
        P(("stream", "dp"), None),
        P(("stream", "dp"), None),
        P(("stream", "dp"), None),
        P(None, ("stream", "dp")),
        P(None, ("stream", "dp")),
        P(None, ("stream", "dp")),
    )
    out_specs = (
        P("dp", "stream", None),
        P("dp", "stream", None),
        P(("stream", "dp"), None),
        P(("stream", "dp"), None),
        P(("stream", "dp"), None),
        P(("stream", "dp"), None),
        P(("stream", "dp"), None),
        P(("stream", "dp"), None),
        P(("stream", "dp"), None),
        P(("stream", "dp"), None),
        P(("stream", "dp"), None),
        P(("stream", "dp"), None),
        P(("stream", "dp"), None),
        P(("stream", "dp"), None),
        P(("stream", "dp"), None),
        P(("stream", "dp"), None),
        P(("stream", "dp"), None),
        P(("stream", "dp"), None),
        P(("stream", "dp"), None),
        P(("stream", "dp"), None),
        P(("stream", "dp"), None),
        P(("stream", "dp"), None),
        P(("stream", "dp"), None),
        P(None, ("stream", "dp")),
        P(None, ("stream", "dp")),
        P(None, ("stream", "dp")),
    )
    return jax.shard_map(
        on_device, mesh=mesh, in_specs=in_specs, out_specs=out_specs, check_vma=False
    )
```

time: 877 us -> 647 us (0.74)
  waiting for transfers between devices: 333 us -> 89.1 us
  starting transfers between devices: 6.55 us -> 57.8 us
  matrix products: 149 us -> 127 us
  local copies, waits for them, and re-layouts: 103 us -> 87.9 us
  other arithmetic: 77.5 us -> 88.7 us
  Pallas kernels: 184 us -> 175 us
    reduce_scatter x3 -> x1, waiting for transfers between devices: 209 us -> 0.01 us  [scatter_whole(): lax.psum_scatter(packed.reshape(-1, D), ('stream', 'dp'), scatter_dimensi...]
    all_gather x2, waiting for transfers between devices: 87 us -> 0.01 us  [the longest x1 0.01 us: gather_whole(): rows = lax.all_gather(packed, ('stream', 'dp'), axis=0, tiled=False)]
    ppermute x4 -> x59, waiting for transfers between devices: 37.6 us -> 89.1 us  [partner(): return lax.ppermute(block, axis, route)]
    ppermute x4 -> x59, starting transfers between devices: 6.34 us -> 57.4 us  [partner(): return lax.ppermute(block, axis, route)]
    reshape x8 -> x2, local copies, waits for them, and re-layouts: 23.1 us -> 0.11 us  [to_rows(): blocks = matrix.astype(jnp.bfloat16).reshape(parts, own, side, D)]
    unnamed x197 -> x284, local copies, waits for them, and re-layouts: 21.8 us -> 41 us
    slice x8 -> x3, local copies, waits for them, and re-layouts: 19.7 us -> 2.47 us  [from_rows(): blocks = rows[:, offset:offset + own * side].reshape(parts, side, own, D)]
    pallas_call x1, Pallas kernels: 38.5 us -> 23.6 us  [run_chars(): pl.pallas_call(chars_ahead, grid=(total // STEP_ROWS,), in_specs=[scalars...]
  transfers between devices with their start and end apart: 9 -> 62, of which waited for: 6 -> 20; matrix products, arithmetic and copies ran while one was open for 22% -> 21% of each run, Pallas kernels for 15% -> 27%
where the time goes in v2:
time: 647 us; the launch traced here: 642 us
  Pallas kernels  175 us (27%)
  matrix products  127 us (20%)
  waiting for transfers between devices  89.1 us (14%)
  other arithmetic  88.7 us (14%)
  local copies, waits for them, and re-layouts  87.9 us (14%)
  starting transfers between devices  57.8 us (9%)
  between operations  16.8 us (3%)
    ppermute x59, waiting for transfers between devices, partner(): return lax.ppermute(block, axis, route)  89.1 us
    pallas_call x3, Pallas kernels, run_attend_back(): pl.pallas_call(attend_back, grid=(pairs,), in_specs=[column(length, 128,...  57.8 us
    ppermute x59, starting transfers between devices, partner(): return lax.ppermute(block, axis, route)  57.4 us
    dot_general x7, matrix products, inner_rows(): lax.dot_general(former, latter, (((0,), (0,)), ((), ())), preferred_eleme...  47.6 us
    pallas_call x1, Pallas kernels, run_chars_back(): pl.pallas_call(chars_back, grid=(blocks,), in_specs=[scalars()] * 4 + [wh...  44.8 us
    dot_general x7, matrix products, inner_cols(): lax.dot_general(former, latter, (((1,), (1,)), ((), ())), preferred_eleme...  41.5 us
    unnamed x284, local copies, waits for them, and re-layouts  41 us
    dot_general x7, matrix products, product(): return jnp.dot(former, latter, preferred_element_type=jnp.float32)  37.5 us
  transfers between devices with their start and end apart: 62, of which 20 were waited for; matrix products, arithmetic and copies ran while one was open for 21% of the time, Pallas kernels for 27%

profile of v2, /device:TPU:0, one launch (start us, length us, event | category | flops | bytes accessed | tf_op | source)
XLA Modules:
  0.0 641.9 jit_solution(13059772946734709083)
XLA Ops:
  19.7 4.3 collective-permute-done.4
  28.0 4.3 collective-permute-done.7
  34.2 7.5 %collective-permute-done.10 = bf16[1,1,2,1,48,768]{5,4,3,2,1,0:T(8,128)(2,1)} collective-permute-done((bf16[1,1,2,1,48,768]{5,4,3,2,1,0:T(8,128)(2,1)S(1)}, bf16[1,1,2,1,48,768]{5,4,3,2,1,0:T(8,128)(2,1)}, u32[]{:S(2)}, u32[]{:S(2)}) %collective-permute-start.10) | collective-permute-done | bytes 147488 | tf_op jit(solution)/shard_map/ppermute | solution.py:24
  48.1 7.6 %scatter_custom_fusion = s32[4096]{0:T(1024)S(1)} fusion(s32[1024]{0:T(1024)S(1)} %bitcast.212, s32[1024]{0:T(1024)S(1)} %broadcast.295, s32[]{:T(128)} %constant.43.clone.1), kind=kCustom, calls=%fused_computation.260 | custom fusion | flops 1024 | bytes 16388 | tf_op jit(solution)/shard_map/scatter-add | solution.py:288
  86.1 11.6 %shard_map.468 = (bf16[1024,256]{1,0:T(8,128)(2,1)S(1)}, f32[32,1024]{1,0:T(8,128)S(1)}) custom-call(bf16[1024,768]{1,0:T(8,128)(2,1)S(1)} %convolution_convert_fusion.6.queries.key_rows.value_rows, bf16[1024,768]{1,0:T(8,128)(2,1)S(1)} %convolution_convert_fusion.6.queries.key_rows.value_rows, ...), custom_call_target="tpu_custom_call" | custom-call | flops 1073741824 | bytes 2097152 | tf_op jit(solution)/shard_map/pallas_call | solution.py:609
  97.8 9.4 %collective-permute-done.15 = bf16[1,2,2,2,48,768]{5,4,3,2,1,0:T(8,128)(2,1)S(1)} collective-permute-done((bf16[1,2,2,2,48,768]{5,4,3,2,1,0:T(8,128)(2,1)S(1)}, bf16[1,2,2,2,48,768]{5,4,3,2,1,0:T(8,128)(2,1)S(1)}, u32[]{:S(2)}, u32[]{:S(2)}) %collective-permute-start.15) | collective-permute-done | bytes 589856 | tf_op jit(solution)/shard_map/ppermute | solution.py:24
  116.9 11.6 %shard_map.470 = (bf16[1024,256]{1,0:T(8,128)(2,1)S(1)}, f32[32,1024]{1,0:T(8,128)S(1)}) custom-call(bf16[1024,768]{1,0:T(8,128)(2,1)S(1)} %convolution_convert_fusion.5.queries.key_rows.value_rows, bf16[1024,768]{1,0:T(8,128)(2,1)S(1)} %convolution_convert_fusion.5.queries.key_rows.value_rows, ...), custom_call_target="tpu_custom_call" | custom-call | flops 1073741824 | bytes 2097152 | tf_op jit(solution)/shard_map/pallas_call | solution.py:609
  137.9 11.8 %shard_map.472 = (bf16[1024,256]{1,0:T(8,128)(2,1)S(1)}, f32[32,1024]{1,0:T(8,128)S(1)}) custom-call(bf16[1024,768]{1,0:T(8,128)(2,1)S(1)} %convolution_convert_fusion.4.queries.key_rows.value_rows, bf16[1024,768]{1,0:T(8,128)(2,1)S(1)} %convolution_convert_fusion.4.queries.key_rows.value_rows, ...), custom_call_target="tpu_custom_call" | custom-call | flops 1073741824 | bytes 2097152 | tf_op jit(solution)/shard_map/pallas_call | solution.py:609
  171.3 23.6 %shard_map.473 = (f32[256,16,128]{2,1,0:T(8,128)}, f32[4096,8,128]{2,1,0:T(8,128)}, bf16[1024,768]{1,0:T(8,128)(2,1)}) custom-call(s32[4096]{0:T(1024)} %bitcast.207, s32[4096]{0:T(1024)} %rev.8.rows_b, s32[1024]{0:T(1024)} %fusion.116.ends, bf16[256,768]{1,0:T(8,128)(2,1)} %get-tuple-element.273.table, bf16[768,1536]{1,0:T(8,128)(2,1)} %bitcast.187, ...), custom_call_target="tpu_custom_call" | custom-call | flops 20000000000 | bytes 41943040 | tf_op jit(solution)/shard_map/pallas_call | solution.py:475
  194.9 13.2 %collective-permute-done.24 = bf16[1,2,2,2,96,768]{5,4,3,2,1,0:T(8,128)(2,1)} collective-permute-done((bf16[1,2,2,2,96,768]{5,4,3,2,1,0:T(8,128)(2,1)}, bf16[1,2,2,2,96,768]{5,4,3,2,1,0:T(8,128)(2,1)}, u32[]{:S(2)}, u32[]{:S(2)}) %collective-permute-start.24) | collective-permute-done | bytes 1179680 | tf_op jit(solution)/shard_map/ppermute | solution.py:24
  220.3 10.7 %fusion.15 = (bf16[1024,3072]{1,0:T(8,128)(2,1)S(1)}, f32[1024,3072]{1,0:T(8,128)}) fusion(bf16[768,3072]{1,0:T(8,128)(2,1)S(1)} %shard_map.474, f32[1024,768]{1,0:T(8,128)S(1)} %multiply_multiply_fusion.5), kind=kOutput, calls=%fused_computation.20 | convolution fusion | flops 4860936192 | bytes 26738688 | tf_op jit(solution)/shard_map/dot_general | solution.py:256
  231.0 5.3 shard_map.475
  236.3 5.3 fusion.79
  248.1 14.3 %fusion.76 = (f32[1024]{0:T(1024)S(1)}, f32[1024,768]{1,0:T(8,128)S(1)}, f32[1024,768]{1,0:T(8,128)}) fusion(bf16[1024,768]{1,0:T(8,128)(2,1)} %copy-done.26, bf16[4608,768]{1,0:T(8,128)(2,1)} %all-gather.4.cloned.1.call-done, bf16[1023,1536]{1,0:T(8,128)(2,1)} %slice_maximum_fusion, bf16[1024,1536]{1,0:T(8,128)(2,1)} %fusion.37, ...), kind=kOutput, calls=%fused_computation.291 | convolution fusion | flops 7303592960 | bytes 22807552 | tf_op jit(solution)/shard_map/dot_general | solution.py:256
  267.4 5.4 fusion.75
  272.8 22.3 %convolution_convert_fusion = bf16[4608,768]{1,0:T(8,128)(2,1)} fusion(bf16[1023,1536]{1,0:T(8,128)(2,1)} %slice_maximum_fusion, bf16[1024,1536]{1,0:T(8,128)(2,1)} %fusion.37, bf16[1024,768]{1,0:T(8,128)(2,1)} %get-tuple-element.293, bf16[1024,768]{1,0:T(8,128)(2,1)} %copy-done.26, f32[1024,768]{1,0:T(8,128)} %get-tuple-element.469, ...), kind=kOutput, calls=%fused_computation.24 | convolution fusion | flops 7314997248 | bytes 22807552 | tf_op jit(solution)/shard_map/dot_general | solution.py:260
  295.1 17.6 %fusion.62 = f32[1024,4608]{1,0:T(8,128)} fusion(bf16[4608,768]{1,0:T(8,128)(2,1)} %all-gather.4.cloned.1.call-done, f32[1024,768]{1,0:T(8,128)} %get-tuple-element.469, f32[1024,768]{1,0:T(8,128)} %get-tuple-element.442, f32[1024]{0:T(1024)S(1)} %negate_multiply_fusion.2), kind=kOutput, calls=%fused_computation.287 | convolution fusion | flops 7264272384 | bytes 32247808 | tf_op jit(solution)/shard_map/dot_general | solution.py:266
  312.7 10.7 %fusion.77 = (f32[1023,1536]{1,0:T(8,128)}, f32[1023,1536]{1,0:T(8,128)}) fusion(f32[1024,4608]{1,0:T(8,128)} %fusion.62), kind=kLoop, calls=%fused_computation.292 | loop fusion | bytes 25141248 | tf_op jit(solution)/shard_map/slice | solution.py:283
  323.4 7.3 %fusion.19 = f32[1024,1536]{1,0:T(8,128)S(1)} fusion(f32[1024,4608]{1,0:T(8,128)} %fusion.62, f32[1023,1536]{1,0:T(8,128)} %get-tuple-element.446, f32[1023,1536]{1,0:T(8,128)} %get-tuple-element.445), kind=kLoop, calls=%fused_computation.26 | loop fusion | flops 3145728 | bytes 25153536 | tf_op jit(solution)/shard_map/add | solution.py:785
  335.2 8.0 %fusion.57 = f32[1024,3072]{1,0:T(8,128)} fusion(bf16[3072,768]{1,0:T(8,128)(2,1)S(1)} %bitcast.165, f32[1024,768]{1,0:T(8,128)S(1)} %get-tuple-element.439, f32[1024]{0:T(1024)S(1)} %negate_multiply_fusion.1), kind=kOutput, calls=%fused_computation.285 | convolution fusion | flops 4833411072 | bytes 20451328 | tf_op jit(solution)/shard_map/dot_general | solution.py:266
  343.2 10.4 %convolution_convert_fusion.2.refs_0_ = bf16[3072,768]{1,0:T(8,128)(2,1)} fusion(bf16[1024,3072]{1,0:T(8,128)(2,1)} %copy-done.118, f32[1024,768]{1,0:T(8,128)S(1)} %get-tuple-element.439, f32[1024]{0:T(1024)S(1)} %negate_multiply_fusion.1), kind=kOutput, calls=%fused_computation.31 | convolution fusion | flops 4835770368 | bytes 14159872 | tf_op jit(solution)/shard_map/dot_general | solution.py:260
  353.6 10.4 %fusion.7 = bf16[1024,3072]{1,0:T(8,128)(2,1)S(1)} fusion(f32[1024,3072]{1,0:T(8,128)S(1)} %bitcast.175, f32[1024,3072]{1,0:T(8,128)} %fusion.57), kind=kLoop, calls=%fused_computation.12 | loop fusion | flops 62914560 | bytes 31457280 | tf_op jit(solution)/shard_map/convert_element_type | solution.py:801
  366.6 9.1 %convolution_convert_fusion.1.refs_0_ = bf16[768,3072]{1,0:T(8,128)(2,1)} fusion(bf16[1024,3072]{1,0:T(8,128)(2,1)S(1)} %fusion.7, f32[1024,768]{1,0:T(8,128)} %copy-done.43), kind=kOutput, calls=%fused_computation.30 | convolution fusion | flops 4834983936 | bytes 14155776 | tf_op jit(solution)/shard_map/dot_general | solution.py:260
  375.8 9.1 %multiply_reduce_fusion = (bf16[768]{0:T(1024)(128)(2,1)S(1)}, f32[1024]{0:T(1024)S(1)}, f32[1024,768]{1,0:T(8,128)}) fusion(f32[1024,768]{1,0:T(8,128)S(1)} %copy-done.25, f32[1024]{0:T(1024)S(1)} %copy-done.108, f32[1024]{0:T(1024)S(1)} %copy-done.102, f32[768]{0:T(1024)S(1)} %copy-done.106, bf16[1024,3072]{1,0:T(8,128)(2,1)} %copy-done.38, ...), kind=kOutput, calls=%fused_computation.64 | convolution fusion | flops 4838914048 | bytes 20468224 | tf_op jit(solution)/shard_map/dot_general | solution.py:266
  402.4 4.1 convert_add_fusion
  414.9 44.8 %shard_map.478 = (bf16[768,1536]{1,0:T(8,128)(2,1)}, bf16[256,768]{1,0:T(8,128)(2,1)}) custom-call(s32[4096]{0:T(1024)} %bitcast.208, s32[4096]{0:T(1024)} %rev.8.rows_b, s32[4096]{0:T(1024)} %get-tuple-element.434.owners_f, s32[4096]{0:T(1024)} %broadcast_add_fusion.1.owners_b, f32[1024,768]{1,0:T(8,128)} %get-tuple-element.302.upstream, ...), custom_call_target="tpu_custom_call" | custom-call | flops 20000000000 | bytes 41943040 | tf_op jit(solution)/shard_map/pallas_call | solution.py:505
  472.6 19.5 %shard_map.479 = (bf16[1024,256]{1,0:T(8,128)(2,1)S(1)}, bf16[1024,256]{1,0:T(8,128)(2,1)S(1)}, bf16[1024,256]{1,0:T(8,128)(2,1)S(1)}) custom-call(bf16[1024,768]{1,0:T(8,128)(2,1)S(1)} %copy-done.21, bf16[1024,768]{1,0:T(8,128)(2,1)S(1)} %copy-done.21, bf16[1024,768]{1,0:T(8,128)(2,1)S(1)} %copy-done.21, f32[32,1024]{1,0:T(8,128)S(1)} %copy-done.23, ...), custom_call_target="tpu_custom_call" | custom-call | flops 2684354560 | bytes 4194304 | tf_op jit(solution)/shard_map/pallas_call | solution.py:628
  507.3 19.1 %shard_map.481 = (bf16[1024,256]{1,0:T(8,128)(2,1)S(1)}, bf16[1024,256]{1,0:T(8,128)(2,1)S(1)}, bf16[1024,256]{1,0:T(8,128)(2,1)S(1)}) custom-call(bf16[1024,768]{1,0:T(8,128)(2,1)S(1)} %copy-done.19, bf16[1024,768]{1,0:T(8,128)(2,1)S(1)} %copy-done.19, bf16[1024,768]{1,0:T(8,128)(2,1)S(1)} %copy-done.19, f32[32,1024]{1,0:T(8,128)S(1)} %get-tuple-element.330.logsum, ...), custom_call_target="tpu_custom_call" | custom-call | flops 2684354560 | bytes 4194304 | tf_op jit(solution)/shard_map/pallas_call | solution.py:628
  536.0 19.2 %shard_map.483 = (bf16[1024,256]{1,0:T(8,128)(2,1)S(1)}, bf16[1024,256]{1,0:T(8,128)(2,1)S(1)}, bf16[1024,256]{1,0:T(8,128)(2,1)S(1)}) custom-call(bf16[1024,768]{1,0:T(8,128)(2,1)S(1)} %copy-done.17, bf16[1024,768]{1,0:T(8,128)(2,1)S(1)} %copy-done.17, bf16[1024,768]{1,0:T(8,128)(2,1)S(1)} %copy-done.17, f32[32,1024]{1,0:T(8,128)S(1)} %get-tuple-element.347.logsum, ...), custom_call_target="tpu_custom_call" | custom-call | flops 2684354560 | bytes 4194304 | tf_op jit(solution)/shard_map/pallas_call | solution.py:628
  568.9 4.8 collective-permute-done.40
  574.8 7.4 %collective-permute-done.42 = bf16[1,2,2,1,80,768]{5,4,3,2,1,0:T(8,128)(2,1)S(1)} collective-permute-done((bf16[1,2,2,1,80,768]{5,4,3,2,1,0:T(8,128)(2,1)S(1)}, bf16[1,2,2,1,80,768]{5,4,3,2,1,0:T(8,128)(2,1)S(1)}, u32[]{:S(2)}, u32[]{:S(2)}) %collective-permute-start.42) | collective-permute-done | bytes 491552 | tf_op jit(solution)/shard_map/ppermute | solution.py:24
  589.2 12.2 %collective-permute-done.47 = bf16[1,2,2,1,32,768]{5,4,3,2,1,0:T(8,128)(2,1)S(1)} collective-permute-done((bf16[1,2,2,1,32,768]{5,4,3,2,1,0:T(8,128)(2,1)S(1)}, bf16[1,2,2,1,32,768]{5,4,3,2,1,0:T(8,128)(2,1)S(1)}, u32[]{:S(2)}, u32[]{:S(2)}) %collective-permute-start.47) | collective-permute-done | bytes 196640 | tf_op jit(solution)/shard_map/ppermute | solution.py:24
  (660 shorter events, 243.1 us)
Async XLA Ops:
  7.2 148.2 %all-gather.6.cloned.1.call-start = ((), (), s32[]{:S(2)}) async-start(), calls=%async_computation.3 | async-start | bytes 3244032 | tf_op jit(solution)/shard_map/all_gather | solution.py:166
  43.2 204.8 %all-gather.4.cloned.1.call-start = ((), (), s32[]{:S(2)}) async-start(), calls=%async_computation.1 | async-start | bytes 7299072 | tf_op jit(solution)/shard_map/all_gather | solution.py:724
  44.3 25.4 %collective-permute-start = (bf16[512,768]{1,0:T(8,128)(2,1)}, bf16[512,768]{1,0:T(8,128)(2,1)}, u32[]{:S(2)}, u32[]{:S(2)}) collective-permute-start(bf16[512,768]{1,0:T(8,128)(2,1)} %get-tuple-element.458), channel_id=1, source_target_pairs={{0,16},{16,0},{1,17},{17,1},{2,18},{18,2},{3,19},{19,3},{4,20},{20... | collective-permute-start | bytes 2359304 | tf_op jit(solution)/shard_map/ppermute | solution.py:24
  46.8 20.9 %collective-permute-start.14 = (bf16[1,1,1,1,96,768]{5,4,3,2,1,0:T(8,128)(2,1)}, bf16[1,1,1,1,96,768]{5,4,3,2,1,0:T(8,128)(2,1)}, u32[]{:S(2)}, u32[]{:S(2)}) collective-permute-start(bf16[1,1,1,1,96,768]{5,4,3,2,1,0:T(8,128)(2,1)} %bitcast.11), channel_id=1, source_target_pairs={{0,4},{4,0},{1,5},{5,1},{2,6},{6,2},{3,7},{7,3},{8,12},{12,8},{9,1... | collective-permute-start | bytes 442376 | tf_op jit(solution)/shard_map/ppermute | solution.py:24
  66.0 566.9 %reduce-scatter.2.cloned.1.call-start = ((), (), s32[]{:S(2)}) async-start(), calls=%async_computation.2 | async-start | bytes 7299072 | tf_op jit(solution)/shard_map/reduce_scatter | solution.py:200
  67.7 30.1 %collective-permute-start.17 = (bf16[1,1,1,1,96,768]{5,4,3,2,1,0:T(8,128)(2,1)}, bf16[1,1,1,1,96,768]{5,4,3,2,1,0:T(8,128)(2,1)S(1)}, u32[]{:S(2)}, u32[]{:S(2)}) collective-permute-start(bf16[1,1,1,1,96,768]{5,4,3,2,1,0:T(8,128)(2,1)} %convert_bitcast_fusion), channel_id=1, source_target_pairs={{0,4},{4,0},{1,5},{5,1},{2,6},{6,2},{3,7},{7,3},{8,12},{12,8},{9,1... | collective-permute-start | bytes 442376 | tf_op jit(solution)/shard_map/ppermute | solution.py:24
  69.7 80.1 %collective-permute-start.21 = (bf16[512,768]{1,0:T(8,128)(2,1)}, bf16[512,768]{1,0:T(8,128)(2,1)}, u32[]{:S(2)}, u32[]{:S(2)}) collective-permute-start(bf16[512,768]{1,0:T(8,128)(2,1)} %get-tuple-element.456), channel_id=1, source_target_pairs={{0,16},{16,0},{1,17},{17,1},{2,18},{18,2},{3,19},{19,3},{4,20},{20... | collective-permute-start | bytes 2359304 | tf_op jit(solution)/shard_map/ppermute | solution.py:24
  76.1 21.7 %collective-permute-start.16 = (bf16[1,1,2,1,96,768]{5,4,3,2,1,0:T(8,128)(2,1)S(1)}, bf16[1,1,2,1,96,768]{5,4,3,2,1,0:T(8,128)(2,1)S(1)}, u32[]{:S(2)}, u32[]{:S(2)}) collective-permute-start(bf16[1,1,2,1,96,768]{5,4,3,2,1,0:T(8,128)(2,1)S(1)} %constant_dynamic-update-slice_fusion.22), channel_id=1, source_target_pairs={{0,8},{8,0},{1,9},{9,1},{2,10},{10,2},{3,11},{11,3},{4,12},{12,4},... | collective-permute-start | bytes 884744 | tf_op jit(solution)/shard_map/ppermute | solution.py:24
  79.6 27.6 %collective-permute-start.15 = (bf16[1,2,2,2,48,768]{5,4,3,2,1,0:T(8,128)(2,1)S(1)}, bf16[1,2,2,2,48,768]{5,4,3,2,1,0:T(8,128)(2,1)S(1)}, u32[]{:S(2)}, u32[]{:S(2)}) collective-permute-start(bf16[1,2,2,2,48,768]{5,4,3,2,1,0:T(8,128)(2,1)S(1)} %constant_dynamic-update-slice_fusion.20), channel_id=1, source_target_pairs={{0,16},{16,0},{1,17},{17,1},{2,18},{18,2},{3,19},{19,3},{4,20},{20... | collective-permute-start | bytes 1769480 | tf_op jit(solution)/shard_map/ppermute | solution.py:24
  107.3 23.8 %collective-permute-start.18 = (bf16[2,2,2,2,48,768]{5,4,3,2,1,0:T(8,128)(2,1)S(1)}, bf16[2,2,2,2,48,768]{5,4,3,2,1,0:T(8,128)(2,1)S(1)}, u32[]{:S(2)}, u32[]{:S(2)}) collective-permute-start(bf16[2,2,2,2,48,768]{5,4,3,2,1,0:T(8,128)(2,1)S(1)} %constant_dynamic-update-slice_fusion.24), channel_id=1, source_target_pairs={{0,1},{1,0},{2,3},{3,2},{4,5},{5,4},{6,7},{7,6},{8,9},{9,8},{10,11... | collective-permute-start | bytes 3538952 | tf_op jit(solution)/shard_map/ppermute | solution.py:24
  111.4 17.2 %collective-permute-start.20 = (bf16[1,1,2,1,96,768]{5,4,3,2,1,0:T(8,128)(2,1)S(1)}, bf16[1,1,2,1,96,768]{5,4,3,2,1,0:T(8,128)(2,1)S(1)}, u32[]{:S(2)}, u32[]{:S(2)}) collective-permute-start(bf16[1,1,2,1,96,768]{5,4,3,2,1,0:T(8,128)(2,1)S(1)} %constant_dynamic-update-slice_fusion.28), channel_id=1, source_target_pairs={{0,8},{8,0},{1,9},{9,1},{2,10},{10,2},{3,11},{11,3},{4,12},{12,4},... | collective-permute-start | bytes 884744 | tf_op jit(solution)/shard_map/ppermute | solution.py:24
  114.0 17.1 %collective-permute-start.19 = (bf16[1,2,2,1,96,768]{5,4,3,2,1,0:T(8,128)(2,1)S(1)}, bf16[1,2,2,1,96,768]{5,4,3,2,1,0:T(8,128)(2,1)S(1)}, u32[]{:S(2)}, u32[]{:S(2)}) collective-permute-start(bf16[1,2,2,1,96,768]{5,4,3,2,1,0:T(8,128)(2,1)S(1)} %constant_dynamic-update-slice_fusion.26), channel_id=1, source_target_pairs={{0,2},{2,0},{1,3},{3,1},{4,6},{6,4},{5,7},{7,5},{8,10},{10,8},{9,1... | collective-permute-start | bytes 1769480 | tf_op jit(solution)/shard_map/ppermute | solution.py:24
  132.8 34.0 %collective-permute-start.23 = (bf16[1,2,2,2,96,768]{5,4,3,2,1,0:T(8,128)(2,1)}, bf16[1,2,2,2,96,768]{5,4,3,2,1,0:T(8,128)(2,1)}, u32[]{:S(2)}, u32[]{:S(2)}) collective-permute-start(bf16[1,2,2,2,96,768]{5,4,3,2,1,0:T(8,128)(2,1)} %constant_dynamic-update-slice_fusion.35), channel_id=1, source_target_pairs={{0,16},{16,0},{1,17},{17,1},{2,18},{18,2},{3,19},{19,3},{4,20},{20... | collective-permute-start | bytes 3538952 | tf_op jit(solution)/shard_map/ppermute | solution.py:24
  133.5 17.4 %collective-permute-start.22 = (bf16[1,2,2,1,96,768]{5,4,3,2,1,0:T(8,128)(2,1)S(1)}, bf16[1,2,2,1,96,768]{5,4,3,2,1,0:T(8,128)(2,1)S(1)}, u32[]{:S(2)}, u32[]{:S(2)}) collective-permute-start(bf16[1,2,2,1,96,768]{5,4,3,2,1,0:T(8,128)(2,1)S(1)} %constant_dynamic-update-slice_fusion.30), channel_id=1, source_target_pairs={{0,2},{2,0},{1,3},{3,1},{4,6},{6,4},{5,7},{7,5},{8,10},{10,8},{9,1... | collective-permute-start | bytes 1769480 | tf_op jit(solution)/shard_map/ppermute | solution.py:24
  169.6 38.6 %collective-permute-start.25 = (bf16[2,2,2,2,96,768]{5,4,3,2,1,0:T(8,128)(2,1)S(1)}, bf16[2,2,2,2,96,768]{5,4,3,2,1,0:T(8,128)(2,1)}, u32[]{:S(2)}, u32[]{:S(2)}) collective-permute-start(bf16[2,2,2,2,96,768]{5,4,3,2,1,0:T(8,128)(2,1)S(1)} %constant_dynamic-update-slice_fusion.39), channel_id=1, source_target_pairs={{0,1},{1,0},{2,3},{3,2},{4,5},{5,4},{6,7},{7,6},{8,9},{9,8},{10,11... | collective-permute-start | bytes 7077896 | tf_op jit(solution)/shard_map/ppermute | solution.py:24
  170.5 37.6 %collective-permute-start.24 = (bf16[1,2,2,2,96,768]{5,4,3,2,1,0:T(8,128)(2,1)}, bf16[1,2,2,2,96,768]{5,4,3,2,1,0:T(8,128)(2,1)}, u32[]{:S(2)}, u32[]{:S(2)}) collective-permute-start(bf16[1,2,2,2,96,768]{5,4,3,2,1,0:T(8,128)(2,1)} %constant_dynamic-update-slice_fusion.37), channel_id=1, source_target_pairs={{0,16},{16,0},{1,17},{17,1},{2,18},{18,2},{3,19},{19,3},{4,20},{20... | collective-permute-start | bytes 3538952 | tf_op jit(solution)/shard_map/ppermute | solution.py:24
  212.9 18.1 %collective-permute-start.26 = (bf16[2,2,2,2,96,768]{5,4,3,2,1,0:T(8,128)(2,1)}, bf16[2,2,2,2,96,768]{5,4,3,2,1,0:T(8,128)(2,1)}, u32[]{:S(2)}, u32[]{:S(2)}) collective-permute-start(bf16[2,2,2,2,96,768]{5,4,3,2,1,0:T(8,128)(2,1)} %constant_dynamic-update-slice_fusion.41), channel_id=1, source_target_pairs={{0,1},{1,0},{2,3},{3,2},{4,5},{5,4},{6,7},{7,6},{8,9},{9,8},{10,11... | collective-permute-start | bytes 7077896 | tf_op jit(solution)/shard_map/ppermute | solution.py:24
  393.8 104.4 %collective-permute-start.31 = (bf16[512,768]{1,0:T(8,128)(2,1)}, bf16[512,768]{1,0:T(8,128)(2,1)}, u32[]{:S(2)}, u32[]{:S(2)}) collective-permute-start(bf16[512,768]{1,0:T(8,128)(2,1)} %broadcast_select_fusion.2), channel_id=1, source_target_pairs={{0,16},{16,0},{1,17},{17,1},{2,18},{18,2},{3,19},{19,3},{4,20},{20... | collective-permute-start | bytes 2359304 | tf_op jit(solution)/shard_map/ppermute | solution.py:24
  411.1 48.6 %collective-permute-start.29 = (bf16[1,2,2,2,96,768]{5,4,3,2,1,0:T(8,128)(2,1)S(1)}, bf16[1,2,2,2,96,768]{5,4,3,2,1,0:T(8,128)(2,1)}, u32[]{:S(2)}, u32[]{:S(2)}) collective-permute-start(bf16[1,2,2,2,96,768]{5,4,3,2,1,0:T(8,128)(2,1)S(1)} %bitcast.189), channel_id=1, source_target_pairs={{0,16},{16,0},{1,17},{17,1},{2,18},{18,2},{3,19},{19,3},{4,20},{20... | collective-permute-start | bytes 3538952 | tf_op jit(solution)/shard_map/ppermute | solution.py:24
  413.0 46.7 %collective-permute-start.30 = (bf16[2,2,2,1,96,768]{5,4,3,2,1,0:T(8,128)(2,1)}, bf16[2,2,2,1,96,768]{5,4,3,2,1,0:T(8,128)(2,1)}, u32[]{:S(2)}, u32[]{:S(2)}) collective-permute-start(bf16[2,2,2,1,96,768]{5,4,3,2,1,0:T(8,128)(2,1)} %slice.586), channel_id=1, source_target_pairs={{0,2},{2,0},{1,3},{3,1},{4,6},{6,4},{5,7},{7,5},{8,10},{10,8},{9,1... | collective-permute-start | bytes 3538952 | tf_op jit(solution)/shard_map/ppermute | solution.py:24
  463.3 34.9 %collective-permute-start.34 = (bf16[16,80,768]{2,1,0:T(8,128)(2,1)S(1)}, bf16[16,80,768]{2,1,0:T(8,128)(2,1)S(1)}, u32[]{:S(2)}, u32[]{:S(2)}) collective-permute-start(bf16[16,80,768]{2,1,0:T(8,128)(2,1)S(1)} %get-tuple-element.326), channel_id=1, source_target_pairs={{0,1},{1,0},{2,3},{3,2},{4,5},{5,4},{6,7},{7,6},{8,9},{9,8},{10,11... | collective-permute-start | bytes 5898248 | tf_op jit(solution)/shard_map/ppermute | solution.py:24
  470.0 28.3 %collective-permute-start.33 = (bf16[1,2,2,1,96,768]{5,4,3,2,1,0:T(8,128)(2,1)S(1)}, bf16[1,2,2,1,96,768]{5,4,3,2,1,0:T(8,128)(2,1)S(1)}, u32[]{:S(2)}, u32[]{:S(2)}) collective-permute-start(bf16[1,2,2,1,96,768]{5,4,3,2,1,0:T(8,128)(2,1)S(1)} %slice.589), channel_id=1, source_target_pairs={{0,16},{16,0},{1,17},{17,1},{2,18},{18,2},{3,19},{19,3},{4,20},{20... | collective-permute-start | bytes 1769480 | tf_op jit(solution)/shard_map/ppermute | solution.py:24
  470.4 27.9 %collective-permute-start.32 = (bf16[1,2,2,1,96,768]{5,4,3,2,1,0:T(8,128)(2,1)S(1)}, bf16[1,2,2,1,96,768]{5,4,3,2,1,0:T(8,128)(2,1)S(1)}, u32[]{:S(2)}, u32[]{:S(2)}) collective-permute-start(bf16[1,2,2,1,96,768]{5,4,3,2,1,0:T(8,128)(2,1)S(1)} %slice.590), channel_id=1, source_target_pairs={{0,2},{2,0},{1,3},{3,1},{4,6},{6,4},{5,7},{7,5},{8,10},{10,8},{9,1... | collective-permute-start | bytes 1769480 | tf_op jit(solution)/shard_map/ppermute | solution.py:24
  503.2 32.7 %collective-permute-start.38 = (bf16[16,32,768]{2,1,0:T(8,128)(2,1)S(1)}, bf16[16,32,768]{2,1,0:T(8,128)(2,1)S(1)}, u32[]{:S(2)}, u32[]{:S(2)}) collective-permute-start(bf16[16,32,768]{2,1,0:T(8,128)(2,1)S(1)} %get-tuple-element.344), channel_id=1, source_target_pairs={{0,1},{1,0},{2,3},{3,2},{4,5},{5,4},{6,7},{7,6},{8,9},{9,8},{10,11... | collective-permute-start | bytes 2359304 | tf_op jit(solution)/shard_map/ppermute | solution.py:24
  503.7 32.3 %collective-permute-start.37 = (bf16[1,2,2,2,80,768]{5,4,3,2,1,0:T(8,128)(2,1)S(1)}, bf16[1,2,2,2,80,768]{5,4,3,2,1,0:T(8,128)(2,1)S(1)}, u32[]{:S(2)}, u32[]{:S(2)}) collective-permute-start(bf16[1,2,2,2,80,768]{5,4,3,2,1,0:T(8,128)(2,1)S(1)} %bitcast.193), channel_id=1, source_target_pairs={{0,16},{16,0},{1,17},{17,1},{2,18},{18,2},{3,19},{19,3},{4,20},{20... | collective-permute-start | bytes 2949128 | tf_op jit(solution)/shard_map/ppermute | solution.py:24
  504.3 30.2 %collective-permute-start.36 = (bf16[1,1,2,1,96,768]{5,4,3,2,1,0:T(8,128)(2,1)S(1)}, bf16[1,1,2,1,96,768]{5,4,3,2,1,0:T(8,128)(2,1)S(1)}, u32[]{:S(2)}, u32[]{:S(2)}) collective-permute-start(bf16[1,1,2,1,96,768]{5,4,3,2,1,0:T(8,128)(2,1)S(1)} %slice.595), channel_id=1, source_target_pairs={{0,8},{8,0},{1,9},{9,1},{2,10},{10,2},{3,11},{11,3},{4,12},{12,4},... | collective-permute-start | bytes 884744 | tf_op jit(solution)/shard_map/ppermute | solution.py:24
  506.8 29.1 %collective-permute-start.35 = (bf16[1,1,2,1,96,768]{5,4,3,2,1,0:T(8,128)(2,1)S(1)}, bf16[1,1,2,1,96,768]{5,4,3,2,1,0:T(8,128)(2,1)S(1)}, u32[]{:S(2)}, u32[]{:S(2)}) collective-permute-start(bf16[1,1,2,1,96,768]{5,4,3,2,1,0:T(8,128)(2,1)S(1)} %slice.596), channel_id=1, source_target_pairs={{0,8},{8,0},{1,9},{9,1},{2,10},{10,2},{3,11},{11,3},{4,12},{12,4},... | collective-permute-start | bytes 884744 | tf_op jit(solution)/shard_map/ppermute | solution.py:24
  559.8 22.5 %collective-permute-start.45 = (bf16[16,24,768]{2,1,0:T(8,128)(2,1)S(1)}, bf16[16,24,768]{2,1,0:T(8,128)(2,1)S(1)}, u32[]{:S(2)}, u32[]{:S(2)}) collective-permute-start(bf16[16,24,768]{2,1,0:T(8,128)(2,1)S(1)} %get-tuple-element.364), channel_id=1, source_target_pairs={{0,1},{1,0},{2,3},{3,2},{4,5},{5,4},{6,7},{7,6},{8,9},{9,8},{10,11... | collective-permute-start | bytes 1769480 | tf_op jit(solution)/shard_map/ppermute | solution.py:24
  562.1 20.2 %collective-permute-start.42 = (bf16[1,2,2,1,80,768]{5,4,3,2,1,0:T(8,128)(2,1)S(1)}, bf16[1,2,2,1,80,768]{5,4,3,2,1,0:T(8,128)(2,1)S(1)}, u32[]{:S(2)}, u32[]{:S(2)}) collective-permute-start(bf16[1,2,2,1,80,768]{5,4,3,2,1,0:T(8,128)(2,1)S(1)} %slice.591), channel_id=1, source_target_pairs={{0,2},{2,0},{1,3},{3,1},{4,6},{6,4},{5,7},{7,5},{8,10},{10,8},{9,1... | collective-permute-start | bytes 1474568 | tf_op jit(solution)/shard_map/ppermute | solution.py:24
  563.7 18.6 %collective-permute-start.44 = (bf16[16,24,768]{2,1,0:T(8,128)(2,1)S(1)}, bf16[16,24,768]{2,1,0:T(8,128)(2,1)S(1)}, u32[]{:S(2)}, u32[]{:S(2)}) collective-permute-start(bf16[16,24,768]{2,1,0:T(8,128)(2,1)S(1)} %get-tuple-element.362), channel_id=1, source_target_pairs={{0,1},{1,0},{2,3},{3,2},{4,5},{5,4},{6,7},{7,6},{8,9},{9,8},{10,11... | collective-permute-start | bytes 1769480 | tf_op jit(solution)/shard_map/ppermute | solution.py:24
  573.6 54.7 %collective-permute-start.39 = (bf16[512,768]{1,0:T(8,128)(2,1)S(1)}, bf16[512,768]{1,0:T(8,128)(2,1)S(1)}, u32[]{:S(2)}, u32[]{:S(2)}) collective-permute-start(bf16[512,768]{1,0:T(8,128)(2,1)S(1)} %broadcast_select_fusion), channel_id=1, source_target_pairs={{0,16},{16,0},{1,17},{17,1},{2,18},{18,2},{3,19},{19,3},{4,20},{20... | collective-permute-start | bytes 2359304 | tf_op jit(solution)/shard_map/ppermute | solution.py:24
  582.7 18.7 %collective-permute-start.49 = (bf16[2,2,2,1,24,768]{5,4,3,2,1,0:T(8,128)(2,1)S(1)}, bf16[2,2,2,1,24,768]{5,4,3,2,1,0:T(8,128)(2,1)S(1)}, u32[]{:S(2)}, u32[]{:S(2)}) collective-permute-start(bf16[2,2,2,1,24,768]{5,4,3,2,1,0:T(8,128)(2,1)S(1)} %slice.593), channel_id=1, source_target_pairs={{0,2},{2,0},{1,3},{3,1},{4,6},{6,4},{5,7},{7,5},{8,10},{10,8},{9,1... | collective-permute-start | bytes 884744 | tf_op jit(solution)/shard_map/ppermute | solution.py:24
  (168 other events, 1428.7 us)
Sparse Core Ops, SparseCore 0:
  43.4 69.8 all-gather.5
  116.8 89.3 all-gather.3
  385.0 141.5 reduce-scatter.1

commit v3 on v2

--- a/solution.py
+++ b/solution.py
@@ -14,16 +14,6 @@
 STEP = 5
 
 
-def partner(block, axis, apart):
-    count = lax.axis_size(axis)
-    route = []
-    for low in range(count):
-        high = low | 1 << apart
-        if high != low and high < count:
-            route += [(low, high), (high, low)]
-    return lax.ppermute(block, axis, route)
-
-
 def to_rows(matrix, parts):
     side = matrix.shape[1] // D
     own = matrix.shape[0] // parts
@@ -41,21 +31,13 @@
     return jnp.pad(gains.reshape(1, -1), ((0, 7), (0, D - gains.size)))
 
 
-def swap_bit(block, bit):
-    inner = lax.axis_size("dp").bit_length() - 1
-    if bit < inner:
-        return partner(block, "dp", bit)
-    return partner(block, "stream", bit - inner)
+def swap(block, mask):
+    parts = lax.axis_size("dp") * lax.axis_size("stream")
+    return lax.ppermute(block, ("stream", "dp"), [(place, place ^ mask) for place in range(parts)])
 
 
 def pair_bits():
     return (lax.axis_size("dp") * lax.axis_size("stream")).bit_length() - 2
-
-
-def hop_order(turned):
-    top = pair_bits()
-    order = list(range(2, top)) + ([1, top] if turned else [top, 1])
-    return order
 
 
 def in_pairs(shapes):
@@ -146,30 +128,86 @@
         return self.ended.pop(name)
 
 
-def gather_chain(shards, turned):
+def gather_chain(shards, near_first=False):
+    shapes = shapes_of(shards, 1)
+    packed = jnp.concatenate([to_rows(shard, 1)[0] for shard in shards], 0)
+    if not in_pairs(shapes):
+        return gather_whole(packed, shapes)
+    top = pair_bits()
+    far = 1 << (top - 2)
+    high = packed.shape[0]
+    corner = 1 << top
+    near = (2, corner, corner | 2)
+    held = packed[None, None, None]
+    for turn in range(2):
+        if near_first == (turn == 0):
+            held, *got = yield (held, *[swap(held, mask) for mask in near])
+            held = jnp.concatenate(
+                [jnp.concatenate([held, got[0]], 2), jnp.concatenate(got[1:], 2)], 0
+            )
+        else:
+            held, *got = yield (held, *[swap(held, step << 2) for step in range(1, far)])
+            held = jnp.concatenate([held, *got], 1)
+    held = held.reshape(4 * far, high, D)
+    held, other = yield (held, swap(held, 1))
+    return join_halves(shapes, held, other)
+
+
+def gather_steps(shards, turned):
     shapes = shapes_of(shards, 1)
     packed = jnp.concatenate([to_rows(shard, 1)[0] for shard in shards], 0)
     if not in_pairs(shapes):
         return gather_whole(packed, shapes)
     top = pair_bits()
     held = packed.reshape((1,) * top + packed.shape)
-    for bit in hop_order(turned):
-        other = swap_bit(held, bit)
-        held, other = yield (held, other)
+    for bit in list(range(2, top)) + ([1, top] if turned else [top, 1]):
+        held, other = yield (held, swap(held, 1 << bit))
         held = jnp.concatenate([held, other], top - bit)
-    other = swap_bit(held, 0)
-    held, other = yield (held, other)
+    held = held.reshape(1 << top, *packed.shape)
+    held, other = yield (held, swap(held, 1))
     return join_halves(shapes, held, other)
 
 
-def gather_whole(packed, shapes):
-    rows = lax.all_gather(packed, ("stream", "dp"), axis=0, tiled=False)
+def unpack(shapes, rows, *weights):
+    pieces = [rows[number].astype(jnp.float32) for number in range(8)]
+    offset = 0
+    for (own, side), weight in zip(shapes, weights):
+        for number in range(side):
+            block = jnp.concatenate([piece[offset : offset + own] for piece in pieces], 0)
+            weight[:, number * D : number * D + D] = block.astype(weight.dtype)
+            offset += own
+
+
+def unpack_rows(rows, shapes):
+    parts, high = rows.shape[:2]
+    if not in_pairs(shapes):
+        return unpack_plain(rows, shapes)
+    return pl.pallas_call(
+        functools.partial(unpack, shapes),
+        grid=(parts // 8,),
+        in_specs=[pl.BlockSpec((8, high, D), lambda group: (group, 0, 0))],
+        out_specs=[
+            pl.BlockSpec((8 * own, side * D), lambda group: (group, 0)) for own, side in shapes
+        ],
+        out_shape=[
+            jax.ShapeDtypeStruct((parts * own, side * D), jnp.bfloat16) for own, side in shapes
+        ],
+        compiler_params=pltpu.CompilerParams(vmem_limit_bytes=40 << 20),
+        cost_estimate=spent(3),
+    )(rows)
+
+
+def unpack_plain(rows, shapes):
     pieces = []
     offset = 0
     for own, side in shapes:
         pieces.append(from_rows(rows, offset, own, side))
         offset += own * side
     return pieces
+
+
+def gather_whole(packed, shapes):
+    return unpack_rows(lax.all_gather(packed, ("stream", "dp"), axis=0, tiled=False), shapes)
 
 
 def join_halves(shapes, mine, theirs):
@@ -188,9 +226,7 @@
             jax.ShapeDtypeStruct((parts * rows, side * D), jnp.bfloat16) for rows, side in shapes
         ],
         compiler_params=pltpu.CompilerParams(vmem_limit_bytes=40 << 20),
-        cost_estimate=pl.CostEstimate(
-            flops=0, bytes_accessed=4 * parts * high * D, transcendentals=0
-        ),
+        cost_estimate=spent(4),
     )(my_place(), mine.reshape(pairs, high, D), theirs.reshape(pairs, high, D))
 
 
@@ -212,7 +248,7 @@
     return pieces
 
 
-def scatter_chain(grads, turned):
+def scatter_chain(grads, split=False):
     parts = lax.axis_size("dp") * lax.axis_size("stream")
     shapes = shapes_of(grads, parts)
     if not in_pairs(shapes):
@@ -230,25 +266,50 @@
         ),
         out_shape=[half, half],
         compiler_params=pltpu.CompilerParams(vmem_limit_bytes=40 << 20),
-        cost_estimate=pl.CostEstimate(
-            flops=0, bytes_accessed=4 * parts * high * D, transcendentals=0
-        ),
+        cost_estimate=spent(4),
     )(my_place(), *[grad.astype(jnp.bfloat16) for grad in grads])
-    other = swap_bit(sent, 0)
-    kept, other = yield (kept, other)
-    total = kept.astype(jnp.float32) + other.astype(jnp.float32)
+    kept, other = yield (kept, swap(sent, 1))
     top = pair_bits()
-    total = total.reshape((2,) * top + (high, D))
-    for bit in reversed(hop_order(turned)):
-        axis = top - bit
-        other = swap_bit(lax.slice_in_dim(total, 1, 2, axis=axis).astype(jnp.bfloat16), bit)
-        kept, other = yield (lax.slice_in_dim(total, 0, 1, axis=axis), other)
-        total = kept + other.astype(jnp.float32)
-    return own_pieces(total.reshape(high, D), shapes)
+    far = 1 << (top - 2)
+    corner = 1 << top
+    near = [(1, 0), (0, 1), (1, 1)]
+    quarter = jax.ShapeDtypeStruct((far, high, D), jnp.bfloat16)
+    views = [
+        pl.BlockSpec((1, 1, 1, high, D), lambda row, x=x, y=y: (x, row, y, 0, 0))
+        for x, y in [(0, 0)] + near
+    ]
+    total, *sent = pl.pallas_call(
+        sum_quarters,
+        grid=(far,),
+        in_specs=views + views,
+        out_specs=[pl.BlockSpec((1, high, D), lambda row: (row, 0, 0))] * 4,
+        out_shape=[jax.ShapeDtypeStruct(quarter.shape, jnp.float32)] + [quarter] * 3,
+        compiler_params=pltpu.CompilerParams(vmem_limit_bytes=40 << 20),
+        cost_estimate=spent(3),
+    )(*[kept.reshape(2, far, 2, high, D)] * 4, *[other.reshape(2, far, 2, high, D)] * 4)
+    got = [swap(sent[0], corner), swap(sent[1], 2)]
+    if split:
+        total, last, *got = yield (total, sent[2], *got)
+        total, got, last = yield (total, got, swap(last, corner | 2))
+    else:
+        total, last, *got = yield (total, swap(sent[2], corner | 2), *got)
+    total = total + sum(block.astype(jnp.float32) for block in [last, *got])
+    others = [
+        swap(total[number].astype(jnp.bfloat16), number << 2) for number in range(1, far)
+    ]
+    kept, *others = yield (total[0], *others)
+    total = kept + sum(other.astype(jnp.float32) for other in others)
+    return own_pieces(total, shapes)
+
+
+def sum_quarters(*refs):
+    for former, latter, out in zip(refs[:4], refs[4:8], refs[8:]):
+        total = former[0, 0, 0].astype(jnp.float32) + latter[0, 0, 0].astype(jnp.float32)
+        out[0] = total.astype(out.dtype)
 
 
 def swap_chain(block):
-    other = yield partner(block, "stream", 0)
+    other = yield swap(block, lax.axis_size("dp"))
     return other
 
 
@@ -313,7 +374,15 @@
 
 
 STEP_ROWS = 512
-UNROLL = 8
+
+
+def spent(microseconds):
+    return pl.CostEstimate(
+        flops=int(microseconds * 1e9), bytes_accessed=1, transcendentals=0
+    )
+
+
+UNROLL = 16
 
 
 def contract(former, latter, left, right):
@@ -389,22 +458,44 @@
             pooled[:, at : at + 128] = (spans[:, place, :] * shares[...]).astype(pooled.dtype)
 
 
-def chars_back(
-    rows_f, rows_b, owners_f, owners_b, upstream, shares, table, w_gru, letters, before,
-    grad_gru, grad_table, spread, sums_f, sums_b, more_f, more_b, full, carry
-):
-    block = pl.num_programs(0) - 1 - pl.program_id(0)
-    width = full.shape[1] // 4
-
-    @pl.when(pl.program_id(0) == 0)
+def chars_back(blocks, opening, closing, *refs):
+    rows_f, rows_b, owners_f, owners_b, letters, before = refs[:6]
+    rest = list(refs[6:])
+    take = lambda count: [rest.pop(0) for _ in range(count)]
+    if opening:
+        upstream, shares = take(2)
+    else:
+        spread, carry_in, *sums_in = take(6)
+    if closing:
+        table, w_gru = take(2)
+    if opening:
+        (spread,) = take(1)
+    if closing:
+        grad_gru, grad_table = take(2)
+    else:
+        carry_out, *sums_out = take(5)
+    *sums, carry = take(5)
+    if closing:
+        (full,) = take(1)
+    sums_f, sums_b, more_f, more_b = sums
+    step_number = pl.program_id(0)
+    block = blocks[0] - 1 - step_number
+    width = 384
+
+    @pl.when(step_number == 0)
     def start():
-        for held in (sums_f, sums_b, more_f, more_b):
-            held[...] = jnp.zeros_like(held)
-        carry[...] = jnp.zeros_like(carry)
-        for at, _, place in lane_blocks(width):
-            spread[:, place, :] = upstream[:, at : at + 128] * shares[...]
-        for place in (3, 7):
-            spread[:, place, :] = jnp.zeros((spread.shape[0], 128), jnp.float32)
+        if opening:
+            for held in sums:
+                held[...] = jnp.zeros_like(held)
+            carry[...] = jnp.zeros_like(carry)
+            for at, _, place in lane_blocks(width):
+                spread[:, place, :] = upstream[:, at : at + 128] * shares[...]
+            for place in (3, 7):
+                spread[:, place, :] = jnp.zeros((spread.shape[0], 128), jnp.float32)
+        else:
+            for held, given in zip(sums, sums_in):
+                held[...] = given[...]
+            carry[...] = carry_in[...]
 
     leading = lax.broadcasted_iota(jnp.int32, (8, 128), 0) < 4
 
@@ -424,16 +515,29 @@
             moved = carried * priors[inner]
             id_f, id_b = owned[inner]
             for held, row, value in (
-                ((sums_f, more_f)[inner % 2], id_f, jnp.where(leading, carried, pltpu.roll(moved, 4, 0))),
-                ((sums_b, more_b)[inner % 2], id_b, jnp.where(leading, pltpu.roll(carried, 4, 0), moved)),
+                (
+                    (sums_f, more_f)[inner % 2],
+                    id_f,
+                    jnp.where(leading, carried, pltpu.roll(moved, 4, 0)),
+                ),
+                (
+                    (sums_b, more_b)[inner % 2],
+                    id_b,
+                    jnp.where(leading, pltpu.roll(carried, 4, 0), moved),
+                ),
             ):
                 held[row] += value
         return passed
 
     carry[...] = lax.fori_loop(0, STEP_ROWS // UNROLL, several, carry[...])
 
-    @pl.when(block == 0)
+    @pl.when(step_number == pl.num_programs(0) - 1)
     def finish():
+        if not closing:
+            carry_out[...] = carry[...]
+            for held, given in zip(sums, sums_out):
+                given[...] = held[...]
+            return
         sums_f[...] += more_f[...]
         sums_b[...] += more_b[...]
         for _, left, place in lane_blocks(width):
@@ -488,154 +592,351 @@
             pltpu.VMEM((2, 8, 128), f32),
         ],
         compiler_params=pltpu.CompilerParams(vmem_limit_bytes=56 << 20),
-        cost_estimate=pl.CostEstimate(
-            flops=20_000_000_000, bytes_accessed=40 << 20, transcendentals=0
-        ),
+        cost_estimate=spent(24),
     )(ids, jnp.flip(ids), ends, table, w_gru, shares)
 
 
-def run_chars_back(ids, owners, upstream, shares, table, w_gru, letters, before):
-    total, count = ids.shape[0], shares.shape[0]
+def run_chars_back(last, count, ids, owners, letters, before, *, upstream=None, held=None, ends=None):
     f32 = jnp.float32
-    blocks = total // STEP_ROWS
-    outs = (
-        jax.ShapeDtypeStruct(w_gru.shape, jnp.bfloat16),
-        jax.ShapeDtypeStruct(table.shape, jnp.bfloat16),
-    )
+    tile = jax.ShapeDtypeStruct((letters.shape[0], 8, 128), f32)
+    flat = jax.ShapeDtypeStruct((8, 128), f32)
+    inputs = [ids, jnp.flip(ids), owners, jnp.flip(owners), letters, before]
+    blocks = [scalars()] * 4 + [
+        whole(letters),
+        pl.BlockSpec((STEP_ROWS, 8, 128), lambda block: (last - 1 - block, 0, 0)),
+    ]
+    outs = []
+    if upstream is not None:
+        inputs += upstream
+        outs.append(jax.ShapeDtypeStruct((upstream[0].shape[0], 8, 128), f32))
+    else:
+        inputs += held
+    if ends is not None:
+        inputs += ends
+        outs.append(jax.ShapeDtypeStruct(ends[1].shape, jnp.bfloat16))
+        outs.append(jax.ShapeDtypeStruct(ends[0].shape, jnp.bfloat16))
+    else:
+        outs += [flat] + [tile] * 4
+    blocks += [whole(array) for array in inputs[6:]]
+    scratch = [pltpu.VMEM(tile.shape, f32)] * 4 + [pltpu.VMEM(flat.shape, f32)]
+    if ends is not None:
+        scratch.append(pltpu.VMEM((ends[0].shape[0], ends[1].shape[1]), f32))
     return pl.pallas_call(
-        chars_back,
-        grid=(blocks,),
-        in_specs=[scalars()] * 4
-        + [
-            whole(upstream),
-            whole(shares),
-            whole(table),
-            whole(w_gru),
-            whole(letters),
-            pl.BlockSpec((STEP_ROWS, 8, 128), lambda block: (blocks - 1 - block, 0, 0)),
-        ],
-        out_specs=[whole(outs[0]), whole(outs[1])],
+        functools.partial(chars_back, (last,), upstream is not None, ends is not None),
+        grid=(count,),
+        in_specs=blocks,
+        out_specs=[whole(out) for out in outs],
         out_shape=outs,
-        scratch_shapes=[
-            pltpu.VMEM((count, 8, 128), f32),
-            pltpu.VMEM((table.shape[0], 8, 128), f32),
-            pltpu.VMEM((table.shape[0], 8, 128), f32),
-            pltpu.VMEM((table.shape[0], 8, 128), f32),
-            pltpu.VMEM((table.shape[0], 8, 128), f32),
-            pltpu.VMEM((table.shape[0], w_gru.shape[1]), f32),
-            pltpu.VMEM((8, 128), f32),
-        ],
+        scratch_shapes=scratch,
         compiler_params=pltpu.CompilerParams(vmem_limit_bytes=56 << 20),
-        cost_estimate=pl.CostEstimate(
-            flops=20_000_000_000, bytes_accessed=40 << 20, transcendentals=0
-        ),
-    )(ids, jnp.flip(ids), owners, jnp.flip(owners), upstream, shares, table, w_gru, letters, before)
-
-
-ROWS = 256
+        cost_estimate=spent(6 * count),
+    )(*inputs)
 
 
 def attend(queries, key_rows, value_rows, context, logsum):
     size = key_rows.shape[1] // 2
     lanes = lax.broadcasted_iota(jnp.int32, (1, 2 * size), 1)
     scale = size ** (-0.5)
-
-    def some_rows(number, _):
-        at = pl.ds(pl.multiple_of(number * ROWS, ROWS), ROWS)
-        row_block = queries[at, :]
-        parts = []
-        sums = []
-        for head in range(2):
-            own = (lanes < size) if head == 0 else (lanes >= size)
-            scores = contract(jnp.where(own, row_block, 0) * scale, key_rows[...], 1, 1)
-            row_max = jnp.max(scores, axis=-1, keepdims=True)
-            exponent = jnp.exp(scores - row_max)
-            row_total = jnp.sum(exponent, axis=-1, keepdims=True)
-            probs = (exponent * (1.0 / row_total)).astype(jnp.bfloat16)
-            parts.append(contract(probs, value_rows[...], 1, 0))
-            sums.append(row_max + jnp.log(row_total))
-        context[at, :] = jnp.where(lanes < size, parts[0], parts[1]).astype(context.dtype)
-        both = jnp.where(lanes < size, sums[0], sums[1])
-        turned = jnp.transpose(both)
-        logsum[0:8, at] = turned[0:8]
-        logsum[8:16, at] = turned[size : size + 8]
-        return 0
-
-    lax.fori_loop(0, queries.shape[0] // ROWS, some_rows, 0)
-
-
-def attend_back(queries, key_rows, value_rows, logsum, grads, query_grad, key_grad, value_grad, key_sum, value_sum):
+    parts = []
+    sums = []
+    for head in range(2):
+        own = (lanes < size) if head == 0 else (lanes >= size)
+        scores = contract(jnp.where(own, queries[...], 0) * scale, key_rows[...], 1, 1)
+        row_max = jnp.max(scores, axis=-1, keepdims=True)
+        exponent = jnp.exp(scores - row_max)
+        row_total = jnp.sum(exponent, axis=-1, keepdims=True)
+        parts.append(
+            contract(exponent.astype(jnp.bfloat16), value_rows[...], 1, 0) * (1.0 / row_total)
+        )
+        sums.append(row_max + jnp.log(row_total))
+    context[...] = jnp.where(lanes < size, parts[0], parts[1]).astype(context.dtype)
+    turned = jnp.transpose(jnp.where(lanes < size, sums[0], sums[1]))
+    logsum[0:8, :] = turned[0:8]
+    logsum[8:16, :] = turned[size : size + 8]
+
+
+def attend_back(queries, key_rows, value_rows, logsum, grads, query_grad, key_grad, value_grad):
     size = key_rows.shape[1] // 2
     lanes = lax.broadcasted_iota(jnp.int32, (1, 2 * size), 1)
     scale = size ** (-0.5)
-    key_sum[...] = jnp.zeros_like(key_sum)
-    value_sum[...] = jnp.zeros_like(value_sum)
-
-    def some_rows(number, _):
-        at = pl.ds(pl.multiple_of(number * ROWS, ROWS), ROWS)
-        row_block = queries[at, :]
-        grad_block = grads[at, :]
-        parts = []
-        for head in range(2):
-            own = (lanes < size) if head == 0 else (lanes >= size)
-            own_rows = jnp.where(own, row_block, 0) * scale
-            own_grads = jnp.where(own, grad_block, 0)
-            scores = contract(key_rows[...], own_rows, 1, 1)
-            probs = jnp.exp(scores - logsum[8 * head : 8 * head + 1, at])
-            value_sum[...] += contract(probs.astype(jnp.bfloat16), own_grads, 1, 0)
-            prob_grad = contract(value_rows[...], own_grads, 1, 1)
-            center = jnp.sum(prob_grad * probs, axis=0, keepdims=True)
-            score_grad = (probs * (prob_grad - center)).astype(jnp.bfloat16)
-            key_sum[...] += contract(score_grad, own_rows, 1, 0)
-            parts.append(contract(score_grad, key_rows[...], 0, 0))
-        query_grad[at, :] = (
-            jnp.where(lanes < size, parts[0], parts[1]) * scale
-        ).astype(query_grad.dtype)
-        return 0
-
-    lax.fori_loop(0, queries.shape[0] // ROWS, some_rows, 0)
-    key_grad[...] = key_sum[...].astype(key_grad.dtype)
-    value_grad[...] = value_sum[...].astype(value_grad.dtype)
+    parts = []
+    key_sum, value_sum = 0.0, 0.0
+    for head in range(2):
+        own = (lanes < size) if head == 0 else (lanes >= size)
+        own_rows = jnp.where(own, queries[...], 0) * scale
+        own_grads = jnp.where(own, grads[...], 0)
+        scores = contract(key_rows[...], own_rows, 1, 1)
+        probs = jnp.exp(scores - logsum[8 * head : 8 * head + 1, :])
+        value_sum = value_sum + contract(probs.astype(jnp.bfloat16), own_grads, 1, 0)
+        prob_grad = contract(value_rows[...], own_grads, 1, 1)
+        center = jnp.sum(prob_grad * probs, axis=0, keepdims=True)
+        score_grad = (probs * (prob_grad - center)).astype(jnp.bfloat16)
+        key_sum = key_sum + contract(score_grad, own_rows, 1, 0)
+        parts.append(contract(score_grad, key_rows[...], 0, 0))
+    query_grad[...] = (jnp.where(lanes < size, parts[0], parts[1]) * scale).astype(query_grad.dtype)
+    key_grad[...] = key_sum.astype(key_grad.dtype)
+    value_grad[...] = value_sum.astype(value_grad.dtype)
 
 
 def column(rows, width, offset):
     return pl.BlockSpec((rows, width), lambda pair: (0, offset + pair))
 
 
-def run_attend(qkv):
+def run_attend(qkv, first, pairs):
     length, across = qkv.shape
-    model = across // 3
-    pairs = model // 128
+    every = across // 384
     return pl.pallas_call(
         attend,
         grid=(pairs,),
-        in_specs=[column(length, 128, pairs * part) for part in range(3)],
+        in_specs=[column(length, 128, every * part + first) for part in range(3)],
         out_specs=[column(length, 128, 0), pl.BlockSpec((16, length), lambda pair: (pair, 0))],
         out_shape=(
-            jax.ShapeDtypeStruct((length, model), jnp.bfloat16),
+            jax.ShapeDtypeStruct((length, 128 * pairs), jnp.bfloat16),
             jax.ShapeDtypeStruct((16 * pairs, length), jnp.float32),
         ),
         compiler_params=pltpu.CompilerParams(vmem_limit_bytes=40 << 20),
-        cost_estimate=pl.CostEstimate(flops=4 * length * length * model, bytes_accessed=8 * length * model, transcendentals=length * length * 12),
+        cost_estimate=spent(5 * pairs),
     )(qkv, qkv, qkv)
 
 
-def run_attend_back(qkv, logsum, grads):
+def run_attend_back(qkv, logsum, grads, first, pairs):
     length, across = qkv.shape
-    model = across // 3
-    pairs = model // 128
-    part = jax.ShapeDtypeStruct((length, model), jnp.bfloat16)
+    every = across // 384
+    part = jax.ShapeDtypeStruct((length, 128 * pairs), jnp.bfloat16)
     return pl.pallas_call(
         attend_back,
         grid=(pairs,),
-        in_specs=[column(length, 128, pairs * part) for part in range(3)]
-        + [pl.BlockSpec((16, length), lambda pair: (pair, 0)), column(length, 128, 0)],
+        in_specs=[column(length, 128, every * part + first) for part in range(3)]
+        + [
+            pl.BlockSpec((16, length), lambda pair: (first + pair, 0)),
+            column(length, 128, first),
+        ],
         out_specs=[column(length, 128, 0)] * 3,
         out_shape=(part, part, part),
-        scratch_shapes=[pltpu.VMEM((length, 128), jnp.float32)] * 2,
         compiler_params=pltpu.CompilerParams(vmem_limit_bytes=40 << 20),
-        cost_estimate=pl.CostEstimate(flops=10 * length * length * model, bytes_accessed=16 * length * model, transcendentals=length * length * 12),
+        cost_estimate=spent(1),
     )(qkv, qkv, qkv, logsum, grads)
+
+
+CHUNK = 512
+SLOPE = 0.7978845608028654
+
+
+def gelu_pair(values):
+    square = values * values
+    curve = jnp.tanh(SLOPE * values * (1.0 + 0.044715 * square))
+    half = 0.5 * (1.0 + curve)
+    slope = half + (0.5 * SLOPE) * values * (1.0 - curve * curve) * (1.0 + 3 * 0.044715 * square)
+    return values * half, slope
+
+
+def unit(values):
+    center = jnp.mean(values, axis=-1, keepdims=True)
+    shifted = values - center
+    spread = jnp.mean(shifted * shifted, axis=-1, keepdims=True)
+    root = lax.rsqrt(spread + 1e-05)
+    return shifted * root, root
+
+
+def unit_back(normal, root, given):
+    return (
+        given
+        - jnp.mean(given, axis=-1, keepdims=True)
+        - normal * jnp.mean(given * normal, axis=-1, keepdims=True)
+    ) * root
+
+
+def column_sum(values):
+    return jnp.sum(values.reshape(-1, 8, values.shape[1]), axis=0)
+
+
+def feed_ahead(mixed, gains, up, down, summed, feature):
+    normal, _ = unit(mixed[...])
+    normed = normal * gains[0:1]
+    hidden = contract(normed.astype(jnp.bfloat16), up[...], 1, 0)
+    active, _ = gelu_pair(hidden)
+    total = normed + contract(active.astype(jnp.bfloat16), down[...], 1, 0)
+    summed[...] = total
+    normal, _ = unit(total)
+    feature[...] = (normal * gains[1:2]).astype(feature.dtype)
+
+
+def feed_back(
+    mixed, summed, feature_grad, gains, up, down, out,
+    active_out, hidden_grad, ffn_out, normed_out, mixed_grad, attended, context_grad, gain_sums
+):
+    @pl.when(pl.program_id(0) == 0)
+    def start():
+        gain_sums[...] = jnp.zeros_like(gain_sums)
+
+    normal, root = unit(summed[...])
+    given = feature_grad[...].astype(jnp.float32)
+    gain_sums[8:16] += column_sum(given * normal)
+    summed_grad = unit_back(normal, root, given * gains[1:2])
+    ffn_grad = summed_grad.astype(jnp.bfloat16)
+    ffn_out[...] = ffn_grad
+    normal, root = unit(mixed[...])
+    normed = (normal * gains[0:1]).astype(jnp.bfloat16)
+    normed_out[...] = normed
+    hidden = contract(normed, up[...], 1, 0)
+    active, slope = gelu_pair(hidden)
+    active_out[...] = active.astype(jnp.bfloat16)
+    hidden_grad[...] = (slope * contract(ffn_grad, down[...], 1, 1)).astype(jnp.bfloat16)
+    normed_grad = summed_grad + contract(hidden_grad[...], up[...], 1, 1)
+    gain_sums[0:8] += column_sum(normed_grad * normal)
+    total = unit_back(normal, root, normed_grad * gains[0:1])
+    mixed_grad[...] = total
+    attended[...] = total.astype(jnp.bfloat16)
+    context_grad[...] = contract(attended[...], out[...], 1, 1).astype(jnp.bfloat16)
+
+
+def blend_both(
+    feature, pooled, out_grad, gains, blend,
+    result, feature_grad, state_grad, grads, gain_sum, early, middle, late, spread, total
+):
+    length = feature.shape[0]
+    pair = 2 * D
+    rows = 128
+    chunks = [slice(at, at + rows) for at in range(0, length, rows)]
+
+    def ahead(number):
+        return contract(feature[...], blend[number * pair : number * pair + D, :], 1, 0) + contract(
+            pooled[...], blend[number * pair + D : number * pair + pair, :], 1, 0
+        )
+
+    edge = jnp.zeros((8, D), jnp.float32)
+    early[0:8] = edge
+    late[length : length + 8] = edge
+    spread[0:8] = edge
+    spread[length + 8 : length + 16] = edge
+    early[8 : length + 8] = ahead(0)
+    middle[...] = ahead(1)
+    late[0:length] = ahead(2)
+    gain_sum[...] = jnp.zeros_like(gain_sum)
+    for chunk in chunks:
+        before = slice(chunk.start + 7, chunk.stop + 7)
+        after = slice(chunk.start + 1, chunk.stop + 1)
+        blended, slope = gelu_pair(middle[chunk] + early[before] + late[after])
+        normal, root = unit(feature[chunk].astype(jnp.float32) + blended)
+        result[chunk] = (normal * gains[2:3]).astype(result.dtype)
+        given = out_grad[chunk].astype(jnp.float32)
+        gain_sum[...] += column_sum(given * normal)
+        whole_grad = unit_back(normal, root, given * gains[2:3])
+        total[chunk] = whole_grad
+        spread[slice(chunk.start + 8, chunk.stop + 8)] = whole_grad * slope
+    for chunk in chunks:
+        for number, offset in ((0, 9), (1, 8), (2, 7)):
+            grads[chunk, number * D : number * D + D] = spread[
+                slice(chunk.start + offset, chunk.stop + offset)
+            ].astype(jnp.bfloat16)
+
+    def back(left):
+        return sum(
+            contract(
+                grads[:, number * D : number * D + D],
+                blend[number * pair + left : number * pair + left + D, :],
+                1,
+                1,
+            )
+            for number in range(3)
+        )
+
+    feature_grad[...] = (total[...] + back(0)).astype(feature_grad.dtype)
+    state_grad[...] = back(D)
+
+
+def params(size):
+    return pltpu.CompilerParams(vmem_limit_bytes=size << 20)
+
+
+def rows_block(width):
+    return pl.BlockSpec((CHUNK, width), lambda step: (step, 0))
+
+
+def fixed(*shape):
+    return pl.BlockSpec(shape, lambda step: (0,) * len(shape))
+
+
+def run_feed(mixed, gains, up, down):
+    length = mixed.shape[0]
+    wide = up.shape[1]
+    return pl.pallas_call(
+        feed_ahead,
+        grid=(length // CHUNK,),
+        in_specs=[rows_block(D), fixed(3, D), fixed(D, wide), fixed(wide, D)],
+        out_specs=[rows_block(D), rows_block(D)],
+        out_shape=[
+            jax.ShapeDtypeStruct((length, D), jnp.float32),
+            jax.ShapeDtypeStruct((length, D), jnp.bfloat16),
+        ],
+        compiler_params=params(56),
+        cost_estimate=spent(18),
+    )(mixed, gains, up, down)
+
+
+def run_feed_back(mixed, summed, feature_grad, gains, up, down, out):
+    length = mixed.shape[0]
+    wide = up.shape[1]
+    bf = jnp.bfloat16
+    f32 = jnp.float32
+    widths = [(wide, bf), (wide, bf), (D, bf), (D, bf), (D, f32), (D, bf), (D, bf)]
+    return pl.pallas_call(
+        feed_back,
+        grid=(length // CHUNK,),
+        in_specs=[rows_block(D)] * 3 + [fixed(3, D), fixed(D, wide), fixed(wide, D), fixed(D, D)],
+        out_specs=[rows_block(width) for width, _ in widths] + [fixed(16, D)],
+        out_shape=[jax.ShapeDtypeStruct((length, width), kind) for width, kind in widths]
+        + [jax.ShapeDtypeStruct((16, D), f32)],
+        compiler_params=params(60),
+        cost_estimate=spent(32),
+    )(mixed, summed, feature_grad, gains, up, down, out)
+
+
+def run_blend(feature, pooled, out_grad, gains, blend):
+    length = feature.shape[0]
+    bf = jnp.bfloat16
+    f32 = jnp.float32
+    return pl.pallas_call(
+        blend_both,
+        out_shape=[
+            jax.ShapeDtypeStruct((length, D), bf),
+            jax.ShapeDtypeStruct((length, D), bf),
+            jax.ShapeDtypeStruct((length, D), f32),
+            jax.ShapeDtypeStruct((length, 3 * D), bf),
+            jax.ShapeDtypeStruct((8, D), f32),
+        ],
+        scratch_shapes=[
+            pltpu.VMEM((length + 8, D), f32),
+            pltpu.VMEM((length, D), f32),
+            pltpu.VMEM((length + 8, D), f32),
+            pltpu.VMEM((length + 16, D), f32),
+            pltpu.VMEM((length, D), f32),
+        ],
+        compiler_params=params(60),
+        cost_estimate=spent(26),
+    )(feature, pooled, out_grad, gains, blend)
+
+
+def blend_weight_grad(feature, pooled, grads, out):
+    out[0:D, :] = contract(feature[...], grads[...], 0, 0).astype(out.dtype)
+    out[D : 2 * D, :] = contract(pooled[...], grads[...], 0, 0).astype(out.dtype)
+
+
+def run_blend_grad(feature, pooled, grads):
+    length = feature.shape[0]
+    return pl.pallas_call(
+        blend_weight_grad,
+        grid=(3,),
+        in_specs=[
+            fixed(length, D),
+            fixed(length, D),
+            pl.BlockSpec((length, D), lambda third: (0, third)),
+        ],
+        out_specs=pl.BlockSpec((2 * D, D), lambda third: (third, 0)),
+        out_shape=jax.ShapeDtypeStruct((6 * D, D), jnp.bfloat16),
+        compiler_params=params(48),
+        cost_estimate=spent(12),
+    )(feature, pooled, grads)
 
 
 def on_device(
@@ -700,152 +1001,130 @@
             on_first, jnp.concatenate([kept, got], 0), jnp.concatenate([got, kept], 0)
         )
 
+    ids_row = jnp.where(on_first, char_ids[0], char_ids[1])
+    lengths_row = jnp.where(on_first, char_lengths[0], char_lengths[1])
+
+    queries = HEADS // 2
     groups = 3
+    pairs = queries // groups
+    wide = 128 * pairs
+    everyone = ("stream", "dp")
     by_group = w_qkv.reshape(w_qkv.shape[0], 3, groups, -1).transpose(0, 2, 1, 3)
     by_group = by_group.reshape(w_qkv.shape[0], groups, -1)
-    ids_row = jnp.where(on_first, char_ids[0], char_ids[1])
-    lengths_row = jnp.where(on_first, char_lengths[0], char_lengths[1])
-    segment = char_segments(lengths_row, ids_row.shape[0])
-    shares = 1.0 / lengths_row.astype(jnp.float32)[:, None]
-    ends = jnp.cumsum(lengths_row)
-
     flow.begin("tokens", swap_chain(jnp.where(on_first, tokens_in[1], tokens_in[0])), [4])
-    flow.begin("first", gather_chain([by_group[:, 0]], False))
-    flow.begin("second", gather_chain([by_group[:, 1]], True))
+    flow.begin("group0", gather_steps([by_group[:, 0]], False))
+    flow.begin("group1", gather_steps([by_group[:, 1]], True))
     flow.slot(())
     flow.slot(())
-    flow.begin("third", gather_chain([by_group[:, 2], w_out], True))
+    flow.begin("group2", gather_steps([by_group[:, 2], w_out], True))
+    flow.begin("up", gather_steps([w_up], True), [0, 1, 0, 1, 0])
     flow.slot(())
     shards = flow.slot((char_table, w_gru, gains_row(gains), w_blend))
-    flow.begin("up", gather_chain([w_up], True), [0, 0, 0, 1, 0])
     shapes = shapes_of(shards[:3], 1)
     packed = jnp.concatenate([to_rows(shard, 1)[0] for shard in shards[:3]], 0)
-    rest = gather_whole(packed, shapes)
+    rest = lax.all_gather(packed, everyone, axis=0, tiled=False)
     blend_all = lax.all_gather(
-        shards[3].astype(jnp.bfloat16), ("stream", "dp"), axis=0, tiled=True
-    )
+        shards[3].astype(jnp.bfloat16), everyone, axis=0, tiled=True
+    )
+    flow.begin("down", gather_steps([w_down], True), [0, 0, 1, 0, 0])
     flow.slot(())
     tokens = both_halves(tokens_in, flow.end("tokens"))
-    (w_first,) = flow.end("first")
-    (w_second,) = flow.end("second")
-    flow.begin("down", gather_chain([w_down], True), [0, 0, 0, 1, 0])
-    flow.begin("out_grad", swap_chain(jnp.where(on_first, out_grad[1], out_grad[0])), [2])
-    qkv_parts, contexts, logsums = [], [], []
-
-    def attend_group(w_group):
+    weights, parts_qkv, contexts, logsums = [], [], [], []
+    for number in range(groups):
+        w_group, *w_more = flow.end("group%d" % number)
+        if number == 2:
+            segment = char_segments(lengths_row, ids_row.shape[0])
+            shares = 1.0 / lengths_row.astype(jnp.float32)[:, None]
+            ends = jnp.cumsum(lengths_row)
+            lengths_row = (segment, shares, ends)
         qkv = product(tokens, w_group).astype(jnp.bfloat16)
-        context, logsum = run_attend(qkv)
-        return qkv, context, logsum
-
-    qkv, context, logsum = attend_group(w_first)
-    qkv, context, logsum, tokens = flow.slot((qkv, context, logsum, tokens))
-    qkv_parts.append(qkv)
-    contexts.append(context)
-    logsums.append(logsum)
-    qkv, context, logsum = attend_group(w_second)
-    qkv, context, logsum, tokens = flow.slot((qkv, context, logsum, tokens))
-    qkv_parts.append(qkv)
-    contexts.append(context)
-    logsums.append(logsum)
-    w_third, out_all = flow.end("third")
-    qkv, context, logsum = attend_group(w_third)
-    qkv, context, logsum, tokens = flow.slot((qkv, context, logsum, tokens))
-    qkv_parts.append(qkv)
-    contexts.append(context)
-    logsums.append(logsum)
+        context, logsum = run_attend(qkv, 0, pairs)
+        qkv, context, logsum, tokens, lengths_row = flow.slot(
+            (qkv, context, logsum, tokens, lengths_row)
+        )
+        weights.append(w_group)
+        parts_qkv.append(qkv)
+        contexts.append(context)
+        logsums.append(logsum)
+    (out_all,) = w_more
+    segment, shares, ends = lengths_row
     context = jnp.concatenate(contexts, 1)
-    mixed_sum = tokens.astype(jnp.float32) + product(context, out_all)
-    mixed_sum, rest = flow.slot((mixed_sum, rest))
-    table_all, gru_all, gain_all = rest
+    table_all, gru_all, gain_all = unpack_rows(rest, shapes)
     gain_all = gain_all.reshape(parts, -1, D)[:, 0, : gains.size]
     gain_all = gain_all.reshape(parts, 3, -1).transpose(1, 0, 2).reshape(3, -1).astype(jnp.float32)
     letters, before, pooled = run_chars(ids_row, ends, table_all, gru_all, shares)
-    letters, before, pooled, mixed_sum = flow.slot((letters, before, pooled, mixed_sum))
-    normed = norm_gain(mixed_sum, gain_all[0])
+    letters, before, pooled, context, tokens = flow.slot((letters, before, pooled, context, tokens))
+    mixed_sum = tokens.astype(jnp.float32) + product(context, out_all)
+    mixed_sum, gain_all = flow.slot((mixed_sum, gain_all))
+    flow.begin("out_grad", swap_chain(jnp.where(on_first, out_grad[1], out_grad[0])))
     (up_all,) = flow.end("up")
-    hidden = product(normed.astype(jnp.bfloat16), up_all)
-    active = jax.nn.gelu(hidden).astype(jnp.bfloat16)
-    active, hidden, normed = flow.slot((active, hidden, normed))
     (down_all,) = flow.end("down")
-    summed = normed + product(active, down_all)
-    feature = norm_gain(summed, gain_all[1]).astype(jnp.bfloat16)
-
+    summed, feature = run_feed(mixed_sum, gain_all, up_all, down_all)
+    summed, feature, blend_all = flow.slot((summed, feature, blend_all))
     whole_grad = both_halves(out_grad, flow.end("out_grad"))
-    joined = jnp.concatenate([feature, pooled], 1)
-    stacked = jnp.concatenate([rows_before(joined), joined, rows_after(joined)], 1)
-    blend_in = product(stacked, blend_all)
-    blended, gelu_pull = jax.vjp(jax.nn.gelu, blend_in)
-    result, norm_pull = jax.vjp(norm_gain, feature.astype(jnp.float32) + blended, gain_all[2])
-    total_grad, gain_blend = norm_pull(whole_grad.astype(jnp.float32))
-    blend_grad = gelu_pull(total_grad)[0].astype(jnp.bfloat16)
-    grad_blend = inner_rows(stacked, blend_grad)
-    stacked_grad = inner_cols(blend_grad, blend_all)
-    pair_width = joined.shape[1]
-    joined_grad = (
-        stacked_grad[:, pair_width : 2 * pair_width]
-        + rows_after(stacked_grad[:, :pair_width])
-        + rows_before(stacked_grad[:, 2 * pair_width :])
-    )
-    feature_grad = (total_grad + joined_grad[:, :D]).astype(jnp.bfloat16)
-    result = result.astype(jnp.bfloat16)
-    flow.begin(
-        "result", swap_chain(jnp.where(on_first, result[half_len:], result[:half_len])), [2]
-    )
+    result, feature_grad, state_grad, blend_grads, gain_blend = run_blend(
+        feature, pooled, whole_grad, gain_all, blend_all
+    )
+    grad_blend = run_blend_grad(feature, pooled, blend_grads)
+    result, grad_blend, feature_grad = flow.slot((result, grad_blend, feature_grad))
     (blend_sum,) = scatter_whole([grad_blend])
-
-    summed_grad, gain_ffn = jax.vjp(norm_gain, summed, gain_all[1])[1](
-        feature_grad.astype(jnp.float32)
-    )
-    ffn_grad = summed_grad.astype(jnp.bfloat16)
-    grad_down = inner_rows(active, ffn_grad).astype(jnp.bfloat16)
-    hidden_grad = jax.vjp(jax.nn.gelu, hidden)[1](inner_cols(ffn_grad, down_all))[0].astype(
-        jnp.bfloat16
-    )
-    grad_up = inner_rows(normed.astype(jnp.bfloat16), hidden_grad).astype(jnp.bfloat16)
-    normed_grad = summed_grad + inner_cols(hidden_grad, up_all)
-    flow.begin("down", scatter_chain([grad_down], True))
-    flow.begin("up", scatter_chain([grad_up], False))
-    mixed_grad, gain_attn = jax.vjp(norm_gain, mixed_sum, gain_all[0])[1](normed_grad)
-    attended_grad = mixed_grad.astype(jnp.bfloat16)
-    grad_out = inner_rows(context, attended_grad).astype(jnp.bfloat16)
-    context_grad = inner_cols(attended_grad, out_all).astype(jnp.bfloat16)
-    gain_grads = jnp.stack([gain_attn, gain_ffn, gain_blend])
-    state_grad = joined_grad[:, D:]
-    context_grad, grad_out, gain_grads, mixed_grad, state_grad = flow.slot(
-        (context_grad, grad_out, gain_grads, mixed_grad, state_grad)
-    )
-    grad_gru, grad_table = run_chars_back(
-        ids_row, segment, state_grad, shares, table_all, gru_all, letters, before
-    )
-    context_grad, grad_gru, grad_table = flow.slot((context_grad, grad_gru, grad_table))
-    flow.begin("letters", scatter_chain([grad_gru, grad_table, grad_out], True))
+    flow.begin("result", swap_chain(jnp.where(on_first, result[half_len:], result[:half_len])))
+    active, hidden_grad, ffn_grad, normed, mixed_grad, attended_grad, context_grad, gain_sums = (
+        run_feed_back(mixed_sum, summed, feature_grad, gain_all, up_all, down_all, out_all)
+    )
+    gain_grads = jnp.stack(
+        [jnp.sum(gain_sums[:8], 0), jnp.sum(gain_sums[8:], 0), jnp.sum(gain_blend, 0)]
+    )
     gain_rows = gain_grads.reshape(3, parts, -1).transpose(1, 0, 2).reshape(parts, -1)
     gain_rows = jnp.pad(gain_rows[:, None], ((0, 0), (0, 7), (0, D - gain_rows.shape[1])))
     gain_rows = gain_rows.reshape(8 * parts, D)
+    grad_down = inner_rows(active, ffn_grad).astype(jnp.bfloat16)
+    grad_up = inner_rows(normed, hidden_grad).astype(jnp.bfloat16)
+    grad_out = inner_rows(context, attended_grad).astype(jnp.bfloat16)
+    grad_down, grad_up, grad_out, state_grad, context_grad, gain_rows = flow.slot(
+        (grad_down, grad_up, grad_out, state_grad, context_grad, gain_rows)
+    )
+    flow.begin("feed", scatter_chain([grad_down, grad_up]))
     tokens_grad = mixed_grad
-    weights = (w_first, w_second, w_third)
+    group_grads = []
     for number in range(groups):
-        width = context_grad.shape[1] // groups
+        left = wide * number
         qkv_grad = jnp.concatenate(
             run_attend_back(
-                qkv_parts[number],
-                logsums[number],
-                context_grad[:, number * width : number * width + width],
+                parts_qkv[number], logsums[number], context_grad[:, left : left + wide], 0, pairs
             ),
             1,
         )
+        tokens_grad = tokens_grad + inner_cols(qkv_grad, weights[number])
         grad_group = inner_rows(tokens, qkv_grad).astype(jnp.bfloat16)
-        tokens_grad = tokens_grad + inner_cols(qkv_grad, weights[number])
-        if number < 2:
-            context_grad, grad_group, tokens_grad = flow.slot(
-                (context_grad, grad_group, tokens_grad)
-            )
-        grads = [grad_group, gain_rows] if number == 0 else [grad_group]
-        flow.begin("qkv%d" % number, scatter_chain(grads, number % 2 == 1))
-    tokens_grad = tokens_grad.astype(jnp.bfloat16)
+        if number == groups - 1:
+            tokens_grad = tokens_grad.astype(jnp.bfloat16)
+        if number != 1:
+            done = (context_grad, grad_group, tokens_grad, state_grad)
+            done, blend_sum = flow.slot((done, blend_sum)) if number else (flow.slot(done), blend_sum)
+            context_grad, grad_group, tokens_grad, state_grad = done
+        group_grads.append(grad_group)
     flow.begin(
-        "tokens", swap_chain(jnp.where(on_first, tokens_grad[half_len:], tokens_grad[:half_len])), [4]
-    )
+        "tokens", swap_chain(jnp.where(on_first, tokens_grad[half_len:], tokens_grad[:half_len]))
+    )
+    flow.begin("qkv", scatter_chain(group_grads + [grad_out, gain_rows]), [0, 0, 1])
+    blocks = ids_row.shape[0] // STEP_ROWS
+    spread, *held = run_chars_back(
+        blocks, blocks // 2, ids_row, segment, letters, before, upstream=[state_grad, shares]
+    )
+    spread, held = flow.slot((spread, held))
+    grad_gru, grad_table = run_chars_back(
+        blocks // 2,
+        blocks // 2,
+        ids_row,
+        segment,
+        letters,
+        before,
+        held=[spread, *held],
+        ends=[table_all, gru_all],
+    )
+    grad_gru, grad_table = flow.slot((grad_gru, grad_table))
+    flow.begin("letters", scatter_chain([grad_gru, grad_table]))
     while flow.live:
         flow.slot(())
     own_result = jnp.where(on_first, result[:half_len], result[half_len:])
@@ -859,15 +1138,16 @@
         jnp.where(on_first, own_grad, back_grad),
         jnp.where(on_first, back_grad, own_grad),
     ]
-    first_sum, gain_sum = flow.end("qkv0")
-    group_sums = jnp.stack([first_sum, flow.end("qkv1")[0], flow.end("qkv2")[0]], 1)
+    *group_sums, out_sum, gain_sum = flow.end("qkv")
+    group_sums = jnp.stack(group_sums, 1)
     qkv_sum = group_sums.reshape(w_qkv.shape[0], groups, 3, -1).transpose(0, 2, 1, 3)
     letter_sums = flow.end("letters")
+    feed_sums = flow.end("feed")
     sums = (
         qkv_sum.reshape(w_qkv.shape),
-        letter_sums[2],
-        flow.end("up")[0],
-        flow.end("down")[0],
+        out_sum,
+        feed_sums[1],
+        feed_sums[0],
         letter_sums[0],
         blend_sum,
         letter_sums[1],

time: 647 us -> 522 us (0.81)
  matrix products: 127 us -> 40 us
  Pallas kernels: 175 us -> 244 us
  local copies, waits for them, and re-layouts: 87.9 us -> 46.6 us
  waiting for transfers between devices: 89.1 us -> 57.3 us
  other arithmetic: 88.7 us -> 59.2 us
    pallas_call x4 -> x13, Pallas kernels: 79.9 us -> 166 us  [the longest x2 51.5 us: run_chars_back(): pl.pallas_call(functools.partial(chars_back, (last,), upstream is not Non...]
    dot_general x7 -> x3, matrix products: 41.5 us -> 4.26 us  [inner_cols(): lax.dot_general(former, latter, (((1,), (1,)), ((), ())), preferred_eleme...]
    ppermute x59 -> x50, waiting for transfers between devices: 89.1 us -> 56.3 us  [swap(): lax.ppermute(block, ('stream', 'dp'), [(place, place ^ mask) for place in...]
    dot_general x7 -> x4, matrix products: 37.5 us -> 7.26 us  [product(): return jnp.dot(former, latter, preferred_element_type=jnp.float32)]
    slice x69 -> x3, local copies, waits for them, and re-layouts: 24.4 us -> 1.82 us  [the longest x2 1.15 us: on_device(): context_grad[:, left:left + wide]]
    dot_general x7 -> x6, matrix products: 47.6 us -> 28.5 us  [inner_rows(): lax.dot_general(former, latter, (((0,), (0,)), ((), ())), preferred_eleme...]
    add x27 -> x0, other arithmetic: 18.9 us -> none  [the longest x1 7.29 us: on_device(): stacked_grad[:, pair_width:2 * pair_width]]
    reduce_sum x9 -> x2, other arithmetic: 18.7 us -> 0.05 us  [the longest x1 0.03 us: on_device(): jnp.sum(gain_sums[:8], 0)]
  transfers between devices with their start and end apart: 62 -> 53, of which waited for: 20 -> 16; matrix products, arithmetic and copies ran while one was open for 21% -> 22% of each run, Pallas kernels for 27% -> 40%
where the time goes in v3:
time: 522 us; the launch traced here: 517 us
  Pallas kernels  244 us (47%)
  other arithmetic  59.2 us (11%)
  waiting for transfers between devices  57.3 us (11%)
  starting transfers between devices  53.6 us (10%)
  local copies, waits for them, and re-layouts  46.6 us (9%)
  matrix products  40 us (8%)
  between operations  15.7 us (3%)
    ppermute x50, waiting for transfers between devices, swap(): lax.ppermute(block, ('stream', 'dp'), [(place, place ^ mask) for place in...  56.3 us
    ppermute x50, starting transfers between devices, swap(): lax.ppermute(block, ('stream', 'dp'), [(place, place ^ mask) for place in...  53.4 us
    pallas_call x2, Pallas kernels, run_chars_back(): pl.pallas_call(functools.partial(chars_back, (last,), upstream is not Non...  51.5 us
    pallas_call x3, Pallas kernels, run_attend_back(): pl.pallas_call(attend_back, grid=(pairs,), in_specs=[column(length, 128,...  39.6 us
    pallas_call x1, Pallas kernels, run_feed_back(): pl.pallas_call(feed_back, grid=(length // CHUNK,), in_specs=[rows_block(D...  32 us
    unnamed x233, local copies, waits for them, and re-layouts  29.7 us
    dot_general x6, matrix products, inner_rows(): lax.dot_general(former, latter, (((0,), (0,)), ((), ())), preferred_eleme...  28.5 us
    pallas_call x1, Pallas kernels, run_blend(): pl.pallas_call(blend_both, out_shape=[jax.ShapeDtypeStruct((length, D), b...  25.7 us
  transfers between devices with their start and end apart: 53, of which 16 were waited for; matrix products, arithmetic and copies ran while one was open for 22% of the time, Pallas kernels for 40%

profile of v3, /device:TPU:0, one launch (start us, length us, event | category | flops | bytes accessed | tf_op | source)
XLA Modules:
  0.0 516.7 jit_solution(13472600867970252720)
XLA Ops:
  19.3 4.4 collective-permute-done.4
  27.9 4.3 collective-permute-done.7
  35.5 6.0 %collective-permute-done.12 = bf16[1,1,2,1,48,768]{5,4,3,2,1,0:T(8,128)(2,1)S(1)} collective-permute-done((bf16[1,1,2,1,48,768]{5,4,3,2,1,0:T(8,128)(2,1)S(1)}, bf16[1,1,2,1,48,768]{5,4,3,2,1,0:T(8,128)(2,1)S(1)}, u32[]{:S(2)}, u32[]{:S(2)}) %collective-permute-start.12) | collective-permute-done | bytes 147488 | tf_op jit(solution)/shard_map/ppermute | solution.py:36
  73.1 7.4 %shard_map.468 = (bf16[1024,256]{1,0:T(8,128)(2,1)S(1)}, f32[32,1024]{1,0:T(8,128)S(1)}) custom-call(bf16[1024,768]{1,0:T(8,128)(2,1)S(1)} %convolution_convert_fusion.4.queries.key_rows.value_rows, bf16[1024,768]{1,0:T(8,128)(2,1)S(1)} %convolution_convert_fusion.4.queries.key_rows.value_rows, ...), custom_call_target="tpu_custom_call" | custom-call | flops 10000000000 | bytes 1 | tf_op jit(solution)/shard_map/pallas_call | solution.py:688
  88.4 7.4 %shard_map.470 = (bf16[1024,256]{1,0:T(8,128)(2,1)S(1)}, f32[32,1024]{1,0:T(8,128)S(1)}) custom-call(bf16[1024,768]{1,0:T(8,128)(2,1)S(1)} %convolution_convert_fusion.3.queries.key_rows.value_rows, bf16[1024,768]{1,0:T(8,128)(2,1)S(1)} %convolution_convert_fusion.3.queries.key_rows.value_rows, ...), custom_call_target="tpu_custom_call" | custom-call | flops 10000000000 | bytes 1 | tf_op jit(solution)/shard_map/pallas_call | solution.py:688
  98.3 8.2 %scatter_custom_fusion = s32[4096]{0:T(1024)} fusion(s32[1024]{0:T(1024)S(1)} %get-tuple-element.466, s32[1024]{0:T(1024)S(1)} %broadcast.110, s32[]{:T(128)} %constant.28.clone.1), kind=kCustom, calls=%fused_computation.139 | custom fusion | flops 1024 | bytes 16388 | tf_op jit(solution)/shard_map/scatter-add | solution.py:349
  115.3 7.4 %shard_map.472 = (bf16[1024,256]{1,0:T(8,128)(2,1)S(1)}, f32[32,1024]{1,0:T(8,128)S(1)}) custom-call(bf16[1024,768]{1,0:T(8,128)(2,1)S(1)} %convolution_convert_fusion.2.queries.key_rows.value_rows, bf16[1024,768]{1,0:T(8,128)(2,1)S(1)} %convolution_convert_fusion.2.queries.key_rows.value_rows, ...), custom_call_target="tpu_custom_call" | custom-call | flops 10000000000 | bytes 1 | tf_op jit(solution)/shard_map/pallas_call | solution.py:688
  138.1 20.8 %shard_map.474 = (f32[256,16,128]{2,1,0:T(8,128)}, f32[4096,8,128]{2,1,0:T(8,128)}, bf16[1024,768]{1,0:T(8,128)(2,1)}) custom-call(s32[4096]{0:T(1024)} %bitcast.209, s32[4096]{0:T(1024)} %rev.10.rows_b.refs_1_, s32[1024]{0:T(1024)} %get-tuple-element.282.ends, bf16[256,768]{1,0:T(8,128)(2,1)} %copy-done.31, bf16[768,1536]{1,0:T(8,128)(2,1)} %copy-done.29, ...), custom_call_target="tpu_custom_call" | custom-call | flops 24000000000 | bytes 1 | tf_op jit(solution)/shard_map/pallas_call | solution.py:579
  158.9 5.2 %collective-permute-done.24 = bf16[1,2,2,2,96,768]{5,4,3,2,1,0:T(8,128)(2,1)} collective-permute-done((bf16[1,2,2,2,96,768]{5,4,3,2,1,0:T(8,128)(2,1)}, bf16[1,2,2,2,96,768]{5,4,3,2,1,0:T(8,128)(2,1)}, u32[]{:S(2)}, u32[]{:S(2)}) %collective-permute-start.24) | collective-permute-done | bytes 1179680 | tf_op jit(solution)/shard_map/ppermute | solution.py:36
  164.1 3.4 pad_maximum_fusion.1
  177.7 3.6 shard_map.476.down
  183.5 17.5 %shard_map.477 = (f32[1024,768]{1,0:T(8,128)}, bf16[1024,768]{1,0:T(8,128)(2,1)}) custom-call(f32[1024,768]{1,0:T(8,128)} %convert_add_fusion.mixed, f32[3,768]{1,0:T(4,128)} %reshape.258.gains, bf16[768,3072]{1,0:T(8,128)(2,1)} %copy-done.14, bf16[3072,768]{1,0:T(8,128)(2,1)} %copy-done.15), custom_call_target="tpu_custom_call" | custom-call | flops 17999998976 | bytes 1 | tf_op jit(solution)/shard_map/pallas_call | solution.py:863
  204.1 25.7 %shard_map.478 = (bf16[1024,768]{1,0:T(8,128)(2,1)}, bf16[1024,768]{1,0:T(8,128)(2,1)}, f32[1024,768]{1,0:T(8,128)}, bf16[1024,2304]{1,0:T(8,128)(2,1)}, f32[8,768]{1,0:T(8,128)}) custom-call(bf16[1024,768]{1,0:T(8,128)(2,1)} %get-tuple-element.315.feature, bf16[1024,768]{1,0:T(8,128)(2,1)} %get-tuple-element.316.pooled, ...), custom_call_target="tpu_custom_call" | custom-call | flops 25999998976 | bytes 1 | tf_op jit(solution)/shard_map/pallas_call | solution.py:899
  229.7 10.8 %shard_map.479 = bf16[4608,768]{1,0:T(8,128)(2,1)} custom-call(bf16[1024,768]{1,0:T(8,128)(2,1)S(1)} %copy-done.34, bf16[1024,768]{1,0:T(8,128)(2,1)S(1)} %copy-done.33, bf16[1024,2304]{1,0:T(8,128)(2,1)} %get-tuple-element.320.grads), custom_call_target="tpu_custom_call" | custom-call | flops 12000000000 | bytes 1 | tf_op jit(solution)/shard_map/pallas_call | solution.py:927
  242.4 32.0 %shard_map.480 = (bf16[1024,3072]{1,0:T(8,128)(2,1)}, bf16[1024,3072]{1,0:T(8,128)(2,1)}, bf16[1024,768]{1,0:T(8,128)(2,1)}, bf16[1024,768]{1,0:T(8,128)(2,1)}, ...) custom-call(f32[1024,768]{1,0:T(8,128)} %convert_add_fusion.mixed, ...), custom_call_target="tpu_custom_call" | custom-call | flops 32000000000 | bytes 1 | tf_op jit(solution)/shard_map/pallas_call | solution.py:883
  274.5 10.0 %convolution_convert_fusion.1.refs_0_ = bf16[3072,768]{1,0:T(8,128)(2,1)} fusion(bf16[1024,3072]{1,0:T(8,128)(2,1)} %get-tuple-element.325, bf16[1024,768]{1,0:T(8,128)(2,1)} %get-tuple-element.326), kind=kOutput, calls=%fused_computation.2 | convolution fusion | flops 4834197504 | bytes 12582912 | tf_op jit(solution)/shard_map/dot_general | solution.py:321
  284.5 6.9 %convolution_convert_fusion.refs_1_ = bf16[768,3072]{1,0:T(8,128)(2,1)} fusion(bf16[1024,768]{1,0:T(8,128)(2,1)S(1)} %copy-done.101, bf16[1024,3072]{1,0:T(8,128)(2,1)S(1)} %copy-done.100), kind=kOutput, calls=%fused_computation.1 | convolution fusion | flops 4834197504 | bytes 12582912 | tf_op jit(solution)/shard_map/dot_general | solution.py:321
  292.0 4.1 convolution_convert_fusion.8.refs_3_
  296.1 6.2 %shard_map.482 = (bf16[16,192,768]{2,1,0:T(8,128)(2,1)S(1)}, bf16[16,192,768]{2,1,0:T(8,128)(2,1)}) custom-call(s32[1]{0:T(128)} %bitcast.13.place, bf16[3072,768]{1,0:T(8,128)(2,1)S(1)} %copy-done.16, bf16[768,3072]{1,0:T(8,128)(2,1)} %convolution_convert_fusion.refs_1_), custom_call_target="tpu_custom_call" | custom-call | flops 4000000000 | bytes 1 | tf_op jit(solution)/shard_map/pallas_call | solution.py:259
  306.4 13.1 %shard_map.481 = (bf16[1024,256]{1,0:T(8,128)(2,1)S(1)}, bf16[1024,256]{1,0:T(8,128)(2,1)S(1)}, bf16[1024,256]{1,0:T(8,128)(2,1)S(1)}) custom-call(bf16[1024,768]{1,0:T(8,128)(2,1)S(1)} %copy-done.4, bf16[1024,768]{1,0:T(8,128)(2,1)S(1)} %copy-done.4, bf16[1024,768]{1,0:T(8,128)(2,1)S(1)} %copy-done.4, f32[32,1024]{1,0:T(8,128)S(1)} %copy-done.10, ...), custom_call_target="tpu_custom_call" | custom-call | flops 1000000000 | bytes 1 | tf_op jit(solution)/shard_map/pallas_call | solution.py:706
  329.4 4.9 shard_map.485
  337.9 13.1 %shard_map.483 = (bf16[1024,256]{1,0:T(8,128)(2,1)S(1)}, bf16[1024,256]{1,0:T(8,128)(2,1)S(1)}, bf16[1024,256]{1,0:T(8,128)(2,1)S(1)}) custom-call(bf16[1024,768]{1,0:T(8,128)(2,1)S(1)} %copy-done.6, bf16[1024,768]{1,0:T(8,128)(2,1)S(1)} %copy-done.6, bf16[1024,768]{1,0:T(8,128)(2,1)S(1)} %copy-done.6, f32[32,1024]{1,0:T(8,128)S(1)} %copy-done.12, ...), custom_call_target="tpu_custom_call" | custom-call | flops 1000000000 | bytes 1 | tf_op jit(solution)/shard_map/pallas_call | solution.py:706
  351.1 13.3 %shard_map.484 = (bf16[1024,256]{1,0:T(8,128)(2,1)S(1)}, bf16[1024,256]{1,0:T(8,128)(2,1)S(1)}, bf16[1024,256]{1,0:T(8,128)(2,1)S(1)}) custom-call(bf16[1024,768]{1,0:T(8,128)(2,1)S(1)} %copy-done.2, bf16[1024,768]{1,0:T(8,128)(2,1)S(1)} %copy-done.2, bf16[1024,768]{1,0:T(8,128)(2,1)S(1)} %copy-done.2, f32[32,1024]{1,0:T(8,128)S(1)} %get-tuple-element.355.logsum, ...), custom_call_target="tpu_custom_call" | custom-call | flops 1000000000 | bytes 1 | tf_op jit(solution)/shard_map/pallas_call | solution.py:706
  377.6 13.6 %collective-permute-done.30 = bf16[4,192,768]{2,1,0:T(8,128)(2,1)} collective-permute-done((bf16[4,192,768]{2,1,0:T(8,128)(2,1)}, bf16[4,192,768]{2,1,0:T(8,128)(2,1)}, u32[]{:S(2)}, u32[]{:S(2)}) %collective-permute-start.30) | collective-permute-done | bytes 1179680 | tf_op jit(solution)/shard_map/ppermute | solution.py:36
  400.4 3.9 fusion.20
  404.3 3.4 collective-permute-start.34
  408.8 24.2 %shard_map.486 = (f32[1024,8,128]{2,1,0:T(8,128)}, f32[8,128]{1,0:T(8,128)}, f32[256,8,128]{2,1,0:T(8,128)}, f32[256,8,128]{2,1,0:T(8,128)}, f32[256,8,128]{2,1,0:T(8,128)}, /*index=5*/f32[256,8,128]{2,1,0:T(8,128)}) custom-call(s32[4096]{0:T(1024)} %bitcast.210, s32[4096]{0:T(1024)} %rev.10.rows_b.refs_1_, s32[4096]{0:T(1024)} %add_bitcast_fusion.3.refs_2_, ...), custom_call_target="tpu_custom_call" | custom-call | flops 24000000000 | bytes 1 | tf_op jit(solution)/shard_map/pallas_call | solution.py:624
  441.1 27.3 %shard_map.488 = (bf16[768,1536]{1,0:T(8,128)(2,1)}, bf16[256,768]{1,0:T(8,128)(2,1)}) custom-call(s32[4096]{0:T(1024)} %bitcast.211, s32[4096]{0:T(1024)} %rev.10.rows_b.refs_1_, s32[4096]{0:T(1024)} %add_bitcast_fusion.3.refs_2_, s32[4096]{0:T(1024)} %rev.11.refs_3_, f32[256,16,128]{2,1,0:T(8,128)} %get-tuple-element.369.refs_4_, ...), custom_call_target="tpu_custom_call" | custom-call | flops 24000000000 | bytes 1 | tf_op jit(solution)/shard_map/pallas_call | solution.py:624
  475.7 3.4 collective-permute-start.42
  486.7 6.7 %collective-permute-done.41 = bf16[104,768]{1,0:T(8,128)(2,1)S(1)} collective-permute-done((bf16[104,768]{1,0:T(8,128)(2,1)S(1)}, bf16[104,768]{1,0:T(8,128)(2,1)S(1)}, u32[]{:S(2)}, u32[]{:S(2)}) %collective-permute-start.41) | collective-permute-done | bytes 159776 | tf_op jit(solution)/shard_map/ppermute | solution.py:36
  493.9 4.0 collective-permute-done.45
  499.7 3.7 collective-permute-start.47
  (470 shorter events, 175.3 us)
Async XLA Ops:
  7.2 126.5 %all-gather.6.cloned.1.call-start = ((), (), s32[]{:S(2)}) async-start(), calls=%async_computation.3 | async-start | bytes 3244032 | tf_op jit(solution)/shard_map/all_gather | solution.py:1025
  18.8 13.5 %collective-permute-start.8 = (bf16[1,1,1,1,96,768]{5,4,3,2,1,0:T(8,128)(2,1)S(1)}, bf16[1,1,1,1,96,768]{5,4,3,2,1,0:T(8,128)(2,1)S(1)}, u32[]{:S(2)}, u32[]{:S(2)}) collective-permute-start(bf16[1,1,1,1,96,768]{5,4,3,2,1,0:T(8,128)(2,1)S(1)} %bitcast.197), channel_id=1, source_target_pairs={{0,4},{1,5},{2,6},{3,7},{4,0},{5,1},{6,2},{7,3},{8,12},{9,13},{10,... | collective-permute-start | bytes 442376 | tf_op jit(solution)/shard_map/ppermute | solution.py:36
  42.9 158.0 %all-gather.4.cloned.1.call-start = ((), (), s32[]{:S(2)}) async-start(), calls=%async_computation.1 | async-start | bytes 7299072 | tf_op jit(solution)/shard_map/all_gather | solution.py:1026
  44.7 15.7 %collective-permute-start = (bf16[512,768]{1,0:T(8,128)(2,1)}, bf16[512,768]{1,0:T(8,128)(2,1)}, u32[]{:S(2)}, u32[]{:S(2)}) collective-permute-start(bf16[512,768]{1,0:T(8,128)(2,1)} %get-tuple-element.477), channel_id=1, source_target_pairs={{0,16},{1,17},{2,18},{3,19},{4,20},{5,21},{6,22},{7,23},{8,24},{9,... | collective-permute-start | bytes 2359304 | tf_op jit(solution)/shard_map/ppermute | solution.py:36
  45.5 13.1 %collective-permute-start.9 = (bf16[1,1,2,1,96,768]{5,4,3,2,1,0:T(8,128)(2,1)S(1)}, bf16[1,1,2,1,96,768]{5,4,3,2,1,0:T(8,128)(2,1)}, u32[]{:S(2)}, u32[]{:S(2)}) collective-permute-start(bf16[1,1,2,1,96,768]{5,4,3,2,1,0:T(8,128)(2,1)S(1)} %constant_dynamic-update-slice_fusion.8), channel_id=1, source_target_pairs={{0,8},{1,9},{2,10},{3,11},{4,12},{5,13},{6,14},{7,15},{8,0},{9,1},... | collective-permute-start | bytes 884744 | tf_op jit(solution)/shard_map/ppermute | solution.py:36
  49.6 10.9 %collective-permute-start.15 = (bf16[1,2,2,1,48,768]{5,4,3,2,1,0:T(8,128)(2,1)}, bf16[1,2,2,1,48,768]{5,4,3,2,1,0:T(8,128)(2,1)}, u32[]{:S(2)}, u32[]{:S(2)}) collective-permute-start(bf16[1,2,2,1,48,768]{5,4,3,2,1,0:T(8,128)(2,1)} %constant_dynamic-update-slice_fusion.16), channel_id=1, source_target_pairs={{0,2},{1,3},{2,0},{3,1},{4,6},{5,7},{6,4},{7,5},{8,10},{9,11},{10,... | collective-permute-start | bytes 884744 | tf_op jit(solution)/shard_map/ppermute | solution.py:36
  56.3 320.2 %reduce-scatter.2.cloned.1.call-start = ((), (), s32[]{:S(2)}) async-start(), calls=%async_computation.2 | async-start | bytes 7299072 | tf_op jit(solution)/shard_map/reduce_scatter | solution.py:236
  62.3 20.1 %collective-permute-start.19 = (bf16[1,1,2,1,96,768]{5,4,3,2,1,0:T(8,128)(2,1)S(1)}, bf16[1,1,2,1,96,768]{5,4,3,2,1,0:T(8,128)(2,1)S(1)}, u32[]{:S(2)}, u32[]{:S(2)}) collective-permute-start(bf16[1,1,2,1,96,768]{5,4,3,2,1,0:T(8,128)(2,1)S(1)} %constant_dynamic-update-slice_fusion.22), channel_id=1, source_target_pairs={{0,8},{1,9},{2,10},{3,11},{4,12},{5,13},{6,14},{7,15},{8,0},{9,1},... | collective-permute-start | bytes 884744 | tf_op jit(solution)/shard_map/ppermute | solution.py:36
  65.2 17.2 %collective-permute-start.18 = (bf16[1,2,2,2,48,768]{5,4,3,2,1,0:T(8,128)(2,1)S(1)}, bf16[1,2,2,2,48,768]{5,4,3,2,1,0:T(8,128)(2,1)S(1)}, u32[]{:S(2)}, u32[]{:S(2)}) collective-permute-start(bf16[1,2,2,2,48,768]{5,4,3,2,1,0:T(8,128)(2,1)S(1)} %constant_dynamic-update-slice_fusion.20), channel_id=1, source_target_pairs={{0,16},{1,17},{2,18},{3,19},{4,20},{5,21},{6,22},{7,23},{8,24},{9,... | collective-permute-start | bytes 1769480 | tf_op jit(solution)/shard_map/ppermute | solution.py:36
  67.6 14.8 %collective-permute-start.17 = (bf16[1,2,2,1,96,768]{5,4,3,2,1,0:T(8,128)(2,1)S(1)}, bf16[1,2,2,1,96,768]{5,4,3,2,1,0:T(8,128)(2,1)S(1)}, u32[]{:S(2)}, u32[]{:S(2)}) collective-permute-start(bf16[1,2,2,1,96,768]{5,4,3,2,1,0:T(8,128)(2,1)S(1)} %constant_dynamic-update-slice_fusion.18), channel_id=1, source_target_pairs={{0,2},{1,3},{2,0},{3,1},{4,6},{5,7},{6,4},{7,5},{8,10},{9,11},{10,... | collective-permute-start | bytes 1769480 | tf_op jit(solution)/shard_map/ppermute | solution.py:36
  84.0 40.2 %collective-permute-start.22 = (bf16[1,2,2,1,96,768]{5,4,3,2,1,0:T(8,128)(2,1)}, bf16[1,2,2,1,96,768]{5,4,3,2,1,0:T(8,128)(2,1)}, u32[]{:S(2)}, u32[]{:S(2)}) collective-permute-start(bf16[1,2,2,1,96,768]{5,4,3,2,1,0:T(8,128)(2,1)} %constant_dynamic-update-slice_fusion.26), channel_id=1, source_target_pairs={{0,2},{1,3},{2,0},{3,1},{4,6},{5,7},{6,4},{7,5},{8,10},{9,11},{10,... | collective-permute-start | bytes 1769480 | tf_op jit(solution)/shard_map/ppermute | solution.py:36
  86.1 38.1 %collective-permute-start.21 = (bf16[1,2,2,2,96,768]{5,4,3,2,1,0:T(8,128)(2,1)}, bf16[1,2,2,2,96,768]{5,4,3,2,1,0:T(8,128)(2,1)}, u32[]{:S(2)}, u32[]{:S(2)}) collective-permute-start(bf16[1,2,2,2,96,768]{5,4,3,2,1,0:T(8,128)(2,1)} %constant_dynamic-update-slice_fusion.24), channel_id=1, source_target_pairs={{0,16},{1,17},{2,18},{3,19},{4,20},{5,21},{6,22},{7,23},{8,24},{9,... | collective-permute-start | bytes 3538952 | tf_op jit(solution)/shard_map/ppermute | solution.py:36
  129.1 35.0 %collective-permute-start.24 = (bf16[1,2,2,2,96,768]{5,4,3,2,1,0:T(8,128)(2,1)}, bf16[1,2,2,2,96,768]{5,4,3,2,1,0:T(8,128)(2,1)}, u32[]{:S(2)}, u32[]{:S(2)}) collective-permute-start(bf16[1,2,2,2,96,768]{5,4,3,2,1,0:T(8,128)(2,1)} %constant_dynamic-update-slice_fusion.28), channel_id=1, source_target_pairs={{0,16},{1,17},{2,18},{3,19},{4,20},{5,21},{6,22},{7,23},{8,24},{9,... | collective-permute-start | bytes 3538952 | tf_op jit(solution)/shard_map/ppermute | solution.py:36
  132.2 31.8 %collective-permute-start.23 = (bf16[16,96,768]{2,1,0:T(8,128)(2,1)S(1)}, bf16[16,96,768]{2,1,0:T(8,128)(2,1)}, u32[]{:S(2)}, u32[]{:S(2)}) collective-permute-start(bf16[16,96,768]{2,1,0:T(8,128)(2,1)S(1)} %bitcast.176), channel_id=1, source_target_pairs={{0,1},{1,0},{2,3},{3,2},{4,5},{5,4},{6,7},{7,6},{8,9},{9,8},{10,11... | collective-permute-start | bytes 7077896 | tf_op jit(solution)/shard_map/ppermute | solution.py:36
  167.4 10.2 %collective-permute-start.25 = (bf16[16,96,768]{2,1,0:T(8,128)(2,1)}, bf16[16,96,768]{2,1,0:T(8,128)(2,1)}, u32[]{:S(2)}, u32[]{:S(2)}) collective-permute-start(bf16[16,96,768]{2,1,0:T(8,128)(2,1)} %bitcast.28.mine), channel_id=1, source_target_pairs={{0,1},{1,0},{2,3},{3,2},{4,5},{5,4},{6,7},{7,6},{8,9},{9,8},{10,11... | collective-permute-start | bytes 7077896 | tf_op jit(solution)/shard_map/ppermute | solution.py:36
  168.7 32.2 %collective-permute-start.26 = (bf16[512,768]{1,0:T(8,128)(2,1)}, bf16[512,768]{1,0:T(8,128)(2,1)}, u32[]{:S(2)}, u32[]{:S(2)}) collective-permute-start(bf16[512,768]{1,0:T(8,128)(2,1)} %get-tuple-element.475), channel_id=1, source_target_pairs={{0,16},{1,17},{2,18},{3,19},{4,20},{5,21},{6,22},{7,23},{8,24},{9,... | collective-permute-start | bytes 2359304 | tf_op jit(solution)/shard_map/ppermute | solution.py:36
  242.1 54.1 %collective-permute-start.27 = (bf16[512,768]{1,0:T(8,128)(2,1)S(1)}, bf16[512,768]{1,0:T(8,128)(2,1)}, u32[]{:S(2)}, u32[]{:S(2)}) collective-permute-start(bf16[512,768]{1,0:T(8,128)(2,1)S(1)} %broadcast_select_fusion.2), channel_id=1, source_target_pairs={{0,16},{1,17},{2,18},{3,19},{4,20},{5,21},{6,22},{7,23},{8,24},{9,... | collective-permute-start | bytes 2359304 | tf_op jit(solution)/shard_map/ppermute | solution.py:36
  304.5 24.9 %collective-permute-start.28 = (bf16[16,192,768]{2,1,0:T(8,128)(2,1)}, bf16[16,192,768]{2,1,0:T(8,128)(2,1)}, u32[]{:S(2)}, u32[]{:S(2)}) collective-permute-start(bf16[16,192,768]{2,1,0:T(8,128)(2,1)} %get-tuple-element.346), channel_id=1, source_target_pairs={{0,1},{1,0},{2,3},{3,2},{4,5},{5,4},{6,7},{7,6},{8,9},{9,8},{10,11... | collective-permute-start | bytes 14155784 | tf_op jit(solution)/shard_map/ppermute | solution.py:36
  334.3 43.4 %collective-permute-start.29 = (bf16[4,192,768]{2,1,0:T(8,128)(2,1)}, bf16[4,192,768]{2,1,0:T(8,128)(2,1)}, u32[]{:S(2)}, u32[]{:S(2)}) collective-permute-start(bf16[4,192,768]{2,1,0:T(8,128)(2,1)} %get-tuple-element.364), channel_id=1, source_target_pairs={{0,18},{1,19},{2,16},{3,17},{4,22},{5,23},{6,20},{7,21},{8,26},{9,... | collective-permute-start | bytes 3538952 | tf_op jit(solution)/shard_map/ppermute | solution.py:36
  336.8 54.5 %collective-permute-start.30 = (bf16[4,192,768]{2,1,0:T(8,128)(2,1)}, bf16[4,192,768]{2,1,0:T(8,128)(2,1)}, u32[]{:S(2)}, u32[]{:S(2)}) collective-permute-start(bf16[4,192,768]{2,1,0:T(8,128)(2,1)} %get-tuple-element.365), channel_id=1, source_target_pairs={{0,16},{1,17},{2,18},{3,19},{4,20},{5,21},{6,22},{7,23},{8,24},{9,... | collective-permute-start | bytes 3538952 | tf_op jit(solution)/shard_map/ppermute | solution.py:36
  337.4 53.9 %collective-permute-start.31 = (bf16[4,192,768]{2,1,0:T(8,128)(2,1)}, bf16[4,192,768]{2,1,0:T(8,128)(2,1)}, u32[]{:S(2)}, u32[]{:S(2)}) collective-permute-start(bf16[4,192,768]{2,1,0:T(8,128)(2,1)} %get-tuple-element.366), channel_id=1, source_target_pairs={{0,2},{1,3},{2,0},{3,1},{4,6},{5,7},{6,4},{7,5},{8,10},{9,11},{10,... | collective-permute-start | bytes 3538952 | tf_op jit(solution)/shard_map/ppermute | solution.py:36
  393.6 42.6 %collective-permute-start.35 = (bf16[512,768]{1,0:T(8,128)(2,1)}, bf16[512,768]{1,0:T(8,128)(2,1)}, u32[]{:S(2)}, u32[]{:S(2)}) collective-permute-start(bf16[512,768]{1,0:T(8,128)(2,1)} %broadcast_select_fusion), channel_id=1, source_target_pairs={{0,16},{1,17},{2,18},{3,19},{4,20},{5,21},{6,22},{7,23},{8,24},{9,... | collective-permute-start | bytes 2359304 | tf_op jit(solution)/shard_map/ppermute | solution.py:36
  400.4 35.8 %collective-permute-start.36 = (bf16[16,104,768]{2,1,0:T(8,128)(2,1)}, bf16[16,104,768]{2,1,0:T(8,128)(2,1)S(1)}, u32[]{:S(2)}, u32[]{:S(2)}) collective-permute-start(bf16[16,104,768]{2,1,0:T(8,128)(2,1)} %get-tuple-element.387), channel_id=1, source_target_pairs={{0,1},{1,0},{2,3},{3,2},{4,5},{5,4},{6,7},{7,6},{8,9},{9,8},{10,11... | collective-permute-start | bytes 7667720 | tf_op jit(solution)/shard_map/ppermute | solution.py:36
  404.3 31.8 %collective-permute-start.34 = (bf16[192,768]{1,0:T(8,128)(2,1)S(1)}, bf16[192,768]{1,0:T(8,128)(2,1)S(1)}, u32[]{:S(2)}, u32[]{:S(2)}) collective-permute-start(bf16[192,768]{1,0:T(8,128)(2,1)S(1)} %get-tuple-element.478), channel_id=1, source_target_pairs={{0,12},{1,13},{2,14},{3,15},{4,8},{5,9},{6,10},{7,11},{8,4},{9,5},... | collective-permute-start | bytes 884744 | tf_op jit(solution)/shard_map/ppermute | solution.py:36
  407.8 28.4 %collective-permute-start.33 = (bf16[192,768]{1,0:T(8,128)(2,1)S(1)}, bf16[192,768]{1,0:T(8,128)(2,1)}, u32[]{:S(2)}, u32[]{:S(2)}) collective-permute-start(bf16[192,768]{1,0:T(8,128)(2,1)S(1)} %get-tuple-element.479), channel_id=1, source_target_pairs={{0,8},{1,9},{2,10},{3,11},{4,12},{5,13},{6,14},{7,15},{8,0},{9,1},... | collective-permute-start | bytes 884744 | tf_op jit(solution)/shard_map/ppermute | solution.py:36
  407.8 28.4 %collective-permute-start.32 = (bf16[192,768]{1,0:T(8,128)(2,1)S(1)}, bf16[192,768]{1,0:T(8,128)(2,1)}, u32[]{:S(2)}, u32[]{:S(2)}) collective-permute-start(bf16[192,768]{1,0:T(8,128)(2,1)S(1)} %get-tuple-element.480), channel_id=1, source_target_pairs={{0,4},{1,5},{2,6},{3,7},{4,0},{5,1},{6,2},{7,3},{8,12},{9,13},{10,... | collective-permute-start | bytes 884744 | tf_op jit(solution)/shard_map/ppermute | solution.py:36
  437.5 33.9 %collective-permute-start.37 = (bf16[4,104,768]{2,1,0:T(8,128)(2,1)S(1)}, bf16[4,104,768]{2,1,0:T(8,128)(2,1)S(1)}, u32[]{:S(2)}, u32[]{:S(2)}) collective-permute-start(bf16[4,104,768]{2,1,0:T(8,128)(2,1)S(1)} %get-tuple-element.400), channel_id=1, source_target_pairs={{0,18},{1,19},{2,16},{3,17},{4,22},{5,23},{6,20},{7,21},{8,26},{9,... | collective-permute-start | bytes 1916936 | tf_op jit(solution)/shard_map/ppermute | solution.py:36
  439.0 32.5 %collective-permute-start.38 = (bf16[4,104,768]{2,1,0:T(8,128)(2,1)S(1)}, bf16[4,104,768]{2,1,0:T(8,128)(2,1)S(1)}, u32[]{:S(2)}, u32[]{:S(2)}) collective-permute-start(bf16[4,104,768]{2,1,0:T(8,128)(2,1)S(1)} %get-tuple-element.401), channel_id=1, source_target_pairs={{0,16},{1,17},{2,18},{3,19},{4,20},{5,21},{6,22},{7,23},{8,24},{9,... | collective-permute-start | bytes 1916936 | tf_op jit(solution)/shard_map/ppermute | solution.py:36
  440.5 31.0 %collective-permute-start.39 = (bf16[4,104,768]{2,1,0:T(8,128)(2,1)S(1)}, bf16[4,104,768]{2,1,0:T(8,128)(2,1)S(1)}, u32[]{:S(2)}, u32[]{:S(2)}) collective-permute-start(bf16[4,104,768]{2,1,0:T(8,128)(2,1)S(1)} %get-tuple-element.402), channel_id=1, source_target_pairs={{0,2},{1,3},{2,0},{3,1},{4,6},{5,7},{6,4},{7,5},{8,10},{9,11},{10,... | collective-permute-start | bytes 1916936 | tf_op jit(solution)/shard_map/ppermute | solution.py:36
  479.5 14.4 %collective-permute-start.44 = (bf16[4,56,768]{2,1,0:T(8,128)(2,1)S(1)}, bf16[4,56,768]{2,1,0:T(8,128)(2,1)S(1)}, u32[]{:S(2)}, u32[]{:S(2)}) collective-permute-start(bf16[4,56,768]{2,1,0:T(8,128)(2,1)S(1)} %get-tuple-element.414), channel_id=1, source_target_pairs={{0,18},{1,19},{2,16},{3,17},{4,22},{5,23},{6,20},{7,21},{8,26},{9,... | collective-permute-start | bytes 1032200 | tf_op jit(solution)/shard_map/ppermute | solution.py:36
  481.0 16.9 %collective-permute-start.45 = (bf16[4,56,768]{2,1,0:T(8,128)(2,1)S(1)}, bf16[4,56,768]{2,1,0:T(8,128)(2,1)S(1)}, u32[]{:S(2)}, u32[]{:S(2)}) collective-permute-start(bf16[4,56,768]{2,1,0:T(8,128)(2,1)S(1)} %get-tuple-element.415), channel_id=1, source_target_pairs={{0,16},{1,17},{2,18},{3,19},{4,20},{5,21},{6,22},{7,23},{8,24},{9,... | collective-permute-start | bytes 1032200 | tf_op jit(solution)/shard_map/ppermute | solution.py:36
  482.5 15.4 %collective-permute-start.46 = (bf16[4,56,768]{2,1,0:T(8,128)(2,1)S(1)}, bf16[4,56,768]{2,1,0:T(8,128)(2,1)S(1)}, u32[]{:S(2)}, u32[]{:S(2)}) collective-permute-start(bf16[4,56,768]{2,1,0:T(8,128)(2,1)S(1)} %get-tuple-element.416), channel_id=1, source_target_pairs={{0,2},{1,3},{2,0},{3,1},{4,6},{5,7},{6,4},{7,5},{8,10},{9,11},{10,... | collective-permute-start | bytes 1032200 | tf_op jit(solution)/shard_map/ppermute | solution.py:36
  (125 other events, 940.7 us)
Sparse Core Ops, SparseCore 0:
  43.0 66.3 all-gather.5
  113.0 82.8 all-gather.3
  240.7 135.7 reduce-scatter.1

commit v4 on v3

--- a/solution.py
+++ b/solution.py
@@ -27,8 +27,9 @@
     return blocks.transpose(0, 2, 1, 3).reshape(parts * own, side * D)
 
 
-def gains_row(gains):
-    return jnp.pad(gains.reshape(1, -1), ((0, 7), (0, D - gains.size)))
+def gains_rows(gains):
+    blank = jnp.zeros((8, D), jnp.float32)
+    return lax.dynamic_update_slice(blank, gains, (0, my_place()[0] * gains.shape[1]))
 
 
 def swap(block, mask):
@@ -42,7 +43,7 @@
 
 def in_pairs(shapes):
     parts = lax.axis_size("dp") * lax.axis_size("stream")
-    return parts >= 8 and parts & (parts - 1) == 0 and all(rows % 8 == 0 for rows, _ in shapes)
+    return parts == 32 and all(rows % 8 == 0 for rows, _ in shapes)
 
 
 def my_place():
@@ -192,7 +193,7 @@
         out_shape=[
             jax.ShapeDtypeStruct((parts * own, side * D), jnp.bfloat16) for own, side in shapes
         ],
-        compiler_params=pltpu.CompilerParams(vmem_limit_bytes=40 << 20),
+        compiler_params=pltpu.CompilerParams(vmem_limit_bytes=16 << 20),
         cost_estimate=spent(3),
     )(rows)
 
@@ -225,7 +226,7 @@
         out_shape=[
             jax.ShapeDtypeStruct((parts * rows, side * D), jnp.bfloat16) for rows, side in shapes
         ],
-        compiler_params=pltpu.CompilerParams(vmem_limit_bytes=40 << 20),
+        compiler_params=pltpu.CompilerParams(vmem_limit_bytes=16 << 20),
         cost_estimate=spent(4),
     )(my_place(), mine.reshape(pairs, high, D), theirs.reshape(pairs, high, D))
 
@@ -248,15 +249,82 @@
     return pieces
 
 
-def scatter_chain(grads, split=False):
+def feed_grads(place, former, latter, given, source, keep, send, held):
+    step = pl.program_id(0)
+    core = place[0] & 1
+    low = place[0] >> 1
+
+    @pl.when(step < 4)
+    def down():
+        whole_grad = contract(former[...], given[...], 0, 0)
+        rows = whole_grad.shape[0] // 8
+        for pair in range(4):
+            there = (4 * step + pair) ^ low
+            first = whole_grad[2 * pair * rows : (2 * pair + 1) * rows]
+            second = whole_grad[(2 * pair + 1) * rows : (2 * pair + 2) * rows]
+            keep[there, 0:rows] = jnp.where(core == 0, first, second).astype(keep.dtype)
+            send[there, 0:rows] = jnp.where(core == 0, second, first).astype(send.dtype)
+
+    rows = D // held.shape[0]
+    for number in range(4):
+
+        @pl.when(step == 4 + number)
+        def up():
+            whole_grad = contract(source[...], latter[...], 0, 0)
+            held[:, number * rows : number * rows + rows] = whole_grad.reshape(-1, rows, D)
+
+    @pl.when(step == 7)
+    def finish():
+        start = 4 * rows
+        for pair in range(held.shape[0] // 2):
+            first, second = held[2 * pair], held[2 * pair + 1]
+            there = pair ^ low
+            keep[there, start:] = jnp.where(core == 0, first, second).astype(keep.dtype)
+            send[there, start:] = jnp.where(core == 0, second, first).astype(send.dtype)
+
+
+def run_feed_grads(active, ffn_grad, normed, hidden_grad):
+    length, wide = active.shape
+    parts = lax.axis_size("dp") * lax.axis_size("stream")
+    pairs = parts // 2
+    high = 2 * wide // parts
+    half = jax.ShapeDtypeStruct((pairs, high, D), jnp.bfloat16)
+    whole_half = pl.BlockSpec(half.shape, lambda step, place: (0, 0, 0))
+    kept_rows = pl.BlockSpec((length, D), lambda step, place: (0, 0))
+    return pl.pallas_call(
+        feed_grads,
+        grid_spec=pltpu.PrefetchScalarGridSpec(
+            num_scalar_prefetch=1,
+            grid=(8,),
+            in_specs=[
+                pl.BlockSpec((length, D), lambda step, place: (0, jnp.minimum(step, 3))),
+                pl.BlockSpec((length, D), lambda step, place: (0, jnp.maximum(step - 4, 0))),
+                kept_rows,
+                kept_rows,
+            ],
+            out_specs=[whole_half, whole_half],
+            scratch_shapes=[pltpu.VMEM((parts, high // 2, D), jnp.float32)],
+        ),
+        out_shape=[half, half],
+        compiler_params=params(56),
+        cost_estimate=spent(16),
+    )(my_place(), active, hidden_grad, ffn_grad, normed)
+
+
+def scatter_chain(grads):
     parts = lax.axis_size("dp") * lax.axis_size("stream")
     shapes = shapes_of(grads, parts)
     if not in_pairs(shapes):
         return scatter_whole(grads)
+    total = yield from halves_chain(*core_halves(grads, shapes, parts))
+    return own_pieces(total, shapes)
+
+
+def core_halves(grads, shapes, parts):
     pairs = parts // 2
     high = sum(rows * side for rows, side in shapes)
     half = jax.ShapeDtypeStruct((pairs, high, D), jnp.bfloat16)
-    kept, sent = pl.pallas_call(
+    return pl.pallas_call(
         functools.partial(apart, shapes),
         grid_spec=pltpu.PrefetchScalarGridSpec(
             num_scalar_prefetch=1,
@@ -265,9 +333,13 @@
             out_specs=[turned_block(high)] * 2,
         ),
         out_shape=[half, half],
-        compiler_params=pltpu.CompilerParams(vmem_limit_bytes=40 << 20),
+        compiler_params=pltpu.CompilerParams(vmem_limit_bytes=16 << 20),
         cost_estimate=spent(4),
     )(my_place(), *[grad.astype(jnp.bfloat16) for grad in grads])
+
+
+def halves_chain(kept, sent, split=False):
+    high = kept.shape[1]
     kept, other = yield (kept, swap(sent, 1))
     top = pair_bits()
     far = 1 << (top - 2)
@@ -284,7 +356,7 @@
         in_specs=views + views,
         out_specs=[pl.BlockSpec((1, high, D), lambda row: (row, 0, 0))] * 4,
         out_shape=[jax.ShapeDtypeStruct(quarter.shape, jnp.float32)] + [quarter] * 3,
-        compiler_params=pltpu.CompilerParams(vmem_limit_bytes=40 << 20),
+        compiler_params=pltpu.CompilerParams(vmem_limit_bytes=16 << 20),
         cost_estimate=spent(3),
     )(*[kept.reshape(2, far, 2, high, D)] * 4, *[other.reshape(2, far, 2, high, D)] * 4)
     got = [swap(sent[0], corner), swap(sent[1], 2)]
@@ -294,18 +366,30 @@
     else:
         total, last, *got = yield (total, swap(sent[2], corner | 2), *got)
     total = total + sum(block.astype(jnp.float32) for block in [last, *got])
+    while split and far > 1:
+        far //= 2
+        kept, other = yield (total[:far], swap(total[far:].astype(jnp.bfloat16), far << 2))
+        total = kept + other.astype(jnp.float32)
+    if split:
+        return total[0]
     others = [
         swap(total[number].astype(jnp.bfloat16), number << 2) for number in range(1, far)
     ]
     kept, *others = yield (total[0], *others)
-    total = kept + sum(other.astype(jnp.float32) for other in others)
-    return own_pieces(total, shapes)
+    return kept + sum(other.astype(jnp.float32) for other in others)
 
 
 def sum_quarters(*refs):
     for former, latter, out in zip(refs[:4], refs[4:8], refs[8:]):
         total = former[0, 0, 0].astype(jnp.float32) + latter[0, 0, 0].astype(jnp.float32)
         out[0] = total.astype(out.dtype)
+
+
+def feed_chain(halves, shapes):
+    if not in_pairs(shapes):
+        return scatter_whole(halves)
+    total = yield from halves_chain(*halves, True)
+    return own_pieces(total, shapes)
 
 
 def swap_chain(block):
@@ -344,10 +428,9 @@
     return jnp.concatenate([matrix[1:], jnp.zeros_like(matrix[:1])], 0)
 
 
-def char_segments(lengths, char_count):
-    starts = jnp.cumsum(lengths) - lengths
-    markers = jnp.zeros((char_count,), jnp.int32).at[starts].add(1)
-    return jnp.cumsum(markers) - 1
+def char_segments(ends, char_count):
+    places = lax.broadcasted_iota(jnp.int32, (ends.shape[0], char_count), 1)
+    return jnp.sum((ends[:, None] <= places).astype(jnp.int32), axis=0)
 
 
 def step_rates():
@@ -550,14 +633,9 @@
                 letters[:, 8 + place, :] * total - update * found[:, 4 + lane, :]
             )
             full[:, left + width : left + width + 128] = update * total
-        upper = full[...].astype(jnp.bfloat16)
-        lower = (full[...] - upper.astype(jnp.float32)).astype(jnp.bfloat16)
-        grad_gru[...] = (
-            contract(table[...], upper, 0, 0) + contract(table[...], lower, 0, 0)
-        ).astype(grad_gru.dtype)
-        grad_table[...] = (
-            contract(upper, w_gru[...], 1, 1) + contract(lower, w_gru[...], 1, 1)
-        ).astype(grad_table.dtype)
+        found = full[...].astype(jnp.bfloat16)
+        grad_gru[...] = contract(table[...], found, 0, 0).astype(grad_gru.dtype)
+        grad_table[...] = contract(found, w_gru[...], 1, 1).astype(grad_table.dtype)
 
 
 def whole(array):
@@ -591,7 +669,7 @@
             pltpu.VMEM((count, 8, 128), f32),
             pltpu.VMEM((2, 8, 128), f32),
         ],
-        compiler_params=pltpu.CompilerParams(vmem_limit_bytes=56 << 20),
+        compiler_params=pltpu.CompilerParams(vmem_limit_bytes=44 << 20),
         cost_estimate=spent(24),
     )(ids, jnp.flip(ids), ends, table, w_gru, shares)
 
@@ -628,7 +706,7 @@
         out_specs=[whole(out) for out in outs],
         out_shape=outs,
         scratch_shapes=scratch,
-        compiler_params=pltpu.CompilerParams(vmem_limit_bytes=56 << 20),
+        compiler_params=pltpu.CompilerParams(vmem_limit_bytes=40 << 20),
         cost_estimate=spent(6 * count),
     )(*inputs)
 
@@ -655,7 +733,7 @@
     logsum[8:16, :] = turned[size : size + 8]
 
 
-def attend_back(queries, key_rows, value_rows, logsum, grads, query_grad, key_grad, value_grad):
+def attend_back(queries, key_rows, value_rows, logsum, grads, qkv_grad):
     size = key_rows.shape[1] // 2
     lanes = lax.broadcasted_iota(jnp.int32, (1, 2 * size), 1)
     scale = size ** (-0.5)
@@ -673,9 +751,10 @@
         score_grad = (probs * (prob_grad - center)).astype(jnp.bfloat16)
         key_sum = key_sum + contract(score_grad, own_rows, 1, 0)
         parts.append(contract(score_grad, key_rows[...], 0, 0))
-    query_grad[...] = (jnp.where(lanes < size, parts[0], parts[1]) * scale).astype(query_grad.dtype)
-    key_grad[...] = key_sum.astype(key_grad.dtype)
-    value_grad[...] = value_sum.astype(value_grad.dtype)
+    query_sum = jnp.where(lanes < size, parts[0], parts[1]) * scale
+    for number, total in enumerate((query_sum, key_sum, value_sum)):
+        at = number * (qkv_grad.shape[1] // 3) + pl.program_id(0) * 2 * size
+        qkv_grad[:, pl.ds(pl.multiple_of(at, 2 * size), 2 * size)] = total.astype(qkv_grad.dtype)
 
 
 def column(rows, width, offset):
@@ -694,25 +773,21 @@
             jax.ShapeDtypeStruct((length, 128 * pairs), jnp.bfloat16),
             jax.ShapeDtypeStruct((16 * pairs, length), jnp.float32),
         ),
-        compiler_params=pltpu.CompilerParams(vmem_limit_bytes=40 << 20),
+        compiler_params=pltpu.CompilerParams(vmem_limit_bytes=28 << 20),
         cost_estimate=spent(5 * pairs),
     )(qkv, qkv, qkv)
 
 
-def run_attend_back(qkv, logsum, grads, first, pairs):
+def run_attend_back(qkv, logsum, grads, first):
     length, across = qkv.shape
-    every = across // 384
-    part = jax.ShapeDtypeStruct((length, 128 * pairs), jnp.bfloat16)
+    pairs = across // 384
     return pl.pallas_call(
         attend_back,
         grid=(pairs,),
-        in_specs=[column(length, 128, every * part + first) for part in range(3)]
-        + [
-            pl.BlockSpec((16, length), lambda pair: (first + pair, 0)),
-            column(length, 128, first),
-        ],
-        out_specs=[column(length, 128, 0)] * 3,
-        out_shape=(part, part, part),
+        in_specs=[column(length, 128, pairs * part) for part in range(3)]
+        + [pl.BlockSpec((16, length), lambda pair: (pair, 0)), column(length, 128, first)],
+        out_specs=pl.BlockSpec((length, across), lambda pair: (0, 0)),
+        out_shape=jax.ShapeDtypeStruct((length, across), jnp.bfloat16),
         compiler_params=pltpu.CompilerParams(vmem_limit_bytes=40 << 20),
         cost_estimate=spent(1),
     )(qkv, qkv, qkv, logsum, grads)
@@ -791,7 +866,7 @@
 
 
 def blend_both(
-    feature, pooled, out_grad, gains, blend,
+    order, feature, pooled, mine, theirs, gains, blend,
     result, feature_grad, state_grad, grads, gain_sum, early, middle, late, spread, total
 ):
     length = feature.shape[0]
@@ -819,7 +894,13 @@
         blended, slope = gelu_pair(middle[chunk] + early[before] + late[after])
         normal, root = unit(feature[chunk].astype(jnp.float32) + blended)
         result[chunk] = (normal * gains[2:3]).astype(result.dtype)
-        given = out_grad[chunk].astype(jnp.float32)
+        half = length // 2
+        within = slice(chunk.start % half, chunk.start % half + rows)
+        given = jnp.where(
+            order[0] == chunk.start // half,
+            mine[within].astype(jnp.float32),
+            theirs[within].astype(jnp.float32),
+        )
         gain_sum[...] += column_sum(given * normal)
         whole_grad = unit_back(normal, root, given * gains[2:3])
         total[chunk] = whole_grad
@@ -892,12 +973,13 @@
     )(mixed, summed, feature_grad, gains, up, down, out)
 
 
-def run_blend(feature, pooled, out_grad, gains, blend):
+def run_blend(order, feature, pooled, mine, theirs, gains, blend):
     length = feature.shape[0]
     bf = jnp.bfloat16
     f32 = jnp.float32
     return pl.pallas_call(
         blend_both,
+        in_specs=[scalars()] + [pl.BlockSpec(memory_space=pltpu.VMEM)] * 6,
         out_shape=[
             jax.ShapeDtypeStruct((length, D), bf),
             jax.ShapeDtypeStruct((length, D), bf),
@@ -914,7 +996,7 @@
         ],
         compiler_params=params(60),
         cost_estimate=spent(26),
-    )(feature, pooled, out_grad, gains, blend)
+    )(order, feature, pooled, mine, theirs, gains, blend)
 
 
 def blend_weight_grad(feature, pooled, grads, out):
@@ -1019,7 +1101,7 @@
     flow.begin("group2", gather_steps([by_group[:, 2], w_out], True))
     flow.begin("up", gather_steps([w_up], True), [0, 1, 0, 1, 0])
     flow.slot(())
-    shards = flow.slot((char_table, w_gru, gains_row(gains), w_blend))
+    shards = flow.slot((char_table, w_gru, gains_rows(gains), w_blend))
     shapes = shapes_of(shards[:3], 1)
     packed = jnp.concatenate([to_rows(shard, 1)[0] for shard in shards[:3]], 0)
     rest = lax.all_gather(packed, everyone, axis=0, tiled=False)
@@ -1033,9 +1115,9 @@
     for number in range(groups):
         w_group, *w_more = flow.end("group%d" % number)
         if number == 2:
-            segment = char_segments(lengths_row, ids_row.shape[0])
             shares = 1.0 / lengths_row.astype(jnp.float32)[:, None]
             ends = jnp.cumsum(lengths_row)
+            segment = char_segments(ends, ids_row.shape[0])
             lengths_row = (segment, shares, ends)
         qkv = product(tokens, w_group).astype(jnp.bfloat16)
         context, logsum = run_attend(qkv, 0, pairs)
@@ -1050,8 +1132,7 @@
     segment, shares, ends = lengths_row
     context = jnp.concatenate(contexts, 1)
     table_all, gru_all, gain_all = unpack_rows(rest, shapes)
-    gain_all = gain_all.reshape(parts, -1, D)[:, 0, : gains.size]
-    gain_all = gain_all.reshape(parts, 3, -1).transpose(1, 0, 2).reshape(3, -1).astype(jnp.float32)
+    gain_all = jnp.sum(gain_all.reshape(parts, 8, D)[:, :3].astype(jnp.float32), 0)
     letters, before, pooled = run_chars(ids_row, ends, table_all, gru_all, shares)
     letters, before, pooled, context, tokens = flow.slot((letters, before, pooled, context, tokens))
     mixed_sum = tokens.astype(jnp.float32) + product(context, out_all)
@@ -1061,9 +1142,14 @@
     (down_all,) = flow.end("down")
     summed, feature = run_feed(mixed_sum, gain_all, up_all, down_all)
     summed, feature, blend_all = flow.slot((summed, feature, blend_all))
-    whole_grad = both_halves(out_grad, flow.end("out_grad"))
     result, feature_grad, state_grad, blend_grads, gain_blend = run_blend(
-        feature, pooled, whole_grad, gain_all, blend_all
+        lax.axis_index("stream").reshape(1),
+        feature,
+        pooled,
+        jnp.where(on_first, out_grad[0], out_grad[1]),
+        flow.end("out_grad"),
+        gain_all,
+        blend_all,
     )
     grad_blend = run_blend_grad(feature, pooled, blend_grads)
     result, grad_blend, feature_grad = flow.slot((result, grad_blend, feature_grad))
@@ -1072,28 +1158,32 @@
     active, hidden_grad, ffn_grad, normed, mixed_grad, attended_grad, context_grad, gain_sums = (
         run_feed_back(mixed_sum, summed, feature_grad, gain_all, up_all, down_all, out_all)
     )
-    gain_grads = jnp.stack(
-        [jnp.sum(gain_sums[:8], 0), jnp.sum(gain_sums[8:], 0), jnp.sum(gain_blend, 0)]
-    )
-    gain_rows = gain_grads.reshape(3, parts, -1).transpose(1, 0, 2).reshape(parts, -1)
-    gain_rows = jnp.pad(gain_rows[:, None], ((0, 0), (0, 7), (0, D - gain_rows.shape[1])))
-    gain_rows = gain_rows.reshape(8 * parts, D)
-    grad_down = inner_rows(active, ffn_grad).astype(jnp.bfloat16)
-    grad_up = inner_rows(normed, hidden_grad).astype(jnp.bfloat16)
+    gain_grads = jnp.concatenate(
+        [jnp.sum(sums, 0, keepdims=True) for sums in (gain_sums[:8], gain_sums[8:], gain_blend)], 0
+    )
+    gain_grads = jnp.pad(gain_grads, ((0, 5), (0, 0))).astype(jnp.bfloat16)
+    gain_rows = jnp.broadcast_to(gain_grads[None], (parts, 8, D)).reshape(8 * parts, D)
+    if in_pairs([(w_down.shape[0], 1), (w_up.shape[0], 4)]):
+        feed_grad = run_feed_grads(active, ffn_grad, normed, hidden_grad)
+    else:
+        feed_grad = [
+            inner_rows(active, ffn_grad).astype(jnp.bfloat16),
+            inner_rows(normed, hidden_grad).astype(jnp.bfloat16),
+        ]
     grad_out = inner_rows(context, attended_grad).astype(jnp.bfloat16)
-    grad_down, grad_up, grad_out, state_grad, context_grad, gain_rows = flow.slot(
-        (grad_down, grad_up, grad_out, state_grad, context_grad, gain_rows)
-    )
-    flow.begin("feed", scatter_chain([grad_down, grad_up]))
+    feed_grad, grad_out, state_grad, context_grad, gain_rows = flow.slot(
+        (feed_grad, grad_out, state_grad, context_grad, gain_rows)
+    )
+    flow.begin(
+        "feed",
+        feed_chain(feed_grad, [(w_down.shape[0], 1), (w_up.shape[0], 4)]),
+        [0, 0, 0, 0, 1],
+    )
     tokens_grad = mixed_grad
     group_grads = []
     for number in range(groups):
-        left = wide * number
-        qkv_grad = jnp.concatenate(
-            run_attend_back(
-                parts_qkv[number], logsums[number], context_grad[:, left : left + wide], 0, pairs
-            ),
-            1,
+        qkv_grad = run_attend_back(
+            parts_qkv[number], logsums[number], context_grad, pairs * number
         )
         tokens_grad = tokens_grad + inner_cols(qkv_grad, weights[number])
         grad_group = inner_rows(tokens, qkv_grad).astype(jnp.bfloat16)
@@ -1104,9 +1194,6 @@
             done, blend_sum = flow.slot((done, blend_sum)) if number else (flow.slot(done), blend_sum)
             context_grad, grad_group, tokens_grad, state_grad = done
         group_grads.append(grad_group)
-    flow.begin(
-        "tokens", swap_chain(jnp.where(on_first, tokens_grad[half_len:], tokens_grad[:half_len]))
-    )
     flow.begin("qkv", scatter_chain(group_grads + [grad_out, gain_rows]), [0, 0, 1])
     blocks = ids_row.shape[0] // STEP_ROWS
     spread, *held = run_chars_back(
@@ -1123,8 +1210,13 @@
         held=[spread, *held],
         ends=[table_all, gru_all],
     )
-    grad_gru, grad_table = flow.slot((grad_gru, grad_table))
+    grad_gru, grad_table, tokens_grad = flow.slot((grad_gru, grad_table, tokens_grad))
     flow.begin("letters", scatter_chain([grad_gru, grad_table]))
+    flow.begin(
+        "tokens",
+        swap_chain(jnp.where(on_first, tokens_grad[half_len:], tokens_grad[:half_len])),
+        [1],
+    )
     while flow.live:
         flow.slot(())
     own_result = jnp.where(on_first, result[:half_len], result[half_len:])
@@ -1151,7 +1243,9 @@
         letter_sums[0],
         blend_sum,
         letter_sums[1],
-        gain_sum[0, : gains.size].reshape(gains.shape),
+        lax.dynamic_slice(
+            gain_sum, (0, my_place()[0] * gains.shape[1]), gains.shape
+        ),
     )
     rates = step_rates()
     results = [

time: 522 us -> 501 us (0.960)
  waiting for transfers between devices: 57.3 us -> 84.2 us
  other arithmetic: 59.2 us -> 35.8 us
  matrix products: 40 us -> 24.1 us
  local copies, waits for them, and re-layouts: 46.6 us -> 37.7 us
    dot_general x6 -> x4, matrix products: 28.5 us -> 11.4 us  [inner_rows(): lax.dot_general(former, latter, (((0,), (0,)), ((), ())), preferred_eleme...]
    pallas_call x7, Pallas kernels: 41.3 us -> 54.7 us  [the longest x1 26.1 us: run_blend(): pl.pallas_call(blend_both, in_specs=[scalars()] + [pl.BlockSpec(memory_sp...]
    all_gather x1, waiting for transfers between devices: 0.02 us -> 13.3 us  [on_device(): lax.all_gather(shards[3].astype(jnp.bfloat16), everyone, axis=0, tiled=True)]
    pallas_call x2, Pallas kernels: 51.5 us -> 42.2 us  [run_chars_back(): pl.pallas_call(functools.partial(chars_back, (last,), upstream is not Non...]
    scatter-add x1 -> x0, other arithmetic: 8.19 us -> none  [char_segments(): markers = jnp.zeros((char_count,), jnp.int32).at[starts].add(1)]
    ppermute x50 -> x49, waiting for transfers between devices: 56.3 us -> 64 us  [swap(): lax.ppermute(block, ('stream', 'dp'), [(place, place ^ mask) for place in...]
    another operation x8 -> x6, other arithmetic: 8.68 us -> 1.8 us
    reduce_scatter x1, waiting for transfers between devices: 0.91 us -> 6.85 us  [scatter_whole(): lax.psum_scatter(packed.reshape(-1, D), ('stream', 'dp'), scatter_dimensi...]
  transfers between devices with their start and end apart: 53 -> 52, of which waited for: 16 -> 19; matrix products, arithmetic and copies ran while one was open for 22% -> 12% of each run, Pallas kernels for 40% -> 41%
where the time goes in v4:
time: 501 us; the launch traced here: 497 us
  Pallas kernels  245 us (49%)
  waiting for transfers between devices  84.2 us (17%)
  starting transfers between devices  54.4 us (11%)
  local copies, waits for them, and re-layouts  37.7 us (8%)
  other arithmetic  35.8 us (7%)
  matrix products  24.1 us (5%)
  between operations  15.9 us (3%)
    ppermute x49, waiting for transfers between devices, swap(): lax.ppermute(block, ('stream', 'dp'), [(place, place ^ mask) for place in...  64 us
    ppermute x49, starting transfers between devices, swap(): lax.ppermute(block, ('stream', 'dp'), [(place, place ^ mask) for place in...  54.3 us
    pallas_call x2, Pallas kernels, run_chars_back(): pl.pallas_call(functools.partial(chars_back, (last,), upstream is not Non...  42.2 us
    pallas_call x3, Pallas kernels, run_attend_back(): pl.pallas_call(attend_back, grid=(pairs,), in_specs=[column(length, 128,...  39.4 us
    pallas_call x1, Pallas kernels, run_feed_back(): pl.pallas_call(feed_back, grid=(length // CHUNK,), in_specs=[rows_block(D...  32.2 us
    unnamed x287, local copies, waits for them, and re-layouts  28.8 us
    pallas_call x1, Pallas kernels, run_blend(): pl.pallas_call(blend_both, in_specs=[scalars()] + [pl.BlockSpec(memory_sp...  26.1 us
    pallas_call x3, Pallas kernels, run_attend(): pl.pallas_call(attend, grid=(pairs,), in_specs=[column(length, 128, every...  22.7 us
  transfers between devices with their start and end apart: 52, of which 19 were waited for; matrix products, arithmetic and copies ran while one was open for 12% of the time, Pallas kernels for 41%

profile of v4, /device:TPU:0, one launch (start us, length us, event | category | flops | bytes accessed | tf_op | source)
XLA Modules:
  0.0 497.2 jit_solution(5552405937716641744)
XLA Ops:
  19.3 4.4 collective-permute-done.4
  27.9 4.3 collective-permute-done.7
  35.7 5.9 %collective-permute-done.12 = bf16[1,1,2,1,48,768]{5,4,3,2,1,0:T(8,128)(2,1)} collective-permute-done((bf16[1,1,2,1,48,768]{5,4,3,2,1,0:T(8,128)(2,1)S(1)}, bf16[1,1,2,1,48,768]{5,4,3,2,1,0:T(8,128)(2,1)}, u32[]{:S(2)}, u32[]{:S(2)}) %collective-permute-start.12) | collective-permute-done | bytes 147488 | tf_op jit(solution)/shard_map/ppermute | solution.py:37
  52.8 6.3 %collective-permute-done.9 = bf16[1,1,2,1,96,768]{5,4,3,2,1,0:T(8,128)(2,1)} collective-permute-done((bf16[1,1,2,1,96,768]{5,4,3,2,1,0:T(8,128)(2,1)S(1)}, bf16[1,1,2,1,96,768]{5,4,3,2,1,0:T(8,128)(2,1)}, u32[]{:S(2)}, u32[]{:S(2)}) %collective-permute-start.9) | collective-permute-done | bytes 294944 | tf_op jit(solution)/shard_map/ppermute | solution.py:37
  73.9 7.4 %shard_map.468 = (bf16[1024,256]{1,0:T(8,128)(2,1)S(1)}, f32[32,1024]{1,0:T(8,128)S(1)}) custom-call(bf16[1024,768]{1,0:T(8,128)(2,1)S(1)} %convolution_convert_fusion.2.queries.key_rows.value_rows, bf16[1024,768]{1,0:T(8,128)(2,1)S(1)} %convolution_convert_fusion.2.queries.key_rows.value_rows, ...), custom_call_target="tpu_custom_call" | custom-call | flops 10000000000 | bytes 1 | tf_op jit(solution)/shard_map/pallas_call | solution.py:767
  85.2 7.4 %shard_map.470 = (bf16[1024,256]{1,0:T(8,128)(2,1)S(1)}, f32[32,1024]{1,0:T(8,128)S(1)}) custom-call(bf16[1024,768]{1,0:T(8,128)(2,1)S(1)} %convolution_convert_fusion.1.queries.key_rows.value_rows, bf16[1024,768]{1,0:T(8,128)(2,1)S(1)} %convolution_convert_fusion.1.queries.key_rows.value_rows, ...), custom_call_target="tpu_custom_call" | custom-call | flops 10000000000 | bytes 1 | tf_op jit(solution)/shard_map/pallas_call | solution.py:767
  96.9 7.9 %shard_map.472 = (bf16[1024,256]{1,0:T(8,128)(2,1)S(1)}, f32[32,1024]{1,0:T(8,128)S(1)}) custom-call(bf16[1024,768]{1,0:T(8,128)(2,1)S(1)} %convolution_convert_fusion.queries.key_rows.value_rows, bf16[1024,768]{1,0:T(8,128)(2,1)S(1)} %convolution_convert_fusion.queries.key_rows.value_rows, ...), custom_call_target="tpu_custom_call" | custom-call | flops 10000000000 | bytes 1 | tf_op jit(solution)/shard_map/pallas_call | solution.py:767
  106.8 3.8 convert_reduce_fusion.refs_2_
  119.5 19.1 %shard_map.474 = (f32[256,16,128]{2,1,0:T(8,128)S(1)}, f32[4096,8,128]{2,1,0:T(8,128)}, bf16[1024,768]{1,0:T(8,128)(2,1)S(1)}) custom-call(s32[4096]{0:T(1024)S(1)} %bitcast.167, s32[4096]{0:T(1024)S(1)} %rev.10.rows_b.refs_1_, s32[1024]{0:T(1024)S(1)} %add_bitcast_fusion.2.ends, bf16[256,768]{1,0:T(8,128)(2,1)S(1)} %get-tuple-element.282.table.refs_12_, ...), custom_call_target="tpu_custom_call" | custom-call | flops 24000000000 | bytes 1 | tf_op jit(solution)/shard_map/pallas_call | solution.py:657
  138.6 5.6 %collective-permute-done.24 = bf16[1,2,2,2,96,768]{5,4,3,2,1,0:T(8,128)(2,1)} collective-permute-done((bf16[1,2,2,2,96,768]{5,4,3,2,1,0:T(8,128)(2,1)}, bf16[1,2,2,2,96,768]{5,4,3,2,1,0:T(8,128)(2,1)}, u32[]{:S(2)}, u32[]{:S(2)}) %collective-permute-start.24) | collective-permute-done | bytes 1179680 | tf_op jit(solution)/shard_map/ppermute | solution.py:37
  150.4 3.2 shard_map.475.up
  153.6 3.1 convert_add_fusion.mixed
  160.1 18.0 %shard_map.477 = (f32[1024,768]{1,0:T(8,128)}, bf16[1024,768]{1,0:T(8,128)(2,1)}) custom-call(f32[1024,768]{1,0:T(8,128)} %convert_add_fusion.mixed, f32[3,768]{1,0:T(4,128)} %convert_reduce_fusion.1.gains, bf16[768,3072]{1,0:T(8,128)(2,1)} %copy-done.30, bf16[3072,768]{1,0:T(8,128)(2,1)} %copy-done.31), custom_call_target="tpu_custom_call" | custom-call | flops 17999998976 | bytes 1 | tf_op jit(solution)/shard_map/pallas_call | solution.py:944
  178.1 13.3 %all-gather.4.cloned.1.call-done.blend = bf16[4608,768]{1,0:T(8,128)(2,1)} async-done(((bf16[144,768]{1,0:T(8,128)(2,1)}), bf16[4608,768]{1,0:T(8,128)(2,1)}) %all-gather.4.cloned.1.call-update) | async-done | bytes 7077904 | tf_op jit(solution)/shard_map/all_gather | solution.py:1108
  191.4 26.1 %shard_map.478 = (bf16[1024,768]{1,0:T(8,128)(2,1)}, bf16[1024,768]{1,0:T(8,128)(2,1)}, f32[1024,768]{1,0:T(8,128)}, bf16[1024,2304]{1,0:T(8,128)(2,1)}, f32[8,768]{1,0:T(8,128)}) custom-call(s32[1]{0:T(128)} %bitcast.order, bf16[1024,768]{1,0:T(8,128)(2,1)} %get-tuple-element.311.feature, bf16[1024,768]{1,0:T(8,128)(2,1)} %copy-done.46, ...), custom_call_target="tpu_custom_call" | custom-call | flops 25999998976 | bytes 1 | tf_op jit(solution)/shard_map/pallas_call | solution.py:980
  217.5 10.8 %shard_map.479 = bf16[4608,768]{1,0:T(8,128)(2,1)} custom-call(bf16[1024,768]{1,0:T(8,128)(2,1)S(1)} %copy-done.48, bf16[1024,768]{1,0:T(8,128)(2,1)S(1)} %copy-done.47, bf16[1024,2304]{1,0:T(8,128)(2,1)} %get-tuple-element.316.grads), custom_call_target="tpu_custom_call" | custom-call | flops 12000000000 | bytes 1 | tf_op jit(solution)/shard_map/pallas_call | solution.py:1009
  231.6 32.2 %shard_map.480 = (bf16[1024,3072]{1,0:T(8,128)(2,1)}, bf16[1024,3072]{1,0:T(8,128)(2,1)}, bf16[1024,768]{1,0:T(8,128)(2,1)}, bf16[1024,768]{1,0:T(8,128)(2,1)}, ...) custom-call(f32[1024,768]{1,0:T(8,128)} %convert_add_fusion.mixed, ...), custom_call_target="tpu_custom_call" | custom-call | flops 32000000000 | bytes 1 | tf_op jit(solution)/shard_map/pallas_call | solution.py:964
  263.8 19.9 %shard_map.481 = (bf16[16,192,768]{2,1,0:T(8,128)(2,1)}, bf16[16,192,768]{2,1,0:T(8,128)(2,1)}) custom-call(s32[1]{0:T(128)} %bitcast.14.place, bf16[1024,3072]{1,0:T(8,128)(2,1)} %get-tuple-element.321.former, bf16[1024,3072]{1,0:T(8,128)(2,1)} %get-tuple-element.322.latter, bf16[1024,768]{1,0:T(8,128)(2,1)} %get-tuple-element.323.given, ...), custom_call_target="tpu_custom_call" | custom-call | flops 16000000000 | bytes 1 | tf_op jit(solution)/shard_map/pallas_call | solution.py:294
  283.9 4.0 convolution_convert_fusion.6.refs_3_
  288.2 13.1 %shard_map.482 = bf16[1024,768]{1,0:T(8,128)(2,1)S(1)} custom-call(bf16[1024,768]{1,0:T(8,128)(2,1)S(1)} %copy-done.1, bf16[1024,768]{1,0:T(8,128)(2,1)S(1)} %copy-done.1, bf16[1024,768]{1,0:T(8,128)(2,1)S(1)} %copy-done.1, f32[32,1024]{1,0:T(8,128)S(1)} %copy-done.18, bf16[1024,768]{1,0:T(8,128)(2,1)S(1)} %copy-done.6), custom_call_target="tpu_custom_call" | custom-call | flops 1000000000 | bytes 1 | tf_op jit(solution)/shard_map/pallas_call | solution.py:784
  312.8 13.1 %shard_map.484 = bf16[1024,768]{1,0:T(8,128)(2,1)S(1)} custom-call(bf16[1024,768]{1,0:T(8,128)(2,1)S(1)} %copy-done.3, bf16[1024,768]{1,0:T(8,128)(2,1)S(1)} %copy-done.3, bf16[1024,768]{1,0:T(8,128)(2,1)S(1)} %copy-done.3, f32[32,1024]{1,0:T(8,128)S(1)} %copy-done.20, bf16[1024,768]{1,0:T(8,128)(2,1)S(1)} %copy-done.6), custom_call_target="tpu_custom_call" | custom-call | flops 1000000000 | bytes 1 | tf_op jit(solution)/shard_map/pallas_call | solution.py:784
  329.8 13.3 %shard_map.483 = bf16[1024,768]{1,0:T(8,128)(2,1)S(1)} custom-call(bf16[1024,768]{1,0:T(8,128)(2,1)S(1)} %copy-done.5, bf16[1024,768]{1,0:T(8,128)(2,1)S(1)} %copy-done.5, bf16[1024,768]{1,0:T(8,128)(2,1)S(1)} %copy-done.5, f32[32,1024]{1,0:T(8,128)S(1)} %copy-done.22, bf16[1024,768]{1,0:T(8,128)(2,1)S(1)} %copy-done.6), custom_call_target="tpu_custom_call" | custom-call | flops 1000000000 | bytes 1 | tf_op jit(solution)/shard_map/pallas_call | solution.py:784
  348.2 6.9 %reduce-scatter.2.cloned.1.call-done = bf16[144,768]{1,0:T(8,128)(2,1)} async-done(((bf16[4608,768]{1,0:T(8,128)(2,1)}), bf16[144,768]{1,0:T(8,128)(2,1)}) %reduce-scatter.2.cloned.1.call-update) | async-done | bytes 221200 | tf_op jit(solution)/shard_map/reduce_scatter | solution.py:237
  369.9 20.3 %shard_map.486 = (f32[1024,8,128]{2,1,0:T(8,128)S(1)}, f32[8,128]{1,0:T(8,128)S(1)}, f32[256,8,128]{2,1,0:T(8,128)S(1)}, f32[256,8,128]{2,1,0:T(8,128)S(1)}, f32...) custom-call(s32[4096]{0:T(1024)S(1)} %bitcast.168, s32[4096]{0:T(1024)S(1)} %copy-done.26, s32[4096]{0:T(1024)S(1)} %copy-done.27, ...), custom_call_target="tpu_custom_call" | custom-call | flops 24000000000 | bytes 1 | tf_op jit(solution)/shard_map/pallas_call | solution.py:702
  390.3 3.8 collective-permute-done.31
  398.7 3.8 shard_map.489
  406.1 21.9 %shard_map.488 = (bf16[768,1536]{1,0:T(8,128)(2,1)S(1)}, bf16[256,768]{1,0:T(8,128)(2,1)S(1)}) custom-call(s32[4096]{0:T(1024)S(1)} %bitcast.169, s32[4096]{0:T(1024)S(1)} %copy-done.26, s32[4096]{0:T(1024)S(1)} %copy-done.27, s32[4096]{0:T(1024)S(1)} %rev.11.refs_3_, f32[256,16,128]{2,1,0:T(8,128)S(1)} %copy-done.53, ...), custom_call_target="tpu_custom_call" | custom-call | flops 24000000000 | bytes 1 | tf_op jit(solution)/shard_map/pallas_call | solution.py:702
  428.1 4.4 collective-permute-done.35
  445.2 5.8 %collective-permute-done.40 = bf16[104,768]{1,0:T(8,128)(2,1)S(1)} collective-permute-done((bf16[104,768]{1,0:T(8,128)(2,1)S(1)}, bf16[104,768]{1,0:T(8,128)(2,1)S(1)}, u32[]{:S(2)}, u32[]{:S(2)}) %collective-permute-start.40) | collective-permute-done | bytes 159776 | tf_op jit(solution)/shard_map/ppermute | solution.py:37
  452.8 3.2 collective-permute-done.39
  459.3 7.2 %collective-permute-done.43 = bf16[4,56,768]{2,1,0:T(8,128)(2,1)S(1)} collective-permute-done((bf16[4,56,768]{2,1,0:T(8,128)(2,1)S(1)}, bf16[4,56,768]{2,1,0:T(8,128)(2,1)S(1)}, u32[]{:S(2)}, u32[]{:S(2)}) %collective-permute-start.43) | collective-permute-done | bytes 344096 | tf_op jit(solution)/shard_map/ppermute | solution.py:37
  466.5 5.8 %collective-permute-done.44 = bf16[4,56,768]{2,1,0:T(8,128)(2,1)S(1)} collective-permute-done((bf16[4,56,768]{2,1,0:T(8,128)(2,1)S(1)}, bf16[4,56,768]{2,1,0:T(8,128)(2,1)S(1)}, u32[]{:S(2)}, u32[]{:S(2)}) %collective-permute-start.44) | collective-permute-done | bytes 344096 | tf_op jit(solution)/shard_map/ppermute | solution.py:37
  (507 shorter events, 156.3 us)
Async XLA Ops:
  7.2 110.0 %all-gather.6.cloned.1.call-start = ((), (), s32[]{:S(2)}) async-start(), calls=%async_computation.3 | async-start | bytes 3244032 | tf_op jit(solution)/shard_map/all_gather | solution.py:1107
  18.8 13.5 %collective-permute-start.8 = (bf16[1,1,1,1,96,768]{5,4,3,2,1,0:T(8,128)(2,1)S(1)}, bf16[1,1,1,1,96,768]{5,4,3,2,1,0:T(8,128)(2,1)S(1)}, u32[]{:S(2)}, u32[]{:S(2)}) collective-permute-start(bf16[1,1,1,1,96,768]{5,4,3,2,1,0:T(8,128)(2,1)S(1)} %bitcast.182), channel_id=1, source_target_pairs={{0,4},{1,5},{2,6},{3,7},{4,0},{5,1},{6,2},{7,3},{8,12},{9,13},{10,... | collective-permute-start | bytes 442376 | tf_op jit(solution)/shard_map/ppermute | solution.py:37
  43.1 148.4 %all-gather.4.cloned.1.call-start = ((), (), s32[]{:S(2)}) async-start(), calls=%async_computation.1 | async-start | bytes 7299072 | tf_op jit(solution)/shard_map/all_gather | solution.py:1108
  45.1 15.7 %collective-permute-start = (bf16[512,768]{1,0:T(8,128)(2,1)}, bf16[512,768]{1,0:T(8,128)(2,1)}, u32[]{:S(2)}, u32[]{:S(2)}) collective-permute-start(bf16[512,768]{1,0:T(8,128)(2,1)} %get-tuple-element.463), channel_id=1, source_target_pairs={{0,16},{1,17},{2,18},{3,19},{4,20},{5,21},{6,22},{7,23},{8,24},{9,... | collective-permute-start | bytes 2359304 | tf_op jit(solution)/shard_map/ppermute | solution.py:37
  45.9 13.2 %collective-permute-start.9 = (bf16[1,1,2,1,96,768]{5,4,3,2,1,0:T(8,128)(2,1)S(1)}, bf16[1,1,2,1,96,768]{5,4,3,2,1,0:T(8,128)(2,1)}, u32[]{:S(2)}, u32[]{:S(2)}) collective-permute-start(bf16[1,1,2,1,96,768]{5,4,3,2,1,0:T(8,128)(2,1)S(1)} %constant_dynamic-update-slice_fusion.8), channel_id=1, source_target_pairs={{0,8},{1,9},{2,10},{3,11},{4,12},{5,13},{6,14},{7,15},{8,0},{9,1},... | collective-permute-start | bytes 884744 | tf_op jit(solution)/shard_map/ppermute | solution.py:37
  49.6 11.3 %collective-permute-start.15 = (bf16[1,2,2,1,48,768]{5,4,3,2,1,0:T(8,128)(2,1)S(1)}, bf16[1,2,2,1,48,768]{5,4,3,2,1,0:T(8,128)(2,1)}, u32[]{:S(2)}, u32[]{:S(2)}) collective-permute-start(bf16[1,2,2,1,48,768]{5,4,3,2,1,0:T(8,128)(2,1)S(1)} %constant_dynamic-update-slice_fusion.16), channel_id=1, source_target_pairs={{0,2},{1,3},{2,0},{3,1},{4,6},{5,7},{6,4},{7,5},{8,10},{9,11},{10,... | collective-permute-start | bytes 884744 | tf_op jit(solution)/shard_map/ppermute | solution.py:37
  52.8 302.3 %reduce-scatter.2.cloned.1.call-start = ((), (), s32[]{:S(2)}) async-start(), calls=%async_computation.2 | async-start | bytes 7299072 | tf_op jit(solution)/shard_map/reduce_scatter | solution.py:237
  62.7 19.3 %collective-permute-start.19 = (bf16[1,1,2,1,96,768]{5,4,3,2,1,0:T(8,128)(2,1)S(1)}, bf16[1,1,2,1,96,768]{5,4,3,2,1,0:T(8,128)(2,1)S(1)}, u32[]{:S(2)}, u32[]{:S(2)}) collective-permute-start(bf16[1,1,2,1,96,768]{5,4,3,2,1,0:T(8,128)(2,1)S(1)} %constant_dynamic-update-slice_fusion.22), channel_id=1, source_target_pairs={{0,8},{1,9},{2,10},{3,11},{4,12},{5,13},{6,14},{7,15},{8,0},{9,1},... | collective-permute-start | bytes 884744 | tf_op jit(solution)/shard_map/ppermute | solution.py:37
  64.7 17.4 %collective-permute-start.18 = (bf16[1,2,2,2,48,768]{5,4,3,2,1,0:T(8,128)(2,1)S(1)}, bf16[1,2,2,2,48,768]{5,4,3,2,1,0:T(8,128)(2,1)S(1)}, u32[]{:S(2)}, u32[]{:S(2)}) collective-permute-start(bf16[1,2,2,2,48,768]{5,4,3,2,1,0:T(8,128)(2,1)S(1)} %constant_dynamic-update-slice_fusion.20), channel_id=1, source_target_pairs={{0,16},{1,17},{2,18},{3,19},{4,20},{5,21},{6,22},{7,23},{8,24},{9,... | collective-permute-start | bytes 1769480 | tf_op jit(solution)/shard_map/ppermute | solution.py:37
  67.0 15.0 %collective-permute-start.17 = (bf16[1,2,2,1,96,768]{5,4,3,2,1,0:T(8,128)(2,1)S(1)}, bf16[1,2,2,1,96,768]{5,4,3,2,1,0:T(8,128)(2,1)S(1)}, u32[]{:S(2)}, u32[]{:S(2)}) collective-permute-start(bf16[1,2,2,1,96,768]{5,4,3,2,1,0:T(8,128)(2,1)S(1)} %constant_dynamic-update-slice_fusion.18), channel_id=1, source_target_pairs={{0,2},{1,3},{2,0},{3,1},{4,6},{5,7},{6,4},{7,5},{8,10},{9,11},{10,... | collective-permute-start | bytes 1769480 | tf_op jit(solution)/shard_map/ppermute | solution.py:37
  82.1 28.5 %collective-permute-start.22 = (bf16[1,2,2,1,96,768]{5,4,3,2,1,0:T(8,128)(2,1)S(1)}, bf16[1,2,2,1,96,768]{5,4,3,2,1,0:T(8,128)(2,1)S(1)}, u32[]{:S(2)}, u32[]{:S(2)}) collective-permute-start(bf16[1,2,2,1,96,768]{5,4,3,2,1,0:T(8,128)(2,1)S(1)} %constant_dynamic-update-slice_fusion.26), channel_id=1, source_target_pairs={{0,2},{1,3},{2,0},{3,1},{4,6},{5,7},{6,4},{7,5},{8,10},{9,11},{10,... | collective-permute-start | bytes 1769480 | tf_op jit(solution)/shard_map/ppermute | solution.py:37
  82.8 27.8 %collective-permute-start.21 = (bf16[1,2,2,2,96,768]{5,4,3,2,1,0:T(8,128)(2,1)S(1)}, bf16[1,2,2,2,96,768]{5,4,3,2,1,0:T(8,128)(2,1)}, u32[]{:S(2)}, u32[]{:S(2)}) collective-permute-start(bf16[1,2,2,2,96,768]{5,4,3,2,1,0:T(8,128)(2,1)S(1)} %constant_dynamic-update-slice_fusion.24), channel_id=1, source_target_pairs={{0,16},{1,17},{2,18},{3,19},{4,20},{5,21},{6,22},{7,23},{8,24},{9,... | collective-permute-start | bytes 3538952 | tf_op jit(solution)/shard_map/ppermute | solution.py:37
  112.6 31.7 %collective-permute-start.24 = (bf16[1,2,2,2,96,768]{5,4,3,2,1,0:T(8,128)(2,1)}, bf16[1,2,2,2,96,768]{5,4,3,2,1,0:T(8,128)(2,1)}, u32[]{:S(2)}, u32[]{:S(2)}) collective-permute-start(bf16[1,2,2,2,96,768]{5,4,3,2,1,0:T(8,128)(2,1)} %constant_dynamic-update-slice_fusion.28), channel_id=1, source_target_pairs={{0,16},{1,17},{2,18},{3,19},{4,20},{5,21},{6,22},{7,23},{8,24},{9,... | collective-permute-start | bytes 3538952 | tf_op jit(solution)/shard_map/ppermute | solution.py:37
  115.7 28.5 %collective-permute-start.23 = (bf16[16,96,768]{2,1,0:T(8,128)(2,1)S(1)}, bf16[16,96,768]{2,1,0:T(8,128)(2,1)}, u32[]{:S(2)}, u32[]{:S(2)}) collective-permute-start(bf16[16,96,768]{2,1,0:T(8,128)(2,1)S(1)} %bitcast.155), channel_id=1, source_target_pairs={{0,1},{1,0},{2,3},{3,2},{4,5},{5,4},{6,7},{7,6},{8,9},{9,8},{10,11... | collective-permute-start | bytes 7077896 | tf_op jit(solution)/shard_map/ppermute | solution.py:37
  147.4 30.8 %collective-permute-start.26 = (bf16[512,768]{1,0:T(8,128)(2,1)S(1)}, bf16[512,768]{1,0:T(8,128)(2,1)}, u32[]{:S(2)}, u32[]{:S(2)}) collective-permute-start(bf16[512,768]{1,0:T(8,128)(2,1)S(1)} %get-tuple-element.461), channel_id=1, source_target_pairs={{0,16},{1,17},{2,18},{3,19},{4,20},{5,21},{6,22},{7,23},{8,24},{9,... | collective-permute-start | bytes 2359304 | tf_op jit(solution)/shard_map/ppermute | solution.py:37
  229.8 58.1 %collective-permute-start.27 = (bf16[512,768]{1,0:T(8,128)(2,1)S(1)}, bf16[512,768]{1,0:T(8,128)(2,1)S(1)}, u32[]{:S(2)}, u32[]{:S(2)}) collective-permute-start(bf16[512,768]{1,0:T(8,128)(2,1)S(1)} %broadcast_select_fusion.2), channel_id=1, source_target_pairs={{0,16},{1,17},{2,18},{3,19},{4,20},{5,21},{6,22},{7,23},{8,24},{9,... | collective-permute-start | bytes 2359304 | tf_op jit(solution)/shard_map/ppermute | solution.py:37
  288.0 19.3 %collective-permute-start.28 = (bf16[16,192,768]{2,1,0:T(8,128)(2,1)S(1)}, bf16[16,192,768]{2,1,0:T(8,128)(2,1)S(1)}, u32[]{:S(2)}, u32[]{:S(2)}) collective-permute-start(bf16[16,192,768]{2,1,0:T(8,128)(2,1)S(1)} %copy-done.132), channel_id=1, source_target_pairs={{0,1},{1,0},{2,3},{3,2},{4,5},{5,4},{6,7},{7,6},{8,9},{9,8},{10,11... | collective-permute-start | bytes 14155784 | tf_op jit(solution)/shard_map/ppermute | solution.py:37
  311.0 45.8 %collective-permute-start.29 = (bf16[4,192,768]{2,1,0:T(8,128)(2,1)S(1)}, bf16[4,192,768]{2,1,0:T(8,128)(2,1)}, u32[]{:S(2)}, u32[]{:S(2)}) collective-permute-start(bf16[4,192,768]{2,1,0:T(8,128)(2,1)S(1)} %get-tuple-element.355), channel_id=1, source_target_pairs={{0,16},{1,17},{2,18},{3,19},{4,20},{5,21},{6,22},{7,23},{8,24},{9,... | collective-permute-start | bytes 3538952 | tf_op jit(solution)/shard_map/ppermute | solution.py:37
  311.2 45.6 %collective-permute-start.30 = (bf16[4,192,768]{2,1,0:T(8,128)(2,1)S(1)}, bf16[4,192,768]{2,1,0:T(8,128)(2,1)}, u32[]{:S(2)}, u32[]{:S(2)}) collective-permute-start(bf16[4,192,768]{2,1,0:T(8,128)(2,1)S(1)} %get-tuple-element.356), channel_id=1, source_target_pairs={{0,2},{1,3},{2,0},{3,1},{4,6},{5,7},{6,4},{7,5},{8,10},{9,11},{10,... | collective-permute-start | bytes 3538952 | tf_op jit(solution)/shard_map/ppermute | solution.py:37
  364.5 29.6 %collective-permute-start.32 = (bf16[16,104,768]{2,1,0:T(8,128)(2,1)}, bf16[16,104,768]{2,1,0:T(8,128)(2,1)}, u32[]{:S(2)}, u32[]{:S(2)}) collective-permute-start(bf16[16,104,768]{2,1,0:T(8,128)(2,1)} %get-tuple-element.373), channel_id=1, source_target_pairs={{0,1},{1,0},{2,3},{3,2},{4,5},{5,4},{6,7},{7,6},{8,9},{9,8},{10,11... | collective-permute-start | bytes 7667720 | tf_op jit(solution)/shard_map/ppermute | solution.py:37
  364.6 29.5 %collective-permute-start.31 = (bf16[4,192,768]{2,1,0:T(8,128)(2,1)}, bf16[4,192,768]{2,1,0:T(8,128)(2,1)S(1)}, u32[]{:S(2)}, u32[]{:S(2)}) collective-permute-start(bf16[4,192,768]{2,1,0:T(8,128)(2,1)} %copy-done.29), channel_id=1, source_target_pairs={{0,18},{1,19},{2,16},{3,17},{4,22},{5,23},{6,20},{7,21},{8,26},{9,... | collective-permute-start | bytes 3538952 | tf_op jit(solution)/shard_map/ppermute | solution.py:37
  397.1 30.9 %collective-permute-start.33 = (bf16[2,192,768]{2,1,0:T(8,128)(2,1)}, bf16[2,192,768]{2,1,0:T(8,128)(2,1)}, u32[]{:S(2)}, u32[]{:S(2)}) collective-permute-start(bf16[2,192,768]{2,1,0:T(8,128)(2,1)} %slice.278), channel_id=1, source_target_pairs={{0,8},{1,9},{2,10},{3,11},{4,12},{5,13},{6,14},{7,15},{8,0},{9,1},... | collective-permute-start | bytes 1769480 | tf_op jit(solution)/shard_map/ppermute | solution.py:37
  402.6 25.5 %collective-permute-start.34 = (bf16[4,104,768]{2,1,0:T(8,128)(2,1)S(1)}, bf16[4,104,768]{2,1,0:T(8,128)(2,1)S(1)}, u32[]{:S(2)}, u32[]{:S(2)}) collective-permute-start(bf16[4,104,768]{2,1,0:T(8,128)(2,1)S(1)} %get-tuple-element.390), channel_id=1, source_target_pairs={{0,18},{1,19},{2,16},{3,17},{4,22},{5,23},{6,20},{7,21},{8,26},{9,... | collective-permute-start | bytes 1916936 | tf_op jit(solution)/shard_map/ppermute | solution.py:37
  404.5 27.9 %collective-permute-start.35 = (bf16[4,104,768]{2,1,0:T(8,128)(2,1)S(1)}, bf16[4,104,768]{2,1,0:T(8,128)(2,1)S(1)}, u32[]{:S(2)}, u32[]{:S(2)}) collective-permute-start(bf16[4,104,768]{2,1,0:T(8,128)(2,1)S(1)} %get-tuple-element.391), channel_id=1, source_target_pairs={{0,16},{1,17},{2,18},{3,19},{4,20},{5,21},{6,22},{7,23},{8,24},{9,... | collective-permute-start | bytes 1916936 | tf_op jit(solution)/shard_map/ppermute | solution.py:37
  405.0 27.9 %collective-permute-start.36 = (bf16[4,104,768]{2,1,0:T(8,128)(2,1)S(1)}, bf16[4,104,768]{2,1,0:T(8,128)(2,1)S(1)}, u32[]{:S(2)}, u32[]{:S(2)}) collective-permute-start(bf16[4,104,768]{2,1,0:T(8,128)(2,1)S(1)} %get-tuple-element.392), channel_id=1, source_target_pairs={{0,2},{1,3},{2,0},{3,1},{4,6},{5,7},{6,4},{7,5},{8,10},{9,11},{10,... | collective-permute-start | bytes 1916936 | tf_op jit(solution)/shard_map/ppermute | solution.py:37
  436.7 22.6 %collective-permute-start.37 = (bf16[1,192,768]{2,1,0:T(8,128)(2,1)S(1)}, bf16[1,192,768]{2,1,0:T(8,128)(2,1)S(1)}, u32[]{:S(2)}, u32[]{:S(2)}) collective-permute-start(bf16[1,192,768]{2,1,0:T(8,128)(2,1)S(1)} %slice.279), channel_id=1, source_target_pairs={{0,4},{1,5},{2,6},{3,7},{4,0},{5,1},{6,2},{7,3},{8,12},{9,13},{10,... | collective-permute-start | bytes 884744 | tf_op jit(solution)/shard_map/ppermute | solution.py:37
  438.2 21.1 %collective-permute-start.41 = (bf16[512,768]{1,0:T(8,128)(2,1)S(1)}, bf16[512,768]{1,0:T(8,128)(2,1)S(1)}, u32[]{:S(2)}, u32[]{:S(2)}) collective-permute-start(bf16[512,768]{1,0:T(8,128)(2,1)S(1)} %broadcast_select_fusion), channel_id=1, source_target_pairs={{0,16},{1,17},{2,18},{3,19},{4,20},{5,21},{6,22},{7,23},{8,24},{9,... | collective-permute-start | bytes 2359304 | tf_op jit(solution)/shard_map/ppermute | solution.py:37
  441.7 14.3 %collective-permute-start.39 = (bf16[104,768]{1,0:T(8,128)(2,1)S(1)}, bf16[104,768]{1,0:T(8,128)(2,1)S(1)}, u32[]{:S(2)}, u32[]{:S(2)}) collective-permute-start(bf16[104,768]{1,0:T(8,128)(2,1)S(1)} %get-tuple-element.465), channel_id=1, source_target_pairs={{0,8},{1,9},{2,10},{3,11},{4,12},{5,13},{6,14},{7,15},{8,0},{9,1},... | collective-permute-start | bytes 479240 | tf_op jit(solution)/shard_map/ppermute | solution.py:37
  442.3 15.0 %collective-permute-start.38 = (bf16[104,768]{1,0:T(8,128)(2,1)S(1)}, bf16[104,768]{1,0:T(8,128)(2,1)S(1)}, u32[]{:S(2)}, u32[]{:S(2)}) collective-permute-start(bf16[104,768]{1,0:T(8,128)(2,1)S(1)} %get-tuple-element.466), channel_id=1, source_target_pairs={{0,4},{1,5},{2,6},{3,7},{4,0},{5,1},{6,2},{7,3},{8,12},{9,13},{10,... | collective-permute-start | bytes 479240 | tf_op jit(solution)/shard_map/ppermute | solution.py:37
  451.0 15.5 %collective-permute-start.43 = (bf16[4,56,768]{2,1,0:T(8,128)(2,1)S(1)}, bf16[4,56,768]{2,1,0:T(8,128)(2,1)S(1)}, u32[]{:S(2)}, u32[]{:S(2)}) collective-permute-start(bf16[4,56,768]{2,1,0:T(8,128)(2,1)S(1)} %get-tuple-element.407), channel_id=1, source_target_pairs={{0,18},{1,19},{2,16},{3,17},{4,22},{5,23},{6,20},{7,21},{8,26},{9,... | collective-permute-start | bytes 1032200 | tf_op jit(solution)/shard_map/ppermute | solution.py:37
  456.0 16.2 %collective-permute-start.44 = (bf16[4,56,768]{2,1,0:T(8,128)(2,1)S(1)}, bf16[4,56,768]{2,1,0:T(8,128)(2,1)S(1)}, u32[]{:S(2)}, u32[]{:S(2)}) collective-permute-start(bf16[4,56,768]{2,1,0:T(8,128)(2,1)S(1)} %get-tuple-element.408), channel_id=1, source_target_pairs={{0,16},{1,17},{2,18},{3,19},{4,20},{5,21},{6,22},{7,23},{8,24},{9,... | collective-permute-start | bytes 1032200 | tf_op jit(solution)/shard_map/ppermute | solution.py:37
  457.3 15.0 %collective-permute-start.45 = (bf16[4,56,768]{2,1,0:T(8,128)(2,1)S(1)}, bf16[4,56,768]{2,1,0:T(8,128)(2,1)S(1)}, u32[]{:S(2)}, u32[]{:S(2)}) collective-permute-start(bf16[4,56,768]{2,1,0:T(8,128)(2,1)S(1)} %get-tuple-element.409), channel_id=1, source_target_pairs={{0,2},{1,3},{2,0},{3,1},{4,6},{5,7},{6,4},{7,5},{8,10},{9,11},{10,... | collective-permute-start | bytes 1032200 | tf_op jit(solution)/shard_map/ppermute | solution.py:37
  (158 other events, 1184.3 us)
Sparse Core Ops, SparseCore 0:
  43.2 66.8 all-gather.5
  113.6 77.8 all-gather.3
  228.5 126.5 reduce-scatter.1

commit v5 on v4

--- a/solution.py
+++ b/solution.py
@@ -311,12 +311,12 @@
     )(my_place(), active, hidden_grad, ffn_grad, normed)
 
 
-def scatter_chain(grads):
+def scatter_chain(grads, halving=False):
     parts = lax.axis_size("dp") * lax.axis_size("stream")
     shapes = shapes_of(grads, parts)
     if not in_pairs(shapes):
         return scatter_whole(grads)
-    total = yield from halves_chain(*core_halves(grads, shapes, parts))
+    total = yield from halves_chain(*core_halves(grads, shapes, parts), False, halving)
     return own_pieces(total, shapes)
 
 
@@ -338,7 +338,7 @@
     )(my_place(), *[grad.astype(jnp.bfloat16) for grad in grads])
 
 
-def halves_chain(kept, sent, split=False):
+def halves_chain(kept, sent, split=False, halving=False):
     high = kept.shape[1]
     kept, other = yield (kept, swap(sent, 1))
     top = pair_bits()
@@ -366,11 +366,11 @@
     else:
         total, last, *got = yield (total, swap(sent[2], corner | 2), *got)
     total = total + sum(block.astype(jnp.float32) for block in [last, *got])
-    while split and far > 1:
+    while halving and far > 1:
         far //= 2
         kept, other = yield (total[:far], swap(total[far:].astype(jnp.bfloat16), far << 2))
         total = kept + other.astype(jnp.float32)
-    if split:
+    if halving:
         return total[0]
     others = [
         swap(total[number].astype(jnp.bfloat16), number << 2) for number in range(1, far)
@@ -385,10 +385,10 @@
         out[0] = total.astype(out.dtype)
 
 
-def feed_chain(halves, shapes):
+def feed_chain(halves, shapes, split, halving):
     if not in_pairs(shapes):
         return scatter_whole(halves)
-    total = yield from halves_chain(*halves, True)
+    total = yield from halves_chain(*halves, split, halving)
     return own_pieces(total, shapes)
 
 
@@ -550,7 +550,7 @@
     else:
         spread, carry_in, *sums_in = take(6)
     if closing:
-        table, w_gru = take(2)
+        position, table, w_gru = take(3)
     if opening:
         (spread,) = take(1)
     if closing:
@@ -634,8 +634,28 @@
             )
             full[:, left + width : left + width + 128] = update * total
         found = full[...].astype(jnp.bfloat16)
-        grad_gru[...] = contract(table[...], found, 0, 0).astype(grad_gru.dtype)
-        grad_table[...] = contract(found, w_gru[...], 1, 1).astype(grad_table.dtype)
+        whole_gru = contract(table[...], found, 0, 0)
+        whole_table = contract(found, w_gru[...], 1, 1)
+        if grad_gru.shape[0] == whole_gru.shape[0]:
+            grad_gru[...] = whole_gru.astype(grad_gru.dtype)
+            grad_table[...] = whole_table.astype(grad_table.dtype)
+            return
+        pairs = grad_gru.shape[0]
+        high, low = whole_gru.shape[0] // (2 * pairs), whole_table.shape[0] // (2 * pairs)
+        core = position[0] & 1
+        for pair in range(pairs):
+            halves = []
+            for side in range(2):
+                at = 2 * pair + side
+                rows = whole_gru[at * high : at * high + high]
+                halves.append(
+                    jnp.concatenate(
+                        [rows[:, :D], rows[:, D:], whole_table[at * low : at * low + low]], 0
+                    )
+                )
+            there = pair ^ (position[0] >> 1)
+            grad_gru[there] = jnp.where(core == 0, halves[0], halves[1]).astype(grad_gru.dtype)
+            grad_table[there] = jnp.where(core == 0, halves[1], halves[0]).astype(grad_table.dtype)
 
 
 def whole(array):
@@ -674,6 +694,10 @@
     )(ids, jnp.flip(ids), ends, table, w_gru, shares)
 
 
+def letter_shapes(ends, parts):
+    return [(ends[1].shape[0] // parts, ends[1].shape[1] // D), (ends[0].shape[0] // parts, 1)]
+
+
 def run_chars_back(last, count, ids, owners, letters, before, *, upstream=None, held=None, ends=None):
     f32 = jnp.float32
     tile = jax.ShapeDtypeStruct((letters.shape[0], 8, 128), f32)
@@ -690,12 +714,16 @@
     else:
         inputs += held
     if ends is not None:
-        inputs += ends
-        outs.append(jax.ShapeDtypeStruct(ends[1].shape, jnp.bfloat16))
-        outs.append(jax.ShapeDtypeStruct(ends[0].shape, jnp.bfloat16))
+        inputs += [my_place()] + ends
+        parts = lax.axis_size("dp") * lax.axis_size("stream")
+        if in_pairs(letter_shapes(ends, parts)):
+            high = sum(rows * side for rows, side in letter_shapes(ends, parts))
+            outs += [jax.ShapeDtypeStruct((parts // 2, high, D), jnp.bfloat16)] * 2
+        else:
+            outs += [jax.ShapeDtypeStruct(array.shape, jnp.bfloat16) for array in ends[::-1]]
     else:
         outs += [flat] + [tile] * 4
-    blocks += [whole(array) for array in inputs[6:]]
+    blocks += [scalars() if array.shape == (1,) else whole(array) for array in inputs[6:]]
     scratch = [pltpu.VMEM(tile.shape, f32)] * 4 + [pltpu.VMEM(flat.shape, f32)]
     if ends is not None:
         scratch.append(pltpu.VMEM((ends[0].shape[0], ends[1].shape[1]), f32))
@@ -788,7 +816,7 @@
         + [pl.BlockSpec((16, length), lambda pair: (pair, 0)), column(length, 128, first)],
         out_specs=pl.BlockSpec((length, across), lambda pair: (0, 0)),
         out_shape=jax.ShapeDtypeStruct((length, across), jnp.bfloat16),
-        compiler_params=pltpu.CompilerParams(vmem_limit_bytes=40 << 20),
+        compiler_params=pltpu.CompilerParams(vmem_limit_bytes=30 << 20),
         cost_estimate=spent(1),
     )(qkv, qkv, qkv, logsum, grads)
 
@@ -935,7 +963,7 @@
 
 
 def fixed(*shape):
-    return pl.BlockSpec(shape, lambda step: (0,) * len(shape))
+    return pl.BlockSpec(shape, lambda step: (0,) * len(shape), pipeline_mode=pl.Buffered(1))
 
 
 def run_feed(mixed, gains, up, down):
@@ -1019,6 +1047,39 @@
         compiler_params=params(48),
         cost_estimate=spent(12),
     )(feature, pooled, grads)
+
+
+def group_grads(place, tokens, first, second, third, context, attended, gains, keep, send, held):
+    pairs, high, _ = keep.shape
+    rows = D // (2 * pairs)
+    pieces = [(tokens, first), (tokens, second), (tokens, third), (context, attended)]
+    for number, (former, latter) in enumerate(pieces):
+        whole_grad = contract(former[...], latter[...], 0, 0)
+        held[:, number * rows : number * rows + rows] = whole_grad.reshape(2 * pairs, rows, D)
+    held[:, 4 * rows :] = jnp.broadcast_to(gains[...][None], (2 * pairs, 8, D))
+    core = place[0] & 1
+    for pair in range(pairs):
+        there = pair ^ (place[0] >> 1)
+        former, latter = held[2 * pair], held[2 * pair + 1]
+        keep[there] = jnp.where(core == 0, former, latter).astype(keep.dtype)
+        send[there] = jnp.where(core == 0, latter, former).astype(send.dtype)
+
+
+def run_group_grads(tokens, qkv_grads, context, attended, gains):
+    parts = lax.axis_size("dp") * lax.axis_size("stream")
+    high = 4 * (D // parts) + 8
+    half = jax.ShapeDtypeStruct((parts // 2, high, D), jnp.bfloat16)
+    return pl.pallas_call(
+        group_grads,
+        grid=(1,),
+        in_specs=[scalars()]
+        + [fixed(*array.shape) for array in (tokens, *qkv_grads, context, attended, gains)],
+        out_specs=[fixed(*half.shape)] * 2,
+        out_shape=[half, half],
+        scratch_shapes=[pltpu.VMEM((parts, high, D), jnp.float32)],
+        compiler_params=params(60),
+        cost_estimate=spent(1),
+    )(my_place(), tokens, *qkv_grads, context, attended, gains)
 
 
 def on_device(
@@ -1161,8 +1222,7 @@
     gain_grads = jnp.concatenate(
         [jnp.sum(sums, 0, keepdims=True) for sums in (gain_sums[:8], gain_sums[8:], gain_blend)], 0
     )
-    gain_grads = jnp.pad(gain_grads, ((0, 5), (0, 0))).astype(jnp.bfloat16)
-    gain_rows = jnp.broadcast_to(gain_grads[None], (parts, 8, D)).reshape(8 * parts, D)
+    gain_grads = jnp.pad(gain_grads, ((0, 5), (0, 0)))
     if in_pairs([(w_down.shape[0], 1), (w_up.shape[0], 4)]):
         feed_grad = run_feed_grads(active, ffn_grad, normed, hidden_grad)
     else:
@@ -1170,31 +1230,37 @@
             inner_rows(active, ffn_grad).astype(jnp.bfloat16),
             inner_rows(normed, hidden_grad).astype(jnp.bfloat16),
         ]
-    grad_out = inner_rows(context, attended_grad).astype(jnp.bfloat16)
-    feed_grad, grad_out, state_grad, context_grad, gain_rows = flow.slot(
-        (feed_grad, grad_out, state_grad, context_grad, gain_rows)
+    feed_grad, state_grad, context_grad, gain_grads = flow.slot(
+        (feed_grad, state_grad, context_grad, gain_grads)
     )
     flow.begin(
         "feed",
-        feed_chain(feed_grad, [(w_down.shape[0], 1), (w_up.shape[0], 4)]),
+        feed_chain(feed_grad, [(w_down.shape[0], 1), (w_up.shape[0], 4)], True, True),
         [0, 0, 0, 0, 1],
     )
     tokens_grad = mixed_grad
-    group_grads = []
+    qkv_grads = []
     for number in range(groups):
         qkv_grad = run_attend_back(
             parts_qkv[number], logsums[number], context_grad, pairs * number
         )
         tokens_grad = tokens_grad + inner_cols(qkv_grad, weights[number])
-        grad_group = inner_rows(tokens, qkv_grad).astype(jnp.bfloat16)
-        if number == groups - 1:
-            tokens_grad = tokens_grad.astype(jnp.bfloat16)
-        if number != 1:
-            done = (context_grad, grad_group, tokens_grad, state_grad)
-            done, blend_sum = flow.slot((done, blend_sum)) if number else (flow.slot(done), blend_sum)
-            context_grad, grad_group, tokens_grad, state_grad = done
-        group_grads.append(grad_group)
-    flow.begin("qkv", scatter_chain(group_grads + [grad_out, gain_rows]), [0, 0, 1])
+        qkv_grads.append(qkv_grad)
+        if number == 0:
+            context_grad, tokens_grad, state_grad = flow.slot(
+                (context_grad, tokens_grad, state_grad)
+            )
+    tokens_grad = tokens_grad.astype(jnp.bfloat16)
+    qkv_shapes = [(w_qkv.shape[0], 1)] * 3 + [(w_out.shape[0], 1), (8, 1)]
+    if in_pairs(qkv_shapes):
+        qkv_halves = run_group_grads(tokens, qkv_grads, context, attended_grad, gain_grads)
+    else:
+        qkv_halves = [inner_rows(tokens, grad).astype(jnp.bfloat16) for grad in qkv_grads]
+        qkv_halves.append(inner_rows(context, attended_grad).astype(jnp.bfloat16))
+        gain_rows = jnp.broadcast_to(gain_grads[None], (parts, 8, D)).astype(jnp.bfloat16)
+        qkv_halves.append(gain_rows.reshape(8 * parts, D))
+    qkv_halves, tokens_grad, blend_sum = flow.slot((qkv_halves, tokens_grad, blend_sum))
+    flow.begin("qkv", feed_chain(qkv_halves, qkv_shapes, False, True), [0, 0, 1, 0])
     blocks = ids_row.shape[0] // STEP_ROWS
     spread, *held = run_chars_back(
         blocks, blocks // 2, ids_row, segment, letters, before, upstream=[state_grad, shares]
@@ -1211,7 +1277,10 @@
         ends=[table_all, gru_all],
     )
     grad_gru, grad_table, tokens_grad = flow.slot((grad_gru, grad_table, tokens_grad))
-    flow.begin("letters", scatter_chain([grad_gru, grad_table]))
+    flow.begin(
+        "letters",
+        feed_chain([grad_gru, grad_table], letter_shapes([table_all, gru_all], parts), False, False),
+    )
     flow.begin(
         "tokens",
         swap_chain(jnp.where(on_first, tokens_grad[half_len:], tokens_grad[:half_len])),

time: 501 us -> 494 us (0.986)
  matrix products: 24.1 us -> 14.1 us
    dot_general x4 -> x0, matrix products: 11.4 us -> none  [inner_rows(): lax.dot_general(former, latter, (((0,), (0,)), ((), ())), preferred_eleme...]
    pallas_call x2 -> x1, Pallas kernels: 3.23 us -> 11.6 us  [run_group_grads(): pl.pallas_call(group_grads, grid=(1,), in_specs=[scalars()] + [fixed(*arr...]
    reduce_scatter x1, waiting for transfers between devices: 6.85 us -> 0.01 us  [scatter_whole(): lax.psum_scatter(packed.reshape(-1, D), ('stream', 'dp'), scatter_dimensi...]
    ppermute x49 -> x48, starting transfers between devices: 54.3 us -> 49.9 us  [swap(): lax.ppermute(block, ('stream', 'dp'), [(place, place ^ mask) for place in...]
    ppermute x49 -> x48, waiting for transfers between devices: 64 us -> 67.8 us  [swap(): lax.ppermute(block, ('stream', 'dp'), [(place, place ^ mask) for place in...]
    unnamed x287 -> x251, local copies, waits for them, and re-layouts: 28.8 us -> 28.9 us
  transfers between devices with their start and end apart: 52 -> 51, of which waited for: 19 -> 19; matrix products, arithmetic and copies ran while one was open for 12% -> 11% of each run, Pallas kernels for 41% -> 44%
where the time goes in v5:
time: 494 us; the launch traced here: 490 us
  Pallas kernels  250 us (51%)
  waiting for transfers between devices  81.7 us (17%)
  starting transfers between devices  50 us (10%)
  local copies, waits for them, and re-layouts  39.5 us (8%)
  other arithmetic  38.4 us (8%)
  between operations  15.7 us (3%)
  matrix products  14.1 us (3%)
    ppermute x48, waiting for transfers between devices, swap(): lax.ppermute(block, ('stream', 'dp'), [(place, place ^ mask) for place in...  67.8 us
    ppermute x48, starting transfers between devices, swap(): lax.ppermute(block, ('stream', 'dp'), [(place, place ^ mask) for place in...  49.9 us
    pallas_call x2, Pallas kernels, run_chars_back(): pl.pallas_call(functools.partial(chars_back, (last,), upstream is not Non...  42.4 us
    pallas_call x3, Pallas kernels, run_attend_back(): pl.pallas_call(attend_back, grid=(pairs,), in_specs=[column(length, 128,...  39.3 us
    pallas_call x1, Pallas kernels, run_feed_back(): pl.pallas_call(feed_back, grid=(length // CHUNK,), in_specs=[rows_block(D...  32.2 us
    unnamed x251, local copies, waits for them, and re-layouts  28.9 us
    pallas_call x1, Pallas kernels, run_blend(): pl.pallas_call(blend_both, in_specs=[scalars()] + [pl.BlockSpec(memory_sp...  26.1 us
    pallas_call x3, Pallas kernels, run_attend(): pl.pallas_call(attend, grid=(pairs,), in_specs=[column(length, 128, every...  22.7 us
  transfers between devices with their start and end apart: 51, of which 19 were waited for; matrix products, arithmetic and copies ran while one was open for 11% of the time, Pallas kernels for 44%

profile of v5, /device:TPU:0, one launch (start us, length us, event | category | flops | bytes accessed | tf_op | source)
XLA Modules:
  0.0 490.0 jit_solution(212013130116698230)
XLA Ops:
  8.5 3.1 collective-permute-start.2
  19.3 4.3 collective-permute-done.4
  27.9 4.3 collective-permute-done.7
  35.4 6.4 %collective-permute-done.12 = bf16[1,1,2,1,48,768]{5,4,3,2,1,0:T(8,128)(2,1)S(1)} collective-permute-done((bf16[1,1,2,1,48,768]{5,4,3,2,1,0:T(8,128)(2,1)S(1)}, bf16[1,1,2,1,48,768]{5,4,3,2,1,0:T(8,128)(2,1)S(1)}, u32[]{:S(2)}, u32[]{:S(2)}) %collective-permute-start.12) | collective-permute-done | bytes 147488 | tf_op jit(solution)/shard_map/ppermute | solution.py:37
  56.1 3.5 collective-permute-done.9
  74.9 7.4 %shard_map.468 = (bf16[1024,256]{1,0:T(8,128)(2,1)S(1)}, f32[32,1024]{1,0:T(8,128)S(1)}) custom-call(bf16[1024,768]{1,0:T(8,128)(2,1)S(1)} %convolution_convert_fusion.2.queries.key_rows.value_rows, bf16[1024,768]{1,0:T(8,128)(2,1)S(1)} %convolution_convert_fusion.2.queries.key_rows.value_rows, ...), custom_call_target="tpu_custom_call" | custom-call | flops 10000000000 | bytes 1 | tf_op jit(solution)/shard_map/pallas_call | solution.py:795
  85.4 7.4 %shard_map.470 = (bf16[1024,256]{1,0:T(8,128)(2,1)S(1)}, f32[32,1024]{1,0:T(8,128)S(1)}) custom-call(bf16[1024,768]{1,0:T(8,128)(2,1)S(1)} %convolution_convert_fusion.1.queries.key_rows.value_rows, bf16[1024,768]{1,0:T(8,128)(2,1)S(1)} %convolution_convert_fusion.1.queries.key_rows.value_rows, ...), custom_call_target="tpu_custom_call" | custom-call | flops 10000000000 | bytes 1 | tf_op jit(solution)/shard_map/pallas_call | solution.py:795
  97.1 7.8 %shard_map.472 = (bf16[1024,256]{1,0:T(8,128)(2,1)S(1)}, f32[32,1024]{1,0:T(8,128)S(1)}) custom-call(bf16[1024,768]{1,0:T(8,128)(2,1)S(1)} %convolution_convert_fusion.queries.key_rows.value_rows, bf16[1024,768]{1,0:T(8,128)(2,1)S(1)} %convolution_convert_fusion.queries.key_rows.value_rows, ...), custom_call_target="tpu_custom_call" | custom-call | flops 10000000000 | bytes 1 | tf_op jit(solution)/shard_map/pallas_call | solution.py:795
  107.6 3.7 convert_reduce_fusion.refs_2_
  121.8 18.9 %shard_map.474 = (f32[256,16,128]{2,1,0:T(8,128)S(1)}, f32[4096,8,128]{2,1,0:T(8,128)}, bf16[1024,768]{1,0:T(8,128)(2,1)S(1)}) custom-call(s32[4096]{0:T(1024)S(1)} %bitcast.151, s32[4096]{0:T(1024)S(1)} %copy-done.27, s32[1024]{0:T(1024)S(1)} %copy-done.31, bf16[256,768]{1,0:T(8,128)(2,1)S(1)} %get-tuple-element.278.table.refs_13_, ...), custom_call_target="tpu_custom_call" | custom-call | flops 24000000000 | bytes 1 | tf_op jit(solution)/shard_map/pallas_call | solution.py:677
  140.7 6.9 %collective-permute-done.24 = bf16[1,2,2,2,96,768]{5,4,3,2,1,0:T(8,128)(2,1)} collective-permute-done((bf16[1,2,2,2,96,768]{5,4,3,2,1,0:T(8,128)(2,1)}, bf16[1,2,2,2,96,768]{5,4,3,2,1,0:T(8,128)(2,1)}, u32[]{:S(2)}, u32[]{:S(2)}) %collective-permute-start.24) | collective-permute-done | bytes 1179680 | tf_op jit(solution)/shard_map/ppermute | solution.py:37
  153.9 3.1 shard_map.475.up
  157.1 3.1 convert_add_fusion.mixed
  163.7 17.4 %shard_map.477 = (f32[1024,768]{1,0:T(8,128)}, bf16[1024,768]{1,0:T(8,128)(2,1)}) custom-call(f32[1024,768]{1,0:T(8,128)} %convert_add_fusion.mixed, f32[3,768]{1,0:T(4,128)} %convert_reduce_fusion.1.gains, bf16[768,3072]{1,0:T(8,128)(2,1)} %copy-done.34, bf16[3072,768]{1,0:T(8,128)(2,1)} %copy-done.35), custom_call_target="tpu_custom_call" | custom-call | flops 17999998976 | bytes 1 | tf_op jit(solution)/shard_map/pallas_call | solution.py:972
  181.1 13.9 %all-gather.4.cloned.1.call-done.blend = bf16[4608,768]{1,0:T(8,128)(2,1)} async-done(((bf16[144,768]{1,0:T(8,128)(2,1)}), bf16[4608,768]{1,0:T(8,128)(2,1)}) %all-gather.4.cloned.1.call-update) | async-done | bytes 7077904 | tf_op jit(solution)/shard_map/all_gather | solution.py:1169
  195.0 26.1 %shard_map.478 = (bf16[1024,768]{1,0:T(8,128)(2,1)}, bf16[1024,768]{1,0:T(8,128)(2,1)}, f32[1024,768]{1,0:T(8,128)}, bf16[1024,2304]{1,0:T(8,128)(2,1)}, f32[8,768]{1,0:T(8,128)}) custom-call(s32[1]{0:T(128)} %bitcast.order, bf16[1024,768]{1,0:T(8,128)(2,1)} %get-tuple-element.307.feature, bf16[1024,768]{1,0:T(8,128)(2,1)} %copy-done.45, ...), custom_call_target="tpu_custom_call" | custom-call | flops 25999998976 | bytes 1 | tf_op jit(solution)/shard_map/pallas_call | solution.py:1008
  221.1 10.8 %shard_map.479 = bf16[4608,768]{1,0:T(8,128)(2,1)} custom-call(bf16[1024,768]{1,0:T(8,128)(2,1)S(1)} %copy-done.47, bf16[1024,768]{1,0:T(8,128)(2,1)S(1)} %copy-done.46, bf16[1024,2304]{1,0:T(8,128)(2,1)} %get-tuple-element.312.grads), custom_call_target="tpu_custom_call" | custom-call | flops 12000000000 | bytes 1 | tf_op jit(solution)/shard_map/pallas_call | solution.py:1037
  236.0 32.2 %shard_map.480 = (bf16[1024,3072]{1,0:T(8,128)(2,1)}, bf16[1024,3072]{1,0:T(8,128)(2,1)}, bf16[1024,768]{1,0:T(8,128)(2,1)}, bf16[1024,768]{1,0:T(8,128)(2,1)}, ...) custom-call(f32[1024,768]{1,0:T(8,128)} %convert_add_fusion.mixed, ...), custom_call_target="tpu_custom_call" | custom-call | flops 32000000000 | bytes 1 | tf_op jit(solution)/shard_map/pallas_call | solution.py:992
  268.2 19.9 %shard_map.481 = (bf16[16,192,768]{2,1,0:T(8,128)(2,1)}, bf16[16,192,768]{2,1,0:T(8,128)(2,1)}) custom-call(s32[1]{0:T(128)} %bitcast.14.place.refs_12_, bf16[1024,3072]{1,0:T(8,128)(2,1)} %get-tuple-element.317.former, bf16[1024,3072]{1,0:T(8,128)(2,1)} %get-tuple-element.318.latter, bf16[1024,768]{1,0:T(8,128)(2,1)} %get-tuple-element.319.given, ...), custom_call_target="tpu_custom_call" | custom-call | flops 16000000000 | bytes 1 | tf_op jit(solution)/shard_map/pallas_call | solution.py:294
  288.9 13.1 %shard_map.482.first = bf16[1024,768]{1,0:T(8,128)(2,1)S(1)} custom-call(bf16[1024,768]{1,0:T(8,128)(2,1)S(1)} %copy-done.2, bf16[1024,768]{1,0:T(8,128)(2,1)S(1)} %copy-done.2, bf16[1024,768]{1,0:T(8,128)(2,1)S(1)} %copy-done.2, f32[32,1024]{1,0:T(8,128)S(1)} %get-tuple-element.334.logsum, bf16[1024,768]{1,0:T(8,128)(2,1)S(1)} %copy-done.7), custom_call_target="tpu_custom_call" | custom-call | flops 1000000000 | bytes 1 | tf_op jit(solution)/shard_map/pallas_call | solution.py:812
  314.8 13.2 %shard_map.485.third = bf16[1024,768]{1,0:T(8,128)(2,1)S(1)} custom-call(bf16[1024,768]{1,0:T(8,128)(2,1)S(1)} %copy-done.6, bf16[1024,768]{1,0:T(8,128)(2,1)S(1)} %copy-done.6, bf16[1024,768]{1,0:T(8,128)(2,1)S(1)} %copy-done.6, f32[32,1024]{1,0:T(8,128)S(1)} %copy-done.26, bf16[1024,768]{1,0:T(8,128)(2,1)S(1)} %copy-done.7), custom_call_target="tpu_custom_call" | custom-call | flops 1000000000 | bytes 1 | tf_op jit(solution)/shard_map/pallas_call | solution.py:812
  328.1 13.0 %shard_map.484.second = bf16[1024,768]{1,0:T(8,128)(2,1)S(1)} custom-call(bf16[1024,768]{1,0:T(8,128)(2,1)S(1)} %copy-done.4, bf16[1024,768]{1,0:T(8,128)(2,1)S(1)} %copy-done.4, bf16[1024,768]{1,0:T(8,128)(2,1)S(1)} %copy-done.4, f32[32,1024]{1,0:T(8,128)S(1)} %copy-done.24, bf16[1024,768]{1,0:T(8,128)(2,1)S(1)} %copy-done.7), custom_call_target="tpu_custom_call" | custom-call | flops 1000000000 | bytes 1 | tf_op jit(solution)/shard_map/pallas_call | solution.py:812
  342.3 11.6 %shard_map.486 = (bf16[16,104,768]{2,1,0:T(8,128)(2,1)}, bf16[16,104,768]{2,1,0:T(8,128)(2,1)}) custom-call(s32[1]{0:T(128)} %bitcast.14.place.refs_12_, bf16[1024,768]{1,0:T(8,128)(2,1)} %copy-done.58, bf16[1024,768]{1,0:T(8,128)(2,1)} %copy-done.10, bf16[1024,768]{1,0:T(8,128)(2,1)} %copy-done.11, bf16[1024,768]{1,0:T(8,128)(2,1)} %copy-done.8, ...), custom_call_target="tpu_custom_call" | custom-call | flops 1000000000 | bytes 1 | tf_op jit(solution)/shard_map/pallas_call | solution.py:1072
  366.2 20.2 %shard_map.483 = (f32[1024,8,128]{2,1,0:T(8,128)S(1)}, f32[8,128]{1,0:T(8,128)S(1)}, f32[256,8,128]{2,1,0:T(8,128)S(1)}, f32[256,8,128]{2,1,0:T(8,128)S(1)}, f32...) custom-call(s32[4096]{0:T(1024)S(1)} %bitcast.152, s32[4096]{0:T(1024)S(1)} %copy-done.28, s32[4096]{0:T(1024)S(1)} %copy-done.29, ...), custom_call_target="tpu_custom_call" | custom-call | flops 24000000000 | bytes 1 | tf_op jit(solution)/shard_map/pallas_call | solution.py:730
  386.4 4.5 collective-permute-done.31
  394.6 3.0 collective-permute-start.33
  401.8 22.3 %shard_map.488 = (bf16[16,56,768]{2,1,0:T(8,128)(2,1)S(1)}, bf16[16,56,768]{2,1,0:T(8,128)(2,1)S(1)}) custom-call(s32[4096]{0:T(1024)S(1)} %bitcast.153, s32[4096]{0:T(1024)S(1)} %copy-done.28, s32[4096]{0:T(1024)S(1)} %copy-done.29, s32[4096]{0:T(1024)S(1)} %rev.11.refs_3_, f32[256,16,128]{2,1,0:T(8,128)S(1)} %copy-done.52, ...), custom_call_target="tpu_custom_call" | custom-call | flops 24000000000 | bytes 1 | tf_op jit(solution)/shard_map/pallas_call | solution.py:730
  424.2 3.6 collective-permute-done.35
  435.8 5.4 %collective-permute-done.37 = bf16[1,192,768]{2,1,0:T(8,128)(2,1)S(1)} collective-permute-done((bf16[1,192,768]{2,1,0:T(8,128)(2,1)S(1)}, bf16[1,192,768]{2,1,0:T(8,128)(2,1)S(1)}, u32[]{:S(2)}, u32[]{:S(2)}) %collective-permute-start.37) | collective-permute-done | bytes 294944 | tf_op jit(solution)/shard_map/ppermute | solution.py:37
  444.9 4.3 collective-permute-done.38
  451.1 7.5 %collective-permute-done.41 = bf16[4,56,768]{2,1,0:T(8,128)(2,1)S(1)} collective-permute-done((bf16[4,56,768]{2,1,0:T(8,128)(2,1)S(1)}, bf16[4,56,768]{2,1,0:T(8,128)(2,1)S(1)}, u32[]{:S(2)}, u32[]{:S(2)}) %collective-permute-start.41) | collective-permute-done | bytes 344096 | tf_op jit(solution)/shard_map/ppermute | solution.py:37
  458.6 5.9 %collective-permute-done.42 = bf16[4,56,768]{2,1,0:T(8,128)(2,1)S(1)} collective-permute-done((bf16[4,56,768]{2,1,0:T(8,128)(2,1)S(1)}, bf16[4,56,768]{2,1,0:T(8,128)(2,1)S(1)}, u32[]{:S(2)}, u32[]{:S(2)}) %collective-permute-start.42) | collective-permute-done | bytes 344096 | tf_op jit(solution)/shard_map/ppermute | solution.py:37
  (465 shorter events, 146.3 us)
Async XLA Ops:
  7.2 111.9 %all-gather.6.cloned.1.call-start = ((), (), s32[]{:S(2)}) async-start(), calls=%async_computation.3 | async-start | bytes 3244032 | tf_op jit(solution)/shard_map/all_gather | solution.py:1168
  18.8 13.5 %collective-permute-start.8 = (bf16[1,1,1,1,96,768]{5,4,3,2,1,0:T(8,128)(2,1)S(1)}, bf16[1,1,1,1,96,768]{5,4,3,2,1,0:T(8,128)(2,1)S(1)}, u32[]{:S(2)}, u32[]{:S(2)}) collective-permute-start(bf16[1,1,1,1,96,768]{5,4,3,2,1,0:T(8,128)(2,1)S(1)} %bitcast.166), channel_id=1, source_target_pairs={{0,4},{1,5},{2,6},{3,7},{4,0},{5,1},{6,2},{7,3},{8,12},{9,13},{10,... | collective-permute-start | bytes 442376 | tf_op jit(solution)/shard_map/ppermute | solution.py:37
  43.3 151.7 %all-gather.4.cloned.1.call-start = ((), (), s32[]{:S(2)}) async-start(), calls=%async_computation.1 | async-start | bytes 7299072 | tf_op jit(solution)/shard_map/all_gather | solution.py:1169
  45.1 16.1 %collective-permute-start = (bf16[512,768]{1,0:T(8,128)(2,1)}, bf16[512,768]{1,0:T(8,128)(2,1)}, u32[]{:S(2)}, u32[]{:S(2)}) collective-permute-start(bf16[512,768]{1,0:T(8,128)(2,1)} %get-tuple-element.453), channel_id=1, source_target_pairs={{0,16},{1,17},{2,18},{3,19},{4,20},{5,21},{6,22},{7,23},{8,24},{9,... | collective-permute-start | bytes 2359304 | tf_op jit(solution)/shard_map/ppermute | solution.py:37
  46.3 13.3 %collective-permute-start.9 = (bf16[1,1,2,1,96,768]{5,4,3,2,1,0:T(8,128)(2,1)S(1)}, bf16[1,1,2,1,96,768]{5,4,3,2,1,0:T(8,128)(2,1)}, u32[]{:S(2)}, u32[]{:S(2)}) collective-permute-start(bf16[1,1,2,1,96,768]{5,4,3,2,1,0:T(8,128)(2,1)S(1)} %constant_dynamic-update-slice_fusion.8), channel_id=1, source_target_pairs={{0,8},{1,9},{2,10},{3,11},{4,12},{5,13},{6,14},{7,15},{8,0},{9,1},... | collective-permute-start | bytes 884744 | tf_op jit(solution)/shard_map/ppermute | solution.py:37
  56.0 303.6 %reduce-scatter.2.cloned.1.call-start = ((), (), s32[]{:S(2)}) async-start(), calls=%async_computation.2 | async-start | bytes 7299072 | tf_op jit(solution)/shard_map/reduce_scatter | solution.py:237
  63.0 19.6 %collective-permute-start.19 = (bf16[1,1,2,1,96,768]{5,4,3,2,1,0:T(8,128)(2,1)S(1)}, bf16[1,1,2,1,96,768]{5,4,3,2,1,0:T(8,128)(2,1)S(1)}, u32[]{:S(2)}, u32[]{:S(2)}) collective-permute-start(bf16[1,1,2,1,96,768]{5,4,3,2,1,0:T(8,128)(2,1)S(1)} %constant_dynamic-update-slice_fusion.22), channel_id=1, source_target_pairs={{0,8},{1,9},{2,10},{3,11},{4,12},{5,13},{6,14},{7,15},{8,0},{9,1},... | collective-permute-start | bytes 884744 | tf_op jit(solution)/shard_map/ppermute | solution.py:37
  65.7 17.0 %collective-permute-start.18 = (bf16[1,2,2,2,48,768]{5,4,3,2,1,0:T(8,128)(2,1)S(1)}, bf16[1,2,2,2,48,768]{5,4,3,2,1,0:T(8,128)(2,1)S(1)}, u32[]{:S(2)}, u32[]{:S(2)}) collective-permute-start(bf16[1,2,2,2,48,768]{5,4,3,2,1,0:T(8,128)(2,1)S(1)} %constant_dynamic-update-slice_fusion.20), channel_id=1, source_target_pairs={{0,16},{1,17},{2,18},{3,19},{4,20},{5,21},{6,22},{7,23},{8,24},{9,... | collective-permute-start | bytes 1769480 | tf_op jit(solution)/shard_map/ppermute | solution.py:37
  68.4 14.3 %collective-permute-start.17 = (bf16[1,2,2,1,96,768]{5,4,3,2,1,0:T(8,128)(2,1)S(1)}, bf16[1,2,2,1,96,768]{5,4,3,2,1,0:T(8,128)(2,1)S(1)}, u32[]{:S(2)}, u32[]{:S(2)}) collective-permute-start(bf16[1,2,2,1,96,768]{5,4,3,2,1,0:T(8,128)(2,1)S(1)} %constant_dynamic-update-slice_fusion.18), channel_id=1, source_target_pairs={{0,2},{1,3},{2,0},{3,1},{4,6},{5,7},{6,4},{7,5},{8,10},{9,11},{10,... | collective-permute-start | bytes 1769480 | tf_op jit(solution)/shard_map/ppermute | solution.py:37
  82.7 28.6 %collective-permute-start.22 = (bf16[1,2,2,1,96,768]{5,4,3,2,1,0:T(8,128)(2,1)S(1)}, bf16[1,2,2,1,96,768]{5,4,3,2,1,0:T(8,128)(2,1)S(1)}, u32[]{:S(2)}, u32[]{:S(2)}) collective-permute-start(bf16[1,2,2,1,96,768]{5,4,3,2,1,0:T(8,128)(2,1)S(1)} %constant_dynamic-update-slice_fusion.26), channel_id=1, source_target_pairs={{0,2},{1,3},{2,0},{3,1},{4,6},{5,7},{6,4},{7,5},{8,10},{9,11},{10,... | collective-permute-start | bytes 1769480 | tf_op jit(solution)/shard_map/ppermute | solution.py:37
  83.3 28.0 %collective-permute-start.21 = (bf16[1,2,2,2,96,768]{5,4,3,2,1,0:T(8,128)(2,1)S(1)}, bf16[1,2,2,2,96,768]{5,4,3,2,1,0:T(8,128)(2,1)}, u32[]{:S(2)}, u32[]{:S(2)}) collective-permute-start(bf16[1,2,2,2,96,768]{5,4,3,2,1,0:T(8,128)(2,1)S(1)} %constant_dynamic-update-slice_fusion.24), channel_id=1, source_target_pairs={{0,16},{1,17},{2,18},{3,19},{4,20},{5,21},{6,22},{7,23},{8,24},{9,... | collective-permute-start | bytes 3538952 | tf_op jit(solution)/shard_map/ppermute | solution.py:37
  114.1 33.5 %collective-permute-start.24 = (bf16[1,2,2,2,96,768]{5,4,3,2,1,0:T(8,128)(2,1)}, bf16[1,2,2,2,96,768]{5,4,3,2,1,0:T(8,128)(2,1)}, u32[]{:S(2)}, u32[]{:S(2)}) collective-permute-start(bf16[1,2,2,2,96,768]{5,4,3,2,1,0:T(8,128)(2,1)} %constant_dynamic-update-slice_fusion.28), channel_id=1, source_target_pairs={{0,16},{1,17},{2,18},{3,19},{4,20},{5,21},{6,22},{7,23},{8,24},{9,... | collective-permute-start | bytes 3538952 | tf_op jit(solution)/shard_map/ppermute | solution.py:37
  117.6 30.0 %collective-permute-start.23 = (bf16[16,96,768]{2,1,0:T(8,128)(2,1)S(1)}, bf16[16,96,768]{2,1,0:T(8,128)(2,1)}, u32[]{:S(2)}, u32[]{:S(2)}) collective-permute-start(bf16[16,96,768]{2,1,0:T(8,128)(2,1)S(1)} %bitcast.139), channel_id=1, source_target_pairs={{0,1},{1,0},{2,3},{3,2},{4,5},{5,4},{6,7},{7,6},{8,9},{9,8},{10,11... | collective-permute-start | bytes 7077896 | tf_op jit(solution)/shard_map/ppermute | solution.py:37
  149.6 10.7 %collective-permute-start.25 = (bf16[16,96,768]{2,1,0:T(8,128)(2,1)S(1)}, bf16[16,96,768]{2,1,0:T(8,128)(2,1)S(1)}, u32[]{:S(2)}, u32[]{:S(2)}) collective-permute-start(bf16[16,96,768]{2,1,0:T(8,128)(2,1)S(1)} %bitcast.141), channel_id=1, source_target_pairs={{0,1},{1,0},{2,3},{3,2},{4,5},{5,4},{6,7},{7,6},{8,9},{9,8},{10,11... | collective-permute-start | bytes 7077896 | tf_op jit(solution)/shard_map/ppermute | solution.py:37
  150.7 30.3 %collective-permute-start.26 = (bf16[512,768]{1,0:T(8,128)(2,1)S(1)}, bf16[512,768]{1,0:T(8,128)(2,1)}, u32[]{:S(2)}, u32[]{:S(2)}) collective-permute-start(bf16[512,768]{1,0:T(8,128)(2,1)S(1)} %get-tuple-element.451), channel_id=1, source_target_pairs={{0,16},{1,17},{2,18},{3,19},{4,20},{5,21},{6,22},{7,23},{8,24},{9,... | collective-permute-start | bytes 2359304 | tf_op jit(solution)/shard_map/ppermute | solution.py:37
  234.3 54.6 %collective-permute-start.27 = (bf16[512,768]{1,0:T(8,128)(2,1)}, bf16[512,768]{1,0:T(8,128)(2,1)}, u32[]{:S(2)}, u32[]{:S(2)}) collective-permute-start(bf16[512,768]{1,0:T(8,128)(2,1)} %broadcast_select_fusion.2), channel_id=1, source_target_pairs={{0,16},{1,17},{2,18},{3,19},{4,20},{5,21},{6,22},{7,23},{8,24},{9,... | collective-permute-start | bytes 2359304 | tf_op jit(solution)/shard_map/ppermute | solution.py:37
  288.9 18.3 %collective-permute-start.28 = (bf16[16,192,768]{2,1,0:T(8,128)(2,1)}, bf16[16,192,768]{2,1,0:T(8,128)(2,1)S(1)}, u32[]{:S(2)}, u32[]{:S(2)}) collective-permute-start(bf16[16,192,768]{2,1,0:T(8,128)(2,1)} %get-tuple-element.337), channel_id=1, source_target_pairs={{0,1},{1,0},{2,3},{3,2},{4,5},{5,4},{6,7},{7,6},{8,9},{9,8},{10,11... | collective-permute-start | bytes 14155784 | tf_op jit(solution)/shard_map/ppermute | solution.py:37
  312.8 48.6 %collective-permute-start.29 = (bf16[4,192,768]{2,1,0:T(8,128)(2,1)}, bf16[4,192,768]{2,1,0:T(8,128)(2,1)}, u32[]{:S(2)}, u32[]{:S(2)}) collective-permute-start(bf16[4,192,768]{2,1,0:T(8,128)(2,1)} %get-tuple-element.360), channel_id=1, source_target_pairs={{0,16},{1,17},{2,18},{3,19},{4,20},{5,21},{6,22},{7,23},{8,24},{9,... | collective-permute-start | bytes 3538952 | tf_op jit(solution)/shard_map/ppermute | solution.py:37
  312.9 48.5 %collective-permute-start.30 = (bf16[4,192,768]{2,1,0:T(8,128)(2,1)}, bf16[4,192,768]{2,1,0:T(8,128)(2,1)}, u32[]{:S(2)}, u32[]{:S(2)}) collective-permute-start(bf16[4,192,768]{2,1,0:T(8,128)(2,1)} %get-tuple-element.361), channel_id=1, source_target_pairs={{0,2},{1,3},{2,0},{3,1},{4,6},{5,7},{6,4},{7,5},{8,10},{9,11},{10,... | collective-permute-start | bytes 3538952 | tf_op jit(solution)/shard_map/ppermute | solution.py:37
  361.4 29.6 %collective-permute-start.32 = (bf16[16,104,768]{2,1,0:T(8,128)(2,1)}, bf16[16,104,768]{2,1,0:T(8,128)(2,1)S(1)}, u32[]{:S(2)}, u32[]{:S(2)}) collective-permute-start(bf16[16,104,768]{2,1,0:T(8,128)(2,1)} %get-tuple-element.367), channel_id=1, source_target_pairs={{0,1},{1,0},{2,3},{3,2},{4,5},{5,4},{6,7},{7,6},{8,9},{9,8},{10,11... | collective-permute-start | bytes 7667720 | tf_op jit(solution)/shard_map/ppermute | solution.py:37
  361.5 29.5 %collective-permute-start.31 = (bf16[4,192,768]{2,1,0:T(8,128)(2,1)}, bf16[4,192,768]{2,1,0:T(8,128)(2,1)S(1)}, u32[]{:S(2)}, u32[]{:S(2)}) collective-permute-start(bf16[4,192,768]{2,1,0:T(8,128)(2,1)} %copy-done.33), channel_id=1, source_target_pairs={{0,18},{1,19},{2,16},{3,17},{4,22},{5,23},{6,20},{7,21},{8,26},{9,... | collective-permute-start | bytes 3538952 | tf_op jit(solution)/shard_map/ppermute | solution.py:37
  394.6 29.6 %collective-permute-start.33 = (bf16[2,192,768]{2,1,0:T(8,128)(2,1)S(1)}, bf16[2,192,768]{2,1,0:T(8,128)(2,1)S(1)}, u32[]{:S(2)}, u32[]{:S(2)}) collective-permute-start(bf16[2,192,768]{2,1,0:T(8,128)(2,1)S(1)} %slice.275), channel_id=1, source_target_pairs={{0,8},{1,9},{2,10},{3,11},{4,12},{5,13},{6,14},{7,15},{8,0},{9,1},... | collective-permute-start | bytes 1769480 | tf_op jit(solution)/shard_map/ppermute | solution.py:37
  398.3 25.9 %collective-permute-start.34 = (bf16[4,104,768]{2,1,0:T(8,128)(2,1)S(1)}, bf16[4,104,768]{2,1,0:T(8,128)(2,1)S(1)}, u32[]{:S(2)}, u32[]{:S(2)}) collective-permute-start(bf16[4,104,768]{2,1,0:T(8,128)(2,1)S(1)} %get-tuple-element.384), channel_id=1, source_target_pairs={{0,18},{1,19},{2,16},{3,17},{4,22},{5,23},{6,20},{7,21},{8,26},{9,... | collective-permute-start | bytes 1916936 | tf_op jit(solution)/shard_map/ppermute | solution.py:37
  399.7 28.1 %collective-permute-start.35 = (bf16[4,104,768]{2,1,0:T(8,128)(2,1)S(1)}, bf16[4,104,768]{2,1,0:T(8,128)(2,1)S(1)}, u32[]{:S(2)}, u32[]{:S(2)}) collective-permute-start(bf16[4,104,768]{2,1,0:T(8,128)(2,1)S(1)} %get-tuple-element.385), channel_id=1, source_target_pairs={{0,16},{1,17},{2,18},{3,19},{4,20},{5,21},{6,22},{7,23},{8,24},{9,... | collective-permute-start | bytes 1916936 | tf_op jit(solution)/shard_map/ppermute | solution.py:37
  400.2 28.4 %collective-permute-start.36 = (bf16[4,104,768]{2,1,0:T(8,128)(2,1)S(1)}, bf16[4,104,768]{2,1,0:T(8,128)(2,1)S(1)}, u32[]{:S(2)}, u32[]{:S(2)}) collective-permute-start(bf16[4,104,768]{2,1,0:T(8,128)(2,1)S(1)} %get-tuple-element.386), channel_id=1, source_target_pairs={{0,2},{1,3},{2,0},{3,1},{4,6},{5,7},{6,4},{7,5},{8,10},{9,11},{10,... | collective-permute-start | bytes 1916936 | tf_op jit(solution)/shard_map/ppermute | solution.py:37
  428.8 12.4 %collective-permute-start.37 = (bf16[1,192,768]{2,1,0:T(8,128)(2,1)S(1)}, bf16[1,192,768]{2,1,0:T(8,128)(2,1)S(1)}, u32[]{:S(2)}, u32[]{:S(2)}) collective-permute-start(bf16[1,192,768]{2,1,0:T(8,128)(2,1)S(1)} %slice.277), channel_id=1, source_target_pairs={{0,4},{1,5},{2,6},{3,7},{4,0},{5,1},{6,2},{7,3},{8,12},{9,13},{10,... | collective-permute-start | bytes 884744 | tf_op jit(solution)/shard_map/ppermute | solution.py:37
  430.6 20.5 %collective-permute-start.39 = (bf16[512,768]{1,0:T(8,128)(2,1)S(1)}, bf16[512,768]{1,0:T(8,128)(2,1)S(1)}, u32[]{:S(2)}, u32[]{:S(2)}) collective-permute-start(bf16[512,768]{1,0:T(8,128)(2,1)S(1)} %broadcast_select_fusion), channel_id=1, source_target_pairs={{0,16},{1,17},{2,18},{3,19},{4,20},{5,21},{6,22},{7,23},{8,24},{9,... | collective-permute-start | bytes 2359304 | tf_op jit(solution)/shard_map/ppermute | solution.py:37
  432.6 16.6 %collective-permute-start.38 = (bf16[2,104,768]{2,1,0:T(8,128)(2,1)S(1)}, bf16[2,104,768]{2,1,0:T(8,128)(2,1)S(1)}, u32[]{:S(2)}, u32[]{:S(2)}) collective-permute-start(bf16[2,104,768]{2,1,0:T(8,128)(2,1)S(1)} %slice.276), channel_id=1, source_target_pairs={{0,8},{1,9},{2,10},{3,11},{4,12},{5,13},{6,14},{7,15},{8,0},{9,1},... | collective-permute-start | bytes 958472 | tf_op jit(solution)/shard_map/ppermute | solution.py:37
  433.7 24.9 %collective-permute-start.41 = (bf16[4,56,768]{2,1,0:T(8,128)(2,1)S(1)}, bf16[4,56,768]{2,1,0:T(8,128)(2,1)S(1)}, u32[]{:S(2)}, u32[]{:S(2)}) collective-permute-start(bf16[4,56,768]{2,1,0:T(8,128)(2,1)S(1)} %get-tuple-element.399), channel_id=1, source_target_pairs={{0,18},{1,19},{2,16},{3,17},{4,22},{5,23},{6,20},{7,21},{8,26},{9,... | collective-permute-start | bytes 1032200 | tf_op jit(solution)/shard_map/ppermute | solution.py:37
  434.4 30.1 %collective-permute-start.42 = (bf16[4,56,768]{2,1,0:T(8,128)(2,1)S(1)}, bf16[4,56,768]{2,1,0:T(8,128)(2,1)S(1)}, u32[]{:S(2)}, u32[]{:S(2)}) collective-permute-start(bf16[4,56,768]{2,1,0:T(8,128)(2,1)S(1)} %get-tuple-element.400), channel_id=1, source_target_pairs={{0,16},{1,17},{2,18},{3,19},{4,20},{5,21},{6,22},{7,23},{8,24},{9,... | collective-permute-start | bytes 1032200 | tf_op jit(solution)/shard_map/ppermute | solution.py:37
  441.3 23.2 %collective-permute-start.43 = (bf16[4,56,768]{2,1,0:T(8,128)(2,1)S(1)}, bf16[4,56,768]{2,1,0:T(8,128)(2,1)S(1)}, u32[]{:S(2)}, u32[]{:S(2)}) collective-permute-start(bf16[4,56,768]{2,1,0:T(8,128)(2,1)S(1)} %get-tuple-element.401), channel_id=1, source_target_pairs={{0,2},{1,3},{2,0},{3,1},{4,6},{5,7},{6,4},{7,5},{8,10},{9,11},{10,... | collective-permute-start | bytes 1032200 | tf_op jit(solution)/shard_map/ppermute | solution.py:37
  466.8 11.6 %collective-permute-start.44 = (bf16[1,104,768]{2,1,0:T(8,128)(2,1)S(1)}, bf16[1,104,768]{2,1,0:T(8,128)(2,1)S(1)}, u32[]{:S(2)}, u32[]{:S(2)}) collective-permute-start(bf16[1,104,768]{2,1,0:T(8,128)(2,1)S(1)} %slice.278), channel_id=1, source_target_pairs={{0,4},{1,5},{2,6},{3,7},{4,0},{5,1},{6,2},{7,3},{8,12},{9,13},{10,... | collective-permute-start | bytes 479240 | tf_op jit(solution)/shard_map/ppermute | solution.py:37
  (138 other events, 942.4 us)
Sparse Core Ops, SparseCore 0:
  43.4 66.8 all-gather.5
  113.7 81.2 all-gather.3
  232.0 126.6 reduce-scatter.1

commit v6 on v5

--- a/solution.py
+++ b/solution.py
@@ -735,7 +735,7 @@
         out_shape=outs,
         scratch_shapes=scratch,
         compiler_params=pltpu.CompilerParams(vmem_limit_bytes=40 << 20),
-        cost_estimate=spent(6 * count),
+        cost_estimate=spent(1),
     )(*inputs)
 
 
@@ -1049,7 +1049,14 @@
     )(feature, pooled, grads)
 
 
-def group_grads(place, tokens, first, second, third, context, attended, gains, keep, send, held):
+def group_grads(
+    place, tokens, first, second, third, context, attended, gains, mixed, early, middle, late,
+    keep, send, tokens_grad, held
+):
+    total = mixed[...]
+    for grads, weight in ((first, early), (second, middle), (third, late)):
+        total = total + contract(grads[...], weight[...], 1, 1)
+    tokens_grad[...] = total.astype(tokens_grad.dtype)
     pairs, high, _ = keep.shape
     rows = D // (2 * pairs)
     pieces = [(tokens, first), (tokens, second), (tokens, third), (context, attended)]
@@ -1065,21 +1072,21 @@
         send[there] = jnp.where(core == 0, latter, former).astype(send.dtype)
 
 
-def run_group_grads(tokens, qkv_grads, context, attended, gains):
+def run_group_grads(tokens, qkv_grads, context, attended, gains, mixed, weights):
     parts = lax.axis_size("dp") * lax.axis_size("stream")
     high = 4 * (D // parts) + 8
     half = jax.ShapeDtypeStruct((parts // 2, high, D), jnp.bfloat16)
+    inputs = (tokens, *qkv_grads, context, attended, gains, mixed, *weights)
     return pl.pallas_call(
         group_grads,
         grid=(1,),
-        in_specs=[scalars()]
-        + [fixed(*array.shape) for array in (tokens, *qkv_grads, context, attended, gains)],
-        out_specs=[fixed(*half.shape)] * 2,
-        out_shape=[half, half],
+        in_specs=[scalars()] + [fixed(*array.shape) for array in inputs],
+        out_specs=[fixed(*half.shape)] * 2 + [fixed(*tokens.shape)],
+        out_shape=[half, half, jax.ShapeDtypeStruct(tokens.shape, jnp.bfloat16)],
         scratch_shapes=[pltpu.VMEM((parts, high, D), jnp.float32)],
         compiler_params=params(60),
         cost_estimate=spent(1),
-    )(my_place(), tokens, *qkv_grads, context, attended, gains)
+    )(my_place(), *inputs)
 
 
 def on_device(
@@ -1238,34 +1245,35 @@
         feed_chain(feed_grad, [(w_down.shape[0], 1), (w_up.shape[0], 4)], True, True),
         [0, 0, 0, 0, 1],
     )
-    tokens_grad = mixed_grad
     qkv_grads = []
     for number in range(groups):
         qkv_grad = run_attend_back(
             parts_qkv[number], logsums[number], context_grad, pairs * number
         )
-        tokens_grad = tokens_grad + inner_cols(qkv_grad, weights[number])
+        if number == 0:
+            qkv_grad, context_grad, state_grad = flow.slot((qkv_grad, context_grad, state_grad))
         qkv_grads.append(qkv_grad)
-        if number == 0:
-            context_grad, tokens_grad, state_grad = flow.slot(
-                (context_grad, tokens_grad, state_grad)
-            )
-    tokens_grad = tokens_grad.astype(jnp.bfloat16)
     qkv_shapes = [(w_qkv.shape[0], 1)] * 3 + [(w_out.shape[0], 1), (8, 1)]
     if in_pairs(qkv_shapes):
-        qkv_halves = run_group_grads(tokens, qkv_grads, context, attended_grad, gain_grads)
+        *qkv_halves, tokens_grad = run_group_grads(
+            tokens, qkv_grads, context, attended_grad, gain_grads, mixed_grad, weights
+        )
     else:
+        tokens_grad = mixed_grad + sum(
+            inner_cols(grad, weight) for grad, weight in zip(qkv_grads, weights)
+        )
+        tokens_grad = tokens_grad.astype(jnp.bfloat16)
         qkv_halves = [inner_rows(tokens, grad).astype(jnp.bfloat16) for grad in qkv_grads]
         qkv_halves.append(inner_rows(context, attended_grad).astype(jnp.bfloat16))
         gain_rows = jnp.broadcast_to(gain_grads[None], (parts, 8, D)).astype(jnp.bfloat16)
         qkv_halves.append(gain_rows.reshape(8 * parts, D))
-    qkv_halves, tokens_grad, blend_sum = flow.slot((qkv_halves, tokens_grad, blend_sum))
+    qkv_halves, tokens_grad = flow.slot((qkv_halves, tokens_grad))
     flow.begin("qkv", feed_chain(qkv_halves, qkv_shapes, False, True), [0, 0, 1, 0])
     blocks = ids_row.shape[0] // STEP_ROWS
     spread, *held = run_chars_back(
         blocks, blocks // 2, ids_row, segment, letters, before, upstream=[state_grad, shares]
     )
-    spread, held = flow.slot((spread, held))
+    spread, held, blend_sum = flow.slot((spread, held, blend_sum))
     grad_gru, grad_table = run_chars_back(
         blocks // 2,
         blocks // 2,

time: 494 us -> 484 us (0.980)
  waiting for transfers between devices: 81.7 us -> 69.2 us
  Pallas kernels: 250 us -> 259 us
  matrix products: 14.1 us -> 7.26 us
    ppermute x48, waiting for transfers between devices: 67.8 us -> 54 us  [swap(): lax.ppermute(block, ('stream', 'dp'), [(place, place ^ mask) for place in...]
    dot_general x3 -> x0, matrix products: 6.83 us -> none  [inner_cols(): lax.dot_general(former, latter, (((1,), (1,)), ((), ())), preferred_eleme...]
    pallas_call x1, Pallas kernels: 11.6 us -> 17.6 us  [run_group_grads(): pl.pallas_call(group_grads, grid=(1,), in_specs=[scalars()] + [fixed(*arr...]
    unnamed x251 -> x239, local copies, waits for them, and re-layouts: 28.9 us -> 33.2 us
  transfers between devices with their start and end apart: 51 -> 51, of which waited for: 19 -> 19; matrix products, arithmetic and copies ran while one was open for 11% -> 10% of each run, Pallas kernels for 44% -> 46%
where the time goes in v6:
time: 484 us; the launch traced here: 480 us
  Pallas kernels  259 us (54%)
  waiting for transfers between devices  69.2 us (14%)
  starting transfers between devices  50.9 us (11%)
  local copies, waits for them, and re-layouts  43.2 us (9%)
  other arithmetic  34.3 us (7%)
  between operations  15.8 us (3%)
  matrix products  7.26 us (2%)
    ppermute x48, waiting for transfers between devices, swap(): lax.ppermute(block, ('stream', 'dp'), [(place, place ^ mask) for place in...  54 us
    ppermute x48, starting transfers between devices, swap(): lax.ppermute(block, ('stream', 'dp'), [(place, place ^ mask) for place in...  50.8 us
    pallas_call x2, Pallas kernels, run_chars_back(): pl.pallas_call(functools.partial(chars_back, (last,), upstream is not Non...  42.6 us
    pallas_call x3, Pallas kernels, run_attend_back(): pl.pallas_call(attend_back, grid=(pairs,), in_specs=[column(length, 128,...  39.1 us
    unnamed x239, local copies, waits for them, and re-layouts  33.2 us
    pallas_call x1, Pallas kernels, run_feed_back(): pl.pallas_call(feed_back, grid=(length // CHUNK,), in_specs=[rows_block(D...  32.2 us
    pallas_call x1, Pallas kernels, run_blend(): pl.pallas_call(blend_both, in_specs=[scalars()] + [pl.BlockSpec(memory_sp...  26.1 us
    pallas_call x3, Pallas kernels, run_attend(): pl.pallas_call(attend, grid=(pairs,), in_specs=[column(length, 128, every...  22.7 us
  transfers between devices with their start and end apart: 51, of which 19 were waited for; matrix products, arithmetic and copies ran while one was open for 10% of the time, Pallas kernels for 46%

profile of v6, /device:TPU:0, one launch (start us, length us, event | category | flops | bytes accessed | tf_op | source)
XLA Modules:
  0.0 479.7 jit_solution(8203665048888330642)
XLA Ops:
  8.5 3.1 collective-permute-start.2
  19.3 4.3 collective-permute-done.4
  27.9 4.3 collective-permute-done.7
  35.4 6.6 %collective-permute-done.12 = bf16[1,1,2,1,48,768]{5,4,3,2,1,0:T(8,128)(2,1)} collective-permute-done((bf16[1,1,2,1,48,768]{5,4,3,2,1,0:T(8,128)(2,1)S(1)}, bf16[1,1,2,1,48,768]{5,4,3,2,1,0:T(8,128)(2,1)}, u32[]{:S(2)}, u32[]{:S(2)}) %collective-permute-start.12) | collective-permute-done | bytes 147488 | tf_op jit(solution)/shard_map/ppermute | solution.py:37
  46.4 2.7 collective-permute-start.9
  55.6 4.4 collective-permute-done.9
  74.8 7.4 %shard_map.468 = (bf16[1024,256]{1,0:T(8,128)(2,1)S(1)}, f32[32,1024]{1,0:T(8,128)S(1)}) custom-call(bf16[1024,768]{1,0:T(8,128)(2,1)S(1)} %convolution_convert_fusion.2.queries.key_rows.value_rows, bf16[1024,768]{1,0:T(8,128)(2,1)S(1)} %convolution_convert_fusion.2.queries.key_rows.value_rows, ...), custom_call_target="tpu_custom_call" | custom-call | flops 10000000000 | bytes 1 | tf_op jit(solution)/shard_map/pallas_call | solution.py:795
  85.8 7.4 %shard_map.470 = (bf16[1024,256]{1,0:T(8,128)(2,1)S(1)}, f32[32,1024]{1,0:T(8,128)S(1)}) custom-call(bf16[1024,768]{1,0:T(8,128)(2,1)S(1)} %convolution_convert_fusion.1.queries.key_rows.value_rows, bf16[1024,768]{1,0:T(8,128)(2,1)S(1)} %convolution_convert_fusion.1.queries.key_rows.value_rows, ...), custom_call_target="tpu_custom_call" | custom-call | flops 10000000000 | bytes 1 | tf_op jit(solution)/shard_map/pallas_call | solution.py:795
  97.5 7.8 %shard_map.472 = (bf16[1024,256]{1,0:T(8,128)(2,1)S(1)}, f32[32,1024]{1,0:T(8,128)S(1)}) custom-call(bf16[1024,768]{1,0:T(8,128)(2,1)S(1)} %convolution_convert_fusion.queries.key_rows.value_rows, bf16[1024,768]{1,0:T(8,128)(2,1)S(1)} %convolution_convert_fusion.queries.key_rows.value_rows, ...), custom_call_target="tpu_custom_call" | custom-call | flops 10000000000 | bytes 1 | tf_op jit(solution)/shard_map/pallas_call | solution.py:795
  107.4 3.8 convert_reduce_fusion.refs_2_
  121.3 18.9 %shard_map.474 = (f32[256,16,128]{2,1,0:T(8,128)S(1)}, f32[4096,8,128]{2,1,0:T(8,128)}, bf16[1024,768]{1,0:T(8,128)(2,1)S(1)}) custom-call(s32[4096]{0:T(1024)S(1)} %bitcast.138, s32[4096]{0:T(1024)S(1)} %rev.10.rows_b.refs_1_, s32[1024]{0:T(1024)S(1)} %add_bitcast_fusion.1.ends, bf16[256,768]{1,0:T(8,128)(2,1)S(1)} %get-tuple-element.279.table.refs_13_, ...), custom_call_target="tpu_custom_call" | custom-call | flops 24000000000 | bytes 1 | tf_op jit(solution)/shard_map/pallas_call | solution.py:677
  149.3 3.2 shard_map.475.up
  152.5 3.1 convert_add_fusion.mixed
  159.1 17.7 %shard_map.477 = (f32[1024,768]{1,0:T(8,128)}, bf16[1024,768]{1,0:T(8,128)(2,1)}) custom-call(f32[1024,768]{1,0:T(8,128)} %convert_add_fusion.mixed, f32[3,768]{1,0:T(4,128)} %convert_reduce_fusion.1.gains, bf16[768,3072]{1,0:T(8,128)(2,1)} %copy-done.48, bf16[3072,768]{1,0:T(8,128)(2,1)} %copy-done.49), custom_call_target="tpu_custom_call" | custom-call | flops 17999998976 | bytes 1 | tf_op jit(solution)/shard_map/pallas_call | solution.py:972
  176.7 15.1 %all-gather.4.cloned.1.call-done.blend = bf16[4608,768]{1,0:T(8,128)(2,1)} async-done(((bf16[144,768]{1,0:T(8,128)(2,1)}), bf16[4608,768]{1,0:T(8,128)(2,1)}) %all-gather.4.cloned.1.call-update) | async-done | bytes 7077904 | tf_op jit(solution)/shard_map/all_gather | solution.py:1176
  191.9 26.1 %shard_map.478 = (bf16[1024,768]{1,0:T(8,128)(2,1)}, bf16[1024,768]{1,0:T(8,128)(2,1)}, f32[1024,768]{1,0:T(8,128)}, bf16[1024,2304]{1,0:T(8,128)(2,1)}, f32[8,768]{1,0:T(8,128)}) custom-call(s32[1]{0:T(128)} %bitcast.order, bf16[1024,768]{1,0:T(8,128)(2,1)} %get-tuple-element.308.feature, bf16[1024,768]{1,0:T(8,128)(2,1)} %copy-done.52, ...), custom_call_target="tpu_custom_call" | custom-call | flops 25999998976 | bytes 1 | tf_op jit(solution)/shard_map/pallas_call | solution.py:1008
  217.9 10.8 %shard_map.479 = bf16[4608,768]{1,0:T(8,128)(2,1)} custom-call(bf16[1024,768]{1,0:T(8,128)(2,1)S(1)} %copy-done.54, bf16[1024,768]{1,0:T(8,128)(2,1)S(1)} %copy-done.53, bf16[1024,2304]{1,0:T(8,128)(2,1)} %get-tuple-element.313.grads), custom_call_target="tpu_custom_call" | custom-call | flops 12000000000 | bytes 1 | tf_op jit(solution)/shard_map/pallas_call | solution.py:1037
  231.3 32.2 %shard_map.480 = (bf16[1024,3072]{1,0:T(8,128)(2,1)}, bf16[1024,3072]{1,0:T(8,128)(2,1)}, bf16[1024,768]{1,0:T(8,128)(2,1)}, bf16[1024,768]{1,0:T(8,128)(2,1)}, ...) custom-call(f32[1024,768]{1,0:T(8,128)} %convert_add_fusion.mixed, ...), custom_call_target="tpu_custom_call" | custom-call | flops 32000000000 | bytes 1 | tf_op jit(solution)/shard_map/pallas_call | solution.py:992
  263.6 19.9 %shard_map.481 = (bf16[16,192,768]{2,1,0:T(8,128)(2,1)}, bf16[16,192,768]{2,1,0:T(8,128)(2,1)}) custom-call(s32[1]{0:T(128)} %bitcast.14.place.refs_12_, bf16[1024,3072]{1,0:T(8,128)(2,1)} %get-tuple-element.318.former, bf16[1024,3072]{1,0:T(8,128)(2,1)} %get-tuple-element.319.latter, bf16[1024,768]{1,0:T(8,128)(2,1)} %get-tuple-element.320.given, ...), custom_call_target="tpu_custom_call" | custom-call | flops 16000000000 | bytes 1 | tf_op jit(solution)/shard_map/pallas_call | solution.py:294
  284.3 12.9 %shard_map.482.first = bf16[1024,768]{1,0:T(8,128)(2,1)S(1)} custom-call(bf16[1024,768]{1,0:T(8,128)(2,1)S(1)} %copy-done.3, bf16[1024,768]{1,0:T(8,128)(2,1)S(1)} %copy-done.3, bf16[1024,768]{1,0:T(8,128)(2,1)S(1)} %copy-done.3, f32[32,1024]{1,0:T(8,128)S(1)} %copy-done.42, bf16[1024,768]{1,0:T(8,128)(2,1)S(1)} %copy-done.8), custom_call_target="tpu_custom_call" | custom-call | flops 1000000000 | bytes 1 | tf_op jit(solution)/shard_map/pallas_call | solution.py:812
  305.5 13.2 %shard_map.485.third = bf16[1024,768]{1,0:T(8,128)(2,1)S(1)} custom-call(bf16[1024,768]{1,0:T(8,128)(2,1)S(1)} %copy-done.7, bf16[1024,768]{1,0:T(8,128)(2,1)S(1)} %copy-done.7, bf16[1024,768]{1,0:T(8,128)(2,1)S(1)} %copy-done.7, f32[32,1024]{1,0:T(8,128)S(1)} %copy-done.46, bf16[1024,768]{1,0:T(8,128)(2,1)S(1)} %copy-done.8), custom_call_target="tpu_custom_call" | custom-call | flops 1000000000 | bytes 1 | tf_op jit(solution)/shard_map/pallas_call | solution.py:812
  318.7 13.0 %shard_map.484.second = bf16[1024,768]{1,0:T(8,128)(2,1)S(1)} custom-call(bf16[1024,768]{1,0:T(8,128)(2,1)S(1)} %copy-done.5, bf16[1024,768]{1,0:T(8,128)(2,1)S(1)} %copy-done.5, bf16[1024,768]{1,0:T(8,128)(2,1)S(1)} %copy-done.5, f32[32,1024]{1,0:T(8,128)S(1)} %copy-done.44, bf16[1024,768]{1,0:T(8,128)(2,1)S(1)} %copy-done.8), custom_call_target="tpu_custom_call" | custom-call | flops 1000000000 | bytes 1 | tf_op jit(solution)/shard_map/pallas_call | solution.py:812
  332.9 17.6 %shard_map.486 = (bf16[16,104,768]{2,1,0:T(8,128)(2,1)}, bf16[16,104,768]{2,1,0:T(8,128)(2,1)}, bf16[1024,768]{1,0:T(8,128)(2,1)}) custom-call(s32[1]{0:T(128)} %bitcast.14.place.refs_12_, bf16[1024,768]{1,0:T(8,128)(2,1)} %copy-done.55, bf16[1024,768]{1,0:T(8,128)(2,1)} %copy-done.12, bf16[1024,768]{1,0:T(8,128)(2,1)} %copy-done.14, ...), custom_call_target="tpu_custom_call" | custom-call | flops 1000000000 | bytes 1 | tf_op jit(solution)/shard_map/pallas_call | solution.py:1080
  354.5 20.2 %shard_map.483 = (f32[1024,8,128]{2,1,0:T(8,128)S(1)}, f32[8,128]{1,0:T(8,128)S(1)}, f32[256,8,128]{2,1,0:T(8,128)S(1)}, f32[256,8,128]{2,1,0:T(8,128)S(1)}, f32...) custom-call(s32[4096]{0:T(1024)S(1)} %bitcast.139, s32[4096]{0:T(1024)S(1)} %rev.10.rows_b.refs_1_, ...), custom_call_target="tpu_custom_call" | custom-call | flops 1000000000 | bytes 1 | tf_op jit(solution)/shard_map/pallas_call | solution.py:730
  381.6 3.0 shard_map.489
  384.7 2.8 collective-permute-start.34
  390.9 2.9 collective-permute-start.33
  394.0 22.5 %shard_map.488 = (bf16[16,56,768]{2,1,0:T(8,128)(2,1)S(1)}, bf16[16,56,768]{2,1,0:T(8,128)(2,1)S(1)}) custom-call(s32[4096]{0:T(1024)S(1)} %bitcast.140, s32[4096]{0:T(1024)S(1)} %rev.10.rows_b.refs_1_, s32[4096]{0:T(1024)S(1)} %copy-done.40, s32[4096]{0:T(1024)S(1)} %rev.11.refs_3_, f32[256,16,128]{2,1,0:T(8,128)S(1)} %copy-done.11, ...), custom_call_target="tpu_custom_call" | custom-call | flops 1000000000 | bytes 1 | tf_op jit(solution)/shard_map/pallas_call | solution.py:730
  416.5 2.8 collective-permute-done.33
  427.7 5.4 %collective-permute-done.37 = bf16[1,192,768]{2,1,0:T(8,128)(2,1)S(1)} collective-permute-done((bf16[1,192,768]{2,1,0:T(8,128)(2,1)S(1)}, bf16[1,192,768]{2,1,0:T(8,128)(2,1)S(1)}, u32[]{:S(2)}, u32[]{:S(2)}) %collective-permute-start.37) | collective-permute-done | bytes 294944 | tf_op jit(solution)/shard_map/ppermute | solution.py:37
  441.8 8.5 %collective-permute-done.41 = bf16[4,56,768]{2,1,0:T(8,128)(2,1)S(1)} collective-permute-done((bf16[4,56,768]{2,1,0:T(8,128)(2,1)S(1)}, bf16[4,56,768]{2,1,0:T(8,128)(2,1)S(1)}, u32[]{:S(2)}, u32[]{:S(2)}) %collective-permute-start.41) | collective-permute-done | bytes 344096 | tf_op jit(solution)/shard_map/ppermute | solution.py:37
  450.3 4.3 collective-permute-done.42
  (448 shorter events, 136.2 us)
Async XLA Ops:
  7.2 111.9 %all-gather.6.cloned.1.call-start = ((), (), s32[]{:S(2)}) async-start(), calls=%async_computation.3 | async-start | bytes 3244032 | tf_op jit(solution)/shard_map/all_gather | solution.py:1175
  18.8 13.5 %collective-permute-start.8 = (bf16[1,1,1,1,96,768]{5,4,3,2,1,0:T(8,128)(2,1)S(1)}, bf16[1,1,1,1,96,768]{5,4,3,2,1,0:T(8,128)(2,1)S(1)}, u32[]{:S(2)}, u32[]{:S(2)}) collective-permute-start(bf16[1,1,1,1,96,768]{5,4,3,2,1,0:T(8,128)(2,1)S(1)} %bitcast.154), channel_id=1, source_target_pairs={{0,4},{1,5},{2,6},{3,7},{4,0},{5,1},{6,2},{7,3},{8,12},{9,13},{10,... | collective-permute-start | bytes 442376 | tf_op jit(solution)/shard_map/ppermute | solution.py:37
  42.8 149.1 %all-gather.4.cloned.1.call-start = ((), (), s32[]{:S(2)}) async-start(), calls=%async_computation.1 | async-start | bytes 7299072 | tf_op jit(solution)/shard_map/all_gather | solution.py:1176
  42.9 10.2 %collective-permute-start.16 = (bf16[1,1,1,1,96,768]{5,4,3,2,1,0:T(8,128)(2,1)S(1)}, bf16[1,1,1,1,96,768]{5,4,3,2,1,0:T(8,128)(2,1)}, u32[]{:S(2)}, u32[]{:S(2)}) collective-permute-start(bf16[1,1,1,1,96,768]{5,4,3,2,1,0:T(8,128)(2,1)S(1)} %convert_bitcast_fusion), channel_id=1, source_target_pairs={{0,4},{1,5},{2,6},{3,7},{4,0},{5,1},{6,2},{7,3},{8,12},{9,13},{10,... | collective-permute-start | bytes 442376 | tf_op jit(solution)/shard_map/ppermute | solution.py:37
  44.1 16.0 %collective-permute-start = (bf16[512,768]{1,0:T(8,128)(2,1)}, bf16[512,768]{1,0:T(8,128)(2,1)}, u32[]{:S(2)}, u32[]{:S(2)}) collective-permute-start(bf16[512,768]{1,0:T(8,128)(2,1)} %get-tuple-element.455), channel_id=1, source_target_pairs={{0,16},{1,17},{2,18},{3,19},{4,20},{5,21},{6,22},{7,23},{8,24},{9,... | collective-permute-start | bytes 2359304 | tf_op jit(solution)/shard_map/ppermute | solution.py:37
  46.4 13.6 %collective-permute-start.9 = (bf16[1,1,2,1,96,768]{5,4,3,2,1,0:T(8,128)(2,1)}, bf16[1,1,2,1,96,768]{5,4,3,2,1,0:T(8,128)(2,1)}, u32[]{:S(2)}, u32[]{:S(2)}) collective-permute-start(bf16[1,1,2,1,96,768]{5,4,3,2,1,0:T(8,128)(2,1)} %constant_dynamic-update-slice_fusion.8), channel_id=1, source_target_pairs={{0,8},{1,9},{2,10},{3,11},{4,12},{5,13},{6,14},{7,15},{8,0},{9,1},... | collective-permute-start | bytes 884744 | tf_op jit(solution)/shard_map/ppermute | solution.py:37
  55.6 325.1 %reduce-scatter.2.cloned.1.call-start = ((), (), s32[]{:S(2)}) async-start(), calls=%async_computation.2 | async-start | bytes 7299072 | tf_op jit(solution)/shard_map/reduce_scatter | solution.py:237
  61.9 21.0 %collective-permute-start.19 = (bf16[1,1,2,1,96,768]{5,4,3,2,1,0:T(8,128)(2,1)S(1)}, bf16[1,1,2,1,96,768]{5,4,3,2,1,0:T(8,128)(2,1)S(1)}, u32[]{:S(2)}, u32[]{:S(2)}) collective-permute-start(bf16[1,1,2,1,96,768]{5,4,3,2,1,0:T(8,128)(2,1)S(1)} %constant_dynamic-update-slice_fusion.22), channel_id=1, source_target_pairs={{0,8},{1,9},{2,10},{3,11},{4,12},{5,13},{6,14},{7,15},{8,0},{9,1},... | collective-permute-start | bytes 884744 | tf_op jit(solution)/shard_map/ppermute | solution.py:37
  65.5 17.4 %collective-permute-start.18 = (bf16[1,2,2,2,48,768]{5,4,3,2,1,0:T(8,128)(2,1)S(1)}, bf16[1,2,2,2,48,768]{5,4,3,2,1,0:T(8,128)(2,1)S(1)}, u32[]{:S(2)}, u32[]{:S(2)}) collective-permute-start(bf16[1,2,2,2,48,768]{5,4,3,2,1,0:T(8,128)(2,1)S(1)} %constant_dynamic-update-slice_fusion.20), channel_id=1, source_target_pairs={{0,16},{1,17},{2,18},{3,19},{4,20},{5,21},{6,22},{7,23},{8,24},{9,... | collective-permute-start | bytes 1769480 | tf_op jit(solution)/shard_map/ppermute | solution.py:37
  68.2 14.7 %collective-permute-start.17 = (bf16[1,2,2,1,96,768]{5,4,3,2,1,0:T(8,128)(2,1)S(1)}, bf16[1,2,2,1,96,768]{5,4,3,2,1,0:T(8,128)(2,1)S(1)}, u32[]{:S(2)}, u32[]{:S(2)}) collective-permute-start(bf16[1,2,2,1,96,768]{5,4,3,2,1,0:T(8,128)(2,1)S(1)} %constant_dynamic-update-slice_fusion.18), channel_id=1, source_target_pairs={{0,2},{1,3},{2,0},{3,1},{4,6},{5,7},{6,4},{7,5},{8,10},{9,11},{10,... | collective-permute-start | bytes 1769480 | tf_op jit(solution)/shard_map/ppermute | solution.py:37
  83.0 28.2 %collective-permute-start.22 = (bf16[1,2,2,1,96,768]{5,4,3,2,1,0:T(8,128)(2,1)S(1)}, bf16[1,2,2,1,96,768]{5,4,3,2,1,0:T(8,128)(2,1)S(1)}, u32[]{:S(2)}, u32[]{:S(2)}) collective-permute-start(bf16[1,2,2,1,96,768]{5,4,3,2,1,0:T(8,128)(2,1)S(1)} %constant_dynamic-update-slice_fusion.26), channel_id=1, source_target_pairs={{0,2},{1,3},{2,0},{3,1},{4,6},{5,7},{6,4},{7,5},{8,10},{9,11},{10,... | collective-permute-start | bytes 1769480 | tf_op jit(solution)/shard_map/ppermute | solution.py:37
  83.7 28.5 %collective-permute-start.21 = (bf16[1,2,2,2,96,768]{5,4,3,2,1,0:T(8,128)(2,1)S(1)}, bf16[1,2,2,2,96,768]{5,4,3,2,1,0:T(8,128)(2,1)}, u32[]{:S(2)}, u32[]{:S(2)}) collective-permute-start(bf16[1,2,2,2,96,768]{5,4,3,2,1,0:T(8,128)(2,1)S(1)} %constant_dynamic-update-slice_fusion.24), channel_id=1, source_target_pairs={{0,16},{1,17},{2,18},{3,19},{4,20},{5,21},{6,22},{7,23},{8,24},{9,... | collective-permute-start | bytes 3538952 | tf_op jit(solution)/shard_map/ppermute | solution.py:37
  114.2 29.3 %collective-permute-start.24 = (bf16[1,2,2,2,96,768]{5,4,3,2,1,0:T(8,128)(2,1)}, bf16[1,2,2,2,96,768]{5,4,3,2,1,0:T(8,128)(2,1)}, u32[]{:S(2)}, u32[]{:S(2)}) collective-permute-start(bf16[1,2,2,2,96,768]{5,4,3,2,1,0:T(8,128)(2,1)} %constant_dynamic-update-slice_fusion.28), channel_id=1, source_target_pairs={{0,16},{1,17},{2,18},{3,19},{4,20},{5,21},{6,22},{7,23},{8,24},{9,... | collective-permute-start | bytes 3538952 | tf_op jit(solution)/shard_map/ppermute | solution.py:37
  117.8 25.7 %collective-permute-start.23 = (bf16[16,96,768]{2,1,0:T(8,128)(2,1)S(1)}, bf16[16,96,768]{2,1,0:T(8,128)(2,1)}, u32[]{:S(2)}, u32[]{:S(2)}) collective-permute-start(bf16[16,96,768]{2,1,0:T(8,128)(2,1)S(1)} %bitcast.127), channel_id=1, source_target_pairs={{0,1},{1,0},{2,3},{3,2},{4,5},{5,4},{6,7},{7,6},{8,9},{9,8},{10,11... | collective-permute-start | bytes 7077896 | tf_op jit(solution)/shard_map/ppermute | solution.py:37
  146.6 30.1 %collective-permute-start.26 = (bf16[512,768]{1,0:T(8,128)(2,1)S(1)}, bf16[512,768]{1,0:T(8,128)(2,1)}, u32[]{:S(2)}, u32[]{:S(2)}) collective-permute-start(bf16[512,768]{1,0:T(8,128)(2,1)S(1)} %get-tuple-element.453), channel_id=1, source_target_pairs={{0,16},{1,17},{2,18},{3,19},{4,20},{5,21},{6,22},{7,23},{8,24},{9,... | collective-permute-start | bytes 2359304 | tf_op jit(solution)/shard_map/ppermute | solution.py:37
  231.1 53.1 %collective-permute-start.27 = (bf16[512,768]{1,0:T(8,128)(2,1)}, bf16[512,768]{1,0:T(8,128)(2,1)}, u32[]{:S(2)}, u32[]{:S(2)}) collective-permute-start(bf16[512,768]{1,0:T(8,128)(2,1)} %broadcast_select_fusion.2), channel_id=1, source_target_pairs={{0,16},{1,17},{2,18},{3,19},{4,20},{5,21},{6,22},{7,23},{8,24},{9,... | collective-permute-start | bytes 2359304 | tf_op jit(solution)/shard_map/ppermute | solution.py:37
  284.2 14.2 %collective-permute-start.28 = (bf16[16,192,768]{2,1,0:T(8,128)(2,1)}, bf16[16,192,768]{2,1,0:T(8,128)(2,1)S(1)}, u32[]{:S(2)}, u32[]{:S(2)}) collective-permute-start(bf16[16,192,768]{2,1,0:T(8,128)(2,1)} %get-tuple-element.337), channel_id=1, source_target_pairs={{0,1},{1,0},{2,3},{3,2},{4,5},{5,4},{6,7},{7,6},{8,9},{9,8},{10,11... | collective-permute-start | bytes 14155784 | tf_op jit(solution)/shard_map/ppermute | solution.py:37
  302.2 48.3 %collective-permute-start.29 = (bf16[4,192,768]{2,1,0:T(8,128)(2,1)}, bf16[4,192,768]{2,1,0:T(8,128)(2,1)}, u32[]{:S(2)}, u32[]{:S(2)}) collective-permute-start(bf16[4,192,768]{2,1,0:T(8,128)(2,1)} %get-tuple-element.362), channel_id=1, source_target_pairs={{0,16},{1,17},{2,18},{3,19},{4,20},{5,21},{6,22},{7,23},{8,24},{9,... | collective-permute-start | bytes 3538952 | tf_op jit(solution)/shard_map/ppermute | solution.py:37
  304.0 46.5 %collective-permute-start.30 = (bf16[4,192,768]{2,1,0:T(8,128)(2,1)S(1)}, bf16[4,192,768]{2,1,0:T(8,128)(2,1)}, u32[]{:S(2)}, u32[]{:S(2)}) collective-permute-start(bf16[4,192,768]{2,1,0:T(8,128)(2,1)S(1)} %get-tuple-element.363), channel_id=1, source_target_pairs={{0,2},{1,3},{2,0},{3,1},{4,6},{5,7},{6,4},{7,5},{8,10},{9,11},{10,... | collective-permute-start | bytes 3538952 | tf_op jit(solution)/shard_map/ppermute | solution.py:37
  350.5 31.1 %collective-permute-start.32 = (bf16[16,104,768]{2,1,0:T(8,128)(2,1)}, bf16[16,104,768]{2,1,0:T(8,128)(2,1)}, u32[]{:S(2)}, u32[]{:S(2)}) collective-permute-start(bf16[16,104,768]{2,1,0:T(8,128)(2,1)} %get-tuple-element.369), channel_id=1, source_target_pairs={{0,1},{1,0},{2,3},{3,2},{4,5},{5,4},{6,7},{7,6},{8,9},{9,8},{10,11... | collective-permute-start | bytes 7667720 | tf_op jit(solution)/shard_map/ppermute | solution.py:37
  350.6 31.0 %collective-permute-start.31 = (bf16[4,192,768]{2,1,0:T(8,128)(2,1)}, bf16[4,192,768]{2,1,0:T(8,128)(2,1)}, u32[]{:S(2)}, u32[]{:S(2)}) collective-permute-start(bf16[4,192,768]{2,1,0:T(8,128)(2,1)} %get-tuple-element.367), channel_id=1, source_target_pairs={{0,18},{1,19},{2,16},{3,17},{4,22},{5,23},{6,20},{7,21},{8,26},{9,... | collective-permute-start | bytes 3538952 | tf_op jit(solution)/shard_map/ppermute | solution.py:37
  384.7 34.6 %collective-permute-start.34 = (bf16[4,104,768]{2,1,0:T(8,128)(2,1)S(1)}, bf16[4,104,768]{2,1,0:T(8,128)(2,1)S(1)}, u32[]{:S(2)}, u32[]{:S(2)}) collective-permute-start(bf16[4,104,768]{2,1,0:T(8,128)(2,1)S(1)} %get-tuple-element.386), channel_id=1, source_target_pairs={{0,18},{1,19},{2,16},{3,17},{4,22},{5,23},{6,20},{7,21},{8,26},{9,... | collective-permute-start | bytes 1916936 | tf_op jit(solution)/shard_map/ppermute | solution.py:37
  387.4 31.9 %collective-permute-start.35 = (bf16[4,104,768]{2,1,0:T(8,128)(2,1)S(1)}, bf16[4,104,768]{2,1,0:T(8,128)(2,1)S(1)}, u32[]{:S(2)}, u32[]{:S(2)}) collective-permute-start(bf16[4,104,768]{2,1,0:T(8,128)(2,1)S(1)} %get-tuple-element.387), channel_id=1, source_target_pairs={{0,16},{1,17},{2,18},{3,19},{4,20},{5,21},{6,22},{7,23},{8,24},{9,... | collective-permute-start | bytes 1916936 | tf_op jit(solution)/shard_map/ppermute | solution.py:37
  387.6 31.7 %collective-permute-start.36 = (bf16[4,104,768]{2,1,0:T(8,128)(2,1)S(1)}, bf16[4,104,768]{2,1,0:T(8,128)(2,1)S(1)}, u32[]{:S(2)}, u32[]{:S(2)}) collective-permute-start(bf16[4,104,768]{2,1,0:T(8,128)(2,1)S(1)} %get-tuple-element.388), channel_id=1, source_target_pairs={{0,2},{1,3},{2,0},{3,1},{4,6},{5,7},{6,4},{7,5},{8,10},{9,11},{10,... | collective-permute-start | bytes 1916936 | tf_op jit(solution)/shard_map/ppermute | solution.py:37
  390.9 28.4 %collective-permute-start.33 = (bf16[2,192,768]{2,1,0:T(8,128)(2,1)S(1)}, bf16[2,192,768]{2,1,0:T(8,128)(2,1)S(1)}, u32[]{:S(2)}, u32[]{:S(2)}) collective-permute-start(bf16[2,192,768]{2,1,0:T(8,128)(2,1)S(1)} %slice.275), channel_id=1, source_target_pairs={{0,8},{1,9},{2,10},{3,11},{4,12},{5,13},{6,14},{7,15},{8,0},{9,1},... | collective-permute-start | bytes 1769480 | tf_op jit(solution)/shard_map/ppermute | solution.py:37
  419.6 13.5 %collective-permute-start.37 = (bf16[1,192,768]{2,1,0:T(8,128)(2,1)S(1)}, bf16[1,192,768]{2,1,0:T(8,128)(2,1)S(1)}, u32[]{:S(2)}, u32[]{:S(2)}) collective-permute-start(bf16[1,192,768]{2,1,0:T(8,128)(2,1)S(1)} %slice.277), channel_id=1, source_target_pairs={{0,4},{1,5},{2,6},{3,7},{4,0},{5,1},{6,2},{7,3},{8,12},{9,13},{10,... | collective-permute-start | bytes 884744 | tf_op jit(solution)/shard_map/ppermute | solution.py:37
  421.2 20.5 %collective-permute-start.39 = (bf16[512,768]{1,0:T(8,128)(2,1)S(1)}, bf16[512,768]{1,0:T(8,128)(2,1)S(1)}, u32[]{:S(2)}, u32[]{:S(2)}) collective-permute-start(bf16[512,768]{1,0:T(8,128)(2,1)S(1)} %broadcast_select_fusion), channel_id=1, source_target_pairs={{0,16},{1,17},{2,18},{3,19},{4,20},{5,21},{6,22},{7,23},{8,24},{9,... | collective-permute-start | bytes 2359304 | tf_op jit(solution)/shard_map/ppermute | solution.py:37
  423.2 16.0 %collective-permute-start.38 = (bf16[2,104,768]{2,1,0:T(8,128)(2,1)S(1)}, bf16[2,104,768]{2,1,0:T(8,128)(2,1)S(1)}, u32[]{:S(2)}, u32[]{:S(2)}) collective-permute-start(bf16[2,104,768]{2,1,0:T(8,128)(2,1)S(1)} %slice.276), channel_id=1, source_target_pairs={{0,8},{1,9},{2,10},{3,11},{4,12},{5,13},{6,14},{7,15},{8,0},{9,1},... | collective-permute-start | bytes 958472 | tf_op jit(solution)/shard_map/ppermute | solution.py:37
  424.7 25.6 %collective-permute-start.41 = (bf16[4,56,768]{2,1,0:T(8,128)(2,1)S(1)}, bf16[4,56,768]{2,1,0:T(8,128)(2,1)S(1)}, u32[]{:S(2)}, u32[]{:S(2)}) collective-permute-start(bf16[4,56,768]{2,1,0:T(8,128)(2,1)S(1)} %get-tuple-element.401), channel_id=1, source_target_pairs={{0,18},{1,19},{2,16},{3,17},{4,22},{5,23},{6,20},{7,21},{8,26},{9,... | collective-permute-start | bytes 1032200 | tf_op jit(solution)/shard_map/ppermute | solution.py:37
  426.2 28.3 %collective-permute-start.42 = (bf16[4,56,768]{2,1,0:T(8,128)(2,1)S(1)}, bf16[4,56,768]{2,1,0:T(8,128)(2,1)S(1)}, u32[]{:S(2)}, u32[]{:S(2)}) collective-permute-start(bf16[4,56,768]{2,1,0:T(8,128)(2,1)S(1)} %get-tuple-element.402), channel_id=1, source_target_pairs={{0,16},{1,17},{2,18},{3,19},{4,20},{5,21},{6,22},{7,23},{8,24},{9,... | collective-permute-start | bytes 1032200 | tf_op jit(solution)/shard_map/ppermute | solution.py:37
  433.1 21.5 %collective-permute-start.43 = (bf16[4,56,768]{2,1,0:T(8,128)(2,1)S(1)}, bf16[4,56,768]{2,1,0:T(8,128)(2,1)S(1)}, u32[]{:S(2)}, u32[]{:S(2)}) collective-permute-start(bf16[4,56,768]{2,1,0:T(8,128)(2,1)S(1)} %get-tuple-element.403), channel_id=1, source_target_pairs={{0,2},{1,3},{2,0},{3,1},{4,6},{5,7},{6,4},{7,5},{8,10},{9,11},{10,... | collective-permute-start | bytes 1032200 | tf_op jit(solution)/shard_map/ppermute | solution.py:37
  456.8 11.3 %collective-permute-start.44 = (bf16[1,104,768]{2,1,0:T(8,128)(2,1)S(1)}, bf16[1,104,768]{2,1,0:T(8,128)(2,1)S(1)}, u32[]{:S(2)}, u32[]{:S(2)}) collective-permute-start(bf16[1,104,768]{2,1,0:T(8,128)(2,1)S(1)} %slice.278), channel_id=1, source_target_pairs={{0,4},{1,5},{2,6},{3,7},{4,0},{5,1},{6,2},{7,3},{8,12},{9,13},{10,... | collective-permute-start | bytes 479240 | tf_op jit(solution)/shard_map/ppermute | solution.py:37
  (132 other events, 936.8 us)
Sparse Core Ops, SparseCore 0:
  42.9 70.6 all-gather.5
  117.0 74.7 all-gather.3
  228.9 124.9 reduce-scatter.1
